TPU v7x, 32 devices: a whole 2x2x4 slice. The times are simulated.
32 devices in a mesh: group: 2 (over y), dom: 4 (over x, core), img: 4 (over z).
Axes of the slice: x: 2, y: 2, z: 4, core: 2. Of those that a mesh axis runs over, the one named last changes fastest.
Arguments:
- disp: float32 [8, 3, 2048], P(('group', 'img'), None, 'dom'), parts along dimension 0, may hold values from -0.3 to 0.3
- veloc: float32 [8, 3, 2048], P(('group', 'img'), None, 'dom'), parts along dimension 0, may hold values from -1.5 to 1.5
- time_step: float32 [8], P(('group', 'img')), parts along dimension 0, may hold values from 0.05 to 0.4
- reset_flags: int32 [2, 8], P(None, ('group', 'img')), parts along dimension 1, may hold values 0 or 1
- climb: int32 [2], P('group'), parts along dimension 0, may hold values from 1 to 2
- species: int32 [4096], P(('group', 'dom')), parts along dimension 0, may hold values 0 or 1
- neighbours: int32 [8, 4096], P(None, ('group', 'dom')), parts along dimension 1, may hold values from 0 to 767, as said below
- counts: int32 [4096], P(('group', 'dom')), parts along dimension 0, may hold values from 4 to 8, as said below
- lattice: float32 [8, 3, 4096], P(None, None, ('group', 'dom')), parts along dimension 2, may hold values from -1.8 to 1.8, as said below
- embed: float32 [2, 64], replicated, may hold values from -6 to 6
- radial_weight: float32 [2, 8, 64], replicated, may hold values from -2 to 2
- mix_weight: float32 [2, 64, 64], replicated, may hold values from -0.75 to 0.75
- update_weight: float32 [2, 64, 64], replicated, may hold values from -0.75 to 0.75
- readout: float32 [64], replicated, may hold values from -0.75 to 0.75
Outputs:
- new_disp: float32 [8, 3, 2048], P(('group', 'img'), None, 'dom'), parts along dimension 0
- new_veloc: float32 [8, 3, 2048], P(('group', 'img'), None, 'dom'), parts along dimension 0
- band_forces: float32 [2, 2, 8], P(None, None, ('group', 'img')), parts along dimension 2
- path_coordinate: float32 [8], P(('group', 'img')), parts along dimension 0
There are 2 independent parts, one for each index of `group`. A program takes and returns all parts, laid end to end along the dimension named above; an argument that names none is the same for every part. Nothing has to cross between parts.
Inputs may be any that keep to these rules, and one draw needn't show every extreme that they name: `lattice`: each component has magnitude between 1.3 and 1.8. neighbours[k, a] - 128 - (a mod 512) lies between -128 and 128 and is never 0. `counts`: some atom has all 8 slots live.
All inputs are finite; a program needn't handle non-finite values. No bound on the sum of `reset_flags` or of `species` on one device may be relied on, other than what follows from the above.
Results may differ from a plain program's by a relative error of at most 0.0003.
Values sent between devices are 32-bit elements; how exact they have to be, the bound alone decides.
No kernel may reach another device: no remote copies, remote signals or barrier semaphores. Data moves between devices by JAX's collectives and lax.ppermute only.
A program may use at most 64 MiB of HBM per device.

v0:
```python
import jax
import jax.numpy as jnp
from jax import lax
from jax.sharding import PartitionSpec as P

PRECISE = lax.Precision.HIGHEST
SPRING_CONSTANT = 0.5
ALPHA_START = 0.1
STEP_LIMIT = 0.3
TINY_VALUE = 1e-06
SOFTENING = 0.25


def padded_2(block, sides, width, periodic):
    for axis, dim in sides:
        count = lax.axis_size(axis)
        forward = [(i, i + 1) for i in range(count - 1)]
        if periodic:
            forward.append((count - 1, 0))
        backward = [(target, source) for source, target in forward]
        low = lax.ppermute(
            lax.slice_in_dim(block, block.shape[dim] - width, None, axis=dim), axis, forward
        )
        high = lax.ppermute(lax.slice_in_dim(block, 0, width, axis=dim), axis, backward)
        block = jnp.concatenate([low, block, high], axis=dim)
    return block


def shifted(array, axis, by):
    devices = lax.axis_size(axis)
    pairs = [(i, i + by) for i in range(devices) if 0 <= i + by < devices]
    return lax.ppermute(array, axis, pairs)


def carried_in(array, axis, combine, identity):
    devices, here = (lax.axis_size(axis), lax.axis_index(axis))
    everything = lax.all_gather(array, axis)
    start = jnp.broadcast_to(jnp.asarray(identity, array.dtype), array.shape)

    def lap(k, before):
        reached = k < here
        new = combine(before, everything[k])
        return jnp.where(reached, new, before)

    return lax.fori_loop(0, devices, lap, start)


def radial_basis(distance, number):
    centres = 2.0 + 0.5 * jnp.arange(number, dtype=jnp.float32)
    centres = centres.reshape((number,) + (1,) * distance.ndim)
    envelope = 0.5 * (1.0 + jnp.cos(jnp.pi * distance / 6.0))
    return jnp.exp(-(((distance[None] - centres) / 0.5) ** 2)) * envelope[None]


def messages(displace, features, centre_disp, lattice, index, live, radial_w):
    slots = index.shape[0]
    number = radial_w.shape[0]
    others = jnp.moveaxis(jnp.take(displace, index, axis=1), 0, 1)
    vectors = lattice + others - centre_disp[None]
    distance = jnp.sqrt(jnp.sum(vectors * vectors, axis=1) + SOFTENING)
    radial = jnp.einsum("nc,nka->cka", radial_w, radial_basis(distance, number), precision=PRECISE)
    gathered = jnp.take(features, index, axis=1)
    return jnp.sum(radial * gathered * live[None], axis=1) / slots**0.5


def layer(displace, hidden, features, centre, lattice, index, live, radial_w, update_w):
    count = index.shape[1]
    centre_disp = lax.slice_in_dim(displace, centre, centre + count, axis=1)
    message = messages(displace, features, centre_disp, lattice, index, live, radial_w)
    own_hidden = lax.slice_in_dim(hidden, centre, centre + count, axis=1)
    return own_hidden + jnp.einsum("cd,ca->da", update_w, jax.nn.silu(message), precision=PRECISE)


def ghost_ends(values, width):
    return jnp.concatenate([values[..., :width], values[..., -width:]], axis=-1)


def add_returned(values, returned, width):
    owned = values[..., width:-width]
    middle = jnp.zeros(owned.shape[:-1] + (owned.shape[-1] - 2 * width,), jnp.float32)
    padded = jnp.concatenate([returned[..., :width], middle, returned[..., -width:]], axis=-1)
    return owned + padded


def add_values(earlier, later):
    return earlier + later


def local(
    disp,
    veloc,
    time_step,
    reset_flags,
    climb,
    species,
    neighbours,
    counts,
    lattice,
    embed,
    radial_weight,
    mix_weight,
    update_weight,
    readout,
):
    images = disp.shape[0]
    atoms = disp.shape[2]
    slots = neighbours.shape[0]
    ghosts = atoms // 4
    live = (jnp.arange(slots)[:, None] < counts[None, :]).astype(jnp.float32)
    kinds = padded_2(species, (("dom", 0),), ghosts, True)
    base = embed[0][:, None] + (embed[1] - embed[0])[:, None] * kinds.astype(jnp.float32)[None, :]
    base_features = jnp.einsum("cd,ca->da", mix_weight[0], base, precision=PRECISE)

    def first_single(region):
        return layer(
            region,
            base,
            base_features,
            ghosts,
            lattice,
            neighbours,
            live,
            radial_weight[0],
            update_weight[0],
        )

    def second_energy(region, hidden_wide):
        features_two = jnp.einsum("cd,ca->da", mix_weight[1], hidden_wide, precision=PRECISE)
        hidden_two = layer(
            region,
            hidden_wide,
            features_two,
            ghosts,
            lattice,
            neighbours,
            live,
            radial_weight[1],
            update_weight[1],
        )
        return jnp.sum(jnp.dot(readout, hidden_two, precision=PRECISE))

    second_grads = jax.vmap(jax.grad(second_energy, argnums=(0, 1)))
    image_ids = lax.axis_index("img") * images + jnp.arange(images)
    total_images = images * lax.axis_size("img")
    inside = (image_ids >= 1) & (image_ids <= total_images - 2)
    climbing = image_ids == climb[0]
    position = disp
    speed = veloc
    step_size = time_step
    alpha = jnp.full((images,), ALPHA_START, jnp.float32)
    records = []
    for repeat in range(reset_flags.shape[0]):
        forces_region = padded_2(position, (("dom", 2),), ghosts, True)
        hidden_one, pullback = jax.vjp(jax.vmap(first_single), forces_region)
        forces_hidden_wide = padded_2(hidden_one, (("dom", 2),), ghosts, True)
        region_grad, hidden_grad = second_grads(forces_region, forces_hidden_wide)
        returned = padded_2(ghost_ends(hidden_grad, ghosts), (("dom", 2),), ghosts, True)
        (further,) = pullback(add_returned(hidden_grad, returned, ghosts))
        combined = region_grad + further
        returned_two = padded_2(ghost_ends(combined, ghosts), (("dom", 2),), ghosts, True)
        force = -add_returned(combined, returned_two, ghosts)
        widened = padded_2(position, (("img", 0),), 1, False)
        before = widened[:-2]
        after = widened[2:]
        plus = after - position
        minus = position - before
        tangent = after - before
        plus_sq, minus_sq, tangent_sq = lax.psum(
            (
                jnp.sum(plus * plus, axis=(1, 2)),
                jnp.sum(minus * minus, axis=(1, 2)),
                jnp.sum(tangent * tangent, axis=(1, 2)),
            ),
            "dom",
        )
        unit = tangent / jnp.sqrt(tangent_sq + TINY_VALUE)[:, None, None]
        along = lax.psum(jnp.sum(force * unit, axis=(1, 2)), "dom")
        spring = SPRING_CONSTANT * (jnp.sqrt(plus_sq) - jnp.sqrt(minus_sq))
        factor = jnp.where(climbing, -2.0 * along, spring - along)
        band = jnp.where(inside[:, None, None], force + factor[:, None, None] * unit, 0.0)
        speed_sq, band_sq = lax.psum(
            (jnp.sum(speed * speed, axis=(1, 2)), jnp.sum(band * band, axis=(1, 2))), "dom"
        )
        flagged = reset_flags[repeat] == 1
        new_size = jnp.where(flagged, 0.5 * step_size, jnp.minimum(1.1 * step_size, STEP_LIMIT))
        mixed = (1.0 - alpha)[:, None, None] * speed + (
            alpha * jnp.sqrt(speed_sq / (band_sq + TINY_VALUE))
        )[:, None, None] * band
        mixed = jnp.where(flagged[:, None, None], 0.0, mixed)
        alpha = jnp.where(flagged, ALPHA_START, 0.99 * alpha)
        speed = jnp.where(inside[:, None, None], mixed + new_size[:, None, None] * band, 0.0)
        position = position + new_size[:, None, None] * speed
        step_size = new_size
        records.append(jnp.stack([jnp.where(inside, along, 0.0), jnp.where(inside, spring, 0.0)]))
    previous = shifted(position[-1], "img", 1)
    earlier = jnp.concatenate([previous[None], position[:-1]], axis=0)
    spacing = lax.psum(jnp.sum((position - earlier) ** 2, axis=(1, 2)), "dom")
    total_atoms = atoms * lax.axis_size("dom")
    segment = jnp.sqrt(spacing / (3.0 * total_atoms))
    local_path = jnp.cumsum(segment)
    local_total = local_path[-1]
    preceding = carried_in(local_total, "img", add_values, jnp.zeros((), jnp.float32))
    return (position, speed, jnp.stack(records), preceding + local_path)


def solution(mesh):
    in_specs = (
        P(("group", "img"), None, "dom"),
        P(("group", "img"), None, "dom"),
        P(("group", "img")),
        P(None, ("group", "img")),
        P("group"),
        P(("group", "dom")),
        P(None, ("group", "dom")),
        P(("group", "dom")),
        P(None, None, ("group", "dom")),
        P(),
        P(),
        P(),
        P(),
        P(),
    )
    out_specs = (
        P(("group", "img"), None, "dom"),
        P(("group", "img"), None, "dom"),
        P(None, None, ("group", "img")),
        P(("group", "img")),
    )
    return jax.shard_map(local, mesh=mesh, in_specs=in_specs, out_specs=out_specs, check_vma=False)
```

profile of v0, /device:TPU:0, one launch (start us, length us, event | category | flops | bytes accessed | tf_op | source)
XLA Modules:
  0.0 377.9 jit_solution(11129502087165018547)
XLA Ops:
  0.6 1.3 collective-permute-start.10
  1.9 6.2 %collective-permute-start.11 = (f32[1,3,512]{2,0,1:T(1,128)}, f32[1,3,512]{2,0,1:T(1,128)}, u32[]{:S(2)}, u32[]{:S(2)}) collective-permute-start(f32[1,3,512]{2,0,1:T(1,128)} %param.22), channel_id=1, source_target_pairs={{0,1},{1,2},{2,3},{4,5},{5,6},{6,7},{8,9},{9,10},{10,11},{12,13},{... | collective-permute-start | bytes 18440 | tf_op jit(solution)/shard_map/ppermute | solution.py:21
  9.6 2.0 collective-permute-start.2
  13.8 1.3 fusion.190
  15.7 1.3 copy.270
  20.0 10.8 %gather_fusion.1 = f32[4096,64]{1,0:T(8,128)S(1)} fusion(f32[64,768]{0,1:T(8,128)S(1)} %copy.216, s32[4096]{0:T(1024)S(1)} %broadcast_clamp_fusion), kind=kCustom, calls=%fused_computation.1.clone | custom fusion | bytes 2113536 | tf_op jit(solution)/shard_map/jvp(vmap(jit(_take)))/gather | solution.py:62
  31.7 12.7 %gather_fusion = f32[4096,3]{1,0:T(8,128)S(1)} fusion(f32[3,768]{0,1:T(8,128)S(1)} %bitcast.427, s32[4096]{0:T(1024)} %copy-done.6), kind=kCustom, calls=%fused_computation.clone | custom fusion | bytes 114688 | tf_op jit(solution)/shard_map/vmap(jvp(jit(_take)))/gather | solution.py:58
  45.2 1.3 multiply_reduce_fusion.1
  49.8 1.5 collective-permute-start.5
  53.4 12.7 %gather_fusion.2 = f32[4096,64]{1,0:T(8,128)S(1)} fusion(f32[64,768]{0,1:T(8,128)S(1)} %copy.219, s32[4096]{0:T(1024)} %copy-done.6), kind=kCustom, calls=%fused_computation.2.clone | custom fusion | bytes 2113536 | tf_op jit(solution)/shard_map/vmap(jvp(jit(_take)))/gather | solution.py:62
  66.2 1.6 copy.221
  67.8 2.4 fusion.15
  71.5 2.0 copy.250
  73.5 22.8 %scatter_custom_fusion.1 = f32[64,768]{0,1:T(8,128)S(1)} fusion(s32[4096]{0:T(1024)} %bitcast.430, f32[4096,64]{1,0:T(8,128)} %bitcast.425, f32[]{:T(128)} %copy.286), kind=kCustom, calls=%fused_computation.98 | custom fusion | flops 262144 | bytes 197120 | tf_op jit(solution)/shard_map/vmap(transpose(jvp(jit(_take))))/scatter-add | solution.py:62
  97.1 2.1 collective-permute-start.6
  106.0 22.8 %scatter_fusion.1 = f32[3,768]{0,1:T(8,128)S(1)} fusion(f32[3,768]{0,1:T(8,128)S(1)} %pad_bitcast_fusion.2, s32[4096]{0:T(1024)} %bitcast.431, f32[4096,3]{1,0:T(8,128)S(1)} %bitcast.421), kind=kCustom, calls=%fused_computation.7 | custom fusion | flops 12288 | bytes 163840 | tf_op jit(solution)/shard_map/transpose(jvp(vmap(jit(_take))))/scatter-add | solution.py:58
  129.6 1.4 copy.249
  131.3 22.7 %scatter_fusion = f32[3,768]{0,1:T(8,128)S(1)} fusion(f32[3,768]{0,1:T(8,128)S(1)} %pad_bitcast_fusion.3, s32[4096]{0:T(1024)} %bitcast.432, f32[4096,3]{1,0:T(8,128)S(1)} %bitcast.420), kind=kCustom, calls=%fused_computation.5 | custom fusion | flops 12288 | bytes 163840 | tf_op jit(solution)/shard_map/vmap(transpose(jvp(jit(_take))))/scatter-add | solution.py:58
  156.6 1.4 multiply_reduce_fusion.14
  158.0 6.4 %psum.92 = f32[1]{0:T(128)} all-reduce(f32[1]{0:T(128)} %bitcast.70), channel_id=1, replica_groups=mesh['group'=2,'dom'=4,'img'=4] {'dom'}, use_global_device_ids=true, to_apply=%region_15.19 | all-reduce | flops 1 | bytes 8 | tf_op jit(solution)/shard_map/psum | solution.py:168
  165.1 1.3 multiply_reduce_fusion.16
  166.4 7.3 %all-reduce.9 = (f32[1]{0:T(128)}, f32[1]{0:T(128)}, f32[1]{0:T(128)}) all-reduce(f32[1]{0:T(128)} %bitcast.72, f32[1]{0:T(128)} %bitcast.73, f32[1]{0:T(128)} %bitcast.74), channel_id=1, replica_groups=mesh['group'=2,'dom'=4,'img'=4] {'dom'}, use_global_device_ids=true, to_apply=%region_17.21 | all-reduce | flops 3 | bytes 24 | tf_op jit(solution)/shard_map/psum | solution.py:177
  176.8 6.4 %all-reduce.8 = (f32[1]{0:T(128)}, f32[1]{0:T(128)}) all-reduce(f32[1]{0:T(128)} %bitcast.6, f32[1]{0:T(128)} %bitcast.76), channel_id=1, replica_groups=mesh['group'=2,'dom'=4,'img'=4] {'dom'}, use_global_device_ids=true, to_apply=%region_1.2 | all-reduce | flops 2 | bytes 16 | tf_op jit(solution)/shard_map/psum | solution.py:181
  184.6 1.3 multiply_reduce_fusion.12
  185.9 1.3 multiply_add_fusion.3
  187.9 1.7 collective-permute-start.13
  189.6 1.3 copy.269
  191.8 12.7 %gather_fusion.3 = f32[4096,3]{1,0:T(8,128)S(1)} fusion(f32[3,768]{0,1:T(8,128)S(1)} %bitcast.428, s32[4096]{0:T(1024)} %copy-done.6), kind=kCustom, calls=%fused_computation.3.clone | custom fusion | bytes 114688 | tf_op jit(solution)/shard_map/vmap(jvp(jit(_take)))/gather | solution.py:58
  205.4 1.3 multiply_reduce_fusion
  213.9 5.1 %collective-permute-start.21 = (f32[1,3,512]{2,0,1:T(1,128)}, f32[1,3,512]{2,0,1:T(1,128)}, u32[]{:S(2)}, u32[]{:S(2)}) collective-permute-start(f32[1,3,512]{2,0,1:T(1,128)} %multiply_add_fusion.3), channel_id=1, source_target_pairs={{0,1},{1,2},{2,3},{4,5},{5,6},{6,7},{8,9},{9,10},{10,11},{12,13},{... | collective-permute-start | bytes 18440 | tf_op jit(solution)/shard_map/ppermute | solution.py:21
  220.2 12.7 %gather_fusion.4 = f32[4096,64]{1,0:T(8,128)S(1)} fusion(f32[64,768]{0,1:T(8,128)S(1)} %copy.233, s32[4096]{0:T(1024)} %copy-done.6), kind=kCustom, calls=%fused_computation.4.clone | custom fusion | bytes 2113536 | tf_op jit(solution)/shard_map/vmap(jvp(jit(_take)))/gather | solution.py:62
  233.0 1.6 copy.235
  234.6 2.5 fusion.13
  237.4 2.0 copy.256
  239.4 23.1 %scatter_custom_fusion.4 = f32[64,768]{0,1:T(8,128)S(1)} fusion(s32[4096]{0:T(1024)S(1)} %bitcast.433, f32[4096,64]{1,0:T(8,128)} %bitcast.426, f32[]{:T(128)} %copy.286), kind=kCustom, calls=%fused_computation.96 | custom fusion | flops 262144 | bytes 197120 | tf_op jit(solution)/shard_map/vmap(transpose(jvp(jit(_take))))/scatter-add | solution.py:62
  263.1 1.7 collective-permute-start.17
  270.3 22.5 %scatter_fusion.3 = f32[3,768]{0,1:T(8,128)S(1)} fusion(f32[3,768]{0,1:T(8,128)S(1)} %pad_bitcast_fusion, s32[4096]{0:T(1024)S(1)} %bitcast.434, f32[4096,3]{1,0:T(8,128)S(1)} %bitcast.422), kind=kCustom, calls=%fused_computation.10 | custom fusion | flops 12288 | bytes 163840 | tf_op jit(solution)/shard_map/transpose(jvp(vmap(jit(_take))))/scatter-add | solution.py:58
  293.9 22.5 %scatter_fusion.2 = f32[3,768]{0,1:T(8,128)S(1)} fusion(f32[3,768]{0,1:T(8,128)S(1)} %pad_bitcast_fusion.1, s32[4096]{0:T(1024)S(1)} %bitcast.435, f32[4096,3]{1,0:T(8,128)S(1)} %bitcast.419), kind=kCustom, calls=%fused_computation.8 | custom fusion | flops 12288 | bytes 163840 | tf_op jit(solution)/shard_map/vmap(transpose(jvp(jit(_take))))/scatter-add | solution.py:58
  318.5 1.4 multiply_reduce_fusion.8
  319.9 6.7 %psum.98 = f32[1]{0:T(128)} all-reduce(f32[1]{0:T(128)} %bitcast.131), channel_id=1, replica_groups=mesh['group'=2,'dom'=4,'img'=4] {'dom'}, use_global_device_ids=true, to_apply=%region_39.43 | all-reduce | flops 1 | bytes 8 | tf_op jit(solution)/shard_map/psum | solution.py:168
  328.0 6.3 %all-reduce.7 = (f32[1]{0:T(128)}, f32[1]{0:T(128)}, f32[1]{0:T(128)}) all-reduce(f32[1]{0:T(128)} %bitcast.133, f32[1]{0:T(128)} %bitcast.134, f32[1]{0:T(128)} %bitcast.135), channel_id=1, replica_groups=mesh['group'=2,'dom'=4,'img'=4] {'dom'}, use_global_device_ids=true, to_apply=%region_41.45 | all-reduce | flops 3 | bytes 24 | tf_op jit(solution)/shard_map/psum | solution.py:177
  338.2 6.4 %all-reduce.6 = (f32[1]{0:T(128)}, f32[1]{0:T(128)}) all-reduce(f32[1]{0:T(128)} %bitcast.82, f32[1]{0:T(128)} %bitcast.137), channel_id=1, replica_groups=mesh['group'=2,'dom'=4,'img'=4] {'dom'}, use_global_device_ids=true, to_apply=%region_25.29 | all-reduce | flops 2 | bytes 16 | tf_op jit(solution)/shard_map/psum | solution.py:181
  346.0 1.3 multiply_add_fusion.2
  347.3 2.6 collective-permute-start.22
  351.9 6.3 %psum.103 = f32[1]{0:T(128)} all-reduce(f32[1]{0:T(128)} %bitcast.145), channel_id=1, replica_groups=mesh['group'=2,'dom'=4,'img'=4] {'dom'}, use_global_device_ids=true, to_apply=%region_49.53 | all-reduce | flops 1 | bytes 8 | tf_op jit(solution)/shard_map/psum | solution.py:197
  358.1 1.3 fusion.228
  360.0 12.1 %all-reduce.5 = f32[4]{0:T(128)S(1)} all-reduce(f32[4]{0:T(128)S(1)} %fusion.228), channel_id=1, replica_groups=mesh['group'=2,'dom'=4,'img'=4] {'img'}, use_global_device_ids=true, to_apply=%add.5 | all-reduce | flops 4 | bytes 32
  372.1 4.6 %while.13 = (s32[]{:T(128)}, f32[]{:T(128)}, s32[]{:T(128)}, f32[4]{0:T(128)S(1)}, s32[]{:T(128)}) while((s32[]{:T(128)}, f32[]{:T(128)}, s32[]{:T(128)}, f32[4]{0:T(128)S(1)}, s32[]{:T(128)}) %tuple.106), condition=%wide.region_51.55_spmd, body=%wide.region_50.54_spmd.sunk | while | flops 5 | bytes 107 | solution.py:45
  (255 shorter events, 50.0 us)
Async XLA Ops:
  0.6 156.0 %collective-permute-start.10 = (f32[1,3,512]{2,0,1:T(1,128)}, f32[1,3,512]{2,0,1:T(1,128)}, u32[]{:S(2)}, u32[]{:S(2)}) collective-permute-start(f32[1,3,512]{2,0,1:T(1,128)} %param.22), channel_id=1, source_target_pairs={{1,0},{2,1},{3,2},{5,4},{6,5},{7,6},{9,8},{10,9},{11,10},{13,12},{... | collective-permute-start | bytes 18440 | tf_op jit(solution)/shard_map/ppermute | solution.py:24
  1.9 154.7 %collective-permute-start.11 = (f32[1,3,512]{2,0,1:T(1,128)}, f32[1,3,512]{2,0,1:T(1,128)}, u32[]{:S(2)}, u32[]{:S(2)}) collective-permute-start(f32[1,3,512]{2,0,1:T(1,128)} %param.22), channel_id=1, source_target_pairs={{0,1},{1,2},{2,3},{4,5},{5,6},{6,7},{8,9},{9,10},{10,11},{12,13},{... | collective-permute-start | bytes 18440 | tf_op jit(solution)/shard_map/ppermute | solution.py:21
  8.8 22.6 %collective-permute-start = (f32[1,3,128]{2,0,1:T(1,128)S(1)}, f32[1,3,128]{2,0,1:T(1,128)S(1)}, u32[]{:S(2)}, u32[]{:S(2)}) collective-permute-start(f32[1,3,128]{2,0,1:T(1,128)S(1)} %get-tuple-element.207), channel_id=1, source_target_pairs={{0,4},{4,8},{8,12},{12,0},{1,5},{5,9},{9,13},{13,1},{2,6},{6,10},{... | collective-permute-start | bytes 4616 | tf_op jit(solution)/shard_map/ppermute | solution.py:21
  9.6 7.4 %collective-permute-start.2 = (s32[128]{0:T(128)S(1)}, s32[128]{0:T(128)S(1)}, u32[]{:S(2)}, u32[]{:S(2)}) collective-permute-start(s32[128]{0:T(128)S(1)} %get-tuple-element.209), channel_id=1, source_target_pairs={{0,4},{4,8},{8,12},{12,0},{1,5},{5,9},{9,13},{13,1},{2,6},{6,10},{... | collective-permute-start | bytes 1544 | tf_op jit(solution)/shard_map/ppermute | solution.py:21
  11.6 5.6 %collective-permute-start.3 = (s32[128]{0:T(128)S(1)}, s32[128]{0:T(128)S(1)}, u32[]{:S(2)}, u32[]{:S(2)}) collective-permute-start(s32[128]{0:T(128)S(1)} %get-tuple-element.210), channel_id=1, source_target_pairs={{4,0},{8,4},{12,8},{0,12},{5,1},{9,5},{13,9},{1,13},{6,2},{10,6},{... | collective-permute-start | bytes 1544 | tf_op jit(solution)/shard_map/ppermute | solution.py:24
  13.8 5.3 %copy-start.4 = (s32[1,4,8,128]{3,1,2,0:T(4,128)}, s32[1,4,8,128]{3,1,2,0:T(4,128)S(1)}, u32[]{:S(2)}) copy-start(s32[1,4,8,128]{3,1,2,0:T(4,128)S(1)} %copy.263) | copy-start | bytes 49156
  13.8 17.0 %copy-start.6 = (s32[4096]{0:T(1024)}, s32[4096]{0:T(1024)S(1)}, u32[]{:S(2)}) copy-start(s32[4096]{0:T(1024)S(1)} %broadcast_clamp_fusion) | copy-start | bytes 49156
  17.0 14.4 %collective-permute-start.1 = (f32[1,3,128]{2,0,1:T(1,128)S(1)}, f32[1,3,128]{2,0,1:T(1,128)S(1)}, u32[]{:S(2)}, u32[]{:S(2)}) collective-permute-start(f32[1,3,128]{2,0,1:T(1,128)S(1)} %get-tuple-element.208), channel_id=1, source_target_pairs={{4,0},{8,4},{12,8},{0,12},{5,1},{9,5},{13,9},{1,13},{6,2},{10,6},{... | collective-permute-start | bytes 4616 | tf_op jit(solution)/shard_map/ppermute | solution.py:24
  44.5 8.4 %copy-start.7 = (f32[2,64,64]{2,1,0:T(8,128)S(1)}, f32[2,64,64]{2,1,0:T(8,128)}, u32[]{:S(2)}) copy-start(f32[2,64,64]{2,1,0:T(8,128)} %param.33) | copy-start | bytes 98308
  45.1 6.2 %copy-start.43 = (f32[1,3,512]{2,0,1:T(1,128)S(1)}, f32[1,3,512]{2,0,1:T(1,128)}, u32[]{:S(2)}) copy-start(f32[1,3,512]{2,0,1:T(1,128)} %param.23) | copy-start | bytes 18436
  49.5 3.4 collective-permute-start.4
  49.8 3.1 collective-permute-start.5
  71.5 24.9 %copy-start.8 = (f32[2,64,64]{2,1,0:T(8,128)S(1)}, f32[2,64,64]{2,1,0:T(8,128)}, u32[]{:S(2)}) copy-start(f32[2,64,64]{2,1,0:T(8,128)} %param.33) | copy-start | bytes 98308
  71.5 27.6 %copy-start.52 = (s32[2,1]{0,1:T(1,128)S(1)}, s32[2,1]{0,1:T(1,128)}, u32[]{:S(2)}) copy-start(s32[2,1]{0,1:T(1,128)} %param.25) | copy-start | bytes 28
  71.5 30.3 %copy-start.56 = (f32[2,64,64]{2,1,0:T(8,128)S(1)}, f32[2,64,64]{2,1,0:T(8,128)}, u32[]{:S(2)}) copy-start(f32[2,64,64]{2,1,0:T(8,128)} %param.34) | copy-start | bytes 98308
  71.5 30.3 %copy-start.61 = (f32[64,512]{1,0:T(8,128)S(1)}, f32[64,512]{1,0:T(8,128)}, u32[]{:S(2)}) copy-start(f32[64,512]{1,0:T(8,128)} %copy-done.60) | copy-start | bytes 393220
  73.5 29.4 %copy-start = (f32[8,512,64]{1,2,0:T(8,128)S(1)}, f32[8,512,64]{1,2,0:T(8,128)}, u32[]{:S(2)}) copy-start(f32[8,512,64]{1,2,0:T(8,128)} %copy.221) | copy-start | bytes 3145732
  73.5 29.4 %copy-start.48 = (f32[8]{0:T(128)S(1)}, f32[8]{0:T(128)}, u32[]{:S(2)}) copy-start(f32[8]{0:T(128)} %multiply_add_fusion.4) | copy-start | bytes 100
  97.1 6.7 %copy-start.24 = (f32[8,512]{1,0:T(8,128)S(1)}, f32[8,512]{1,0:T(8,128)}, u32[]{:S(2)}) copy-start(f32[8,512]{1,0:T(8,128)} %copy-done.23) | copy-start | bytes 49156
  97.1 4.7 %collective-permute-start.6 = (f32[1,64,128]{2,1,0:T(8,128)S(1)}, f32[1,64,128]{2,1,0:T(8,128)S(1)}, u32[]{:S(2)}, u32[]{:S(2)}) collective-permute-start(f32[1,64,128]{2,1,0:T(8,128)S(1)} %get-tuple-element.179), channel_id=1, source_target_pairs={{0,4},{4,8},{8,12},{12,0},{1,5},{5,9},{9,13},{13,1},{2,6},{6,10},{... | collective-permute-start | bytes 98312 | tf_op jit(solution)/shard_map/ppermute | solution.py:21
  99.1 2.7 collective-permute-start.7
  154.8 10.2 %collective-permute-start.8 = (f32[1,3,128]{2,0,1:T(1,128)S(1)}, f32[1,3,128]{2,0,1:T(1,128)S(1)}, u32[]{:S(2)}, u32[]{:S(2)}) collective-permute-start(f32[1,3,128]{2,0,1:T(1,128)S(1)} %get-tuple-element.203), channel_id=1, source_target_pairs={{0,4},{4,8},{8,12},{12,0},{1,5},{5,9},{9,13},{13,1},{2,6},{6,10},{... | collective-permute-start | bytes 4616 | tf_op jit(solution)/shard_map/ppermute | solution.py:21
  155.6 9.5 %collective-permute-start.9 = (f32[1,3,128]{2,0,1:T(1,128)S(1)}, f32[1,3,128]{2,0,1:T(1,128)S(1)}, u32[]{:S(2)}, u32[]{:S(2)}) collective-permute-start(f32[1,3,128]{2,0,1:T(1,128)S(1)} %get-tuple-element.204), channel_id=1, source_target_pairs={{4,0},{8,4},{12,8},{0,12},{5,1},{9,5},{13,9},{1,13},{6,2},{10,6},{... | collective-permute-start | bytes 4616 | tf_op jit(solution)/shard_map/ppermute | solution.py:24
  185.9 5.1 %copy-start.36 = (f32[1,3,512]{2,0,1:T(1,128)}, f32[1,3,512]{2,0,1:T(1,128)S(1)}, u32[]{:S(2)}) copy-start(f32[1,3,512]{2,0,1:T(1,128)S(1)} %get-tuple-element.160) | copy-start | bytes 18436
  187.9 3.0 collective-permute-start.12
  187.9 3.0 collective-permute-start.13
  204.6 15.1 %copy-start.9 = (f32[2,64,64]{2,1,0:T(8,128)S(1)}, f32[2,64,64]{2,1,0:T(8,128)}, u32[]{:S(2)}) copy-start(f32[2,64,64]{2,1,0:T(8,128)} %param.33) | copy-start | bytes 98308
  205.2 6.8 %copy-start.58 = (u32[32]{0:T(128)S(1)}, u32[32]{0:T(128)}, u32[]{:S(2)}) copy-start(u32[32]{0:T(128)} %constant.181) | copy-start | bytes 388
  208.5 11.2 %copy-start.59 = (f32[64,512]{1,0:T(8,128)}, f32[64,512]{1,0:T(8,128)S(1)}, u32[]{:S(2)}) copy-start(f32[64,512]{1,0:T(8,128)S(1)} %fusion.5) | copy-start | bytes 393220
  209.6 10.1 %collective-permute-start.14 = (f32[1,64,128]{2,1,0:T(8,128)S(1)}, f32[1,64,128]{2,1,0:T(8,128)S(1)}, u32[]{:S(2)}, u32[]{:S(2)}) collective-permute-start(f32[1,64,128]{2,1,0:T(8,128)S(1)} %get-tuple-element.181), channel_id=1, source_target_pairs={{0,4},{4,8},{8,12},{12,0},{1,5},{5,9},{9,13},{13,1},{2,6},{6,10},{... | collective-permute-start | bytes 98312 | tf_op jit(solution)/shard_map/ppermute | solution.py:21
  210.4 9.3 %collective-permute-start.15 = (f32[1,64,128]{2,1,0:T(8,128)S(1)}, f32[1,64,128]{2,1,0:T(8,128)S(1)}, u32[]{:S(2)}, u32[]{:S(2)}) collective-permute-start(f32[1,64,128]{2,1,0:T(8,128)S(1)} %get-tuple-element.182), channel_id=1, source_target_pairs={{4,0},{8,4},{12,8},{0,12},{5,1},{9,5},{13,9},{1,13},{6,2},{10,6},{... | collective-permute-start | bytes 98312 | tf_op jit(solution)/shard_map/ppermute | solution.py:24
  212.7 105.8 %collective-permute-start.20 = (f32[1,3,512]{2,0,1:T(1,128)}, f32[1,3,512]{2,0,1:T(1,128)}, u32[]{:S(2)}, u32[]{:S(2)}) collective-permute-start(f32[1,3,512]{2,0,1:T(1,128)} %multiply_add_fusion.3), channel_id=1, source_target_pairs={{1,0},{2,1},{3,2},{5,4},{6,5},{7,6},{9,8},{10,9},{11,10},{13,12},{... | collective-permute-start | bytes 18440 | tf_op jit(solution)/shard_map/ppermute | solution.py:24
  213.9 104.5 %collective-permute-start.21 = (f32[1,3,512]{2,0,1:T(1,128)}, f32[1,3,512]{2,0,1:T(1,128)}, u32[]{:S(2)}, u32[]{:S(2)}) collective-permute-start(f32[1,3,512]{2,0,1:T(1,128)} %multiply_add_fusion.3), channel_id=1, source_target_pairs={{0,1},{1,2},{2,3},{4,5},{5,6},{6,7},{8,9},{9,10},{10,11},{12,13},{... | collective-permute-start | bytes 18440 | tf_op jit(solution)/shard_map/ppermute | solution.py:21
  237.4 25.1 %copy-start.3 = (f32[64,512]{1,0:T(8,128)S(1)}, f32[64,512]{1,0:T(8,128)}, u32[]{:S(2)}) copy-start(f32[64,512]{1,0:T(8,128)} %copy-done.2) | copy-start | bytes 393220
  237.4 25.1 %copy-start.10 = (f32[2,64,64]{2,1,0:T(8,128)S(1)}, f32[2,64,64]{2,1,0:T(8,128)}, u32[]{:S(2)}) copy-start(f32[2,64,64]{2,1,0:T(8,128)} %param.33) | copy-start | bytes 98308
  237.4 29.1 %copy-start.45 = (f32[512]{0:T(512)S(1)}, f32[512]{0:T(512)}, u32[]{:S(2)}) copy-start(f32[512]{0:T(512)} %copy-done.44) | copy-start | bytes 6148
  237.4 29.1 %copy-start.57 = (f32[2,64,64]{2,1,0:T(8,128)S(1)}, f32[2,64,64]{2,1,0:T(8,128)}, u32[]{:S(2)}) copy-start(f32[2,64,64]{2,1,0:T(8,128)} %param.34) | copy-start | bytes 98308
  239.4 29.1 %copy-start.1 = (f32[8,512,64]{1,2,0:T(8,128)S(1)}, f32[8,512,64]{1,2,0:T(8,128)}, u32[]{:S(2)}) copy-start(f32[8,512,64]{1,2,0:T(8,128)} %copy.235) | copy-start | bytes 3145732
  239.4 29.1 %copy-start.51 = (f32[8]{0:T(128)S(1)}, f32[8]{0:T(128)}, u32[]{:S(2)}) copy-start(f32[8]{0:T(128)} %multiply_add_fusion.4) | copy-start | bytes 100
  263.0 6.3 %copy-start.22 = (f32[8,512]{1,0:T(8,128)S(1)}, f32[8,512]{1,0:T(8,128)}, u32[]{:S(2)}) copy-start(f32[8,512]{1,0:T(8,128)} %copy-done.21) | copy-start | bytes 49156
  263.1 3.4 collective-permute-start.16
  263.1 3.3 collective-permute-start.17
  293.7 52.3 %copy-start.37 = (f32[1,3,512]{2,0,1:T(1,128)S(1)}, f32[1,3,512]{2,0,1:T(1,128)}, u32[]{:S(2)}) copy-start(f32[1,3,512]{2,0,1:T(1,128)} %copy-done.36) | copy-start | bytes 18436
  293.7 65.8 %copy-start.54 = (f32[1,2,1]{1,2,0:T(1,128)S(1)}, f32[1,2,1]{1,2,0:T(1,128)}, u32[]{:S(2)}) copy-start(f32[1,2,1]{1,2,0:T(1,128)} %maximum_bitcast_fusion.4) | copy-start | bytes 28
  316.6 10.7 %collective-permute-start.18 = (f32[1,3,128]{2,0,1:T(1,128)S(1)}, f32[1,3,128]{2,0,1:T(1,128)S(1)}, u32[]{:S(2)}, u32[]{:S(2)}) collective-permute-start(f32[1,3,128]{2,0,1:T(1,128)S(1)} %get-tuple-element.201), channel_id=1, source_target_pairs={{0,4},{4,8},{8,12},{12,0},{1,5},{5,9},{9,13},{13,1},{2,6},{6,10},{... | collective-permute-start | bytes 4616 | tf_op jit(solution)/shard_map/ppermute | solution.py:21
  317.4 9.9 %collective-permute-start.19 = (f32[1,3,128]{2,0,1:T(1,128)S(1)}, f32[1,3,128]{2,0,1:T(1,128)S(1)}, u32[]{:S(2)}, u32[]{:S(2)}) collective-permute-start(f32[1,3,128]{2,0,1:T(1,128)S(1)} %get-tuple-element.202), channel_id=1, source_target_pairs={{4,0},{8,4},{12,8},{0,12},{5,1},{9,5},{13,9},{1,13},{6,2},{10,6},{... | collective-permute-start | bytes 4616 | tf_op jit(solution)/shard_map/ppermute | solution.py:24
  347.3 30.6 %copy-start.35 = (f32[1,3,512]{2,0,1:T(1,128)}, f32[1,3,512]{2,0,1:T(1,128)S(1)}, u32[]{:S(2)}) copy-start(f32[1,3,512]{2,0,1:T(1,128)S(1)} %get-tuple-element.155) | copy-start | bytes 18436
  347.3 4.0 %collective-permute-start.22 = (f32[3,512]{1,0:T(4,128)S(1)}, f32[3,512]{1,0:T(4,128)S(1)}, u32[]{:S(2)}, u32[]{:S(2)}) collective-permute-start(f32[3,512]{1,0:T(4,128)S(1)} %bitcast.438), channel_id=1, source_target_pairs={{0,1},{1,2},{2,3},{4,5},{5,6},{6,7},{8,9},{9,10},{10,11},{12,13},{... | collective-permute-start | bytes 18440 | tf_op jit(solution)/shard_map/ppermute | solution.py:32
  (37 other events, 69.0 us)
where the time goes:
time: 381 us; the launch traced here: 378 us
  other arithmetic  161 us (42%)
  local copies, waits for them, and re-layouts  87.6 us (23%)
  blocking collectives  57.9 us (15%)
  starting transfers between devices  31.6 us (8%)
  matrix products  18.1 us (5%)
  between operations  16.1 us (4%)
    scatter-add x4, other arithmetic, messages(): others = jnp.moveaxis(jnp.take(displace, index, axis=1), 0, 1)  90.5 us
    scatter-add x2, other arithmetic, messages(): gathered = jnp.take(features, index, axis=1)  45.9 us
    gather x6, local copies, waits for them, and re-layouts, messages(): gathered = jnp.take(features, index, axis=1)  40 us
    gather x4, local copies, waits for them, and re-layouts, messages(): others = jnp.moveaxis(jnp.take(displace, index, axis=1), 0, 1)  26.7 us
    ppermute x11, starting transfers between devices, padded_2(): lax.ppermute(lax.slice_in_dim(block, block.shape[dim] - width, None, axis...  18.1 us
    psum x2, blocking collectives, local(): along = lax.psum(jnp.sum(force * unit, axis=(1, 2)), 'dom')  13.6 us
    psum x2, blocking collectives, local(): lax.psum((jnp.sum(plus * plus, axis=(1, 2)), jnp.sum(minus * minus, axis=...  13.1 us
    psum x2, blocking collectives, local(): lax.psum((jnp.sum(speed * speed, axis=(1, 2)), jnp.sum(band * band, axis=...  12.8 us
  transfers between devices with their start and end apart: 23, of which 3 were waited for; matrix products, arithmetic and copies ran while one was open for 62% of the time, Pallas kernels for 0%

commit v1 on v0

v1 whole, which is shorter than its diff:
```python
import functools
import math

import jax
import jax.numpy as jnp
from jax import lax
from jax.experimental import pallas as pl
from jax.experimental.pallas import tpu as pltpu
from jax.sharding import PartitionSpec as P

F32 = jnp.float32
BF16 = jnp.bfloat16
PRECISE = lax.Precision.HIGHEST
SPRING_CONSTANT = 0.5
ALPHA_START = 0.1
STEP_LIMIT = 0.3
TINY_VALUE = 1e-06
SOFTENING = 0.25
LANES = 128
SLOTS = 8
BASIS = 8
CHANNELS = 64
SLAB_BLOCKS = 4
ROW_X = 32
ROW_COUNT = 35
ROW_KIND = 36
PACK_ROWS = 40
NT = (((1,), (1,)), ((), ()))


def split(x):
    high = x.astype(BF16).astype(F32)
    return high, x - high


def left_stack(w):
    high, low = split(w)
    return jnp.concatenate([high, high, low], axis=1)


def right_stack(x):
    high, low = split(x)
    high = high.astype(BF16)
    return jnp.concatenate([high, low.astype(BF16), high], axis=0)


def pair_stack(x):
    high, low = split(x)
    return jnp.concatenate([high.astype(BF16), low.astype(BF16)], axis=0)


def mm(a, b):
    return jnp.dot(a, b, preferred_element_type=F32)


def mm_nt(a, b):
    return lax.dot_general(a, b, NT, preferred_element_type=F32)


def pack_kernel(x_ref, species_ref, nbr_ref, counts_ref, lattice_ref, out_ref):
    out_ref[0:8, :] = nbr_ref[...].astype(F32)
    for c in range(3):
        out_ref[8 + 8 * c : 16 + 8 * c, :] = lattice_ref[:, c, :]
    out_ref[ROW_X : ROW_X + 3, :] = x_ref[0]
    out_ref[ROW_COUNT : ROW_COUNT + 1, :] = counts_ref[...].astype(F32).reshape(1, -1)
    out_ref[ROW_KIND : ROW_KIND + 1, :] = species_ref[...].astype(F32).reshape(1, -1)
    out_ref[ROW_KIND + 1 : PACK_ROWS, :] = jnp.zeros((PACK_ROWS - ROW_KIND - 1, out_ref.shape[1]), F32)


def weight_kernel(
    embed_ref, radial_ref, mix_ref, update_ref, readout_ref, l1_ref, l2_ref, l3_ref, l4_ref, l5_ref, l6_ref, col_ref
):
    eye = (
        lax.broadcasted_iota(jnp.int32, (CHANNELS, CHANNELS), 0)
        == lax.broadcasted_iota(jnp.int32, (CHANNELS, CHANNELS), 1)
    ).astype(F32)

    def turned(x):
        return lax.dot_general(eye, x, NT, precision=PRECISE, preferred_element_type=F32)

    base0 = embed_ref[0:1, :]
    base1 = embed_ref[1:2, :] - base0
    rows = jnp.concatenate([base0, base1], axis=0)
    sent = jnp.dot(rows, mix_ref[0], precision=PRECISE, preferred_element_type=F32)
    scale = 1.0 / math.sqrt(SLOTS)
    first = jnp.concatenate([radial_ref[0] * sent[0:1], radial_ref[0] * sent[1:2]], axis=0) * scale
    second = radial_ref[1] * scale
    folded = jnp.dot(update_ref[0], mix_ref[1], precision=PRECISE, preferred_element_type=F32)
    mix_t = turned(mix_ref[1])
    l1_ref[...] = left_stack(turned(first)).astype(BF16)
    l2_ref[...] = left_stack(turned(folded)).astype(BF16)
    high, low = split(turned(second))
    l3_ref[...] = jnp.concatenate([high, high, low, jnp.zeros_like(high)], axis=1).astype(BF16)
    l4_ref[...] = left_stack(jnp.concatenate([second, jnp.zeros_like(second)], axis=0)).astype(BF16)
    l5_ref[...] = left_stack(folded).astype(BF16)
    l6_ref[...] = left_stack(first).astype(BF16)
    readout = readout_ref[...].reshape(1, CHANNELS)
    wide = (CHANNELS, LANES)
    col_ref[0] = jnp.broadcast_to(jnp.sum(mix_t * base0, axis=1, keepdims=True), wide)
    col_ref[1] = jnp.broadcast_to(jnp.sum(mix_t * base1, axis=1, keepdims=True), wide)
    col_ref[2] = jnp.broadcast_to(jnp.sum(update_ref[0] * readout, axis=1, keepdims=True), wide)
    col_ref[3] = jnp.broadcast_to(jnp.sum(update_ref[1] * readout, axis=1, keepdims=True), wide)


def sin_cos(t):
    q = t * t
    s = -1.0 / 39916800.0
    for c in (1.0 / 362880.0, -1.0 / 5040.0, 1.0 / 120.0, -1.0 / 6.0, 1.0):
        s = s * q + c
    k = 1.0 / 479001600.0
    for c in (-1.0 / 3628800.0, 1.0 / 40320.0, -1.0 / 720.0, 1.0 / 24.0, -0.5, 1.0):
        k = k * q + c
    return s * t, k


def wide_row(x, row):
    return jnp.broadcast_to(x[row : row + 1, :], (8, x.shape[1]))


def silu_parts(m):
    sig = 1.0 / (1.0 + jnp.exp(-m))
    return m * sig, sig * (1.0 + m * (1.0 - sig))


def force_parts(packs, weights, scr):
    l1, l2, l3, l4, l5, l6, col = weights
    (xs, widx, kinds, geo, bst, bpr, sst, ghl, slope, hot, dg, dmat, acc) = scr
    centre = 2.0 + 0.5 * lax.broadcasted_iota(jnp.int32, (BASIS, LANES), 0).astype(F32)
    slot = lax.broadcasted_iota(jnp.int32, (SLOTS, LANES), 0)

    for b in range(1, 11):
        pack = packs[b // 4]
        lanes = slice((b % 4) * LANES, (b % 4 + 1) * LANES)
        index = pack[0:8, lanes].astype(jnp.int32) - LANES * (b % 4)
        widx[b] = index
        inner = index & (LANES - 1)
        part = index >> 7

        def taken(row):
            got = [
                jnp.take_along_axis(jnp.broadcast_to(xs[b - 1 + w, row : row + 1, :], (SLOTS, LANES)), inner, axis=1)
                for w in range(3)
            ]
            return jnp.where(part == 0, got[0], jnp.where(part == 1, got[1], got[2]))

        vec = [
            pack[8 + 8 * c : 16 + 8 * c, lanes] + taken(c) - jnp.broadcast_to(xs[b, c : c + 1, :], (SLOTS, LANES))
            for c in range(3)
        ]
        kind = taken(3)
        dist = jnp.sqrt(vec[0] * vec[0] + vec[1] * vec[1] + vec[2] * vec[2] + SOFTENING)
        live = (slot.astype(F32) < jnp.broadcast_to(pack[ROW_COUNT : ROW_COUNT + 1, lanes], (SLOTS, LANES))).astype(F32)
        turns = dist * (1.0 / 12.0)
        turns = turns - jnp.floor(turns + 0.5)
        sine, cosine = sin_cos(turns * math.pi)
        envelope = cosine * cosine * live
        slant = cosine * sine * live * (-math.pi / 6.0)
        kinds[b] = kind
        if 3 <= b <= 8:
            for c in range(3):
                geo[b, c] = vec[c]
            geo[b, 3] = 1.0 / dist
        total = jnp.zeros((BASIS, LANES), F32)
        total_kind = jnp.zeros((BASIS, LANES), F32)
        for k in range(SLOTS):
            away = wide_row(dist, k) - centre
            gauss = jnp.exp(-4.0 * (away * away))
            env_k = wide_row(envelope, k)
            value = gauss * env_k
            total = total + value
            total_kind = total_kind + value * wide_row(kind, k)
            cols = slice(k * LANES, (k + 1) * LANES)
            if 2 <= b <= 9:
                high, low = split(value)
                bst[b, 0:8, cols] = high
                bst[b, 8:16, cols] = low
            if 3 <= b <= 8:
                bpr[b, :, cols] = gauss * (wide_row(slant, k) - 8.0 * away * env_k)
        both = jnp.concatenate([total, total_kind], axis=0)
        high, low = split(both)
        sst[b] = jnp.concatenate([high, low, high], axis=0).astype(BF16)

    for b in range(1, 11):
        message = mm(l1[...], sst[b])
        value, steep = silu_parts(message)
        sent = mm(l2[...], right_stack(value))
        sent = sent + col[0] + col[1] * jnp.broadcast_to(xs[b, 3:4, :], (CHANNELS, LANES))
        ghl[b] = pair_stack(sent)
        if 3 <= b <= 8:
            slope[b] = steep

    for b in range(1, 11):
        dg[b] = jnp.zeros((CHANNELS, LANES), F32)

    row_id = lax.broadcasted_iota(jnp.int32, (3 * LANES, LANES), 0)

    def second(b, carry):
        index = widx[b]
        for k in range(SLOTS):
            same = row_id == jnp.broadcast_to(index[k : k + 1, :], (3 * LANES, LANES))
            hot[b, :, k * LANES : (k + 1) * LANES] = jnp.where(same, 1.0, 0.0).astype(BF16)
        window = jnp.concatenate([ghl[b - 1], ghl[b], ghl[b + 1]], axis=1)
        got = mm(window, hot[b])
        got = got[:CHANNELS] + got[CHANNELS:]
        basis = bst[b]
        stack = jnp.concatenate([basis, basis], axis=0).astype(BF16)
        radial = mm(l3[...], stack)
        message = jnp.zeros((CHANNELS, LANES), F32)
        for k in range(SLOTS):
            cols = slice(k * LANES, (k + 1) * LANES)
            message = message + radial[:, cols] * got[:, cols]
        _, steep = silu_parts(message)
        back = col[3] * steep
        back = jnp.concatenate([back] * SLOTS, axis=1)
        out = mm_nt(pair_stack(radial * back), hot[b])
        out = out[:CHANNELS] + out[CHANNELS:]
        for w in range(3):
            dg[b - 1 + w] += out[:, w * LANES : (w + 1) * LANES]
        dmat[b] = mm(l4[...], right_stack(got * back))[0:8]
        return carry

    lax.fori_loop(2, 10, second, 0)

    for b in range(3, 9):
        for c in range(3):
            acc[b, c] = jnp.zeros((8, LANES), F32)
    acc[2] = jnp.zeros((3, 8, LANES), F32)
    acc[9] = jnp.zeros((3, 8, LANES), F32)

    def last(b, carry):
        steep = mm(l5[...], right_stack(dg[b])) + col[2]
        sums = mm(l6[...], right_stack(steep * slope[b]))
        kind = kinds[b]
        rows = []
        for k in range(SLOTS):
            cols = slice(k * LANES, (k + 1) * LANES)
            weight = dmat[b, :, cols] + sums[0:8] + wide_row(kind, k) * sums[8:16]
            rows.append(jnp.sum(bpr[b, :, cols] * weight, axis=0, keepdims=True))
        pull = jnp.concatenate(rows, axis=0) * geo[b, 3]
        pieces = []
        for c in range(3):
            value = pull * geo[b, c]
            acc[b, c] -= value
            pieces.append(split(value))
        lines = []
        for h in range(2):
            for c in range(3):
                lines.append(
                    jnp.concatenate([jnp.where(slot == k, pieces[c][h], 0.0) for k in range(SLOTS)], axis=1)
                )
        out = mm_nt(jnp.concatenate(lines, axis=0).astype(BF16), hot[b])
        for c in range(3):
            both = out[8 * c : 8 * c + 8] + out[24 + 8 * c : 32 + 8 * c]
            for w in range(3):
                acc[b - 1 + w, c] += both[:, w * LANES : (w + 1) * LANES]
        return carry

    lax.fori_loop(3, 9, last, 0)


def own_force(acc, c):
    return jnp.concatenate(
        [-jnp.sum(acc[4 + i, c], axis=0, keepdims=True) for i in range(SLAB_BLOCKS)], axis=1
    )


def fill_region(xs, packs, rows_of):
    for b in range(12):
        lanes = slice((b % 4) * LANES, (b % 4 + 1) * LANES)
        pack = packs[b // 4]
        xs[b, 0:3, :] = rows_of(b // 4)[:, lanes]
        xs[b, 3:4, :] = pack[ROW_KIND : ROW_KIND + 1, lanes]


def lane_total(x):
    x = x[:, 0:LANES] + x[:, LANES : 2 * LANES] + x[:, 2 * LANES : 3 * LANES] + x[:, 3 * LANES : 4 * LANES]
    return jnp.sum(x, axis=1, keepdims=True)


def dot3(a, b):
    return jnp.sum(a * b, axis=0, keepdims=True)


def scratch():
    return [
        pltpu.VMEM((12, 8, LANES), F32),
        pltpu.VMEM((12, 8, LANES), jnp.int32),
        pltpu.VMEM((12, 8, LANES), F32),
        pltpu.VMEM((12, 4, 8, LANES), F32),
        pltpu.VMEM((12, 16, SLOTS * LANES), F32),
        pltpu.VMEM((12, 8, SLOTS * LANES), F32),
        pltpu.VMEM((12, 48, LANES), BF16),
        pltpu.VMEM((12, 2 * CHANNELS, LANES), BF16),
        pltpu.VMEM((12, CHANNELS, LANES), F32),
        pltpu.VMEM((12, 3 * LANES, SLOTS * LANES), BF16),
        pltpu.VMEM((12, CHANNELS, LANES), F32),
        pltpu.VMEM((12, 8, SLOTS * LANES), F32),
        pltpu.VMEM((12, 3, 8, LANES), F32),
    ]


def first_kernel(images, pl_ref, po_ref, pr_ref, v_ref, before_ref, after_ref, *rest):
    weights, out_ref, scr = rest[:7], rest[7], rest[8:]
    packs = [pl_ref, po_ref, pr_ref]
    fill_region(scr[0], packs, lambda s: packs[s][ROW_X : ROW_X + 3, :])
    force_parts(packs, weights, scr)
    acc = scr[-1]
    force = jnp.concatenate([own_force(acc, c) for c in range(3)], axis=0)
    here = lax.axis_index("img")
    x = po_ref[ROW_X : ROW_X + 3, :]
    v = v_ref[0]
    before = jnp.where(here > 0, before_ref[0], 0.0)
    after = jnp.where(here < images - 1, after_ref[0], 0.0)
    tangent = after - before
    plus = after - x
    minus = x - before
    sums = jnp.concatenate(
        [
            dot3(force, tangent),
            dot3(force, force),
            dot3(tangent, tangent),
            dot3(plus, plus),
            dot3(minus, minus),
            dot3(v, v),
            jnp.zeros((2, x.shape[1]), F32),
        ],
        axis=0,
    )
    out_ref[0:3, :] = force
    out_ref[3:6, :] = tangent
    out_ref[6:9, :] = v
    out_ref[9:15, :] = jnp.broadcast_to(lane_total(sums)[0:6], (6, x.shape[1]))
    out_ref[15:16, :] = jnp.zeros((1, x.shape[1]), F32)


def step_numbers(ft, ff, tt, pp, mn, vv, dt, alpha, flagged, climbing, inside):
    root = jnp.sqrt(tt + TINY_VALUE)
    along = ft / root
    spring = SPRING_CONSTANT * (jnp.sqrt(pp) - jnp.sqrt(mn))
    factor = jnp.where(climbing, -2.0 * along, spring - along)
    band = jnp.maximum(ff + 2.0 * factor * along + factor * factor * (tt / (tt + TINY_VALUE)), 0.0)
    new_dt = jnp.where(flagged, 0.5 * dt, jnp.minimum(1.1 * dt, STEP_LIMIT))
    pull = jnp.where(flagged, 0.0, alpha * jnp.sqrt(vv / (band + TINY_VALUE))) + new_dt
    keep = jnp.where(flagged, 0.0, 1.0 - alpha)
    new_alpha = jnp.where(flagged, ALPHA_START, 0.99 * alpha)
    keep = jnp.where(inside, keep, 0.0)
    pull = jnp.where(inside, pull, 0.0)
    return (
        jnp.where(inside, along, 0.0),
        jnp.where(inside, spring, 0.0),
        keep,
        pull,
        pull * factor / root,
        new_dt,
        new_alpha,
    )


def second_kernel(images, others, dt_ref, flag_ref, climb_ref, pl_ref, po_ref, pr_ref, own_ref, *rest):
    heard, rest = rest[:others], rest[others:]
    weights, out_ref, scr = rest[:7], rest[7], rest[8:]
    packs = [pl_ref, po_ref, pr_ref]
    here = lax.axis_index("img")
    sums = own_ref[8:16, 0:LANES]
    for one in heard:
        sums = sums + one[8:16, 0:LANES]
    ft, ff, tt, pp, mn, vv = (sums[1 + i : 2 + i, :] for i in range(6))
    shape = (1, LANES)
    along, spring, keep, pull, side, dt, alpha = step_numbers(
        ft,
        ff,
        tt,
        pp,
        mn,
        vv,
        jnp.full(shape, dt_ref[0], F32),
        jnp.full(shape, ALPHA_START, F32),
        jnp.full(shape, flag_ref[0, 0], jnp.int32) == 1,
        jnp.full(shape, here - climb_ref[0], jnp.int32) == 0,
        jnp.full(shape, jnp.where((here >= 1) & (here <= images - 2), 1, 0), jnp.int32) == 1,
    )
    messages = [heard[0], own_ref, heard[others - 1]]

    def wide(s):
        return jnp.concatenate([s] * SLAB_BLOCKS, axis=1)

    def speed(m):
        return wide(keep) * m[6:9, :] + wide(pull) * m[0:3, :] + wide(side) * m[3:6, :]

    moved = [p[ROW_X : ROW_X + 3, :] + wide(dt) * speed(m) for p, m in zip(packs, messages)]
    fill_region(scr[0], packs, lambda s: moved[s])
    force_parts(packs, weights, scr)
    acc = scr[-1]
    out_ref[0:3, :] = moved[1]
    out_ref[3:6, :] = speed(own_ref)
    out_ref[6:9, :] = jnp.concatenate([own_force(acc, c) for c in range(3)], axis=0)
    out_ref[9:10, :] = wide(dt)
    out_ref[10:11, :] = wide(alpha)
    out_ref[11:12, :] = jnp.full((1, out_ref.shape[1]), flag_ref[1, 0], jnp.int32).astype(F32)
    out_ref[12:13, :] = wide(along)
    out_ref[13:14, :] = wide(spring)
    out_ref[14:16, :] = jnp.zeros((2, out_ref.shape[1]), F32)


PRODUCTS = (
    [("f", "t"), ("f", "f"), ("t", "t"), ("p", "p"), ("d", "d"), ("v", "v")]
    + [("d", "v"), ("d", "f"), ("d", "t"), ("d", "V"), ("d", "F"), ("d", "T"), ("v", "f"), ("v", "t")]
    + [(a, b) for a in "vft" for b in "VFT"]
)


def gram_kernel(images, *refs):
    messages, out_ref, state_ref = refs[:images], refs[images], refs[images + 1]
    rows = 8 * ((images + 7) // 8)
    here = lax.axis_index("img")
    width = state_ref.shape[1]
    blank = jnp.zeros((rows - images, width), F32)

    def gathered(row):
        lines = [m[row : row + 1, :] for m in messages]
        return jnp.concatenate(lines + ([blank] if rows > images else []), axis=0)

    def shifted(value, by):
        lines = [value[(s + by) % images : (s + by) % images + 1, :] for s in range(images)]
        return jnp.concatenate(lines + ([blank] if rows > images else []), axis=0)

    offset = lax.broadcasted_iota(jnp.int32, (rows, width), 0)
    number = here - offset
    number = jnp.where(number < 0, number + images, number)
    has_after = (number < images - 1) & (offset < images)
    has_before = (number > 0) & (offset < images)
    totals = [jnp.zeros((rows, width), F32) for _ in PRODUCTS]
    for c in range(3):
        x, v, f = gathered(c), gathered(3 + c), gathered(6 + c)
        after = jnp.where(has_after, shifted(x, -1), 0.0)
        before = jnp.where(has_before, shifted(x, 1), 0.0)
        t = after - before
        table = {"f": f, "v": v, "t": t, "p": after - x, "d": x - before}
        table["F"] = jnp.where(has_before, shifted(f, 1), 0.0)
        table["V"] = jnp.where(has_before, shifted(v, 1), 0.0)
        table["T"] = jnp.where(has_before, shifted(t, 1), 0.0)
        totals = [old + table[a] * table[b] for old, (a, b) in zip(totals, PRODUCTS)]
        state_ref[c : c + 1, :] = t[0:1]
    lane = lax.broadcasted_iota(jnp.int32, (rows, LANES), 1)
    result = jnp.zeros((rows, LANES), F32)
    for q, one in enumerate(totals):
        result = jnp.where(lane == q, jnp.broadcast_to(lane_total(one), (rows, LANES)), result)
    out_ref[...] = result
    for i in range(3):
        state_ref[8 + rows * i : 8 + rows * (i + 1), :] = gathered(9 + i)


def final_kernel(images, others, atoms, climb_ref, own_ref, state_ref, sums_ref, *rest):
    heard, (x_ref, v_ref, band_ref, path_ref) = rest[:others], rest[others:]
    rows = sums_ref.shape[0]
    here = lax.axis_index("img")
    sums = sums_ref[...]
    for one in heard:
        sums = sums + one[...]
    got = {
        pair: jnp.broadcast_to(sums[:, q : q + 1], (rows, LANES)) for q, pair in enumerate(PRODUCTS)
    }
    offset = lax.broadcasted_iota(jnp.int32, (rows, LANES), 0)
    number = here - offset
    number = jnp.where(number < 0, number + images, number)
    inside = (number >= 1) & (number <= images - 2) & (offset < images)
    has_before = (number > 0) & (offset < images)
    climb = jnp.full((rows, LANES), climb_ref[0], jnp.int32)
    dt0, alpha0, flag = (state_ref[8 + rows * i : 8 + rows * (i + 1), 0:LANES] for i in range(3))
    along, spring, keep, pull, side, dt, _ = step_numbers(
        got["f", "t"],
        got["f", "f"],
        got["t", "t"],
        got["p", "p"],
        got["d", "d"],
        got["v", "v"],
        dt0,
        alpha0,
        flag == 1.0,
        number == climb,
        inside,
    )

    def shifted(value):
        lines = [value[(s + 1) % images : (s + 1) % images + 1, :] for s in range(images)]
        if rows > images:
            lines.append(jnp.zeros((rows - images, LANES), F32))
        return jnp.where(has_before, jnp.concatenate(lines, axis=0), 0.0)

    now = {"v": dt * keep, "f": dt * pull, "t": dt * side}
    old = {a.upper(): shifted(value) for a, value in now.items()}
    mine = now["v"] * now["v"] * got["v", "v"] + now["f"] * now["f"] * got["f", "f"]
    mine = mine + now["t"] * now["t"] * got["t", "t"]
    cross = now["v"] * now["f"] * got["v", "f"] + now["v"] * now["t"] * got["v", "t"]
    mine = mine + 2.0 * (cross + now["f"] * now["t"] * got["f", "t"])
    both = jnp.zeros((rows, LANES), F32)
    for a in "vft":
        both = both + now[a] * got["d", a]
    for b in "VFT":
        both = both - old[b] * got["d", b]
    for a in "vft":
        for b in "VFT":
            both = both - now[a] * old[b] * got[a, b]
    squared = got["d", "d"] + mine + shifted(mine) + 2.0 * both
    segment = jnp.sqrt(jnp.maximum(squared, 0.0) * (1.0 / (3.0 * atoms)))
    path = jnp.sum(jnp.where(offset <= here, segment, 0.0), axis=0, keepdims=True)
    path_ref[...] = path

    def wide(s):
        return jnp.concatenate([s[0:1, :]] * SLAB_BLOCKS, axis=1)

    speed = wide(keep) * own_ref[3:6, :] + wide(pull) * own_ref[6:9, :] + wide(side) * state_ref[0:3, :]
    v_ref[0] = speed
    x_ref[0] = own_ref[0:3, :] + wide(dt) * speed
    band_ref[...] = jnp.concatenate(
        [own_ref[12:14, 0:LANES], along[0:1], spring[0:1], jnp.zeros((4, LANES), F32)], axis=0
    )


VMEM_SPEC = pl.BlockSpec(memory_space=pltpu.VMEM)
SMEM_SPEC = pl.BlockSpec(memory_space=pltpu.SMEM)


def call(body, outs, scalars, arrays, scratch_shapes=(), flops=0):
    return pl.pallas_call(
        body,
        out_shape=outs,
        in_specs=[SMEM_SPEC] * len(scalars) + [VMEM_SPEC] * len(arrays),
        out_specs=jax.tree.map(lambda _: VMEM_SPEC, outs),
        scratch_shapes=list(scratch_shapes),
        compiler_params=pltpu.CompilerParams(vmem_limit_bytes=48 * 1024 * 1024),
        cost_estimate=pl.CostEstimate(flops=flops, bytes_accessed=1 << 18, transcendentals=0),
    )(*scalars, *arrays)


def around(array, axis):
    count = lax.axis_size(axis)
    return [lax.ppermute(array, axis, [(i, (i + s) % count) for i in range(count)]) for s in range(1, count)]


def ring(array, axis, by):
    count = lax.axis_size(axis)
    return lax.ppermute(array, axis, [(i, (i + by) % count) for i in range(count)])


def local(
    disp,
    veloc,
    time_step,
    reset_flags,
    climb,
    species,
    neighbours,
    counts,
    lattice,
    embed,
    radial_weight,
    mix_weight,
    update_weight,
    readout,
):
    atoms = disp.shape[2]
    images = lax.axis_size("img")
    domains = lax.axis_size("dom")
    assert disp.shape[0] == 1 and atoms == SLAB_BLOCKS * LANES and domains >= 3
    shape = jax.ShapeDtypeStruct
    before, after = ring(disp, "img", 1), ring(disp, "img", -1)
    pack = call(pack_kernel, shape((PACK_ROWS, atoms), F32), (), (disp, species, neighbours, counts, lattice))
    left, right = ring(pack, "dom", 1), ring(pack, "dom", -1)
    weights = call(
        weight_kernel,
        (
            shape((CHANNELS, 48), BF16),
            shape((CHANNELS, 192), BF16),
            shape((CHANNELS, 32), BF16),
            shape((16, 192), BF16),
            shape((CHANNELS, 192), BF16),
            shape((16, 192), BF16),
            shape((4, CHANNELS, LANES), F32),
        ),
        (),
        (embed, radial_weight, mix_weight, update_weight, readout),
        flops=10000000,
    )
    message = call(
        functools.partial(first_kernel, images),
        shape((16, atoms), F32),
        (),
        (left, pack, right, veloc, before, after, *weights),
        scratch(),
        flops=1000000000,
    )
    heard = around(message, "dom")
    state = call(
        functools.partial(second_kernel, images, len(heard)),
        shape((16, atoms), F32),
        (time_step, reset_flags, climb),
        (left, pack, right, message, *heard, *weights),
        scratch(),
        flops=1000000000,
    )
    band = around(state, "img")
    rows = 8 * ((images + 7) // 8)
    sums, extra = call(
        functools.partial(gram_kernel, images),
        (shape((rows, LANES), F32), shape((8 + 3 * rows, atoms), F32)),
        (),
        (state, *band),
    )
    others = around(sums, "dom")
    new_disp, new_veloc, records, path = call(
        functools.partial(final_kernel, images, len(others), atoms * domains),
        (shape(disp.shape, F32), shape(disp.shape, F32), shape((8, LANES), F32), shape((1, LANES), F32)),
        (climb,),
        (state, extra, sums, *others),
    )
    return new_disp, new_veloc, records[0:4, 0].reshape(2, 2, 1), path[0, 0:1]


def solution(mesh):
    in_specs = (
        P(("group", "img"), None, "dom"),
        P(("group", "img"), None, "dom"),
        P(("group", "img")),
        P(None, ("group", "img")),
        P("group"),
        P(("group", "dom")),
        P(None, ("group", "dom")),
        P(("group", "dom")),
        P(None, None, ("group", "dom")),
        P(),
        P(),
        P(),
        P(),
        P(),
    )
    out_specs = (
        P(("group", "img"), None, "dom"),
        P(("group", "img"), None, "dom"),
        P(None, None, ("group", "img")),
        P(("group", "img")),
    )
    return jax.shard_map(local, mesh=mesh, in_specs=in_specs, out_specs=out_specs, check_vma=False)
```

time: 381 us -> 57.5 us (0.15)
  other arithmetic: 161 us -> 0 us
  local copies, waits for them, and re-layouts: 87.6 us -> 3.68 us
  blocking collectives: 57.9 us -> 0 us
  Pallas kernels: 0 us -> 26.5 us
  starting transfers between devices: 31.6 us -> 10.8 us
  matrix products: 18.1 us -> 0 us
  between operations: 16.1 us -> 2.12 us
  waiting for transfers between devices: 3.28 us -> 14.2 us
    scatter-add x6 -> x0, other arithmetic: 136 us -> none  [the longest x4 90.5 us: messages(): others = jnp.moveaxis(jnp.take(displace, index, axis=1), 0, 1)]
    gather x10 -> x0, local copies, waits for them, and re-layouts: 66.7 us -> none  [the longest x6 40 us: messages(): gathered = jnp.take(features, index, axis=1)]
    psum x7 -> x0, blocking collectives: 45.8 us -> none  [the longest x2 13.6 us: local(): along = lax.psum(jnp.sum(force * unit, axis=(1, 2)), 'dom')]
    pallas_call x0 -> x6, Pallas kernels: none -> 26.5 us  [call(): pl.pallas_call(body, out_shape=outs, in_specs=[SMEM_SPEC] * len(scalars)...]
    ppermute x23 -> x13, starting transfers between devices: 31.6 us -> 10.8 us  [the longest x4 6.04 us: ring(): lax.ppermute(array, axis, [(i, (i + by) % count) for i in range(count)])]
    dot_general x18 -> x0, matrix products: 18.1 us -> none  [the longest x8 10.3 us: messages(): jnp.einsum('nc,nka->cka', radial_w, radial_basis(distance, number), preci...]
    reduce_sum x13 -> x0, other arithmetic: 12.5 us -> none  [the longest x2 2.78 us: local(): jnp.sum(minus * minus, axis=(1, 2))]
    unnamed x1 -> x0, blocking collectives: 12.1 us -> none
  transfers between devices with their start and end apart: 23 -> 13, of which waited for: 3 -> 9; matrix products, arithmetic and copies ran while one was open for 62% -> 0% of each run, Pallas kernels for 0% -> 1%
where the time goes in v1:
time: 57.5 us; the launch traced here: 57.2 us
  Pallas kernels  26.5 us (46%)
  waiting for transfers between devices  14.2 us (25%)
  starting transfers between devices  10.8 us (19%)
  local copies, waits for them, and re-layouts  3.68 us (6%)
  between operations  2.12 us (4%)
    pallas_call x6, Pallas kernels, call(): pl.pallas_call(body, out_shape=outs, in_specs=[SMEM_SPEC] * len(scalars)...  26.5 us
    ppermute x9, waiting for transfers between devices, around(): lax.ppermute(array, axis, [(i, (i + s) % count) for i in range(count)])  9.32 us
    ppermute x4, starting transfers between devices, ring(): lax.ppermute(array, axis, [(i, (i + by) % count) for i in range(count)])  6.04 us
    ppermute x4, waiting for transfers between devices, ring(): lax.ppermute(array, axis, [(i, (i + by) % count) for i in range(count)])  4.86 us
    ppermute x9, starting transfers between devices, around(): lax.ppermute(array, axis, [(i, (i + s) % count) for i in range(count)])  4.77 us
    unnamed x26, local copies, waits for them, and re-layouts  2.92 us
  transfers between devices with their start and end apart: 13, of which 9 were waited for; matrix products, arithmetic and copies ran while one was open for 0% of the time, Pallas kernels for 1%

profile of v1, /device:TPU:0, one launch (start us, length us, event | category | flops | bytes accessed | tf_op | source)
XLA Modules:
  0.0 57.2 jit_solution(6093547614513278309)
XLA Ops:
  0.6 0.7 %copy.27.x_ref = f32[1,3,512]{2,1,0:T(4,128)S(1)} copy(f32[1,3,512]{2,0,1:T(1,128)} %param.14) | data formatting | bytes 12288 | tf_op args[0]
  1.3 0.9 %copy.28.lattice_ref = f32[8,3,512]{2,1,0:T(4,128)S(1)} copy(f32[8,3,512]{2,0,1:T(8,128)} %param.22) | data formatting | bytes 98304 | tf_op args[8]
  2.2 0.0 copy-done.2
  2.2 0.0 copy-done.4
  2.2 0.0 copy-done.5
  2.2 0.0 copy-start.8
  2.3 0.0 copy-start
  2.3 0.0 copy-start.1
  2.3 0.0 copy-start.3
  2.3 0.0 copy-start.6
  2.3 0.0 copy-start.7
  2.3 2.4 %collective-permute-start.1 = (f32[40,512]{1,0:T(8,128)S(1)}, f32[40,512]{1,0:T(8,128)S(1)}, u32[]{:S(2)}, u32[]{:S(2)}) collective-permute-start(f32[40,512]{1,0:T(8,128)S(1)} %shard_map.165.po_ref), channel_id=1, source_target_pairs={{0,12},{4,0},{8,4},{12,8},{1,13},{5,1},{9,5},{13,9},{2,14},{6,2},{... | collective-permute-start | bytes 245768 | tf_op jit(solution)/shard_map/ppermute | solution.py:543
  4.8 0.0 collective-permute-start
  4.8 3.6 %collective-permute-start.3 = (f32[1,3,512]{2,1,0:T(4,128)S(1)}, f32[1,3,512]{2,1,0:T(4,128)S(1)}, u32[]{:S(2)}, u32[]{:S(2)}) collective-permute-start(f32[1,3,512]{2,1,0:T(4,128)S(1)} %copy.27.x_ref), channel_id=1, source_target_pairs={{0,3},{1,0},{2,1},{3,2},{4,7},{5,4},{6,5},{7,6},{8,11},{9,8},{10,9... | collective-permute-start | bytes 18440 | tf_op jit(solution)/shard_map/ppermute | solution.py:543
  8.4 0.0 collective-permute-start.2
  8.4 0.5 shard_map.166
  9.0 0.8 %collective-permute-done.3.after_ref = f32[1,3,512]{2,1,0:T(4,128)S(1)} collective-permute-done((f32[1,3,512]{2,1,0:T(4,128)S(1)}, f32[1,3,512]{2,1,0:T(4,128)S(1)}, u32[]{:S(2)}, u32[]{:S(2)}) %collective-permute-start.3) | collective-permute-done | bytes 6176 | tf_op jit(solution)/shard_map/ppermute | solution.py:543
  9.7 4.1 %collective-permute-done.2.before_ref = f32[1,3,512]{2,1,0:T(4,128)S(1)} collective-permute-done((f32[1,3,512]{2,1,0:T(4,128)S(1)}, f32[1,3,512]{2,1,0:T(4,128)S(1)}, u32[]{:S(2)}, u32[]{:S(2)}) %collective-permute-start.2) | collective-permute-done | bytes 6176 | tf_op jit(solution)/shard_map/ppermute | solution.py:543
  13.8 0.0 collective-permute-done.1.pr_ref
  13.8 0.0 collective-permute-done.pl_ref
  13.8 12.2 %shard_map.167.own_ref = f32[16,512]{1,0:T(8,128)S(1)} custom-call(f32[40,512]{1,0:T(8,128)S(1)} %collective-permute-done.pl_ref, f32[40,512]{1,0:T(8,128)S(1)} %shard_map.165.po_ref, f32[40,512]{1,0:T(8,128)S(1)} %collective-permute-done.1.pr_ref, f32[1,3,512]{2,1,0:T(4,128)S(1)} %copy.31.v_ref, f32[1,3,512]{2,1,0:T(4,128)S(1)} %collective-permute-done.2.before_ref, ...), custom_call_target="tpu_custom_call" | custom-call | flops 1000000000 | bytes 262144 | tf_op jit(solution)/shard_map/pallas_call | solution.py:525
  26.1 0.3 collective-permute-start.6
  26.4 0.8 %collective-permute-start.5 = (f32[16,512]{1,0:T(8,128)S(1)}, f32[16,512]{1,0:T(8,128)S(1)}, u32[]{:S(2)}, u32[]{:S(2)}) collective-permute-start(f32[16,512]{1,0:T(8,128)S(1)} %shard_map.167.own_ref), channel_id=1, source_target_pairs={{0,8},{4,12},{8,0},{12,4},{1,9},{5,13},{9,1},{13,5},{2,10},{6,14},... | collective-permute-start | bytes 98312 | tf_op jit(solution)/shard_map/ppermute | solution.py:538
  27.2 0.2 collective-permute-start.4
  28.0 0.0 copy-start.9
  28.7 0.1 copy.32.flag_ref
  28.8 0.0 collective-permute-done.6.rest_2_
  28.8 1.6 %collective-permute-done.5.rest_1_ = f32[16,512]{1,0:T(8,128)S(1)} collective-permute-done((f32[16,512]{1,0:T(8,128)S(1)}, f32[16,512]{1,0:T(8,128)S(1)}, u32[]{:S(2)}, u32[]{:S(2)}) %collective-permute-start.5) | collective-permute-done | bytes 32800 | tf_op jit(solution)/shard_map/ppermute | solution.py:538
  30.4 0.2 collective-permute-done.4.rest_0_
  30.7 12.8 %shard_map.168.refs_0_.own_ref = f32[16,512]{1,0:T(8,128)S(1)} custom-call(f32[1]{0:T(128)S(6)} %copy.36.dt_ref, s32[2,1]{1,0:T(2,128)S(1)} %copy.32.flag_ref, s32[1]{0:T(128)S(6)} %copy.37.climb_ref, f32[40,512]{1,0:T(8,128)S(1)} %collective-permute-done.pl_ref, f32[40,512]{1,0:T(8,128)S(1)} %shard_map.165.po_ref, ...), custom_call_target="tpu_custom_call" | custom-call | flops 1000000000 | bytes 262144 | tf_op jit(solution)/shard_map/pallas_call | solution.py:525
  43.4 0.4 collective-permute-start.9
  43.8 0.0 collective-permute-start.8
  43.9 1.7 %collective-permute-start.7 = (f32[16,512]{1,0:T(8,128)S(1)}, f32[16,512]{1,0:T(8,128)S(1)}, u32[]{:S(2)}, u32[]{:S(2)}) collective-permute-start(f32[16,512]{1,0:T(8,128)S(1)} %shard_map.168.refs_0_.own_ref), channel_id=1, source_target_pairs={{0,1},{1,2},{2,3},{3,0},{4,5},{5,6},{6,7},{7,4},{8,9},{9,10},{10,1... | collective-permute-start | bytes 98312 | tf_op jit(solution)/shard_map/ppermute | solution.py:538
  45.5 1.9 %collective-permute-done.9.refs_3_ = f32[16,512]{1,0:T(8,128)S(1)} collective-permute-done((f32[16,512]{1,0:T(8,128)S(1)}, f32[16,512]{1,0:T(8,128)S(1)}, u32[]{:S(2)}, u32[]{:S(2)}) %collective-permute-start.9) | collective-permute-done | bytes 32800 | tf_op jit(solution)/shard_map/ppermute | solution.py:538
  47.4 1.3 %collective-permute-done.8.refs_2_ = f32[16,512]{1,0:T(8,128)S(1)} collective-permute-done((f32[16,512]{1,0:T(8,128)S(1)}, f32[16,512]{1,0:T(8,128)S(1)}, u32[]{:S(2)}, u32[]{:S(2)}) %collective-permute-start.8) | collective-permute-done | bytes 32800 | tf_op jit(solution)/shard_map/ppermute | solution.py:538
  48.7 1.5 %collective-permute-done.7.refs_1_ = f32[16,512]{1,0:T(8,128)S(1)} collective-permute-done((f32[16,512]{1,0:T(8,128)S(1)}, f32[16,512]{1,0:T(8,128)S(1)}, u32[]{:S(2)}, u32[]{:S(2)}) %collective-permute-start.7) | collective-permute-done | bytes 32800 | tf_op jit(solution)/shard_map/ppermute | solution.py:538
  50.1 0.2 shard_map.169
  50.4 0.1 collective-permute-start.12
  50.4 1.2 %collective-permute-start.11 = (f32[8,128]{1,0:T(8,128)S(1)}, f32[8,128]{1,0:T(8,128)S(1)}, u32[]{:S(2)}, u32[]{:S(2)}) collective-permute-start(f32[8,128]{1,0:T(8,128)S(1)} %get-tuple-element.25.sums_ref), channel_id=1, source_target_pairs={{0,8},{4,12},{8,0},{12,4},{1,9},{5,13},{9,1},{13,5},{2,10},{6,14},... | collective-permute-start | bytes 12296 | tf_op jit(solution)/shard_map/ppermute | solution.py:538
  51.6 0.2 collective-permute-start.10
  51.7 0.0 collective-permute-done.12.rest_2_
  51.7 2.3 %collective-permute-done.11.rest_1_ = f32[8,128]{1,0:T(8,128)S(1)} collective-permute-done((f32[8,128]{1,0:T(8,128)S(1)}, f32[8,128]{1,0:T(8,128)S(1)}, u32[]{:S(2)}, u32[]{:S(2)}) %collective-permute-start.11) | collective-permute-done | bytes 4128 | tf_op jit(solution)/shard_map/ppermute | solution.py:538
  54.1 0.5 collective-permute-done.10.rest_0_
  54.6 0.7 %shard_map.170 = (f32[1,3,512]{2,1,0:T(4,128)S(1)}, f32[1,3,512]{2,1,0:T(4,128)S(1)}, f32[8,128]{1,0:T(8,128)S(1)}, f32[1,128]{1,0:T(1,128)}) custom-call(s32[1]{0:T(128)S(6)} %copy.37.climb_ref, f32[16,512]{1,0:T(8,128)S(1)} %shard_map.168.refs_0_.own_ref, f32[32,512]{1,0:T(8,128)S(1)} %get-tuple-element.24.state_ref, ...), custom_call_target="tpu_custom_call" | custom-call | bytes 262144 | tf_op jit(solution)/shard_map/pallas_call | solution.py:525
  55.3 0.6 %copy.33 = f32[1,3,512]{2,0,1:T(1,128)} copy(f32[1,3,512]{2,1,0:T(4,128)S(1)} %get-tuple-element.34) | data formatting | bytes 12288
  55.9 0.1 slice_reduce_fusion
  56.0 0.6 %reshape_squeeze.3 = f32[2,2,1]{1,0,2:T(2,128)} reshape(f32[4]{0:T(128)S(1)} %slice_reduce_fusion) | data formatting | bytes 32 | tf_op jit(solution)/shard_map/reshape;squeeze | solution.py:617
  56.6 0.6 %copy.34 = f32[1,3,512]{2,0,1:T(1,128)} copy(f32[1,3,512]{2,1,0:T(4,128)S(1)} %get-tuple-element.35) | data formatting | bytes 12288
  (12 shorter events, 0.0 us)
Async XLA Ops:
  1.3 0.9 %copy-start.2 = (s32[8,512]{1,0:T(8,128)S(1)}, s32[8,512]{1,0:T(8,128)}, u32[]{:S(2)}) copy-start(s32[8,512]{1,0:T(8,128)} %nbr_ref.1) | copy-start | bytes 49156
  1.3 0.9 %copy-start.4 = (s32[512]{0:T(512)S(1)}, s32[512]{0:T(512)}, u32[]{:S(2)}) copy-start(s32[512]{0:T(512)} %species_ref.1) | copy-start | bytes 6148
  1.3 0.9 %copy-start.5 = (s32[512]{0:T(512)S(1)}, s32[512]{0:T(512)}, u32[]{:S(2)}) copy-start(s32[512]{0:T(512)} %counts_ref.1) | copy-start | bytes 6148
  2.2 6.1 %copy-start.8 = (f32[1,3,512]{2,0,1:T(1,128)S(1)}, f32[1,3,512]{2,0,1:T(1,128)}, u32[]{:S(2)}) copy-start(f32[1,3,512]{2,0,1:T(1,128)} %param.15) | copy-start | bytes 18436
  2.3 6.1 %copy-start = (f32[2,64,64]{2,1,0:T(8,128)S(1)}, f32[2,64,64]{2,1,0:T(8,128)}, u32[]{:S(2)}) copy-start(f32[2,64,64]{2,1,0:T(8,128)} %mix_ref.1) | copy-start | bytes 98308
  2.3 6.1 %copy-start.1 = (f32[2,64,64]{2,1,0:T(8,128)S(1)}, f32[2,64,64]{2,1,0:T(8,128)}, u32[]{:S(2)}) copy-start(f32[2,64,64]{2,1,0:T(8,128)} %update_ref.1) | copy-start | bytes 98308
  2.3 6.1 %copy-start.3 = (f32[2,8,64]{2,1,0:T(8,128)S(1)}, f32[2,8,64]{2,1,0:T(8,128)}, u32[]{:S(2)}) copy-start(f32[2,8,64]{2,1,0:T(8,128)} %radial_ref.1) | copy-start | bytes 12292
  2.3 6.1 %copy-start.6 = (f32[2,64]{1,0:T(2,128)S(1)}, f32[2,64]{1,0:T(2,128)}, u32[]{:S(2)}) copy-start(f32[2,64]{1,0:T(2,128)} %embed_ref.1) | copy-start | bytes 1540
  2.3 6.1 %copy-start.7 = (f32[64]{0:T(128)S(1)}, f32[64]{0:T(128)}, u32[]{:S(2)}) copy-start(f32[64]{0:T(128)} %readout_ref.1) | copy-start | bytes 772
  2.3 11.5 %collective-permute-start.1 = (f32[40,512]{1,0:T(8,128)S(1)}, f32[40,512]{1,0:T(8,128)S(1)}, u32[]{:S(2)}, u32[]{:S(2)}) collective-permute-start(f32[40,512]{1,0:T(8,128)S(1)} %shard_map.165.po_ref), channel_id=1, source_target_pairs={{0,12},{4,0},{8,4},{12,8},{1,13},{5,1},{9,5},{13,9},{2,14},{6,2},{... | collective-permute-start | bytes 245768 | tf_op jit(solution)/shard_map/ppermute | solution.py:543
  4.8 9.1 %collective-permute-start = (f32[40,512]{1,0:T(8,128)S(1)}, f32[40,512]{1,0:T(8,128)S(1)}, u32[]{:S(2)}, u32[]{:S(2)}) collective-permute-start(f32[40,512]{1,0:T(8,128)S(1)} %shard_map.165.po_ref), channel_id=1, source_target_pairs={{0,4},{4,8},{8,12},{12,0},{1,5},{5,9},{9,13},{13,1},{2,6},{6,10},{... | collective-permute-start | bytes 245768 | tf_op jit(solution)/shard_map/ppermute | solution.py:543
  4.8 5.0 %collective-permute-start.3 = (f32[1,3,512]{2,1,0:T(4,128)S(1)}, f32[1,3,512]{2,1,0:T(4,128)S(1)}, u32[]{:S(2)}, u32[]{:S(2)}) collective-permute-start(f32[1,3,512]{2,1,0:T(4,128)S(1)} %copy.27.x_ref), channel_id=1, source_target_pairs={{0,3},{1,0},{2,1},{3,2},{4,7},{5,4},{6,5},{7,6},{8,11},{9,8},{10,9... | collective-permute-start | bytes 18440 | tf_op jit(solution)/shard_map/ppermute | solution.py:543
  8.4 5.4 %collective-permute-start.2 = (f32[1,3,512]{2,1,0:T(4,128)S(1)}, f32[1,3,512]{2,1,0:T(4,128)S(1)}, u32[]{:S(2)}, u32[]{:S(2)}) collective-permute-start(f32[1,3,512]{2,1,0:T(4,128)S(1)} %copy.27.x_ref), channel_id=1, source_target_pairs={{0,1},{1,2},{2,3},{3,0},{4,5},{5,6},{6,7},{7,4},{8,9},{9,10},{10,1... | collective-permute-start | bytes 18440 | tf_op jit(solution)/shard_map/ppermute | solution.py:543
  26.1 2.7 %collective-permute-start.6 = (f32[16,512]{1,0:T(8,128)S(1)}, f32[16,512]{1,0:T(8,128)S(1)}, u32[]{:S(2)}, u32[]{:S(2)}) collective-permute-start(f32[16,512]{1,0:T(8,128)S(1)} %shard_map.167.own_ref), channel_id=1, source_target_pairs={{0,12},{4,0},{8,4},{12,8},{1,13},{5,1},{9,5},{13,9},{2,14},{6,2},{... | collective-permute-start | bytes 98312 | tf_op jit(solution)/shard_map/ppermute | solution.py:538
  26.4 4.0 %collective-permute-start.5 = (f32[16,512]{1,0:T(8,128)S(1)}, f32[16,512]{1,0:T(8,128)S(1)}, u32[]{:S(2)}, u32[]{:S(2)}) collective-permute-start(f32[16,512]{1,0:T(8,128)S(1)} %shard_map.167.own_ref), channel_id=1, source_target_pairs={{0,8},{4,12},{8,0},{12,4},{1,9},{5,13},{9,1},{13,5},{2,10},{6,14},... | collective-permute-start | bytes 98312 | tf_op jit(solution)/shard_map/ppermute | solution.py:538
  27.2 3.5 %collective-permute-start.4 = (f32[16,512]{1,0:T(8,128)S(1)}, f32[16,512]{1,0:T(8,128)S(1)}, u32[]{:S(2)}, u32[]{:S(2)}) collective-permute-start(f32[16,512]{1,0:T(8,128)S(1)} %shard_map.167.own_ref), channel_id=1, source_target_pairs={{0,4},{4,8},{8,12},{12,0},{1,5},{5,9},{9,13},{13,1},{2,6},{6,10},{... | collective-permute-start | bytes 98312 | tf_op jit(solution)/shard_map/ppermute | solution.py:538
  28.0 0.7 %copy-start.9 = (s32[2,1]{0,1:T(1,128)S(1)}, s32[2,1]{0,1:T(1,128)}, u32[]{:S(2)}) copy-start(s32[2,1]{0,1:T(1,128)} %param.17) | copy-start | bytes 28
  43.4 4.0 %collective-permute-start.9 = (f32[16,512]{1,0:T(8,128)S(1)}, f32[16,512]{1,0:T(8,128)S(1)}, u32[]{:S(2)}, u32[]{:S(2)}) collective-permute-start(f32[16,512]{1,0:T(8,128)S(1)} %shard_map.168.refs_0_.own_ref), channel_id=1, source_target_pairs={{0,3},{1,0},{2,1},{3,2},{4,7},{5,4},{6,5},{7,6},{8,11},{9,8},{10,9... | collective-permute-start | bytes 98312 | tf_op jit(solution)/shard_map/ppermute | solution.py:538
  43.8 4.8 %collective-permute-start.8 = (f32[16,512]{1,0:T(8,128)S(1)}, f32[16,512]{1,0:T(8,128)S(1)}, u32[]{:S(2)}, u32[]{:S(2)}) collective-permute-start(f32[16,512]{1,0:T(8,128)S(1)} %shard_map.168.refs_0_.own_ref), channel_id=1, source_target_pairs={{0,2},{1,3},{2,0},{3,1},{4,6},{5,7},{6,4},{7,5},{8,10},{9,11},{10,... | collective-permute-start | bytes 98312 | tf_op jit(solution)/shard_map/ppermute | solution.py:538
  43.9 6.3 %collective-permute-start.7 = (f32[16,512]{1,0:T(8,128)S(1)}, f32[16,512]{1,0:T(8,128)S(1)}, u32[]{:S(2)}, u32[]{:S(2)}) collective-permute-start(f32[16,512]{1,0:T(8,128)S(1)} %shard_map.168.refs_0_.own_ref), channel_id=1, source_target_pairs={{0,1},{1,2},{2,3},{3,0},{4,5},{5,6},{6,7},{7,4},{8,9},{9,10},{10,1... | collective-permute-start | bytes 98312 | tf_op jit(solution)/shard_map/ppermute | solution.py:538
  50.4 1.4 %collective-permute-start.12 = (f32[8,128]{1,0:T(8,128)S(1)}, f32[8,128]{1,0:T(8,128)S(1)}, u32[]{:S(2)}, u32[]{:S(2)}) collective-permute-start(f32[8,128]{1,0:T(8,128)S(1)} %get-tuple-element.25.sums_ref), channel_id=1, source_target_pairs={{0,12},{4,0},{8,4},{12,8},{1,13},{5,1},{9,5},{13,9},{2,14},{6,2},{... | collective-permute-start | bytes 12296 | tf_op jit(solution)/shard_map/ppermute | solution.py:538
  50.4 3.7 %collective-permute-start.11 = (f32[8,128]{1,0:T(8,128)S(1)}, f32[8,128]{1,0:T(8,128)S(1)}, u32[]{:S(2)}, u32[]{:S(2)}) collective-permute-start(f32[8,128]{1,0:T(8,128)S(1)} %get-tuple-element.25.sums_ref), channel_id=1, source_target_pairs={{0,8},{4,12},{8,0},{12,4},{1,9},{5,13},{9,1},{13,5},{2,10},{6,14},... | collective-permute-start | bytes 12296 | tf_op jit(solution)/shard_map/ppermute | solution.py:538
  51.6 3.0 %collective-permute-start.10 = (f32[8,128]{1,0:T(8,128)S(1)}, f32[8,128]{1,0:T(8,128)S(1)}, u32[]{:S(2)}, u32[]{:S(2)}) collective-permute-start(f32[8,128]{1,0:T(8,128)S(1)} %get-tuple-element.25.sums_ref), channel_id=1, source_target_pairs={{0,4},{4,8},{8,12},{12,0},{1,5},{5,9},{9,13},{13,1},{2,6},{6,10},{... | collective-permute-start | bytes 12296 | tf_op jit(solution)/shard_map/ppermute | solution.py:538

commit v2 on v1

--- a/solution.py
+++ b/solution.py
@@ -24,6 +24,7 @@
 ROW_X = 32
 ROW_COUNT = 35
 ROW_KIND = 36
+ROW_V = 37
 PACK_ROWS = 40
 NT = (((1,), (1,)), ((), ()))
 
@@ -57,18 +58,18 @@
     return lax.dot_general(a, b, NT, preferred_element_type=F32)
 
 
-def pack_kernel(x_ref, species_ref, nbr_ref, counts_ref, lattice_ref, out_ref):
+def pack_kernel(x_ref, v_ref, species_ref, nbr_ref, counts_ref, lattice_ref, out_ref):
     out_ref[0:8, :] = nbr_ref[...].astype(F32)
     for c in range(3):
-        out_ref[8 + 8 * c : 16 + 8 * c, :] = lattice_ref[:, c, :]
-    out_ref[ROW_X : ROW_X + 3, :] = x_ref[0]
+        out_ref[8 + 8 * c : 16 + 8 * c, :] = lattice_ref[c]
+        out_ref[ROW_X + c : ROW_X + c + 1, :] = x_ref[c]
+        out_ref[ROW_V + c : ROW_V + c + 1, :] = v_ref[c]
     out_ref[ROW_COUNT : ROW_COUNT + 1, :] = counts_ref[...].astype(F32).reshape(1, -1)
     out_ref[ROW_KIND : ROW_KIND + 1, :] = species_ref[...].astype(F32).reshape(1, -1)
-    out_ref[ROW_KIND + 1 : PACK_ROWS, :] = jnp.zeros((PACK_ROWS - ROW_KIND - 1, out_ref.shape[1]), F32)
 
 
 def weight_kernel(
-    embed_ref, radial_ref, mix_ref, update_ref, readout_ref, l1_ref, l2_ref, l3_ref, l4_ref, l5_ref, l6_ref, col_ref
+    embed_ref, radial_ref, mix_ref, update_ref, readout_ref, l1_ref, l2_ref, l3_ref, l5_ref, l6_ref, col_ref
 ):
     eye = (
         lax.broadcasted_iota(jnp.int32, (CHANNELS, CHANNELS), 0)
@@ -91,7 +92,6 @@
     l2_ref[...] = left_stack(turned(folded)).astype(BF16)
     high, low = split(turned(second))
     l3_ref[...] = jnp.concatenate([high, high, low, jnp.zeros_like(high)], axis=1).astype(BF16)
-    l4_ref[...] = left_stack(jnp.concatenate([second, jnp.zeros_like(second)], axis=0)).astype(BF16)
     l5_ref[...] = left_stack(folded).astype(BF16)
     l6_ref[...] = left_stack(first).astype(BF16)
     readout = readout_ref[...].reshape(1, CHANNELS)
@@ -123,12 +123,17 @@
 
 
 def force_parts(packs, weights, scr):
-    l1, l2, l3, l4, l5, l6, col = weights
-    (xs, widx, kinds, geo, bst, bpr, sst, ghl, slope, hot, dg, dmat, acc) = scr
+    l1, l2, l3, l5, l6, col = weights
+    (xs, widx, kinds, geo, bst, bps, bpr, sst, ghl, slope, hot, dg, pulls, acc) = scr
     centre = 2.0 + 0.5 * lax.broadcasted_iota(jnp.int32, (BASIS, LANES), 0).astype(F32)
     slot = lax.broadcasted_iota(jnp.int32, (SLOTS, LANES), 0)
-
-    for b in range(1, 11):
+    row_id = lax.broadcasted_iota(jnp.int32, (3 * LANES, LANES), 0)
+
+    def part_rows(value):
+        high, low = split(value)
+        return jnp.concatenate([high, low], axis=0).astype(BF16)
+
+    def pairs(b):
         pack = packs[b // 4]
         lanes = slice((b % 4) * LANES, (b % 4 + 1) * LANES)
         index = pack[0:8, lanes].astype(jnp.int32) - LANES * (b % 4)
@@ -155,8 +160,8 @@
         sine, cosine = sin_cos(turns * math.pi)
         envelope = cosine * cosine * live
         slant = cosine * sine * live * (-math.pi / 6.0)
-        kinds[b] = kind
         if 3 <= b <= 8:
+            kinds[b] = kind
             for c in range(3):
                 geo[b, c] = vec[c]
             geo[b, 3] = 1.0 / dist
@@ -171,91 +176,119 @@
             total_kind = total_kind + value * wide_row(kind, k)
             cols = slice(k * LANES, (k + 1) * LANES)
             if 2 <= b <= 9:
-                high, low = split(value)
-                bst[b, 0:8, cols] = high
-                bst[b, 8:16, cols] = low
+                bst[b, :, cols] = part_rows(value)
             if 3 <= b <= 8:
-                bpr[b, :, cols] = gauss * (wide_row(slant, k) - 8.0 * away * env_k)
-        both = jnp.concatenate([total, total_kind], axis=0)
-        high, low = split(both)
-        sst[b] = jnp.concatenate([high, low, high], axis=0).astype(BF16)
+                value = gauss * (wide_row(slant, k) - 8.0 * away * env_k)
+                bpr[b, :, cols] = value
+                bps[b, :, cols] = part_rows(value)
+        high, low = split(jnp.concatenate([total, total_kind], axis=0))
+        sst[:, b * LANES : (b + 1) * LANES] = jnp.concatenate([high, low, high], axis=0).astype(BF16)
 
     for b in range(1, 11):
-        message = mm(l1[...], sst[b])
-        value, steep = silu_parts(message)
+        pairs(b)
+
+    for b in range(1, 11, 2):
+        cols = slice(b * LANES, (b + 2) * LANES)
+        value, steep = silu_parts(mm(l1[...], sst[:, cols]))
         sent = mm(l2[...], right_stack(value))
-        sent = sent + col[0] + col[1] * jnp.broadcast_to(xs[b, 3:4, :], (CHANNELS, LANES))
-        ghl[b] = pair_stack(sent)
-        if 3 <= b <= 8:
-            slope[b] = steep
-
-    for b in range(1, 11):
-        dg[b] = jnp.zeros((CHANNELS, LANES), F32)
-
-    row_id = lax.broadcasted_iota(jnp.int32, (3 * LANES, LANES), 0)
-
-    def second(b, carry):
+        for i in range(2):
+            one = sent[:, i * LANES : (i + 1) * LANES]
+            one = one + col[0] + col[1] * jnp.broadcast_to(xs[b + i, 3:4, :], (CHANNELS, LANES))
+            ghl[:, (b + i) * LANES : (b + i + 1) * LANES] = pair_stack(one)
+        slope[:, cols] = steep
+
+    def mark(b):
         index = widx[b]
         for k in range(SLOTS):
             same = row_id == jnp.broadcast_to(index[k : k + 1, :], (3 * LANES, LANES))
             hot[b, :, k * LANES : (k + 1) * LANES] = jnp.where(same, 1.0, 0.0).astype(BF16)
-        window = jnp.concatenate([ghl[b - 1], ghl[b], ghl[b + 1]], axis=1)
-        got = mm(window, hot[b])
+
+    def reach(b, first, last):
+        return [w for w in range(3) if first <= b - 1 + w <= last]
+
+    def spread(left, b, first, last):
+        ws = reach(b, first, last)
+        return ws, mm_nt(left, hot[b, ws[0] * LANES : (ws[-1] + 1) * LANES, :])
+
+    started = set()
+
+    def gather_and_return(b):
+        got = mm(ghl[:, (b - 1) * LANES : (b + 2) * LANES], hot[b])
+        if b < 9:
+            mark(b + 1)
         got = got[:CHANNELS] + got[CHANNELS:]
         basis = bst[b]
-        stack = jnp.concatenate([basis, basis], axis=0).astype(BF16)
-        radial = mm(l3[...], stack)
+        radial = mm(l3[...], jnp.concatenate([basis, basis], axis=0))
         message = jnp.zeros((CHANNELS, LANES), F32)
         for k in range(SLOTS):
             cols = slice(k * LANES, (k + 1) * LANES)
             message = message + radial[:, cols] * got[:, cols]
         _, steep = silu_parts(message)
-        back = col[3] * steep
-        back = jnp.concatenate([back] * SLOTS, axis=1)
-        out = mm_nt(pair_stack(radial * back), hot[b])
+        back = jnp.concatenate([col[3] * steep] * SLOTS, axis=1)
+        ws, out = spread(pair_stack(radial * back), b, 3, 8)
         out = out[:CHANNELS] + out[CHANNELS:]
-        for w in range(3):
-            dg[b - 1 + w] += out[:, w * LANES : (w + 1) * LANES]
-        dmat[b] = mm(l4[...], right_stack(got * back))[0:8]
-        return carry
-
-    lax.fori_loop(2, 10, second, 0)
-
-    for b in range(3, 9):
-        for c in range(3):
-            acc[b, c] = jnp.zeros((8, LANES), F32)
-    acc[2] = jnp.zeros((3, 8, LANES), F32)
-    acc[9] = jnp.zeros((3, 8, LANES), F32)
-
-    def last(b, carry):
-        steep = mm(l5[...], right_stack(dg[b])) + col[2]
-        sums = mm(l6[...], right_stack(steep * slope[b]))
+        for i, w in enumerate(ws):
+            target = b - 1 + w
+            piece = out[:, i * LANES : (i + 1) * LANES]
+            where = slice(target * LANES, (target + 1) * LANES)
+            if target in started:
+                dg[:, where] += piece
+            else:
+                dg[:, where] = piece
+                started.add(target)
+        if 3 <= b <= 8:
+            basis = bps[b]
+            steepness = mm(l3[...], jnp.concatenate([basis, basis], axis=0))
+            pull = got * back * steepness
+            total = pull[0:8]
+            for i in range(1, CHANNELS // 8):
+                total = total + pull[8 * i : 8 * i + 8]
+            pulls[b] = total
+
+    mark(2)
+    for b in range(2, 10):
+        gather_and_return(b)
+
+    begun = set()
+
+    def put(b, c, value):
+        if (b, c) in begun:
+            acc[b, c] += value
+        else:
+            acc[b, c] = value
+            begun.add((b, c))
+
+    def finish(b, sums):
         kind = kinds[b]
         rows = []
         for k in range(SLOTS):
             cols = slice(k * LANES, (k + 1) * LANES)
-            weight = dmat[b, :, cols] + sums[0:8] + wide_row(kind, k) * sums[8:16]
-            rows.append(jnp.sum(bpr[b, :, cols] * weight, axis=0, keepdims=True))
+            weight = sums[0:8] + wide_row(kind, k) * sums[8:16]
+            rows.append(jnp.sum(bpr[b, :, cols] * weight + pulls[b, :, cols], axis=0, keepdims=True))
         pull = jnp.concatenate(rows, axis=0) * geo[b, 3]
         pieces = []
         for c in range(3):
             value = pull * geo[b, c]
-            acc[b, c] -= value
+            if 4 <= b <= 7:
+                put(b, c, -value)
             pieces.append(split(value))
         lines = []
         for h in range(2):
             for c in range(3):
-                lines.append(
-                    jnp.concatenate([jnp.where(slot == k, pieces[c][h], 0.0) for k in range(SLOTS)], axis=1)
-                )
-        out = mm_nt(jnp.concatenate(lines, axis=0).astype(BF16), hot[b])
+                lines.append(jnp.concatenate([jnp.where(slot == k, pieces[c][h], 0.0) for k in range(SLOTS)], axis=1))
+        ws, out = spread(jnp.concatenate(lines, axis=0).astype(BF16), b, 4, 7)
         for c in range(3):
             both = out[8 * c : 8 * c + 8] + out[24 + 8 * c : 32 + 8 * c]
-            for w in range(3):
-                acc[b - 1 + w, c] += both[:, w * LANES : (w + 1) * LANES]
-        return carry
-
-    lax.fori_loop(3, 9, last, 0)
+            for i, w in enumerate(ws):
+                put(b - 1 + w, c, both[:, i * LANES : (i + 1) * LANES])
+
+    for b in range(3, 9, 2):
+        cols = slice(b * LANES, (b + 2) * LANES)
+        steep = mm(l5[...], right_stack(dg[:, cols]))
+        steep = steep + jnp.concatenate([col[2], col[2]], axis=1)
+        sums = mm(l6[...], right_stack(steep * slope[:, cols]))
+        for i in range(2):
+            finish(b + i, sums[:, i * LANES : (i + 1) * LANES])
 
 
 def own_force(acc, c):
@@ -282,35 +315,51 @@
 
 
 def scratch():
+    wide = 12 * LANES
     return [
         pltpu.VMEM((12, 8, LANES), F32),
         pltpu.VMEM((12, 8, LANES), jnp.int32),
         pltpu.VMEM((12, 8, LANES), F32),
         pltpu.VMEM((12, 4, 8, LANES), F32),
-        pltpu.VMEM((12, 16, SLOTS * LANES), F32),
+        pltpu.VMEM((12, 16, SLOTS * LANES), BF16),
+        pltpu.VMEM((12, 16, SLOTS * LANES), BF16),
         pltpu.VMEM((12, 8, SLOTS * LANES), F32),
-        pltpu.VMEM((12, 48, LANES), BF16),
-        pltpu.VMEM((12, 2 * CHANNELS, LANES), BF16),
-        pltpu.VMEM((12, CHANNELS, LANES), F32),
+        pltpu.VMEM((48, wide), BF16),
+        pltpu.VMEM((2 * CHANNELS, wide), BF16),
+        pltpu.VMEM((CHANNELS, wide), F32),
         pltpu.VMEM((12, 3 * LANES, SLOTS * LANES), BF16),
-        pltpu.VMEM((12, CHANNELS, LANES), F32),
+        pltpu.VMEM((CHANNELS, wide), F32),
         pltpu.VMEM((12, 8, SLOTS * LANES), F32),
         pltpu.VMEM((12, 3, 8, LANES), F32),
     ]
 
 
-def first_kernel(images, pl_ref, po_ref, pr_ref, v_ref, before_ref, after_ref, *rest):
-    weights, out_ref, scr = rest[:7], rest[7], rest[8:]
+def first_kernel(pl_ref, po_ref, pr_ref, *rest):
+    weights, out_ref, scr = rest[:6], rest[6], rest[7:]
     packs = [pl_ref, po_ref, pr_ref]
     fill_region(scr[0], packs, lambda s: packs[s][ROW_X : ROW_X + 3, :])
     force_parts(packs, weights, scr)
-    acc = scr[-1]
-    force = jnp.concatenate([own_force(acc, c) for c in range(3)], axis=0)
+    for c in range(3):
+        out_ref[c : c + 1, :] = own_force(scr[-1], c)
+
+
+def rows_of(ref):
+    return jnp.concatenate([ref[c] for c in range(3)], axis=0)
+
+
+def block_row(*values):
+    values = list(values) + [jnp.zeros((1, LANES), F32)] * (SLAB_BLOCKS - len(values))
+    return jnp.concatenate(values, axis=1)
+
+
+def blend_kernel(images, force_ref, po_ref, *rest):
+    before_ref, after_ref, out_ref = rest[0], rest[images - 2], rest[-1]
     here = lax.axis_index("img")
     x = po_ref[ROW_X : ROW_X + 3, :]
-    v = v_ref[0]
-    before = jnp.where(here > 0, before_ref[0], 0.0)
-    after = jnp.where(here < images - 1, after_ref[0], 0.0)
+    v = po_ref[ROW_V : ROW_V + 3, :]
+    force = force_ref[...]
+    before = jnp.where(here > 0, rows_of(before_ref), 0.0)
+    after = jnp.where(here < images - 1, rows_of(after_ref), 0.0)
     tangent = after - before
     plus = after - x
     minus = x - before
@@ -326,11 +375,11 @@
         ],
         axis=0,
     )
+    sums = jnp.broadcast_to(lane_total(sums), (8, LANES))
     out_ref[0:3, :] = force
     out_ref[3:6, :] = tangent
-    out_ref[6:9, :] = v
-    out_ref[9:15, :] = jnp.broadcast_to(lane_total(sums)[0:6], (6, x.shape[1]))
-    out_ref[15:16, :] = jnp.zeros((1, x.shape[1]), F32)
+    out_ref[6:7, :] = block_row(*[sums[i : i + 1] for i in range(4)])
+    out_ref[7:8, :] = block_row(sums[4:5], sums[5:6])
 
 
 def step_numbers(ft, ff, tt, pp, mn, vv, dt, alpha, flagged, climbing, inside):
@@ -358,13 +407,14 @@
 
 def second_kernel(images, others, dt_ref, flag_ref, climb_ref, pl_ref, po_ref, pr_ref, own_ref, *rest):
     heard, rest = rest[:others], rest[others:]
-    weights, out_ref, scr = rest[:7], rest[7], rest[8:]
+    weights, out_ref, scr = rest[:6], rest[6], rest[7:]
     packs = [pl_ref, po_ref, pr_ref]
     here = lax.axis_index("img")
-    sums = own_ref[8:16, 0:LANES]
+    sums = own_ref[6:8, :]
     for one in heard:
-        sums = sums + one[8:16, 0:LANES]
-    ft, ff, tt, pp, mn, vv = (sums[1 + i : 2 + i, :] for i in range(6))
+        sums = sums + one[6:8, :]
+    ft, ff, tt, pp = (sums[0:1, i * LANES : (i + 1) * LANES] for i in range(4))
+    mn, vv = (sums[1:2, i * LANES : (i + 1) * LANES] for i in range(2))
     shape = (1, LANES)
     along, spring, keep, pull, side, dt, alpha = step_numbers(
         ft,
@@ -384,22 +434,18 @@
     def wide(s):
         return jnp.concatenate([s] * SLAB_BLOCKS, axis=1)
 
-    def speed(m):
-        return wide(keep) * m[6:9, :] + wide(pull) * m[0:3, :] + wide(side) * m[3:6, :]
-
-    moved = [p[ROW_X : ROW_X + 3, :] + wide(dt) * speed(m) for p, m in zip(packs, messages)]
+    speeds = [
+        wide(keep) * p[ROW_V : ROW_V + 3, :] + wide(pull) * m[0:3, :] + wide(side) * m[3:6, :]
+        for p, m in zip(packs, messages)
+    ]
+    moved = [p[ROW_X : ROW_X + 3, :] + wide(dt) * s for p, s in zip(packs, speeds)]
     fill_region(scr[0], packs, lambda s: moved[s])
     force_parts(packs, weights, scr)
-    acc = scr[-1]
-    out_ref[0:3, :] = moved[1]
-    out_ref[3:6, :] = speed(own_ref)
-    out_ref[6:9, :] = jnp.concatenate([own_force(acc, c) for c in range(3)], axis=0)
-    out_ref[9:10, :] = wide(dt)
-    out_ref[10:11, :] = wide(alpha)
-    out_ref[11:12, :] = jnp.full((1, out_ref.shape[1]), flag_ref[1, 0], jnp.int32).astype(F32)
-    out_ref[12:13, :] = wide(along)
-    out_ref[13:14, :] = wide(spring)
-    out_ref[14:16, :] = jnp.zeros((2, out_ref.shape[1]), F32)
+    out_ref[0:3, :] = speeds[1]
+    for c in range(3):
+        out_ref[3 + c : 4 + c, :] = own_force(scr[-1], c)
+    out_ref[6:7, :] = block_row(dt, alpha, jnp.full(shape, flag_ref[0, 1], jnp.int32).astype(F32))
+    out_ref[7:8, :] = block_row(along, spring)
 
 
 PRODUCTS = (
@@ -410,15 +456,22 @@
 
 
 def gram_kernel(images, *refs):
-    messages, out_ref, state_ref = refs[:images], refs[images], refs[images + 1]
+    messages, starts, (out_ref, state_ref) = refs[:images], refs[images : 2 * images], refs[2 * images :]
     rows = 8 * ((images + 7) // 8)
     here = lax.axis_index("img")
     width = state_ref.shape[1]
     blank = jnp.zeros((rows - images, width), F32)
 
+    def padded(lines):
+        return jnp.concatenate(lines + ([blank[:, : lines[0].shape[1]]] if rows > images else []), axis=0)
+
     def gathered(row):
-        lines = [m[row : row + 1, :] for m in messages]
-        return jnp.concatenate(lines + ([blank] if rows > images else []), axis=0)
+        return padded([m[row : row + 1, :] for m in messages])
+
+    def number_of(i):
+        return padded([m[6:7, i * LANES : (i + 1) * LANES] for m in messages])
+
+    steps = jnp.concatenate([number_of(0)] * SLAB_BLOCKS, axis=1)
 
     def shifted(value, by):
         lines = [value[(s + by) % images : (s + by) % images + 1, :] for s in range(images)]
@@ -431,7 +484,8 @@
     has_before = (number > 0) & (offset < images)
     totals = [jnp.zeros((rows, width), F32) for _ in PRODUCTS]
     for c in range(3):
-        x, v, f = gathered(c), gathered(3 + c), gathered(6 + c)
+        v, f = gathered(c), gathered(3 + c)
+        x = padded([s[c] for s in starts]) + steps * v
         after = jnp.where(has_after, shifted(x, -1), 0.0)
         before = jnp.where(has_before, shifted(x, 1), 0.0)
         t = after - before
@@ -441,13 +495,14 @@
         table["T"] = jnp.where(has_before, shifted(t, 1), 0.0)
         totals = [old + table[a] * table[b] for old, (a, b) in zip(totals, PRODUCTS)]
         state_ref[c : c + 1, :] = t[0:1]
+        state_ref[3 + c : 4 + c, :] = x[0:1]
     lane = lax.broadcasted_iota(jnp.int32, (rows, LANES), 1)
     result = jnp.zeros((rows, LANES), F32)
     for q, one in enumerate(totals):
         result = jnp.where(lane == q, jnp.broadcast_to(lane_total(one), (rows, LANES)), result)
     out_ref[...] = result
     for i in range(3):
-        state_ref[8 + rows * i : 8 + rows * (i + 1), :] = gathered(9 + i)
+        state_ref[8 : 8 + rows, i * LANES : (i + 1) * LANES] = number_of(i)
 
 
 def final_kernel(images, others, atoms, climb_ref, own_ref, state_ref, sums_ref, *rest):
@@ -466,7 +521,7 @@
     inside = (number >= 1) & (number <= images - 2) & (offset < images)
     has_before = (number > 0) & (offset < images)
     climb = jnp.full((rows, LANES), climb_ref[0], jnp.int32)
-    dt0, alpha0, flag = (state_ref[8 + rows * i : 8 + rows * (i + 1), 0:LANES] for i in range(3))
+    dt0, alpha0, flag = (state_ref[8 : 8 + rows, i * LANES : (i + 1) * LANES] for i in range(3))
     along, spring, keep, pull, side, dt, _ = step_numbers(
         got["f", "t"],
         got["f", "f"],
@@ -504,17 +559,18 @@
     squared = got["d", "d"] + mine + shifted(mine) + 2.0 * both
     segment = jnp.sqrt(jnp.maximum(squared, 0.0) * (1.0 / (3.0 * atoms)))
     path = jnp.sum(jnp.where(offset <= here, segment, 0.0), axis=0, keepdims=True)
-    path_ref[...] = path
+    path_ref[...] = path[:, 0:1]
 
     def wide(s):
         return jnp.concatenate([s[0:1, :]] * SLAB_BLOCKS, axis=1)
 
-    speed = wide(keep) * own_ref[3:6, :] + wide(pull) * own_ref[6:9, :] + wide(side) * state_ref[0:3, :]
-    v_ref[0] = speed
-    x_ref[0] = own_ref[0:3, :] + wide(dt) * speed
-    band_ref[...] = jnp.concatenate(
-        [own_ref[12:14, 0:LANES], along[0:1], spring[0:1], jnp.zeros((4, LANES), F32)], axis=0
-    )
+    speed = wide(keep) * own_ref[0:3, :] + wide(pull) * own_ref[3:6, :] + wide(side) * state_ref[0:3, :]
+    moved = state_ref[3:6, :] + wide(dt) * speed
+    for c in range(3):
+        v_ref[c] = speed[c : c + 1]
+        x_ref[c] = moved[c : c + 1]
+    band_ref[0] = jnp.concatenate([own_ref[7:8, 0:1], own_ref[7:8, LANES : LANES + 1]], axis=1)
+    band_ref[1] = jnp.concatenate([along[0:1, 0:1], spring[0:1, 0:1]], axis=1)
 
 
 VMEM_SPEC = pl.BlockSpec(memory_space=pltpu.VMEM)
@@ -564,16 +620,22 @@
     domains = lax.axis_size("dom")
     assert disp.shape[0] == 1 and atoms == SLAB_BLOCKS * LANES and domains >= 3
     shape = jax.ShapeDtypeStruct
-    before, after = ring(disp, "img", 1), ring(disp, "img", -1)
-    pack = call(pack_kernel, shape((PACK_ROWS, atoms), F32), (), (disp, species, neighbours, counts, lattice))
+    x = jnp.transpose(disp, (1, 0, 2))
+    v = jnp.transpose(veloc, (1, 0, 2))
+    pack = call(
+        pack_kernel,
+        shape((PACK_ROWS, atoms), F32),
+        (),
+        (x, v, species, neighbours, counts, jnp.transpose(lattice, (1, 0, 2))),
+    )
     left, right = ring(pack, "dom", 1), ring(pack, "dom", -1)
+    starts = around(x, "img")
     weights = call(
         weight_kernel,
         (
             shape((CHANNELS, 48), BF16),
             shape((CHANNELS, 192), BF16),
             shape((CHANNELS, 32), BF16),
-            shape((16, 192), BF16),
             shape((CHANNELS, 192), BF16),
             shape((16, 192), BF16),
             shape((4, CHANNELS, LANES), F32),
@@ -582,19 +644,17 @@
         (embed, radial_weight, mix_weight, update_weight, readout),
         flops=10000000,
     )
+    force = call(
+        first_kernel, shape((3, atoms), F32), (), (left, pack, right, *weights), scratch(), flops=1000000000
+    )
     message = call(
-        functools.partial(first_kernel, images),
-        shape((16, atoms), F32),
-        (),
-        (left, pack, right, veloc, before, after, *weights),
-        scratch(),
-        flops=1000000000,
+        functools.partial(blend_kernel, images), shape((8, atoms), F32), (), (force, pack, *starts)
     )
     heard = around(message, "dom")
     state = call(
         functools.partial(second_kernel, images, len(heard)),
-        shape((16, atoms), F32),
-        (time_step, reset_flags, climb),
+        shape((8, atoms), F32),
+        (time_step, jnp.transpose(reset_flags), climb),
         (left, pack, right, message, *heard, *weights),
         scratch(),
         flops=1000000000,
@@ -603,18 +663,23 @@
     rows = 8 * ((images + 7) // 8)
     sums, extra = call(
         functools.partial(gram_kernel, images),
-        (shape((rows, LANES), F32), shape((8 + 3 * rows, atoms), F32)),
+        (shape((rows, LANES), F32), shape((8 + rows, atoms), F32)),
         (),
-        (state, *band),
+        (state, *band, x, *starts),
     )
     others = around(sums, "dom")
-    new_disp, new_veloc, records, path = call(
+    new_x, new_v, records, path = call(
         functools.partial(final_kernel, images, len(others), atoms * domains),
-        (shape(disp.shape, F32), shape(disp.shape, F32), shape((8, LANES), F32), shape((1, LANES), F32)),
+        (shape(x.shape, F32), shape(x.shape, F32), shape((2, 1, 2), F32), shape((1, 1), F32)),
         (climb,),
         (state, extra, sums, *others),
     )
-    return new_disp, new_veloc, records[0:4, 0].reshape(2, 2, 1), path[0, 0:1]
+    return (
+        jnp.transpose(new_x, (1, 0, 2)),
+        jnp.transpose(new_v, (1, 0, 2)),
+        jnp.transpose(records, (0, 2, 1)),
+        path.reshape(1),
+    )
 
 
 def solution(mesh):

time: 57.5 us -> 48.6 us (0.85)
  Pallas kernels: 26.5 us -> 18.7 us
  waiting for transfers between devices: 14.2 us -> 10.1 us
  starting transfers between devices: 10.8 us -> 14.4 us
  local copies, waits for them, and re-layouts: 3.68 us -> 2.91 us
    pallas_call x6 -> x7, Pallas kernels: 26.5 us -> 18.7 us  [call(): pl.pallas_call(body, out_shape=outs, in_specs=[SMEM_SPEC] * len(scalars)...]
    ppermute x9 -> x12, starting transfers between devices: 4.77 us -> 12 us  [around(): lax.ppermute(array, axis, [(i, (i + s) % count) for i in range(count)])]
    ppermute x4 -> x2, waiting for transfers between devices: 4.86 us -> 0.01 us  [ring(): lax.ppermute(array, axis, [(i, (i + by) % count) for i in range(count)])]
    ppermute x4 -> x2, starting transfers between devices: 6.04 us -> 2.43 us  [ring(): lax.ppermute(array, axis, [(i, (i + by) % count) for i in range(count)])]
    ppermute x9 -> x12, waiting for transfers between devices: 9.32 us -> 10.1 us  [around(): lax.ppermute(array, axis, [(i, (i + s) % count) for i in range(count)])]
    another operation x1 -> x0, local copies, waits for them, and re-layouts: 0.65 us -> none  [local(): return (new_disp, new_veloc, records[0:4, 0].reshape(2, 2, 1), path[0, 0:1])]
    unnamed x26 -> x22, local copies, waits for them, and re-layouts: 2.92 us -> 2.91 us
  transfers between devices with their start and end apart: 13 -> 14, of which waited for: 9 -> 7; matrix products, arithmetic and copies ran while one was open for 0% -> 0% of each run, Pallas kernels for 1% -> 17%
where the time goes in v2:
time: 48.6 us; the launch traced here: 48.2 us
  Pallas kernels  18.7 us (38%)
  starting transfers between devices  14.4 us (30%)
  waiting for transfers between devices  10.1 us (21%)
  local copies, waits for them, and re-layouts  2.91 us (6%)
  between operations  2.08 us (4%)
    pallas_call x7, Pallas kernels, call(): pl.pallas_call(body, out_shape=outs, in_specs=[SMEM_SPEC] * len(scalars)...  18.7 us
    ppermute x12, starting transfers between devices, around(): lax.ppermute(array, axis, [(i, (i + s) % count) for i in range(count)])  12 us
    ppermute x12, waiting for transfers between devices, around(): lax.ppermute(array, axis, [(i, (i + s) % count) for i in range(count)])  10.1 us
    unnamed x22, local copies, waits for them, and re-layouts  2.91 us
    ppermute x2, starting transfers between devices, ring(): lax.ppermute(array, axis, [(i, (i + by) % count) for i in range(count)])  2.43 us
  transfers between devices with their start and end apart: 14, of which 7 were waited for; matrix products, arithmetic and copies ran while one was open for 0% of the time, Pallas kernels for 17%

profile of v2, /device:TPU:0, one launch (start us, length us, event | category | flops | bytes accessed | tf_op | source)
XLA Modules:
  0.0 48.2 jit_solution(10585297459553874686)
XLA Ops:
  0.6 0.0 copy-start.7
  0.6 0.0 copy-start.6
  0.7 0.7 %copy-done.7 = s32[512]{0:T(512)S(1)} copy-done((s32[512]{0:T(512)S(1)}, s32[512]{0:T(512)}, u32[]{:S(2)}) %copy-start.7) | copy-done | bytes 2072
  1.3 0.0 copy-done.6
  1.3 0.8 %copy-done.2 = f32[8,3,512]{2,0,1:T(8,128)S(1)} copy-done((f32[8,3,512]{2,0,1:T(8,128)S(1)}, f32[8,3,512]{2,0,1:T(8,128)}, u32[]{:S(2)}) %copy-start.2) | copy-done | bytes 49176
  2.1 0.7 %copy-done.3 = s32[8,512]{1,0:T(8,128)S(1)} copy-done((s32[8,512]{1,0:T(8,128)S(1)}, s32[8,512]{1,0:T(8,128)}, u32[]{:S(2)}) %copy-start.3) | copy-done | bytes 16408
  2.9 0.7 %copy-done.5 = f32[1,3,512]{2,0,1:T(1,128)S(1)} copy-done((f32[1,3,512]{2,0,1:T(1,128)S(1)}, f32[1,3,512]{2,0,1:T(1,128)}, u32[]{:S(2)}) %copy-start.5) | copy-done | bytes 6168
  3.6 0.0 copy-start.9
  3.6 0.7 %shard_map.165.po_ref = f32[40,512]{1,0:T(8,128)S(1)} custom-call(f32[3,1,512]{2,1,0:T(1,128)} %bitcast.1.x_ref.refs_4_, f32[3,1,512]{2,1,0:T(1,128)S(1)} %bitcast.11, s32[512]{0:T(512)S(1)} %copy-done.6, s32[8,512]{1,0:T(8,128)S(1)} %copy-done.3, s32[512]{0:T(512)S(1)} %copy-done.7, f32[3,8,512]{2,1,0:T(8,128)S(1)} %bitcast.10), custom_call_target="tpu_custom_call" | custom-call | bytes 262144 | tf_op jit(solution)/shard_map/pallas_call | solution.py:581
  4.3 2.4 %collective-permute-start.1 = (f32[40,512]{1,0:T(8,128)S(1)}, f32[40,512]{1,0:T(8,128)S(1)}, u32[]{:S(2)}, u32[]{:S(2)}) collective-permute-start(f32[40,512]{1,0:T(8,128)S(1)} %shard_map.165.po_ref), channel_id=1, source_target_pairs={{0,12},{4,0},{8,4},{12,8},{1,13},{5,1},{9,5},{13,9},{2,14},{6,2},{... | collective-permute-start | bytes 245768 | tf_op jit(solution)/shard_map/ppermute | solution.py:599
  6.7 0.0 collective-permute-start
  6.7 3.6 %collective-permute-start.4 = (f32[3,1,512]{2,1,0:T(1,128)}, f32[3,1,512]{2,1,0:T(1,128)S(1)}, u32[]{:S(2)}, u32[]{:S(2)}) collective-permute-start(f32[3,1,512]{2,1,0:T(1,128)} %bitcast.1.x_ref.refs_4_), channel_id=1, source_target_pairs={{0,3},{1,0},{2,1},{3,2},{4,7},{5,4},{6,5},{7,6},{8,11},{9,8},{10,9... | collective-permute-start | bytes 18440 | tf_op jit(solution)/shard_map/ppermute | solution.py:594
  10.3 0.0 collective-permute-start.3
  10.3 1.0 %collective-permute-start.2 = (f32[3,1,512]{2,1,0:T(1,128)}, f32[3,1,512]{2,1,0:T(1,128)S(1)}, u32[]{:S(2)}, u32[]{:S(2)}) collective-permute-start(f32[3,1,512]{2,1,0:T(1,128)} %bitcast.1.x_ref.refs_4_), channel_id=1, source_target_pairs={{0,1},{1,2},{2,3},{3,0},{4,5},{5,6},{6,7},{7,4},{8,9},{9,10},{10,1... | collective-permute-start | bytes 18440 | tf_op jit(solution)/shard_map/ppermute | solution.py:594
  11.3 0.0 copy-done
  11.4 0.0 copy-done.1
  11.4 0.0 copy-done.4
  11.4 0.0 copy-done.8
  11.4 0.5 %shard_map.166 = (bf16[64,48]{1,0:T(8,128)(2,1)S(1)}, bf16[64,192]{1,0:T(8,128)(2,1)S(1)}, bf16[64,32]{1,0:T(8,128)(2,1)S(1)}, bf16[64,192]{1,0:T(8,128)(2,1)S(1...) custom-call(f32[2,64]{1,0:T(2,128)S(1)} %copy-done.8, f32[2,8,64]{2,1,0:T(8,128)S(1)} %copy-done.4, ...), custom_call_target="tpu_custom_call" | custom-call | flops 10000000 | bytes 262144 | tf_op jit(solution)/shard_map/pallas_call | solution.py:581
  11.9 0.0 collective-permute-done.1.pr_ref
  11.9 0.0 collective-permute-done.pl_ref
  11.9 7.5 %shard_map.167.force_ref = f32[3,512]{1,0:T(4,128)S(1)} custom-call(f32[40,512]{1,0:T(8,128)S(1)} %collective-permute-done.pl_ref, f32[40,512]{1,0:T(8,128)S(1)} %shard_map.165.po_ref, f32[40,512]{1,0:T(8,128)S(1)} %collective-permute-done.1.pr_ref, bf16[64,48]{1,0:T(8,128)(2,1)S(1)} %get-tuple-element.16.rest_0_.rest_3_, ...), custom_call_target="tpu_custom_call" | custom-call | flops 1000000000 | bytes 262144 | tf_op jit(solution)/shard_map/pallas_call | solution.py:581
  19.4 0.0 collective-permute-done.4.rest_2_.refs_7_
  19.4 0.0 collective-permute-done.3.rest_1_.refs_6_
  19.4 0.0 collective-permute-done.2.rest_0_.refs_5_
  19.4 0.1 shard_map.168.own_ref
  19.6 0.9 %collective-permute-start.7 = (f32[8,512]{1,0:T(8,128)S(1)}, f32[8,512]{1,0:T(8,128)S(1)}, u32[]{:S(2)}, u32[]{:S(2)}) collective-permute-start(f32[8,512]{1,0:T(8,128)S(1)} %shard_map.168.own_ref), channel_id=1, source_target_pairs={{0,12},{4,0},{8,4},{12,8},{1,13},{5,1},{9,5},{13,9},{2,14},{6,2},{... | collective-permute-start | bytes 49160 | tf_op jit(solution)/shard_map/ppermute | solution.py:594
  20.5 0.6 %collective-permute-start.6 = (f32[8,512]{1,0:T(8,128)S(1)}, f32[8,512]{1,0:T(8,128)S(1)}, u32[]{:S(2)}, u32[]{:S(2)}) collective-permute-start(f32[8,512]{1,0:T(8,128)S(1)} %shard_map.168.own_ref), channel_id=1, source_target_pairs={{0,8},{4,12},{8,0},{12,4},{1,9},{5,13},{9,1},{13,5},{2,10},{6,14},... | collective-permute-start | bytes 49160 | tf_op jit(solution)/shard_map/ppermute | solution.py:594
  21.1 0.0 collective-permute-start.5
  22.4 0.0 copy-start.10
  22.4 0.0 collective-permute-done.7.rest_2_
  22.4 1.9 %collective-permute-done.6.rest_1_ = f32[8,512]{1,0:T(8,128)S(1)} collective-permute-done((f32[8,512]{1,0:T(8,128)S(1)}, f32[8,512]{1,0:T(8,128)S(1)}, u32[]{:S(2)}, u32[]{:S(2)}) %collective-permute-start.6) | collective-permute-done | bytes 16416 | tf_op jit(solution)/shard_map/ppermute | solution.py:594
  24.3 0.1 collective-permute-done.5.rest_0_
  24.4 8.2 %shard_map.169.refs_0_.own_ref = f32[8,512]{1,0:T(8,128)S(1)} custom-call(f32[1]{0:T(128)S(6)} %copy.19.dt_ref, s32[1,2]{1,0:T(1,128)S(1)} %bitcast.12, s32[1]{0:T(128)S(6)} %copy.20.climb_ref, f32[40,512]{1,0:T(8,128)S(1)} %collective-permute-done.pl_ref, f32[40,512]{1,0:T(8,128)S(1)} %shard_map.165.po_ref, f32[40,512]{1,0:T(8,128)S(1)} %collective-permute-done.1.pr_ref, ...), custom_call_target="tpu_custom_call" | custom-call | flops 1000000000 | bytes 262144 | tf_op jit(solution)/shard_map/pallas_call | solution.py:581
  32.6 3.1 %collective-permute-start.10 = (f32[8,512]{1,0:T(8,128)S(1)}, f32[8,512]{1,0:T(8,128)S(1)}, u32[]{:S(2)}, u32[]{:S(2)}) collective-permute-start(f32[8,512]{1,0:T(8,128)S(1)} %shard_map.169.refs_0_.own_ref), channel_id=1, source_target_pairs={{0,3},{1,0},{2,1},{3,2},{4,7},{5,4},{6,5},{7,6},{8,11},{9,8},{10,9... | collective-permute-start | bytes 49160 | tf_op jit(solution)/shard_map/ppermute | solution.py:594
  35.7 0.8 %collective-permute-start.9 = (f32[8,512]{1,0:T(8,128)S(1)}, f32[8,512]{1,0:T(8,128)S(1)}, u32[]{:S(2)}, u32[]{:S(2)}) collective-permute-start(f32[8,512]{1,0:T(8,128)S(1)} %shard_map.169.refs_0_.own_ref), channel_id=1, source_target_pairs={{0,2},{1,3},{2,0},{3,1},{4,6},{5,7},{6,4},{7,5},{8,10},{9,11},{10,... | collective-permute-start | bytes 49160 | tf_op jit(solution)/shard_map/ppermute | solution.py:594
  36.6 0.3 collective-permute-start.8
  36.9 0.3 collective-permute-done.10.refs_3_
  37.1 3.2 %collective-permute-done.9.refs_2_ = f32[8,512]{1,0:T(8,128)S(1)} collective-permute-done((f32[8,512]{1,0:T(8,128)S(1)}, f32[8,512]{1,0:T(8,128)S(1)}, u32[]{:S(2)}, u32[]{:S(2)}) %collective-permute-start.9) | collective-permute-done | bytes 16416 | tf_op jit(solution)/shard_map/ppermute | solution.py:594
  40.3 1.7 %collective-permute-done.8.refs_1_ = f32[8,512]{1,0:T(8,128)S(1)} collective-permute-done((f32[8,512]{1,0:T(8,128)S(1)}, f32[8,512]{1,0:T(8,128)S(1)}, u32[]{:S(2)}, u32[]{:S(2)}) %collective-permute-start.8) | collective-permute-done | bytes 16416 | tf_op jit(solution)/shard_map/ppermute | solution.py:594
  42.1 0.9 %shard_map.170 = (f32[8,128]{1,0:T(8,128)S(1)}, f32[16,512]{1,0:T(8,128)S(1)}) custom-call(f32[8,512]{1,0:T(8,128)S(1)} %shard_map.169.refs_0_.own_ref, f32[8,512]{1,0:T(8,128)S(1)} %collective-permute-done.8.refs_1_, f32[8,512]{1,0:T(8,128)S(1)} %collective-permute-done.9.refs_2_, f32[8,512]{1,0:T(8,128)S(1)} %collective-permute-done.10.refs_3_, ...), custom_call_target="tpu_custom_call" | custom-call | bytes 262144 | tf_op jit(solution)/shard_map/pallas_call | solution.py:581
  43.0 0.1 collective-permute-start.13
  43.1 1.3 %collective-permute-start.12 = (f32[8,128]{1,0:T(8,128)S(1)}, f32[8,128]{1,0:T(8,128)S(1)}, u32[]{:S(2)}, u32[]{:S(2)}) collective-permute-start(f32[8,128]{1,0:T(8,128)S(1)} %get-tuple-element.23.sums_ref), channel_id=1, source_target_pairs={{0,8},{4,12},{8,0},{12,4},{1,9},{5,13},{9,1},{13,5},{2,10},{6,14},... | collective-permute-start | bytes 12296 | tf_op jit(solution)/shard_map/ppermute | solution.py:594
  44.4 0.2 collective-permute-start.11
  44.6 0.0 collective-permute-done.13.rest_2_
  44.6 2.2 %collective-permute-done.12.rest_1_ = f32[8,128]{1,0:T(8,128)S(1)} collective-permute-done((f32[8,128]{1,0:T(8,128)S(1)}, f32[8,128]{1,0:T(8,128)S(1)}, u32[]{:S(2)}, u32[]{:S(2)}) %collective-permute-start.12) | collective-permute-done | bytes 4128 | tf_op jit(solution)/shard_map/ppermute | solution.py:594
  46.7 0.7 %collective-permute-done.11.rest_0_ = f32[8,128]{1,0:T(8,128)S(1)} collective-permute-done((f32[8,128]{1,0:T(8,128)S(1)}, f32[8,128]{1,0:T(8,128)S(1)}, u32[]{:S(2)}, u32[]{:S(2)}) %collective-permute-start.11) | collective-permute-done | bytes 4128 | tf_op jit(solution)/shard_map/ppermute | solution.py:594
  47.5 0.7 %shard_map.171 = (f32[3,1,512]{2,1,0:T(1,128)}, f32[3,1,512]{2,1,0:T(1,128)}, f32[2,1,2]{2,1,0:T(1,128)}, f32[1,1]{1,0:T(1,128)}) custom-call(s32[1]{0:T(128)S(6)} %copy.20.climb_ref, f32[8,512]{1,0:T(8,128)S(1)} %shard_map.169.refs_0_.own_ref, f32[16,512]{1,0:T(8,128)S(1)} %get-tuple-element.22.state_ref, f32[8,128]{1,0:T(8,128)S(1)} %get-tuple-element.23.sums_ref, ...), custom_call_target="tpu_custom_call" | custom-call | bytes 262144 | tf_op jit(solution)/shard_map/pallas_call | solution.py:581
  (9 shorter events, 0.0 us)
Async XLA Ops:
  0.6 0.7 %copy-start.7 = (s32[512]{0:T(512)S(1)}, s32[512]{0:T(512)}, u32[]{:S(2)}) copy-start(s32[512]{0:T(512)} %counts_ref.1) | copy-start | bytes 6148
  0.6 0.7 %copy-start.6 = (s32[512]{0:T(512)S(1)}, s32[512]{0:T(512)}, u32[]{:S(2)}) copy-start(s32[512]{0:T(512)} %species_ref.1) | copy-start | bytes 6148
  1.3 0.8 %copy-start.2 = (f32[8,3,512]{2,0,1:T(8,128)S(1)}, f32[8,3,512]{2,0,1:T(8,128)}, u32[]{:S(2)}) copy-start(f32[8,3,512]{2,0,1:T(8,128)} %param.22) | copy-start | bytes 147460
  2.1 0.7 %copy-start.3 = (s32[8,512]{1,0:T(8,128)S(1)}, s32[8,512]{1,0:T(8,128)}, u32[]{:S(2)}) copy-start(s32[8,512]{1,0:T(8,128)} %nbr_ref.1) | copy-start | bytes 49156
  2.9 0.7 %copy-start.5 = (f32[1,3,512]{2,0,1:T(1,128)S(1)}, f32[1,3,512]{2,0,1:T(1,128)}, u32[]{:S(2)}) copy-start(f32[1,3,512]{2,0,1:T(1,128)} %param.15) | copy-start | bytes 18436
  3.5 7.8 %copy-start = (f32[2,64,64]{2,1,0:T(8,128)S(1)}, f32[2,64,64]{2,1,0:T(8,128)}, u32[]{:S(2)}) copy-start(f32[2,64,64]{2,1,0:T(8,128)} %mix_ref.1) | copy-start | bytes 98308
  3.5 7.8 %copy-start.1 = (f32[2,64,64]{2,1,0:T(8,128)S(1)}, f32[2,64,64]{2,1,0:T(8,128)}, u32[]{:S(2)}) copy-start(f32[2,64,64]{2,1,0:T(8,128)} %update_ref.1) | copy-start | bytes 98308
  3.5 7.8 %copy-start.4 = (f32[2,8,64]{2,1,0:T(8,128)S(1)}, f32[2,8,64]{2,1,0:T(8,128)}, u32[]{:S(2)}) copy-start(f32[2,8,64]{2,1,0:T(8,128)} %radial_ref.1) | copy-start | bytes 12292
  3.5 7.8 %copy-start.8 = (f32[2,64]{1,0:T(2,128)S(1)}, f32[2,64]{1,0:T(2,128)}, u32[]{:S(2)}) copy-start(f32[2,64]{1,0:T(2,128)} %embed_ref.1) | copy-start | bytes 1540
  3.6 7.8 %copy-start.9 = (f32[64]{0:T(128)S(1)}, f32[64]{0:T(128)}, u32[]{:S(2)}) copy-start(f32[64]{0:T(128)} %readout_ref.1) | copy-start | bytes 772
  4.3 7.6 %collective-permute-start.1 = (f32[40,512]{1,0:T(8,128)S(1)}, f32[40,512]{1,0:T(8,128)S(1)}, u32[]{:S(2)}, u32[]{:S(2)}) collective-permute-start(f32[40,512]{1,0:T(8,128)S(1)} %shard_map.165.po_ref), channel_id=1, source_target_pairs={{0,12},{4,0},{8,4},{12,8},{1,13},{5,1},{9,5},{13,9},{2,14},{6,2},{... | collective-permute-start | bytes 245768 | tf_op jit(solution)/shard_map/ppermute | solution.py:599
  6.7 5.2 %collective-permute-start = (f32[40,512]{1,0:T(8,128)S(1)}, f32[40,512]{1,0:T(8,128)S(1)}, u32[]{:S(2)}, u32[]{:S(2)}) collective-permute-start(f32[40,512]{1,0:T(8,128)S(1)} %shard_map.165.po_ref), channel_id=1, source_target_pairs={{0,4},{4,8},{8,12},{12,0},{1,5},{5,9},{9,13},{13,1},{2,6},{6,10},{... | collective-permute-start | bytes 245768 | tf_op jit(solution)/shard_map/ppermute | solution.py:599
  6.7 12.7 %collective-permute-start.4 = (f32[3,1,512]{2,1,0:T(1,128)}, f32[3,1,512]{2,1,0:T(1,128)S(1)}, u32[]{:S(2)}, u32[]{:S(2)}) collective-permute-start(f32[3,1,512]{2,1,0:T(1,128)} %bitcast.1.x_ref.refs_4_), channel_id=1, source_target_pairs={{0,3},{1,0},{2,1},{3,2},{4,7},{5,4},{6,5},{7,6},{8,11},{9,8},{10,9... | collective-permute-start | bytes 18440 | tf_op jit(solution)/shard_map/ppermute | solution.py:594
  10.3 9.1 %collective-permute-start.3 = (f32[3,1,512]{2,1,0:T(1,128)}, f32[3,1,512]{2,1,0:T(1,128)S(1)}, u32[]{:S(2)}, u32[]{:S(2)}) collective-permute-start(f32[3,1,512]{2,1,0:T(1,128)} %bitcast.1.x_ref.refs_4_), channel_id=1, source_target_pairs={{0,2},{1,3},{2,0},{3,1},{4,6},{5,7},{6,4},{7,5},{8,10},{9,11},{10,... | collective-permute-start | bytes 18440 | tf_op jit(solution)/shard_map/ppermute | solution.py:594
  10.3 9.1 %collective-permute-start.2 = (f32[3,1,512]{2,1,0:T(1,128)}, f32[3,1,512]{2,1,0:T(1,128)S(1)}, u32[]{:S(2)}, u32[]{:S(2)}) collective-permute-start(f32[3,1,512]{2,1,0:T(1,128)} %bitcast.1.x_ref.refs_4_), channel_id=1, source_target_pairs={{0,1},{1,2},{2,3},{3,0},{4,5},{5,6},{6,7},{7,4},{8,9},{9,10},{10,1... | collective-permute-start | bytes 18440 | tf_op jit(solution)/shard_map/ppermute | solution.py:594
  19.6 2.9 %collective-permute-start.7 = (f32[8,512]{1,0:T(8,128)S(1)}, f32[8,512]{1,0:T(8,128)S(1)}, u32[]{:S(2)}, u32[]{:S(2)}) collective-permute-start(f32[8,512]{1,0:T(8,128)S(1)} %shard_map.168.own_ref), channel_id=1, source_target_pairs={{0,12},{4,0},{8,4},{12,8},{1,13},{5,1},{9,5},{13,9},{2,14},{6,2},{... | collective-permute-start | bytes 49160 | tf_op jit(solution)/shard_map/ppermute | solution.py:594
  20.5 3.9 %collective-permute-start.6 = (f32[8,512]{1,0:T(8,128)S(1)}, f32[8,512]{1,0:T(8,128)S(1)}, u32[]{:S(2)}, u32[]{:S(2)}) collective-permute-start(f32[8,512]{1,0:T(8,128)S(1)} %shard_map.168.own_ref), channel_id=1, source_target_pairs={{0,8},{4,12},{8,0},{12,4},{1,9},{5,13},{9,1},{13,5},{2,10},{6,14},... | collective-permute-start | bytes 49160 | tf_op jit(solution)/shard_map/ppermute | solution.py:594
  21.1 3.3 %collective-permute-start.5 = (f32[8,512]{1,0:T(8,128)S(1)}, f32[8,512]{1,0:T(8,128)S(1)}, u32[]{:S(2)}, u32[]{:S(2)}) collective-permute-start(f32[8,512]{1,0:T(8,128)S(1)} %shard_map.168.own_ref), channel_id=1, source_target_pairs={{0,4},{4,8},{8,12},{12,0},{1,5},{5,9},{9,13},{13,1},{2,6},{6,10},{... | collective-permute-start | bytes 49160 | tf_op jit(solution)/shard_map/ppermute | solution.py:594
  22.4 2.0 %copy-start.10 = (s32[2,1]{0,1:T(1,128)S(1)}, s32[2,1]{0,1:T(1,128)}, u32[]{:S(2)}) copy-start(s32[2,1]{0,1:T(1,128)} %param.17) | copy-start | bytes 28
  32.6 4.6 %collective-permute-start.10 = (f32[8,512]{1,0:T(8,128)S(1)}, f32[8,512]{1,0:T(8,128)S(1)}, u32[]{:S(2)}, u32[]{:S(2)}) collective-permute-start(f32[8,512]{1,0:T(8,128)S(1)} %shard_map.169.refs_0_.own_ref), channel_id=1, source_target_pairs={{0,3},{1,0},{2,1},{3,2},{4,7},{5,4},{6,5},{7,6},{8,11},{9,8},{10,9... | collective-permute-start | bytes 49160 | tf_op jit(solution)/shard_map/ppermute | solution.py:594
  35.7 4.6 %collective-permute-start.9 = (f32[8,512]{1,0:T(8,128)S(1)}, f32[8,512]{1,0:T(8,128)S(1)}, u32[]{:S(2)}, u32[]{:S(2)}) collective-permute-start(f32[8,512]{1,0:T(8,128)S(1)} %shard_map.169.refs_0_.own_ref), channel_id=1, source_target_pairs={{0,2},{1,3},{2,0},{3,1},{4,6},{5,7},{6,4},{7,5},{8,10},{9,11},{10,... | collective-permute-start | bytes 49160 | tf_op jit(solution)/shard_map/ppermute | solution.py:594
  36.6 5.5 %collective-permute-start.8 = (f32[8,512]{1,0:T(8,128)S(1)}, f32[8,512]{1,0:T(8,128)S(1)}, u32[]{:S(2)}, u32[]{:S(2)}) collective-permute-start(f32[8,512]{1,0:T(8,128)S(1)} %shard_map.169.refs_0_.own_ref), channel_id=1, source_target_pairs={{0,1},{1,2},{2,3},{3,0},{4,5},{5,6},{6,7},{7,4},{8,9},{9,10},{10,1... | collective-permute-start | bytes 49160 | tf_op jit(solution)/shard_map/ppermute | solution.py:594
  43.0 1.6 %collective-permute-start.13 = (f32[8,128]{1,0:T(8,128)S(1)}, f32[8,128]{1,0:T(8,128)S(1)}, u32[]{:S(2)}, u32[]{:S(2)}) collective-permute-start(f32[8,128]{1,0:T(8,128)S(1)} %get-tuple-element.23.sums_ref), channel_id=1, source_target_pairs={{0,12},{4,0},{8,4},{12,8},{1,13},{5,1},{9,5},{13,9},{2,14},{6,2},{... | collective-permute-start | bytes 12296 | tf_op jit(solution)/shard_map/ppermute | solution.py:594
  43.1 3.7 %collective-permute-start.12 = (f32[8,128]{1,0:T(8,128)S(1)}, f32[8,128]{1,0:T(8,128)S(1)}, u32[]{:S(2)}, u32[]{:S(2)}) collective-permute-start(f32[8,128]{1,0:T(8,128)S(1)} %get-tuple-element.23.sums_ref), channel_id=1, source_target_pairs={{0,8},{4,12},{8,0},{12,4},{1,9},{5,13},{9,1},{13,5},{2,10},{6,14},... | collective-permute-start | bytes 12296 | tf_op jit(solution)/shard_map/ppermute | solution.py:594
  44.4 3.0 %collective-permute-start.11 = (f32[8,128]{1,0:T(8,128)S(1)}, f32[8,128]{1,0:T(8,128)S(1)}, u32[]{:S(2)}, u32[]{:S(2)}) collective-permute-start(f32[8,128]{1,0:T(8,128)S(1)} %get-tuple-element.23.sums_ref), channel_id=1, source_target_pairs={{0,4},{4,8},{8,12},{12,0},{1,5},{5,9},{9,13},{13,1},{2,6},{6,10},{... | collective-permute-start | bytes 12296 | tf_op jit(solution)/shard_map/ppermute | solution.py:594

commit v3 on v2

--- a/solution.py
+++ b/solution.py
@@ -58,14 +58,24 @@
     return lax.dot_general(a, b, NT, preferred_element_type=F32)
 
 
-def pack_kernel(x_ref, v_ref, species_ref, nbr_ref, counts_ref, lattice_ref, out_ref):
-    out_ref[0:8, :] = nbr_ref[...].astype(F32)
+def pack_kernel(x_ref, v_ref, species_ref, nbr_ref, counts_ref, lattice_ref, out_ref, x, v, species, nbr, counts, sems):
+    copies = [
+        pltpu.make_async_copy(source, target, sems.at[i])
+        for i, (source, target) in enumerate(
+            [(x_ref, x), (v_ref, v), (species_ref, species), (nbr_ref, nbr), (counts_ref, counts)]
+            + [(lattice_ref.at[c], out_ref.at[pl.ds(8 + 8 * c, 8)]) for c in range(3)]
+        )
+    ]
+    for one in copies:
+        one.start()
+    for one in copies:
+        one.wait()
+    out_ref[0:8, :] = nbr[...].astype(F32)
     for c in range(3):
-        out_ref[8 + 8 * c : 16 + 8 * c, :] = lattice_ref[c]
-        out_ref[ROW_X + c : ROW_X + c + 1, :] = x_ref[c]
-        out_ref[ROW_V + c : ROW_V + c + 1, :] = v_ref[c]
-    out_ref[ROW_COUNT : ROW_COUNT + 1, :] = counts_ref[...].astype(F32).reshape(1, -1)
-    out_ref[ROW_KIND : ROW_KIND + 1, :] = species_ref[...].astype(F32).reshape(1, -1)
+        out_ref[ROW_X + c : ROW_X + c + 1, :] = x[c]
+        out_ref[ROW_V + c : ROW_V + c + 1, :] = v[c]
+    out_ref[ROW_COUNT : ROW_COUNT + 1, :] = counts[...].astype(F32).reshape(1, -1)
+    out_ref[ROW_KIND : ROW_KIND + 1, :] = species[...].astype(F32).reshape(1, -1)
 
 
 def weight_kernel(
@@ -352,8 +362,7 @@
     return jnp.concatenate(values, axis=1)
 
 
-def blend_kernel(images, force_ref, po_ref, *rest):
-    before_ref, after_ref, out_ref = rest[0], rest[images - 2], rest[-1]
+def blend_kernel(images, force_ref, po_ref, before_ref, after_ref, out_ref):
     here = lax.axis_index("img")
     x = po_ref[ROW_X : ROW_X + 3, :]
     v = po_ref[ROW_V : ROW_V + 3, :]
@@ -407,7 +416,7 @@
 
 def second_kernel(images, others, dt_ref, flag_ref, climb_ref, pl_ref, po_ref, pr_ref, own_ref, *rest):
     heard, rest = rest[:others], rest[others:]
-    weights, out_ref, scr = rest[:6], rest[6], rest[7:]
+    weights, out_ref, record_ref, scr = rest[:6], rest[6], rest[7], rest[8:]
     packs = [pl_ref, po_ref, pr_ref]
     here = lax.axis_index("img")
     sums = own_ref[6:8, :]
@@ -441,11 +450,19 @@
     moved = [p[ROW_X : ROW_X + 3, :] + wide(dt) * s for p, s in zip(packs, speeds)]
     fill_region(scr[0], packs, lambda s: moved[s])
     force_parts(packs, weights, scr)
-    out_ref[0:3, :] = speeds[1]
     for c in range(3):
-        out_ref[3 + c : 4 + c, :] = own_force(scr[-1], c)
-    out_ref[6:7, :] = block_row(dt, alpha, jnp.full(shape, flag_ref[0, 1], jnp.int32).astype(F32))
-    out_ref[7:8, :] = block_row(along, spring)
+        force = own_force(scr[-1], c)
+        for i in range(SLAB_BLOCKS):
+            lanes = slice(i * LANES, (i + 1) * LANES)
+            row = 4 * c + i
+            out_ref[row : row + 1, :] = speeds[1][c : c + 1, lanes]
+            out_ref[12 + row : 13 + row, :] = force[:, lanes]
+            out_ref[24 + row : 25 + row, :] = moved[1][c : c + 1, lanes]
+    out_ref[36:37, :] = dt
+    out_ref[37:38, :] = alpha
+    out_ref[38:40, :] = jnp.full((2, LANES), flag_ref[0, 1], jnp.int32).astype(F32)
+    record_ref[0:1, :] = along
+    record_ref[1:2, :] = spring
 
 
 PRODUCTS = (
@@ -456,36 +473,26 @@
 
 
 def gram_kernel(images, *refs):
-    messages, starts, (out_ref, state_ref) = refs[:images], refs[images : 2 * images], refs[2 * images :]
-    rows = 8 * ((images + 7) // 8)
+    messages, out_ref, state_ref = refs[:images], refs[images], refs[images + 1]
+    rows = out_ref.shape[1]
     here = lax.axis_index("img")
-    width = state_ref.shape[1]
-    blank = jnp.zeros((rows - images, width), F32)
-
-    def padded(lines):
-        return jnp.concatenate(lines + ([blank[:, : lines[0].shape[1]]] if rows > images else []), axis=0)
+    blank = [jnp.zeros((rows - images, LANES), F32)] if rows > images else []
 
     def gathered(row):
-        return padded([m[row : row + 1, :] for m in messages])
-
-    def number_of(i):
-        return padded([m[6:7, i * LANES : (i + 1) * LANES] for m in messages])
-
-    steps = jnp.concatenate([number_of(0)] * SLAB_BLOCKS, axis=1)
+        return jnp.concatenate([m[row : row + 1, :] for m in messages] + blank, axis=0)
 
     def shifted(value, by):
         lines = [value[(s + by) % images : (s + by) % images + 1, :] for s in range(images)]
-        return jnp.concatenate(lines + ([blank] if rows > images else []), axis=0)
-
-    offset = lax.broadcasted_iota(jnp.int32, (rows, width), 0)
+        return jnp.concatenate(lines + blank, axis=0)
+
+    offset = lax.broadcasted_iota(jnp.int32, (rows, LANES), 0)
     number = here - offset
     number = jnp.where(number < 0, number + images, number)
     has_after = (number < images - 1) & (offset < images)
     has_before = (number > 0) & (offset < images)
-    totals = [jnp.zeros((rows, width), F32) for _ in PRODUCTS]
-    for c in range(3):
-        v, f = gathered(c), gathered(3 + c)
-        x = padded([s[c] for s in starts]) + steps * v
+    totals = [jnp.zeros((rows, LANES), F32) for _ in PRODUCTS]
+    for row in range(3 * SLAB_BLOCKS):
+        v, f, x = gathered(row), gathered(12 + row), gathered(24 + row)
         after = jnp.where(has_after, shifted(x, -1), 0.0)
         before = jnp.where(has_before, shifted(x, 1), 0.0)
         t = after - before
@@ -494,24 +501,24 @@
         table["V"] = jnp.where(has_before, shifted(v, 1), 0.0)
         table["T"] = jnp.where(has_before, shifted(t, 1), 0.0)
         totals = [old + table[a] * table[b] for old, (a, b) in zip(totals, PRODUCTS)]
-        state_ref[c : c + 1, :] = t[0:1]
-        state_ref[3 + c : 4 + c, :] = x[0:1]
+        state_ref[row : row + 1, :] = t[0:1]
     lane = lax.broadcasted_iota(jnp.int32, (rows, LANES), 1)
     result = jnp.zeros((rows, LANES), F32)
     for q, one in enumerate(totals):
-        result = jnp.where(lane == q, jnp.broadcast_to(lane_total(one), (rows, LANES)), result)
-    out_ref[...] = result
+        one = jnp.broadcast_to(jnp.sum(one, axis=1, keepdims=True), (rows, LANES))
+        result = jnp.where(lane == q, one, result)
+    for d in range(out_ref.shape[0]):
+        out_ref[d] = result
     for i in range(3):
-        state_ref[8 : 8 + rows, i * LANES : (i + 1) * LANES] = number_of(i)
-
-
-def final_kernel(images, others, atoms, climb_ref, own_ref, state_ref, sums_ref, *rest):
-    heard, (x_ref, v_ref, band_ref, path_ref) = rest[:others], rest[others:]
-    rows = sums_ref.shape[0]
+        state_ref[16 + rows * i : 16 + rows * (i + 1), :] = gathered(36 + i)
+
+
+def final_kernel(images, atoms, climb_ref, own_ref, record_ref, state_ref, sums_ref, x_ref, v_ref, band_ref, path_ref):
+    rows = sums_ref.shape[1]
     here = lax.axis_index("img")
-    sums = sums_ref[...]
-    for one in heard:
-        sums = sums + one[...]
+    sums = sums_ref[0]
+    for d in range(1, sums_ref.shape[0]):
+        sums = sums + sums_ref[d]
     got = {
         pair: jnp.broadcast_to(sums[:, q : q + 1], (rows, LANES)) for q, pair in enumerate(PRODUCTS)
     }
@@ -521,7 +528,7 @@
     inside = (number >= 1) & (number <= images - 2) & (offset < images)
     has_before = (number > 0) & (offset < images)
     climb = jnp.full((rows, LANES), climb_ref[0], jnp.int32)
-    dt0, alpha0, flag = (state_ref[8 : 8 + rows, i * LANES : (i + 1) * LANES] for i in range(3))
+    dt0, alpha0, flag = (state_ref[16 + rows * i : 16 + rows * (i + 1), :] for i in range(3))
     along, spring, keep, pull, side, dt, _ = step_numbers(
         got["f", "t"],
         got["f", "f"],
@@ -561,30 +568,33 @@
     path = jnp.sum(jnp.where(offset <= here, segment, 0.0), axis=0, keepdims=True)
     path_ref[...] = path[:, 0:1]
 
-    def wide(s):
-        return jnp.concatenate([s[0:1, :]] * SLAB_BLOCKS, axis=1)
-
-    speed = wide(keep) * own_ref[0:3, :] + wide(pull) * own_ref[3:6, :] + wide(side) * state_ref[0:3, :]
-    moved = state_ref[3:6, :] + wide(dt) * speed
     for c in range(3):
-        v_ref[c] = speed[c : c + 1]
-        x_ref[c] = moved[c : c + 1]
-    band_ref[0] = jnp.concatenate([own_ref[7:8, 0:1], own_ref[7:8, LANES : LANES + 1]], axis=1)
+        speeds, places = [], []
+        for i in range(SLAB_BLOCKS):
+            row = 4 * c + i
+            speed = keep[0:1] * own_ref[row : row + 1, :] + pull[0:1] * own_ref[12 + row : 13 + row, :]
+            speed = speed + side[0:1] * state_ref[row : row + 1, :]
+            speeds.append(speed)
+            places.append(own_ref[24 + row : 25 + row, :] + dt[0:1] * speed)
+        v_ref[c] = jnp.concatenate(speeds, axis=1)
+        x_ref[c] = jnp.concatenate(places, axis=1)
+    band_ref[0] = jnp.concatenate([record_ref[0:1, 0:1], record_ref[1:2, 0:1]], axis=1)
     band_ref[1] = jnp.concatenate([along[0:1, 0:1], spring[0:1, 0:1]], axis=1)
 
 
 VMEM_SPEC = pl.BlockSpec(memory_space=pltpu.VMEM)
 SMEM_SPEC = pl.BlockSpec(memory_space=pltpu.SMEM)
-
-
-def call(body, outs, scalars, arrays, scratch_shapes=(), flops=0):
+HBM_SPEC = pl.BlockSpec(memory_space=pltpu.HBM)
+
+
+def call(body, outs, scalars, arrays, scratch_shapes=(), flops=0, spec=VMEM_SPEC, vmem=24):
     return pl.pallas_call(
         body,
         out_shape=outs,
-        in_specs=[SMEM_SPEC] * len(scalars) + [VMEM_SPEC] * len(arrays),
+        in_specs=[SMEM_SPEC] * len(scalars) + [spec] * len(arrays),
         out_specs=jax.tree.map(lambda _: VMEM_SPEC, outs),
         scratch_shapes=list(scratch_shapes),
-        compiler_params=pltpu.CompilerParams(vmem_limit_bytes=48 * 1024 * 1024),
+        compiler_params=pltpu.CompilerParams(vmem_limit_bytes=vmem * 1024 * 1024),
         cost_estimate=pl.CostEstimate(flops=flops, bytes_accessed=1 << 18, transcendentals=0),
     )(*scalars, *arrays)
 
@@ -627,9 +637,12 @@
         shape((PACK_ROWS, atoms), F32),
         (),
         (x, v, species, neighbours, counts, jnp.transpose(lattice, (1, 0, 2))),
+        [pltpu.VMEM(a.shape, a.dtype) for a in (x, v, species, neighbours, counts)] + [pltpu.SemaphoreType.DMA((8,))],
+        spec=HBM_SPEC,
+        vmem=63,
     )
     left, right = ring(pack, "dom", 1), ring(pack, "dom", -1)
-    starts = around(x, "img")
+    before, after = ring(x, "img", 1), ring(x, "img", -1)
     weights = call(
         weight_kernel,
         (
@@ -648,12 +661,12 @@
         first_kernel, shape((3, atoms), F32), (), (left, pack, right, *weights), scratch(), flops=1000000000
     )
     message = call(
-        functools.partial(blend_kernel, images), shape((8, atoms), F32), (), (force, pack, *starts)
+        functools.partial(blend_kernel, images), shape((8, atoms), F32), (), (force, pack, before, after)
     )
     heard = around(message, "dom")
-    state = call(
+    state, record = call(
         functools.partial(second_kernel, images, len(heard)),
-        shape((8, atoms), F32),
+        (shape((40, LANES), F32), shape((2, LANES), F32)),
         (time_step, jnp.transpose(reset_flags), climb),
         (left, pack, right, message, *heard, *weights),
         scratch(),
@@ -663,16 +676,16 @@
     rows = 8 * ((images + 7) // 8)
     sums, extra = call(
         functools.partial(gram_kernel, images),
-        (shape((rows, LANES), F32), shape((8 + rows, atoms), F32)),
+        (shape((domains, rows, LANES), F32), shape((16 + 3 * rows, LANES), F32)),
         (),
-        (state, *band, x, *starts),
-    )
-    others = around(sums, "dom")
+        (state, *band),
+    )
+    sums = lax.all_to_all(sums, "dom", 0, 0)
     new_x, new_v, records, path = call(
-        functools.partial(final_kernel, images, len(others), atoms * domains),
+        functools.partial(final_kernel, images, atoms * domains),
         (shape(x.shape, F32), shape(x.shape, F32), shape((2, 1, 2), F32), shape((1, 1), F32)),
         (climb,),
-        (state, extra, sums, *others),
+        (state, record, extra, sums),
     )
     return (
         jnp.transpose(new_x, (1, 0, 2)),

time: 48.6 us -> 46.7 us (0.961)
  blocking collectives: 0 us -> 6.21 us
  waiting for transfers between devices: 10.1 us -> 6.91 us
  local copies, waits for them, and re-layouts: 2.91 us -> 0.04 us
  starting transfers between devices: 14.4 us -> 12.4 us
    all_to_all x0 -> x1, blocking collectives: none -> 6.21 us  [local(): sums = lax.all_to_all(sums, 'dom', 0, 0)]
    ppermute x12 -> x6, starting transfers between devices: 12 us -> 6.32 us  [around(): lax.ppermute(array, axis, [(i, (i + s) % count) for i in range(count)])]
    ppermute x2 -> x4, starting transfers between devices: 2.43 us -> 6.04 us  [ring(): lax.ppermute(array, axis, [(i, (i + by) % count) for i in range(count)])]
    ppermute x12 -> x6, waiting for transfers between devices: 10.1 us -> 6.9 us  [around(): lax.ppermute(array, axis, [(i, (i + s) % count) for i in range(count)])]
    unnamed x22 -> x16, local copies, waits for them, and re-layouts: 2.91 us -> 0.04 us
  transfers between devices with their start and end apart: 14 -> 10, of which waited for: 7 -> 5; matrix products, arithmetic and copies ran while one was open for 0% -> 0% of each run, Pallas kernels for 17% -> 17%
where the time goes in v3:
time: 46.7 us; the launch traced here: 46.4 us
  Pallas kernels  18.8 us (40%)
  starting transfers between devices  12.4 us (27%)
  waiting for transfers between devices  6.91 us (15%)
  blocking collectives  6.21 us (13%)
  between operations  2.11 us (5%)
    pallas_call x7, Pallas kernels, call(): pl.pallas_call(body, out_shape=outs, in_specs=[SMEM_SPEC] * len(scalars)...  18.8 us
    ppermute x6, waiting for transfers between devices, around(): lax.ppermute(array, axis, [(i, (i + s) % count) for i in range(count)])  6.9 us
    ppermute x6, starting transfers between devices, around(): lax.ppermute(array, axis, [(i, (i + s) % count) for i in range(count)])  6.32 us
    all_to_all x1, blocking collectives, local(): sums = lax.all_to_all(sums, 'dom', 0, 0)  6.21 us
    ppermute x4, starting transfers between devices, ring(): lax.ppermute(array, axis, [(i, (i + by) % count) for i in range(count)])  6.04 us
  transfers between devices with their start and end apart: 10, of which 5 were waited for; matrix products, arithmetic and copies ran while one was open for 0% of the time, Pallas kernels for 17%

profile of v3, /device:TPU:0, one launch (start us, length us, event | category | flops | bytes accessed | tf_op | source)
XLA Modules:
  0.0 46.4 jit_solution(2879525079415594102)
XLA Ops:
  0.6 0.0 copy-start.7
  0.6 0.0 copy-start.1
  0.7 0.0 copy-start.2
  0.7 0.0 copy-start.3
  0.7 0.0 copy-start.4
  0.7 0.0 copy-start.5
  0.7 1.6 %shard_map.165.po_ref = f32[40,512]{1,0:T(8,128)} custom-call(f32[3,1,512]{2,1,0:T(1,128)} %bitcast.13, f32[3,1,512]{2,1,0:T(1,128)} %bitcast.12, s32[512]{0:T(512)} %species_ref.1, s32[8,512]{1,0:T(8,128)} %nbr_ref.1, s32[512]{0:T(512)} %counts_ref.1, f32[3,8,512]{2,1,0:T(8,128)} %bitcast.11), custom_call_target="tpu_custom_call" | custom-call | bytes 262144 | tf_op jit(solution)/shard_map/pallas_call | solution.py:591
  2.3 0.0 copy-start
  2.3 2.4 %collective-permute-start.1 = (f32[40,512]{1,0:T(8,128)}, f32[40,512]{1,0:T(8,128)S(1)}, u32[]{:S(2)}, u32[]{:S(2)}) collective-permute-start(f32[40,512]{1,0:T(8,128)} %shard_map.165.po_ref), channel_id=1, source_target_pairs={{0,12},{4,0},{8,4},{12,8},{1,13},{5,1},{9,5},{13,9},{2,14},{6,2},{... | collective-permute-start | bytes 245768 | tf_op jit(solution)/shard_map/ppermute | solution.py:609
  4.7 0.0 collective-permute-start
  4.7 0.0 copy-done.7
  4.7 3.6 %collective-permute-start.3 = (f32[3,1,512]{2,1,0:T(1,128)S(1)}, f32[3,1,512]{2,1,0:T(1,128)S(1)}, u32[]{:S(2)}, u32[]{:S(2)}) collective-permute-start(f32[3,1,512]{2,1,0:T(1,128)S(1)} %bitcast.14), channel_id=1, source_target_pairs={{0,3},{1,0},{2,1},{3,2},{4,7},{5,4},{6,5},{7,6},{8,11},{9,8},{10,9... | collective-permute-start | bytes 18440 | tf_op jit(solution)/shard_map/ppermute | solution.py:609
  8.3 0.0 collective-permute-start.2
  8.3 0.0 copy-done.1
  8.3 0.0 copy-done.2
  8.3 0.0 copy-done.3
  8.3 0.0 copy-done.4
  8.4 0.0 copy-done.5
  8.4 0.5 %shard_map.166 = (bf16[64,48]{1,0:T(8,128)(2,1)S(1)}, bf16[64,192]{1,0:T(8,128)(2,1)S(1)}, bf16[64,32]{1,0:T(8,128)(2,1)S(1)}, bf16[64,192]{1,0:T(8,128)(2,1)S(1...) custom-call(f32[2,64]{1,0:T(2,128)S(1)} %copy-done.4, f32[2,8,64]{2,1,0:T(8,128)S(1)} %copy-done.3, ...), custom_call_target="tpu_custom_call" | custom-call | flops 10000000 | bytes 262144 | tf_op jit(solution)/shard_map/pallas_call | solution.py:591
  8.9 0.0 collective-permute-done.1.pr_ref
  8.9 0.0 collective-permute-done.pl_ref
  8.9 0.0 copy-done
  8.9 7.5 %shard_map.167.force_ref = f32[3,512]{1,0:T(4,128)S(1)} custom-call(f32[40,512]{1,0:T(8,128)S(1)} %collective-permute-done.pl_ref, f32[40,512]{1,0:T(8,128)S(1)} %copy-done, f32[40,512]{1,0:T(8,128)S(1)} %collective-permute-done.1.pr_ref, bf16[64,48]{1,0:T(8,128)(2,1)S(1)} %get-tuple-element.18.rest_0_.rest_3_, ...), custom_call_target="tpu_custom_call" | custom-call | flops 1000000000 | bytes 262144 | tf_op jit(solution)/shard_map/pallas_call | solution.py:591
  16.4 0.0 collective-permute-done.3.after_ref
  16.4 0.0 collective-permute-done.2.before_ref
  16.4 0.1 shard_map.168.own_ref
  16.6 1.5 %collective-permute-start.6 = (f32[8,512]{1,0:T(8,128)S(1)}, f32[8,512]{1,0:T(8,128)S(1)}, u32[]{:S(2)}, u32[]{:S(2)}) collective-permute-start(f32[8,512]{1,0:T(8,128)S(1)} %shard_map.168.own_ref), channel_id=1, source_target_pairs={{0,12},{4,0},{8,4},{12,8},{1,13},{5,1},{9,5},{13,9},{2,14},{6,2},{... | collective-permute-start | bytes 49160 | tf_op jit(solution)/shard_map/ppermute | solution.py:604
  18.0 0.6 %collective-permute-start.5 = (f32[8,512]{1,0:T(8,128)S(1)}, f32[8,512]{1,0:T(8,128)S(1)}, u32[]{:S(2)}, u32[]{:S(2)}) collective-permute-start(f32[8,512]{1,0:T(8,128)S(1)} %shard_map.168.own_ref), channel_id=1, source_target_pairs={{0,8},{4,12},{8,0},{12,4},{1,9},{5,13},{9,1},{13,5},{2,10},{6,14},... | collective-permute-start | bytes 49160 | tf_op jit(solution)/shard_map/ppermute | solution.py:604
  18.7 0.0 collective-permute-start.4
  20.0 0.0 copy-start.6
  20.0 0.0 collective-permute-done.6.rest_2_
  20.0 1.9 %collective-permute-done.5.rest_1_ = f32[8,512]{1,0:T(8,128)S(1)} collective-permute-done((f32[8,512]{1,0:T(8,128)S(1)}, f32[8,512]{1,0:T(8,128)S(1)}, u32[]{:S(2)}, u32[]{:S(2)}) %collective-permute-start.5) | collective-permute-done | bytes 16416 | tf_op jit(solution)/shard_map/ppermute | solution.py:604
  21.9 0.1 collective-permute-done.4.rest_0_
  21.9 0.0 copy-done.6
  21.9 8.1 %shard_map.169 = (f32[40,128]{1,0:T(8,128)S(1)}, f32[2,128]{1,0:T(2,128)S(1)}) custom-call(f32[1]{0:T(128)S(6)} %copy.19.dt_ref, s32[1,2]{1,0:T(1,128)S(1)} %bitcast.10, s32[1]{0:T(128)S(6)} %copy.20.climb_ref, f32[40,512]{1,0:T(8,128)S(1)} %collective-permute-done.pl_ref, f32[40,512]{1,0:T(8,128)S(1)} %copy-done, ...), custom_call_target="tpu_custom_call" | custom-call | flops 1000000000 | bytes 262144 | tf_op jit(solution)/shard_map/pallas_call | solution.py:591
  30.1 3.6 %collective-permute-start.9 = (f32[40,128]{1,0:T(8,128)S(1)}, f32[40,128]{1,0:T(8,128)S(1)}, u32[]{:S(2)}, u32[]{:S(2)}) collective-permute-start(f32[40,128]{1,0:T(8,128)S(1)} %get-tuple-element.24.refs_0_.own_ref), channel_id=1, source_target_pairs={{0,3},{1,0},{2,1},{3,2},{4,7},{5,4},{6,5},{7,6},{8,11},{9,8},{10,9... | collective-permute-start | bytes 61448 | tf_op jit(solution)/shard_map/ppermute | solution.py:604
  33.7 0.0 collective-permute-start.8
  33.7 0.6 %collective-permute-start.7 = (f32[40,128]{1,0:T(8,128)S(1)}, f32[40,128]{1,0:T(8,128)S(1)}, u32[]{:S(2)}, u32[]{:S(2)}) collective-permute-start(f32[40,128]{1,0:T(8,128)S(1)} %get-tuple-element.24.refs_0_.own_ref), channel_id=1, source_target_pairs={{0,1},{1,2},{2,3},{3,0},{4,5},{5,6},{6,7},{7,4},{8,9},{9,10},{10,1... | collective-permute-start | bytes 61448 | tf_op jit(solution)/shard_map/ppermute | solution.py:604
  34.3 0.8 %collective-permute-done.9.refs_3_ = f32[40,128]{1,0:T(8,128)S(1)} collective-permute-done((f32[40,128]{1,0:T(8,128)S(1)}, f32[40,128]{1,0:T(8,128)S(1)}, u32[]{:S(2)}, u32[]{:S(2)}) %collective-permute-start.9) | collective-permute-done | bytes 20512 | tf_op jit(solution)/shard_map/ppermute | solution.py:604
  35.2 3.3 %collective-permute-done.8.refs_2_ = f32[40,128]{1,0:T(8,128)S(1)} collective-permute-done((f32[40,128]{1,0:T(8,128)S(1)}, f32[40,128]{1,0:T(8,128)S(1)}, u32[]{:S(2)}, u32[]{:S(2)}) %collective-permute-start.8) | collective-permute-done | bytes 20512 | tf_op jit(solution)/shard_map/ppermute | solution.py:604
  38.4 0.8 %collective-permute-done.7.refs_1_ = f32[40,128]{1,0:T(8,128)S(1)} collective-permute-done((f32[40,128]{1,0:T(8,128)S(1)}, f32[40,128]{1,0:T(8,128)S(1)}, u32[]{:S(2)}, u32[]{:S(2)}) %collective-permute-start.7) | collective-permute-done | bytes 20512 | tf_op jit(solution)/shard_map/ppermute | solution.py:604
  39.3 0.2 shard_map.170
  39.5 6.2 %all_to_all.5.sums_ref = f32[4,8,128]{2,1,0:T(8,128)S(1)} all-to-all(f32[4,8,128]{2,1,0:T(8,128)S(1)} %get-tuple-element.27), channel_id=1, replica_groups=mesh['group'=2,'dom'=4,'img'=4] {'dom'}, dimensions={0} | all-to-all | bytes 32768 | tf_op jit(solution)/shard_map/all_to_all | solution.py:683
  45.7 0.7 %shard_map.171 = (f32[3,1,512]{2,1,0:T(1,128)}, f32[3,1,512]{2,1,0:T(1,128)}, f32[2,1,2]{2,1,0:T(1,128)}, f32[1,1]{1,0:T(1,128)}) custom-call(s32[1]{0:T(128)S(6)} %copy.20.climb_ref, f32[40,128]{1,0:T(8,128)S(1)} %get-tuple-element.24.refs_0_.own_ref, f32[2,128]{1,0:T(2,128)S(1)} %get-tuple-element.25.record_ref, ...), custom_call_target="tpu_custom_call" | custom-call | bytes 262144 | tf_op jit(solution)/shard_map/pallas_call | solution.py:591
Async XLA Ops:
  0.6 4.1 %copy-start.7 = (f32[1,3,512]{2,0,1:T(1,128)S(1)}, f32[1,3,512]{2,0,1:T(1,128)}, u32[]{:S(2)}) copy-start(f32[1,3,512]{2,0,1:T(1,128)} %param.14) | copy-start | bytes 18436
  0.6 7.7 %copy-start.1 = (f32[2,64,64]{2,1,0:T(8,128)S(1)}, f32[2,64,64]{2,1,0:T(8,128)}, u32[]{:S(2)}) copy-start(f32[2,64,64]{2,1,0:T(8,128)} %mix_ref.1) | copy-start | bytes 98308
  0.7 7.7 %copy-start.2 = (f32[2,64,64]{2,1,0:T(8,128)S(1)}, f32[2,64,64]{2,1,0:T(8,128)}, u32[]{:S(2)}) copy-start(f32[2,64,64]{2,1,0:T(8,128)} %update_ref.1) | copy-start | bytes 98308
  0.7 7.7 %copy-start.3 = (f32[2,8,64]{2,1,0:T(8,128)S(1)}, f32[2,8,64]{2,1,0:T(8,128)}, u32[]{:S(2)}) copy-start(f32[2,8,64]{2,1,0:T(8,128)} %radial_ref.1) | copy-start | bytes 12292
  0.7 7.7 %copy-start.4 = (f32[2,64]{1,0:T(2,128)S(1)}, f32[2,64]{1,0:T(2,128)}, u32[]{:S(2)}) copy-start(f32[2,64]{1,0:T(2,128)} %embed_ref.1) | copy-start | bytes 1540
  0.7 7.7 %copy-start.5 = (f32[64]{0:T(128)S(1)}, f32[64]{0:T(128)}, u32[]{:S(2)}) copy-start(f32[64]{0:T(128)} %readout_ref.1) | copy-start | bytes 772
  2.3 6.6 %copy-start = (f32[40,512]{1,0:T(8,128)S(1)}, f32[40,512]{1,0:T(8,128)}, u32[]{:S(2)}) copy-start(f32[40,512]{1,0:T(8,128)} %shard_map.165.po_ref) | copy-start | bytes 245764
  2.3 6.6 %collective-permute-start.1 = (f32[40,512]{1,0:T(8,128)}, f32[40,512]{1,0:T(8,128)S(1)}, u32[]{:S(2)}, u32[]{:S(2)}) collective-permute-start(f32[40,512]{1,0:T(8,128)} %shard_map.165.po_ref), channel_id=1, source_target_pairs={{0,12},{4,0},{8,4},{12,8},{1,13},{5,1},{9,5},{13,9},{2,14},{6,2},{... | collective-permute-start | bytes 245768 | tf_op jit(solution)/shard_map/ppermute | solution.py:609
  4.7 4.2 %collective-permute-start = (f32[40,512]{1,0:T(8,128)}, f32[40,512]{1,0:T(8,128)S(1)}, u32[]{:S(2)}, u32[]{:S(2)}) collective-permute-start(f32[40,512]{1,0:T(8,128)} %shard_map.165.po_ref), channel_id=1, source_target_pairs={{0,4},{4,8},{8,12},{12,0},{1,5},{5,9},{9,13},{13,1},{2,6},{6,10},{... | collective-permute-start | bytes 245768 | tf_op jit(solution)/shard_map/ppermute | solution.py:609
  4.7 11.7 %collective-permute-start.3 = (f32[3,1,512]{2,1,0:T(1,128)S(1)}, f32[3,1,512]{2,1,0:T(1,128)S(1)}, u32[]{:S(2)}, u32[]{:S(2)}) collective-permute-start(f32[3,1,512]{2,1,0:T(1,128)S(1)} %bitcast.14), channel_id=1, source_target_pairs={{0,3},{1,0},{2,1},{3,2},{4,7},{5,4},{6,5},{7,6},{8,11},{9,8},{10,9... | collective-permute-start | bytes 18440 | tf_op jit(solution)/shard_map/ppermute | solution.py:609
  8.3 8.1 %collective-permute-start.2 = (f32[3,1,512]{2,1,0:T(1,128)S(1)}, f32[3,1,512]{2,1,0:T(1,128)S(1)}, u32[]{:S(2)}, u32[]{:S(2)}) collective-permute-start(f32[3,1,512]{2,1,0:T(1,128)S(1)} %bitcast.15), channel_id=1, source_target_pairs={{0,1},{1,2},{2,3},{3,0},{4,5},{5,6},{6,7},{7,4},{8,9},{9,10},{10,1... | collective-permute-start | bytes 18440 | tf_op jit(solution)/shard_map/ppermute | solution.py:609
  16.6 3.4 %collective-permute-start.6 = (f32[8,512]{1,0:T(8,128)S(1)}, f32[8,512]{1,0:T(8,128)S(1)}, u32[]{:S(2)}, u32[]{:S(2)}) collective-permute-start(f32[8,512]{1,0:T(8,128)S(1)} %shard_map.168.own_ref), channel_id=1, source_target_pairs={{0,12},{4,0},{8,4},{12,8},{1,13},{5,1},{9,5},{13,9},{2,14},{6,2},{... | collective-permute-start | bytes 49160 | tf_op jit(solution)/shard_map/ppermute | solution.py:604
  18.0 3.9 %collective-permute-start.5 = (f32[8,512]{1,0:T(8,128)S(1)}, f32[8,512]{1,0:T(8,128)S(1)}, u32[]{:S(2)}, u32[]{:S(2)}) collective-permute-start(f32[8,512]{1,0:T(8,128)S(1)} %shard_map.168.own_ref), channel_id=1, source_target_pairs={{0,8},{4,12},{8,0},{12,4},{1,9},{5,13},{9,1},{13,5},{2,10},{6,14},... | collective-permute-start | bytes 49160 | tf_op jit(solution)/shard_map/ppermute | solution.py:604
  18.7 3.3 %collective-permute-start.4 = (f32[8,512]{1,0:T(8,128)S(1)}, f32[8,512]{1,0:T(8,128)S(1)}, u32[]{:S(2)}, u32[]{:S(2)}) collective-permute-start(f32[8,512]{1,0:T(8,128)S(1)} %shard_map.168.own_ref), channel_id=1, source_target_pairs={{0,4},{4,8},{8,12},{12,0},{1,5},{5,9},{9,13},{13,1},{2,6},{6,10},{... | collective-permute-start | bytes 49160 | tf_op jit(solution)/shard_map/ppermute | solution.py:604
  20.0 2.0 %copy-start.6 = (s32[2,1]{0,1:T(1,128)S(1)}, s32[2,1]{0,1:T(1,128)}, u32[]{:S(2)}) copy-start(s32[2,1]{0,1:T(1,128)} %param.17) | copy-start | bytes 28
  30.1 5.1 %collective-permute-start.9 = (f32[40,128]{1,0:T(8,128)S(1)}, f32[40,128]{1,0:T(8,128)S(1)}, u32[]{:S(2)}, u32[]{:S(2)}) collective-permute-start(f32[40,128]{1,0:T(8,128)S(1)} %get-tuple-element.24.refs_0_.own_ref), channel_id=1, source_target_pairs={{0,3},{1,0},{2,1},{3,2},{4,7},{5,4},{6,5},{7,6},{8,11},{9,8},{10,9... | collective-permute-start | bytes 61448 | tf_op jit(solution)/shard_map/ppermute | solution.py:604
  33.7 4.7 %collective-permute-start.8 = (f32[40,128]{1,0:T(8,128)S(1)}, f32[40,128]{1,0:T(8,128)S(1)}, u32[]{:S(2)}, u32[]{:S(2)}) collective-permute-start(f32[40,128]{1,0:T(8,128)S(1)} %get-tuple-element.24.refs_0_.own_ref), channel_id=1, source_target_pairs={{0,2},{1,3},{2,0},{3,1},{4,6},{5,7},{6,4},{7,5},{8,10},{9,11},{10,... | collective-permute-start | bytes 61448 | tf_op jit(solution)/shard_map/ppermute | solution.py:604
  33.7 5.6 %collective-permute-start.7 = (f32[40,128]{1,0:T(8,128)S(1)}, f32[40,128]{1,0:T(8,128)S(1)}, u32[]{:S(2)}, u32[]{:S(2)}) collective-permute-start(f32[40,128]{1,0:T(8,128)S(1)} %get-tuple-element.24.refs_0_.own_ref), channel_id=1, source_target_pairs={{0,1},{1,2},{2,3},{3,0},{4,5},{5,6},{6,7},{7,4},{8,9},{9,10},{10,1... | collective-permute-start | bytes 61448 | tf_op jit(solution)/shard_map/ppermute | solution.py:604

commit v4 on v3

--- a/solution.py
+++ b/solution.py
@@ -134,7 +134,7 @@
 
 def force_parts(packs, weights, scr):
     l1, l2, l3, l5, l6, col = weights
-    (xs, widx, kinds, geo, bst, bps, bpr, sst, ghl, slope, hot, dg, pulls, acc) = scr
+    (xs, widx, kinds, geo, bst, bps, bpr, sst, sent_all, slope, hot, dg, pulls, acc) = scr
     centre = 2.0 + 0.5 * lax.broadcasted_iota(jnp.int32, (BASIS, LANES), 0).astype(F32)
     slot = lax.broadcasted_iota(jnp.int32, (SLOTS, LANES), 0)
     row_id = lax.broadcasted_iota(jnp.int32, (3 * LANES, LANES), 0)
@@ -204,7 +204,7 @@
         for i in range(2):
             one = sent[:, i * LANES : (i + 1) * LANES]
             one = one + col[0] + col[1] * jnp.broadcast_to(xs[b + i, 3:4, :], (CHANNELS, LANES))
-            ghl[:, (b + i) * LANES : (b + i + 1) * LANES] = pair_stack(one)
+            sent_all[:, (b + i) * LANES : (b + i + 1) * LANES] = one
         slope[:, cols] = steep
 
     def mark(b):
@@ -223,10 +223,17 @@
     started = set()
 
     def gather_and_return(b):
-        got = mm(ghl[:, (b - 1) * LANES : (b + 2) * LANES], hot[b])
-        if b < 9:
-            mark(b + 1)
-        got = got[:CHANNELS] + got[CHANNELS:]
+        index = widx[b]
+        inner, part = index & (LANES - 1), index >> 7
+        windows = [sent_all[:, (b - 1 + w) * LANES : (b + w) * LANES] for w in range(3)]
+        got = []
+        for k in range(SLOTS):
+            lane = jnp.broadcast_to(inner[k : k + 1, :], (CHANNELS, LANES))
+            which = jnp.broadcast_to(part[k : k + 1, :], (CHANNELS, LANES))
+            pick = [jnp.take_along_axis(window, lane, axis=1) for window in windows]
+            got.append(jnp.where(which == 0, pick[0], jnp.where(which == 1, pick[1], pick[2])))
+        got = jnp.concatenate(got, axis=1)
+        mark(b)
         basis = bst[b]
         radial = mm(l3[...], jnp.concatenate([basis, basis], axis=0))
         message = jnp.zeros((CHANNELS, LANES), F32)
@@ -255,7 +262,6 @@
                 total = total + pull[8 * i : 8 * i + 8]
             pulls[b] = total
 
-    mark(2)
     for b in range(2, 10):
         gather_and_return(b)
 
@@ -335,7 +341,7 @@
         pltpu.VMEM((12, 16, SLOTS * LANES), BF16),
         pltpu.VMEM((12, 8, SLOTS * LANES), F32),
         pltpu.VMEM((48, wide), BF16),
-        pltpu.VMEM((2 * CHANNELS, wide), BF16),
+        pltpu.VMEM((CHANNELS, wide), F32),
         pltpu.VMEM((CHANNELS, wide), F32),
         pltpu.VMEM((12, 3 * LANES, SLOTS * LANES), BF16),
         pltpu.VMEM((CHANNELS, wide), F32),
@@ -362,13 +368,12 @@
     return jnp.concatenate(values, axis=1)
 
 
-def blend_kernel(images, force_ref, po_ref, before_ref, after_ref, out_ref):
-    here = lax.axis_index("img")
+def blend_kernel(force_ref, po_ref, before_ref, after_ref, out_ref):
     x = po_ref[ROW_X : ROW_X + 3, :]
     v = po_ref[ROW_V : ROW_V + 3, :]
     force = force_ref[...]
-    before = jnp.where(here > 0, rows_of(before_ref), 0.0)
-    after = jnp.where(here < images - 1, rows_of(after_ref), 0.0)
+    before = rows_of(before_ref)
+    after = rows_of(after_ref)
     tangent = after - before
     plus = after - x
     minus = x - before
@@ -474,7 +479,7 @@
 
 def gram_kernel(images, *refs):
     messages, out_ref, state_ref = refs[:images], refs[images], refs[images + 1]
-    rows = out_ref.shape[1]
+    rows = out_ref.shape[0]
     here = lax.axis_index("img")
     blank = [jnp.zeros((rows - images, LANES), F32)] if rows > images else []
 
@@ -507,18 +512,18 @@
     for q, one in enumerate(totals):
         one = jnp.broadcast_to(jnp.sum(one, axis=1, keepdims=True), (rows, LANES))
         result = jnp.where(lane == q, one, result)
-    for d in range(out_ref.shape[0]):
-        out_ref[d] = result
+    out_ref[...] = result
     for i in range(3):
         state_ref[16 + rows * i : 16 + rows * (i + 1), :] = gathered(36 + i)
 
 
-def final_kernel(images, atoms, climb_ref, own_ref, record_ref, state_ref, sums_ref, x_ref, v_ref, band_ref, path_ref):
-    rows = sums_ref.shape[1]
+def final_kernel(images, others, atoms, climb_ref, own_ref, record_ref, state_ref, sums_ref, *rest):
+    heard, (x_ref, v_ref, band_ref, path_ref) = rest[:others], rest[others:]
+    rows = sums_ref.shape[0]
     here = lax.axis_index("img")
-    sums = sums_ref[0]
-    for d in range(1, sums_ref.shape[0]):
-        sums = sums + sums_ref[d]
+    sums = sums_ref[...]
+    for one in heard:
+        sums = sums + one[...]
     got = {
         pair: jnp.broadcast_to(sums[:, q : q + 1], (rows, LANES)) for q, pair in enumerate(PRODUCTS)
     }
@@ -607,6 +612,11 @@
 def ring(array, axis, by):
     count = lax.axis_size(axis)
     return lax.ppermute(array, axis, [(i, (i + by) % count) for i in range(count)])
+
+
+def beside(array, axis, by):
+    count = lax.axis_size(axis)
+    return lax.ppermute(array, axis, [(i, i + by) for i in range(count) if 0 <= i + by < count])
 
 
 def local(
@@ -642,7 +652,7 @@
         vmem=63,
     )
     left, right = ring(pack, "dom", 1), ring(pack, "dom", -1)
-    before, after = ring(x, "img", 1), ring(x, "img", -1)
+    before, after = beside(x, "img", 1), beside(x, "img", -1)
     weights = call(
         weight_kernel,
         (
@@ -661,7 +671,7 @@
         first_kernel, shape((3, atoms), F32), (), (left, pack, right, *weights), scratch(), flops=1000000000
     )
     message = call(
-        functools.partial(blend_kernel, images), shape((8, atoms), F32), (), (force, pack, before, after)
+        blend_kernel, shape((8, atoms), F32), (), (force, pack, before, after)
     )
     heard = around(message, "dom")
     state, record = call(
@@ -676,16 +686,16 @@
     rows = 8 * ((images + 7) // 8)
     sums, extra = call(
         functools.partial(gram_kernel, images),
-        (shape((domains, rows, LANES), F32), shape((16 + 3 * rows, LANES), F32)),
+        (shape((rows, LANES), F32), shape((16 + 3 * rows, LANES), F32)),
         (),
         (state, *band),
     )
-    sums = lax.all_to_all(sums, "dom", 0, 0)
+    others = around(sums, "dom")
     new_x, new_v, records, path = call(
-        functools.partial(final_kernel, images, atoms * domains),
+        functools.partial(final_kernel, images, len(others), atoms * domains),
         (shape(x.shape, F32), shape(x.shape, F32), shape((2, 1, 2), F32), shape((1, 1), F32)),
         (climb,),
-        (state, record, extra, sums),
+        (state, record, extra, sums, *others),
     )
     return (
         jnp.transpose(new_x, (1, 0, 2)),

time: 46.7 us -> 44.1 us (0.944)
  blocking collectives: 6.21 us -> 0 us
  starting transfers between devices: 12.4 us -> 16.3 us
  Pallas kernels: 18.8 us -> 16.5 us
  waiting for transfers between devices: 6.91 us -> 8.85 us
    all_to_all x1 -> x0, blocking collectives: 6.21 us -> none  [local(): sums = lax.all_to_all(sums, 'dom', 0, 0)]
    ppermute x0 -> x2, starting transfers between devices: none -> 5.83 us  [beside(): lax.ppermute(array, axis, [(i, i + by) for i in range(count) if 0 <= i +...]
    ppermute x4 -> x2, starting transfers between devices: 6.04 us -> 2.43 us  [ring(): lax.ppermute(array, axis, [(i, (i + by) % count) for i in range(count)])]
    pallas_call x7, Pallas kernels: 18.8 us -> 16.5 us  [call(): pl.pallas_call(body, out_shape=outs, in_specs=[SMEM_SPEC] * len(scalars)...]
    ppermute x6 -> x9, waiting for transfers between devices: 6.9 us -> 8.84 us  [around(): lax.ppermute(array, axis, [(i, (i + s) % count) for i in range(count)])]
    ppermute x6 -> x9, starting transfers between devices: 6.32 us -> 8.03 us  [around(): lax.ppermute(array, axis, [(i, (i + s) % count) for i in range(count)])]
  transfers between devices with their start and end apart: 10 -> 13, of which waited for: 5 -> 5; matrix products, arithmetic and copies ran while one was open for 0% -> 0% of each run, Pallas kernels for 17% -> 16%
where the time goes in v4:
time: 44.1 us; the launch traced here: 43.8 us
  Pallas kernels  16.5 us (37%)
  starting transfers between devices  16.3 us (37%)
  waiting for transfers between devices  8.85 us (20%)
  between operations  2.15 us (5%)
    pallas_call x7, Pallas kernels, call(): pl.pallas_call(body, out_shape=outs, in_specs=[SMEM_SPEC] * len(scalars)...  16.5 us
    ppermute x9, waiting for transfers between devices, around(): lax.ppermute(array, axis, [(i, (i + s) % count) for i in range(count)])  8.84 us
    ppermute x9, starting transfers between devices, around(): lax.ppermute(array, axis, [(i, (i + s) % count) for i in range(count)])  8.03 us
    ppermute x2, starting transfers between devices, beside(): lax.ppermute(array, axis, [(i, i + by) for i in range(count) if 0 <= i +...  5.83 us
    ppermute x2, starting transfers between devices, ring(): lax.ppermute(array, axis, [(i, (i + by) % count) for i in range(count)])  2.43 us
  transfers between devices with their start and end apart: 13, of which 5 were waited for; matrix products, arithmetic and copies ran while one was open for 0% of the time, Pallas kernels for 16%

profile of v4, /device:TPU:0, one launch (start us, length us, event | category | flops | bytes accessed | tf_op | source)
XLA Modules:
  0.0 43.8 jit_solution(1875514407647273074)
XLA Ops:
  0.6 0.0 copy-start.7
  0.6 0.0 copy-start.1
  0.7 0.0 copy-start.2
  0.7 0.0 copy-start.3
  0.7 0.0 copy-start.4
  0.7 0.0 copy-start.5
  0.7 1.6 %shard_map.165.po_ref = f32[40,512]{1,0:T(8,128)} custom-call(f32[3,1,512]{2,1,0:T(1,128)} %bitcast.13, f32[3,1,512]{2,1,0:T(1,128)} %bitcast.12, s32[512]{0:T(512)} %species_ref.1, s32[8,512]{1,0:T(8,128)} %nbr_ref.1, s32[512]{0:T(512)} %counts_ref.1, f32[3,8,512]{2,1,0:T(8,128)} %bitcast.11), custom_call_target="tpu_custom_call" | custom-call | bytes 262144 | tf_op jit(solution)/shard_map/pallas_call | solution.py:596
  2.3 0.0 copy-start
  2.3 2.4 %collective-permute-start.1 = (f32[40,512]{1,0:T(8,128)}, f32[40,512]{1,0:T(8,128)S(1)}, u32[]{:S(2)}, u32[]{:S(2)}) collective-permute-start(f32[40,512]{1,0:T(8,128)} %shard_map.165.po_ref), channel_id=1, source_target_pairs={{0,12},{4,0},{8,4},{12,8},{1,13},{5,1},{9,5},{13,9},{2,14},{6,2},{... | collective-permute-start | bytes 245768 | tf_op jit(solution)/shard_map/ppermute | solution.py:614
  4.7 0.0 collective-permute-start
  4.7 0.0 copy-done.7
  4.7 1.3 %collective-permute-start.3 = (f32[3,1,512]{2,1,0:T(1,128)S(1)}, f32[3,1,512]{2,1,0:T(1,128)S(1)}, u32[]{:S(2)}, u32[]{:S(2)}) collective-permute-start(f32[3,1,512]{2,1,0:T(1,128)S(1)} %bitcast.14), channel_id=1, source_target_pairs={{1,0},{2,1},{3,2},{5,4},{6,5},{7,6},{9,8},{10,9},{11,10},{13,12},{... | collective-permute-start | bytes 18440 | tf_op jit(solution)/shard_map/ppermute | solution.py:619
  6.0 4.5 %collective-permute-start.2 = (f32[3,1,512]{2,1,0:T(1,128)S(1)}, f32[3,1,512]{2,1,0:T(1,128)S(1)}, u32[]{:S(2)}, u32[]{:S(2)}) collective-permute-start(f32[3,1,512]{2,1,0:T(1,128)S(1)} %bitcast.15), channel_id=1, source_target_pairs={{0,1},{1,2},{2,3},{4,5},{5,6},{6,7},{8,9},{9,10},{10,11},{12,13},{... | collective-permute-start | bytes 18440 | tf_op jit(solution)/shard_map/ppermute | solution.py:619
  10.5 0.0 copy-done.1
  10.6 0.0 copy-done.2
  10.6 0.0 copy-done.3
  10.6 0.0 copy-done.4
  10.6 0.0 copy-done.5
  10.6 0.5 %shard_map.166 = (bf16[64,48]{1,0:T(8,128)(2,1)S(1)}, bf16[64,192]{1,0:T(8,128)(2,1)S(1)}, bf16[64,32]{1,0:T(8,128)(2,1)S(1)}, bf16[64,192]{1,0:T(8,128)(2,1)S(1...) custom-call(f32[2,64]{1,0:T(2,128)S(1)} %copy-done.4, f32[2,8,64]{2,1,0:T(8,128)S(1)} %copy-done.3, ...), custom_call_target="tpu_custom_call" | custom-call | flops 10000000 | bytes 262144 | tf_op jit(solution)/shard_map/pallas_call | solution.py:596
  11.1 0.0 collective-permute-done.1.pr_ref
  11.1 0.0 collective-permute-done.pl_ref
  11.1 0.0 copy-done
  11.2 6.4 %shard_map.167.force_ref = f32[3,512]{1,0:T(4,128)S(1)} custom-call(f32[40,512]{1,0:T(8,128)S(1)} %collective-permute-done.pl_ref, f32[40,512]{1,0:T(8,128)S(1)} %copy-done, f32[40,512]{1,0:T(8,128)S(1)} %collective-permute-done.1.pr_ref, bf16[64,48]{1,0:T(8,128)(2,1)S(1)} %get-tuple-element.18.rest_0_.rest_3_, ...), custom_call_target="tpu_custom_call" | custom-call | flops 1000000000 | bytes 262144 | tf_op jit(solution)/shard_map/pallas_call | solution.py:596
  17.5 0.0 collective-permute-done.3.after_ref
  17.6 0.0 collective-permute-done.2.before_ref
  17.6 0.1 shard_map.168.own_ref
  17.7 1.2 %collective-permute-start.6 = (f32[8,512]{1,0:T(8,128)S(1)}, f32[8,512]{1,0:T(8,128)S(1)}, u32[]{:S(2)}, u32[]{:S(2)}) collective-permute-start(f32[8,512]{1,0:T(8,128)S(1)} %shard_map.168.own_ref), channel_id=1, source_target_pairs={{0,12},{4,0},{8,4},{12,8},{1,13},{5,1},{9,5},{13,9},{2,14},{6,2},{... | collective-permute-start | bytes 49160 | tf_op jit(solution)/shard_map/ppermute | solution.py:609
  18.9 0.6 %collective-permute-start.5 = (f32[8,512]{1,0:T(8,128)S(1)}, f32[8,512]{1,0:T(8,128)S(1)}, u32[]{:S(2)}, u32[]{:S(2)}) collective-permute-start(f32[8,512]{1,0:T(8,128)S(1)} %shard_map.168.own_ref), channel_id=1, source_target_pairs={{0,8},{4,12},{8,0},{12,4},{1,9},{5,13},{9,1},{13,5},{2,10},{6,14},... | collective-permute-start | bytes 49160 | tf_op jit(solution)/shard_map/ppermute | solution.py:609
  19.5 0.0 collective-permute-start.4
  20.8 0.0 copy-start.6
  20.8 0.0 collective-permute-done.6.rest_2_
  20.8 1.9 %collective-permute-done.5.rest_1_ = f32[8,512]{1,0:T(8,128)S(1)} collective-permute-done((f32[8,512]{1,0:T(8,128)S(1)}, f32[8,512]{1,0:T(8,128)S(1)}, u32[]{:S(2)}, u32[]{:S(2)}) %collective-permute-start.5) | collective-permute-done | bytes 16416 | tf_op jit(solution)/shard_map/ppermute | solution.py:609
  22.7 0.0 collective-permute-done.4.rest_0_
  22.8 7.0 %shard_map.169 = (f32[40,128]{1,0:T(8,128)S(1)}, f32[2,128]{1,0:T(2,128)S(1)}) custom-call(f32[1]{0:T(128)S(6)} %copy.19.dt_ref, s32[1,2]{1,0:T(1,128)S(1)} %bitcast.10, s32[1]{0:T(128)S(6)} %copy.20.climb_ref, f32[40,512]{1,0:T(8,128)S(1)} %collective-permute-done.pl_ref, f32[40,512]{1,0:T(8,128)S(1)} %copy-done, ...), custom_call_target="tpu_custom_call" | custom-call | flops 1000000000 | bytes 262144 | tf_op jit(solution)/shard_map/pallas_call | solution.py:596
  29.8 1.7 %collective-permute-start.9 = (f32[40,128]{1,0:T(8,128)S(1)}, f32[40,128]{1,0:T(8,128)S(1)}, u32[]{:S(2)}, u32[]{:S(2)}) collective-permute-start(f32[40,128]{1,0:T(8,128)S(1)} %get-tuple-element.24.refs_0_.own_ref), channel_id=1, source_target_pairs={{0,3},{1,0},{2,1},{3,2},{4,7},{5,4},{6,5},{7,6},{8,11},{9,8},{10,9... | collective-permute-start | bytes 61448 | tf_op jit(solution)/shard_map/ppermute | solution.py:609
  31.5 1.4 %collective-permute-start.8 = (f32[40,128]{1,0:T(8,128)S(1)}, f32[40,128]{1,0:T(8,128)S(1)}, u32[]{:S(2)}, u32[]{:S(2)}) collective-permute-start(f32[40,128]{1,0:T(8,128)S(1)} %get-tuple-element.24.refs_0_.own_ref), channel_id=1, source_target_pairs={{0,2},{1,3},{2,0},{3,1},{4,6},{5,7},{6,4},{7,5},{8,10},{9,11},{10,... | collective-permute-start | bytes 61448 | tf_op jit(solution)/shard_map/ppermute | solution.py:609
  32.8 1.6 %collective-permute-start.7 = (f32[40,128]{1,0:T(8,128)S(1)}, f32[40,128]{1,0:T(8,128)S(1)}, u32[]{:S(2)}, u32[]{:S(2)}) collective-permute-start(f32[40,128]{1,0:T(8,128)S(1)} %get-tuple-element.24.refs_0_.own_ref), channel_id=1, source_target_pairs={{0,1},{1,2},{2,3},{3,0},{4,5},{5,6},{6,7},{7,4},{8,9},{9,10},{10,1... | collective-permute-start | bytes 61448 | tf_op jit(solution)/shard_map/ppermute | solution.py:609
  34.4 0.0 collective-permute-done.9.refs_3_
  34.4 1.7 %collective-permute-done.8.refs_2_ = f32[40,128]{1,0:T(8,128)S(1)} collective-permute-done((f32[40,128]{1,0:T(8,128)S(1)}, f32[40,128]{1,0:T(8,128)S(1)}, u32[]{:S(2)}, u32[]{:S(2)}) %collective-permute-start.8) | collective-permute-done | bytes 20512 | tf_op jit(solution)/shard_map/ppermute | solution.py:609
  36.2 2.3 %collective-permute-done.7.refs_1_ = f32[40,128]{1,0:T(8,128)S(1)} collective-permute-done((f32[40,128]{1,0:T(8,128)S(1)}, f32[40,128]{1,0:T(8,128)S(1)}, u32[]{:S(2)}, u32[]{:S(2)}) %collective-permute-start.7) | collective-permute-done | bytes 20512 | tf_op jit(solution)/shard_map/ppermute | solution.py:609
  38.4 0.2 shard_map.170
  38.7 0.1 collective-permute-start.12
  38.7 1.3 %collective-permute-start.11 = (f32[8,128]{1,0:T(8,128)S(1)}, f32[8,128]{1,0:T(8,128)S(1)}, u32[]{:S(2)}, u32[]{:S(2)}) collective-permute-start(f32[8,128]{1,0:T(8,128)S(1)} %get-tuple-element.27.sums_ref), channel_id=1, source_target_pairs={{0,8},{4,12},{8,0},{12,4},{1,9},{5,13},{9,1},{13,5},{2,10},{6,14},... | collective-permute-start | bytes 12296 | tf_op jit(solution)/shard_map/ppermute | solution.py:609
  40.1 0.2 collective-permute-start.10
  40.2 0.0 collective-permute-done.12.rest_2_
  40.2 2.2 %collective-permute-done.11.rest_1_ = f32[8,128]{1,0:T(8,128)S(1)} collective-permute-done((f32[8,128]{1,0:T(8,128)S(1)}, f32[8,128]{1,0:T(8,128)S(1)}, u32[]{:S(2)}, u32[]{:S(2)}) %collective-permute-start.11) | collective-permute-done | bytes 4128 | tf_op jit(solution)/shard_map/ppermute | solution.py:609
  42.4 0.7 %collective-permute-done.10.rest_0_ = f32[8,128]{1,0:T(8,128)S(1)} collective-permute-done((f32[8,128]{1,0:T(8,128)S(1)}, f32[8,128]{1,0:T(8,128)S(1)}, u32[]{:S(2)}, u32[]{:S(2)}) %collective-permute-start.10) | collective-permute-done | bytes 4128 | tf_op jit(solution)/shard_map/ppermute | solution.py:609
  43.1 0.7 %shard_map.171 = (f32[3,1,512]{2,1,0:T(1,128)}, f32[3,1,512]{2,1,0:T(1,128)}, f32[2,1,2]{2,1,0:T(1,128)}, f32[1,1]{1,0:T(1,128)}) custom-call(s32[1]{0:T(128)S(6)} %copy.20.climb_ref, f32[40,128]{1,0:T(8,128)S(1)} %get-tuple-element.24.refs_0_.own_ref, f32[2,128]{1,0:T(2,128)S(1)} %get-tuple-element.25.record_ref, ...), custom_call_target="tpu_custom_call" | custom-call | bytes 262144 | tf_op jit(solution)/shard_map/pallas_call | solution.py:596
  (1 shorter events, 0.0 us)
Async XLA Ops:
  0.6 4.1 %copy-start.7 = (f32[1,3,512]{2,0,1:T(1,128)S(1)}, f32[1,3,512]{2,0,1:T(1,128)}, u32[]{:S(2)}) copy-start(f32[1,3,512]{2,0,1:T(1,128)} %param.14) | copy-start | bytes 18436
  0.6 9.9 %copy-start.1 = (f32[2,64,64]{2,1,0:T(8,128)S(1)}, f32[2,64,64]{2,1,0:T(8,128)}, u32[]{:S(2)}) copy-start(f32[2,64,64]{2,1,0:T(8,128)} %mix_ref.1) | copy-start | bytes 98308
  0.7 9.9 %copy-start.2 = (f32[2,64,64]{2,1,0:T(8,128)S(1)}, f32[2,64,64]{2,1,0:T(8,128)}, u32[]{:S(2)}) copy-start(f32[2,64,64]{2,1,0:T(8,128)} %update_ref.1) | copy-start | bytes 98308
  0.7 9.9 %copy-start.3 = (f32[2,8,64]{2,1,0:T(8,128)S(1)}, f32[2,8,64]{2,1,0:T(8,128)}, u32[]{:S(2)}) copy-start(f32[2,8,64]{2,1,0:T(8,128)} %radial_ref.1) | copy-start | bytes 12292
  0.7 9.9 %copy-start.4 = (f32[2,64]{1,0:T(2,128)S(1)}, f32[2,64]{1,0:T(2,128)}, u32[]{:S(2)}) copy-start(f32[2,64]{1,0:T(2,128)} %embed_ref.1) | copy-start | bytes 1540
  0.7 9.9 %copy-start.5 = (f32[64]{0:T(128)S(1)}, f32[64]{0:T(128)}, u32[]{:S(2)}) copy-start(f32[64]{0:T(128)} %readout_ref.1) | copy-start | bytes 772
  2.3 8.9 %copy-start = (f32[40,512]{1,0:T(8,128)S(1)}, f32[40,512]{1,0:T(8,128)}, u32[]{:S(2)}) copy-start(f32[40,512]{1,0:T(8,128)} %shard_map.165.po_ref) | copy-start | bytes 245764
  2.3 8.9 %collective-permute-start.1 = (f32[40,512]{1,0:T(8,128)}, f32[40,512]{1,0:T(8,128)S(1)}, u32[]{:S(2)}, u32[]{:S(2)}) collective-permute-start(f32[40,512]{1,0:T(8,128)} %shard_map.165.po_ref), channel_id=1, source_target_pairs={{0,12},{4,0},{8,4},{12,8},{1,13},{5,1},{9,5},{13,9},{2,14},{6,2},{... | collective-permute-start | bytes 245768 | tf_op jit(solution)/shard_map/ppermute | solution.py:614
  4.7 6.4 %collective-permute-start = (f32[40,512]{1,0:T(8,128)}, f32[40,512]{1,0:T(8,128)S(1)}, u32[]{:S(2)}, u32[]{:S(2)}) collective-permute-start(f32[40,512]{1,0:T(8,128)} %shard_map.165.po_ref), channel_id=1, source_target_pairs={{0,4},{4,8},{8,12},{12,0},{1,5},{5,9},{9,13},{13,1},{2,6},{6,10},{... | collective-permute-start | bytes 245768 | tf_op jit(solution)/shard_map/ppermute | solution.py:614
  4.7 12.8 %collective-permute-start.3 = (f32[3,1,512]{2,1,0:T(1,128)S(1)}, f32[3,1,512]{2,1,0:T(1,128)S(1)}, u32[]{:S(2)}, u32[]{:S(2)}) collective-permute-start(f32[3,1,512]{2,1,0:T(1,128)S(1)} %bitcast.14), channel_id=1, source_target_pairs={{1,0},{2,1},{3,2},{5,4},{6,5},{7,6},{9,8},{10,9},{11,10},{13,12},{... | collective-permute-start | bytes 18440 | tf_op jit(solution)/shard_map/ppermute | solution.py:619
  6.0 11.6 %collective-permute-start.2 = (f32[3,1,512]{2,1,0:T(1,128)S(1)}, f32[3,1,512]{2,1,0:T(1,128)S(1)}, u32[]{:S(2)}, u32[]{:S(2)}) collective-permute-start(f32[3,1,512]{2,1,0:T(1,128)S(1)} %bitcast.15), channel_id=1, source_target_pairs={{0,1},{1,2},{2,3},{4,5},{5,6},{6,7},{8,9},{9,10},{10,11},{12,13},{... | collective-permute-start | bytes 18440 | tf_op jit(solution)/shard_map/ppermute | solution.py:619
  17.7 3.1 %collective-permute-start.6 = (f32[8,512]{1,0:T(8,128)S(1)}, f32[8,512]{1,0:T(8,128)S(1)}, u32[]{:S(2)}, u32[]{:S(2)}) collective-permute-start(f32[8,512]{1,0:T(8,128)S(1)} %shard_map.168.own_ref), channel_id=1, source_target_pairs={{0,12},{4,0},{8,4},{12,8},{1,13},{5,1},{9,5},{13,9},{2,14},{6,2},{... | collective-permute-start | bytes 49160 | tf_op jit(solution)/shard_map/ppermute | solution.py:609
  18.9 3.9 %collective-permute-start.5 = (f32[8,512]{1,0:T(8,128)S(1)}, f32[8,512]{1,0:T(8,128)S(1)}, u32[]{:S(2)}, u32[]{:S(2)}) collective-permute-start(f32[8,512]{1,0:T(8,128)S(1)} %shard_map.168.own_ref), channel_id=1, source_target_pairs={{0,8},{4,12},{8,0},{12,4},{1,9},{5,13},{9,1},{13,5},{2,10},{6,14},... | collective-permute-start | bytes 49160 | tf_op jit(solution)/shard_map/ppermute | solution.py:609
  19.5 3.3 %collective-permute-start.4 = (f32[8,512]{1,0:T(8,128)S(1)}, f32[8,512]{1,0:T(8,128)S(1)}, u32[]{:S(2)}, u32[]{:S(2)}) collective-permute-start(f32[8,512]{1,0:T(8,128)S(1)} %shard_map.168.own_ref), channel_id=1, source_target_pairs={{0,4},{4,8},{8,12},{12,0},{1,5},{5,9},{9,13},{13,1},{2,6},{6,10},{... | collective-permute-start | bytes 49160 | tf_op jit(solution)/shard_map/ppermute | solution.py:609
  20.8 2.0 %copy-start.6 = (s32[2,1]{0,1:T(1,128)S(1)}, s32[2,1]{0,1:T(1,128)}, u32[]{:S(2)}) copy-start(s32[2,1]{0,1:T(1,128)} %param.17) | copy-start | bytes 28
  29.8 4.7 %collective-permute-start.9 = (f32[40,128]{1,0:T(8,128)S(1)}, f32[40,128]{1,0:T(8,128)S(1)}, u32[]{:S(2)}, u32[]{:S(2)}) collective-permute-start(f32[40,128]{1,0:T(8,128)S(1)} %get-tuple-element.24.refs_0_.own_ref), channel_id=1, source_target_pairs={{0,3},{1,0},{2,1},{3,2},{4,7},{5,4},{6,5},{7,6},{8,11},{9,8},{10,9... | collective-permute-start | bytes 61448 | tf_op jit(solution)/shard_map/ppermute | solution.py:609
  31.5 4.7 %collective-permute-start.8 = (f32[40,128]{1,0:T(8,128)S(1)}, f32[40,128]{1,0:T(8,128)S(1)}, u32[]{:S(2)}, u32[]{:S(2)}) collective-permute-start(f32[40,128]{1,0:T(8,128)S(1)} %get-tuple-element.24.refs_0_.own_ref), channel_id=1, source_target_pairs={{0,2},{1,3},{2,0},{3,1},{4,6},{5,7},{6,4},{7,5},{8,10},{9,11},{10,... | collective-permute-start | bytes 61448 | tf_op jit(solution)/shard_map/ppermute | solution.py:609
  32.8 5.6 %collective-permute-start.7 = (f32[40,128]{1,0:T(8,128)S(1)}, f32[40,128]{1,0:T(8,128)S(1)}, u32[]{:S(2)}, u32[]{:S(2)}) collective-permute-start(f32[40,128]{1,0:T(8,128)S(1)} %get-tuple-element.24.refs_0_.own_ref), channel_id=1, source_target_pairs={{0,1},{1,2},{2,3},{3,0},{4,5},{5,6},{6,7},{7,4},{8,9},{9,10},{10,1... | collective-permute-start | bytes 61448 | tf_op jit(solution)/shard_map/ppermute | solution.py:609
  38.7 1.6 %collective-permute-start.12 = (f32[8,128]{1,0:T(8,128)S(1)}, f32[8,128]{1,0:T(8,128)S(1)}, u32[]{:S(2)}, u32[]{:S(2)}) collective-permute-start(f32[8,128]{1,0:T(8,128)S(1)} %get-tuple-element.27.sums_ref), channel_id=1, source_target_pairs={{0,12},{4,0},{8,4},{12,8},{1,13},{5,1},{9,5},{13,9},{2,14},{6,2},{... | collective-permute-start | bytes 12296 | tf_op jit(solution)/shard_map/ppermute | solution.py:609
  38.7 3.7 %collective-permute-start.11 = (f32[8,128]{1,0:T(8,128)S(1)}, f32[8,128]{1,0:T(8,128)S(1)}, u32[]{:S(2)}, u32[]{:S(2)}) collective-permute-start(f32[8,128]{1,0:T(8,128)S(1)} %get-tuple-element.27.sums_ref), channel_id=1, source_target_pairs={{0,8},{4,12},{8,0},{12,4},{1,9},{5,13},{9,1},{13,5},{2,10},{6,14},... | collective-permute-start | bytes 12296 | tf_op jit(solution)/shard_map/ppermute | solution.py:609
  40.1 3.0 %collective-permute-start.10 = (f32[8,128]{1,0:T(8,128)S(1)}, f32[8,128]{1,0:T(8,128)S(1)}, u32[]{:S(2)}, u32[]{:S(2)}) collective-permute-start(f32[8,128]{1,0:T(8,128)S(1)} %get-tuple-element.27.sums_ref), channel_id=1, source_target_pairs={{0,4},{4,8},{8,12},{12,0},{1,5},{5,9},{9,13},{13,1},{2,6},{6,10},{... | collective-permute-start | bytes 12296 | tf_op jit(solution)/shard_map/ppermute | solution.py:609

commit v5 on v4

--- a/solution.py
+++ b/solution.py
@@ -79,8 +79,12 @@
 
 
 def weight_kernel(
-    embed_ref, radial_ref, mix_ref, update_ref, readout_ref, l1_ref, l2_ref, l3_ref, l5_ref, l6_ref, col_ref
+    dt_ref, flag_ref, climb_ref, x_ref, embed_ref, radial_ref, mix_ref, update_ref, readout_ref, l1_ref, l2_ref, l3_ref, l5_ref, l6_ref, col_ref, copy_ref, number_ref
 ):
+    copy_ref[...] = x_ref[...]
+    flags = [flag_ref[0, s].astype(F32) for s in range(flag_ref.shape[1])]
+    for i, value in enumerate([dt_ref[0], climb_ref[0].astype(F32)] + flags):
+        number_ref[i : i + 1, :] = jnp.full((1, LANES), value, F32)
     eye = (
         lax.broadcasted_iota(jnp.int32, (CHANNELS, CHANNELS), 0)
         == lax.broadcasted_iota(jnp.int32, (CHANNELS, CHANNELS), 1)
@@ -207,14 +211,16 @@
             sent_all[:, (b + i) * LANES : (b + i + 1) * LANES] = one
         slope[:, cols] = steep
 
+    def reach(b, first, last):
+        return [w for w in range(3) if first <= b - 1 + w <= last]
+
     def mark(b):
         index = widx[b]
+        ws = reach(b, 3, 8)
+        rows = slice(ws[0] * LANES, (ws[-1] + 1) * LANES)
         for k in range(SLOTS):
-            same = row_id == jnp.broadcast_to(index[k : k + 1, :], (3 * LANES, LANES))
-            hot[b, :, k * LANES : (k + 1) * LANES] = jnp.where(same, 1.0, 0.0).astype(BF16)
-
-    def reach(b, first, last):
-        return [w for w in range(3) if first <= b - 1 + w <= last]
+            same = row_id[rows] == jnp.broadcast_to(index[k : k + 1, :], (rows.stop - rows.start, LANES))
+            hot[b, rows, k * LANES : (k + 1) * LANES] = jnp.where(same, 1.0, 0.0).astype(BF16)
 
     def spread(left, b, first, last):
         ws = reach(b, first, last)
@@ -350,8 +356,14 @@
     ]
 
 
-def first_kernel(pl_ref, po_ref, pr_ref, *rest):
-    weights, out_ref, scr = rest[:6], rest[6], rest[7:]
+def by_parity(sibling, across):
+    even = jnp.full(sibling.shape, lax.axis_index("dom") % 2, jnp.int32) == 0
+    return jnp.where(even, across, sibling), jnp.where(even, sibling, across)
+
+
+def first_kernel(sibling_ref, po_ref, across_ref, *rest):
+    weights, (out_ref, pl_ref, pr_ref), scr = rest[:6], rest[6:9], rest[9:]
+    pl_ref[...], pr_ref[...] = by_parity(sibling_ref[...], across_ref[...])
     packs = [pl_ref, po_ref, pr_ref]
     fill_region(scr[0], packs, lambda s: packs[s][ROW_X : ROW_X + 3, :])
     force_parts(packs, weights, scr)
@@ -368,12 +380,13 @@
     return jnp.concatenate(values, axis=1)
 
 
-def blend_kernel(force_ref, po_ref, before_ref, after_ref, out_ref):
+def blend_kernel(images, force_ref, po_ref, before_ref, after_ref, out_ref):
     x = po_ref[ROW_X : ROW_X + 3, :]
     v = po_ref[ROW_V : ROW_V + 3, :]
     force = force_ref[...]
-    before = rows_of(before_ref)
-    after = rows_of(after_ref)
+    here = lax.axis_index("img")
+    before = jnp.where(here > 0, rows_of(before_ref), 0.0)
+    after = jnp.where(here < images - 1, rows_of(after_ref), 0.0)
     tangent = after - before
     plus = after - x
     minus = x - before
@@ -419,14 +432,35 @@
     )
 
 
-def second_kernel(images, others, dt_ref, flag_ref, climb_ref, pl_ref, po_ref, pr_ref, own_ref, *rest):
+def forward_kernel(own_ref, sibling_ref, out_ref):
+    out_ref[0:6, :] = sibling_ref[0:6, :]
+    out_ref[6:8, :] = own_ref[6:8, :] + sibling_ref[6:8, :]
+
+
+def add_kernel(a_ref, b_ref, out_ref):
+    out_ref[...] = a_ref[...] + b_ref[...]
+
+
+def join_kernel(a_ref, b_ref, out_ref):
+    count = a_ref.shape[0]
+    out_ref[0:count] = a_ref[...]
+    out_ref[count : 2 * count] = b_ref[...]
+
+
+def second_kernel(images, others, paired, number_ref, pl_ref, po_ref, pr_ref, own_ref, *rest):
     heard, rest = rest[:others], rest[others:]
     weights, out_ref, record_ref, scr = rest[:6], rest[6], rest[7], rest[8:]
     packs = [pl_ref, po_ref, pr_ref]
     here = lax.axis_index("img")
-    sums = own_ref[6:8, :]
-    for one in heard:
-        sums = sums + one[6:8, :]
+    if others == 3 and paired:
+        sibling, both, far = heard
+        sums = both[6:8, :] + far[6:8, :]
+        beside = by_parity(sibling[0:6, :], far[0:6, :])
+    else:
+        sums = own_ref[6:8, :]
+        for one in heard:
+            sums = sums + one[6:8, :]
+        beside = heard[0][0:6, :], heard[others - 1][0:6, :]
     ft, ff, tt, pp = (sums[0:1, i * LANES : (i + 1) * LANES] for i in range(4))
     mn, vv = (sums[1:2, i * LANES : (i + 1) * LANES] for i in range(2))
     shape = (1, LANES)
@@ -437,13 +471,13 @@
         pp,
         mn,
         vv,
-        jnp.full(shape, dt_ref[0], F32),
+        number_ref[0:1, :],
         jnp.full(shape, ALPHA_START, F32),
-        jnp.full(shape, flag_ref[0, 0], jnp.int32) == 1,
-        jnp.full(shape, here - climb_ref[0], jnp.int32) == 0,
+        number_ref[2:3, :] == 1.0,
+        number_ref[1:2, :] == jnp.full(shape, here, jnp.int32).astype(F32),
         jnp.full(shape, jnp.where((here >= 1) & (here <= images - 2), 1, 0), jnp.int32) == 1,
     )
-    messages = [heard[0], own_ref, heard[others - 1]]
+    messages = [beside[0], own_ref[0:6, :], beside[1]]
 
     def wide(s):
         return jnp.concatenate([s] * SLAB_BLOCKS, axis=1)
@@ -460,12 +494,12 @@
         for i in range(SLAB_BLOCKS):
             lanes = slice(i * LANES, (i + 1) * LANES)
             row = 4 * c + i
-            out_ref[row : row + 1, :] = speeds[1][c : c + 1, lanes]
-            out_ref[12 + row : 13 + row, :] = force[:, lanes]
-            out_ref[24 + row : 25 + row, :] = moved[1][c : c + 1, lanes]
-    out_ref[36:37, :] = dt
-    out_ref[37:38, :] = alpha
-    out_ref[38:40, :] = jnp.full((2, LANES), flag_ref[0, 1], jnp.int32).astype(F32)
+            out_ref[0, row : row + 1, :] = speeds[1][c : c + 1, lanes]
+            out_ref[0, 12 + row : 13 + row, :] = force[:, lanes]
+            out_ref[0, 24 + row : 25 + row, :] = moved[1][c : c + 1, lanes]
+    out_ref[0, 36:37, :] = dt
+    out_ref[0, 37:38, :] = alpha
+    out_ref[0, 38:40, :] = jnp.broadcast_to(number_ref[3:4, :], (2, LANES))
     record_ref[0:1, :] = along
     record_ref[1:2, :] = spring
 
@@ -477,36 +511,33 @@
 )
 
 
-def gram_kernel(images, *refs):
-    messages, out_ref, state_ref = refs[:images], refs[images], refs[images + 1]
+def gram_kernel(images, messages_ref, out_ref, state_ref):
     rows = out_ref.shape[0]
     here = lax.axis_index("img")
     blank = [jnp.zeros((rows - images, LANES), F32)] if rows > images else []
+    zero = jnp.zeros((1, LANES), F32)
 
     def gathered(row):
-        return jnp.concatenate([m[row : row + 1, :] for m in messages] + blank, axis=0)
-
-    def shifted(value, by):
-        lines = [value[(s + by) % images : (s + by) % images + 1, :] for s in range(images)]
-        return jnp.concatenate(lines + blank, axis=0)
-
-    offset = lax.broadcasted_iota(jnp.int32, (rows, LANES), 0)
-    number = here - offset
-    number = jnp.where(number < 0, number + images, number)
-    has_after = (number < images - 1) & (offset < images)
-    has_before = (number > 0) & (offset < images)
+        return jnp.concatenate([messages_ref[here ^ i, row : row + 1, :] for i in range(images)] + blank, axis=0)
+
+    def earlier(value):
+        return jnp.concatenate([zero, value[0 : rows - 1]], axis=0)
+
+    def later(value):
+        return jnp.concatenate([value[1:images], zero] + blank, axis=0)
+
+    number = lax.broadcasted_iota(jnp.int32, (rows, LANES), 0)
+    held = number < images
     totals = [jnp.zeros((rows, LANES), F32) for _ in PRODUCTS]
     for row in range(3 * SLAB_BLOCKS):
         v, f, x = gathered(row), gathered(12 + row), gathered(24 + row)
-        after = jnp.where(has_after, shifted(x, -1), 0.0)
-        before = jnp.where(has_before, shifted(x, 1), 0.0)
+        before = jnp.where(held, earlier(x), 0.0)
+        after = later(x)
         t = after - before
         table = {"f": f, "v": v, "t": t, "p": after - x, "d": x - before}
-        table["F"] = jnp.where(has_before, shifted(f, 1), 0.0)
-        table["V"] = jnp.where(has_before, shifted(v, 1), 0.0)
-        table["T"] = jnp.where(has_before, shifted(t, 1), 0.0)
+        table["F"], table["V"], table["T"] = earlier(f), earlier(v), earlier(t)
         totals = [old + table[a] * table[b] for old, (a, b) in zip(totals, PRODUCTS)]
-        state_ref[row : row + 1, :] = t[0:1]
+        state_ref[row : row + 1, :] = jnp.sum(jnp.where(number == here, t, 0.0), axis=0, keepdims=True)
     lane = lax.broadcasted_iota(jnp.int32, (rows, LANES), 1)
     result = jnp.zeros((rows, LANES), F32)
     for q, one in enumerate(totals):
@@ -517,22 +548,17 @@
         state_ref[16 + rows * i : 16 + rows * (i + 1), :] = gathered(36 + i)
 
 
-def final_kernel(images, others, atoms, climb_ref, own_ref, record_ref, state_ref, sums_ref, *rest):
-    heard, (x_ref, v_ref, band_ref, path_ref) = rest[:others], rest[others:]
+def final_kernel(images, atoms, number_ref, own_ref, record_ref, state_ref, sums_ref, more_ref, *rest):
+    x_ref, v_ref, band_ref, path_ref = rest
     rows = sums_ref.shape[0]
     here = lax.axis_index("img")
-    sums = sums_ref[...]
-    for one in heard:
-        sums = sums + one[...]
+    sums = sums_ref[...] + more_ref[...]
     got = {
         pair: jnp.broadcast_to(sums[:, q : q + 1], (rows, LANES)) for q, pair in enumerate(PRODUCTS)
     }
-    offset = lax.broadcasted_iota(jnp.int32, (rows, LANES), 0)
-    number = here - offset
-    number = jnp.where(number < 0, number + images, number)
-    inside = (number >= 1) & (number <= images - 2) & (offset < images)
-    has_before = (number > 0) & (offset < images)
-    climb = jnp.full((rows, LANES), climb_ref[0], jnp.int32)
+    number = lax.broadcasted_iota(jnp.int32, (rows, LANES), 0)
+    inside = (number >= 1) & (number <= images - 2)
+    climb = jnp.broadcast_to(number_ref[1:2, :], (rows, LANES))
     dt0, alpha0, flag = (state_ref[16 + rows * i : 16 + rows * (i + 1), :] for i in range(3))
     along, spring, keep, pull, side, dt, _ = step_numbers(
         got["f", "t"],
@@ -544,15 +570,12 @@
         dt0,
         alpha0,
         flag == 1.0,
-        number == climb,
+        number.astype(F32) == climb,
         inside,
     )
 
     def shifted(value):
-        lines = [value[(s + 1) % images : (s + 1) % images + 1, :] for s in range(images)]
-        if rows > images:
-            lines.append(jnp.zeros((rows - images, LANES), F32))
-        return jnp.where(has_before, jnp.concatenate(lines, axis=0), 0.0)
+        return jnp.concatenate([jnp.zeros((1, LANES), F32), value[0 : rows - 1]], axis=0)
 
     now = {"v": dt * keep, "f": dt * pull, "t": dt * side}
     old = {a.upper(): shifted(value) for a, value in now.items()}
@@ -570,21 +593,25 @@
             both = both - now[a] * old[b] * got[a, b]
     squared = got["d", "d"] + mine + shifted(mine) + 2.0 * both
     segment = jnp.sqrt(jnp.maximum(squared, 0.0) * (1.0 / (3.0 * atoms)))
-    path = jnp.sum(jnp.where(offset <= here, segment, 0.0), axis=0, keepdims=True)
+    path = jnp.sum(jnp.where(number <= here, segment, 0.0), axis=0, keepdims=True)
     path_ref[...] = path[:, 0:1]
+    keep, pull, side, dt, along, spring = (
+        jnp.sum(jnp.where(number == here, value, 0.0), axis=0, keepdims=True)
+        for value in (keep, pull, side, dt, along, spring)
+    )
 
     for c in range(3):
         speeds, places = [], []
         for i in range(SLAB_BLOCKS):
             row = 4 * c + i
-            speed = keep[0:1] * own_ref[row : row + 1, :] + pull[0:1] * own_ref[12 + row : 13 + row, :]
-            speed = speed + side[0:1] * state_ref[row : row + 1, :]
+            speed = keep * own_ref[0, row : row + 1, :] + pull * own_ref[0, 12 + row : 13 + row, :]
+            speed = speed + side * state_ref[row : row + 1, :]
             speeds.append(speed)
-            places.append(own_ref[24 + row : 25 + row, :] + dt[0:1] * speed)
+            places.append(own_ref[0, 24 + row : 25 + row, :] + dt * speed)
         v_ref[c] = jnp.concatenate(speeds, axis=1)
         x_ref[c] = jnp.concatenate(places, axis=1)
     band_ref[0] = jnp.concatenate([record_ref[0:1, 0:1], record_ref[1:2, 0:1]], axis=1)
-    band_ref[1] = jnp.concatenate([along[0:1, 0:1], spring[0:1, 0:1]], axis=1)
+    band_ref[1] = jnp.concatenate([along[:, 0:1], spring[:, 0:1]], axis=1)
 
 
 VMEM_SPEC = pl.BlockSpec(memory_space=pltpu.VMEM)
@@ -614,9 +641,8 @@
     return lax.ppermute(array, axis, [(i, (i + by) % count) for i in range(count)])
 
 
-def beside(array, axis, by):
-    count = lax.axis_size(axis)
-    return lax.ppermute(array, axis, [(i, i + by) for i in range(count) if 0 <= i + by < count])
+def swap(array, axis, partner):
+    return lax.ppermute(array, axis, [(i, partner(i)) for i in range(lax.axis_size(axis))])
 
 
 def local(
@@ -638,7 +664,8 @@
     atoms = disp.shape[2]
     images = lax.axis_size("img")
     domains = lax.axis_size("dom")
-    assert disp.shape[0] == 1 and atoms == SLAB_BLOCKS * LANES and domains >= 3
+    assert disp.shape[0] == 1 and atoms == SLAB_BLOCKS * LANES and domains >= 4
+    assert domains & (domains - 1) == 0 and images & (images - 1) == 0
     shape = jax.ShapeDtypeStruct
     x = jnp.transpose(disp, (1, 0, 2))
     v = jnp.transpose(veloc, (1, 0, 2))
@@ -651,9 +678,9 @@
         spec=HBM_SPEC,
         vmem=63,
     )
-    left, right = ring(pack, "dom", 1), ring(pack, "dom", -1)
-    before, after = beside(x, "img", 1), beside(x, "img", -1)
-    weights = call(
+    sibling = swap(pack, "dom", lambda i: i ^ 1)
+    across = swap(pack, "dom", lambda i: (i + 2 * (i % 2) - 1) % domains)
+    *weights, x_copy, numbers = call(
         weight_kernel,
         (
             shape((CHANNELS, 48), BF16),
@@ -662,40 +689,64 @@
             shape((CHANNELS, 192), BF16),
             shape((16, 192), BF16),
             shape((4, CHANNELS, LANES), F32),
+            shape(x.shape, F32),
+            shape((8, LANES), F32),
         ),
+        (time_step, jnp.transpose(reset_flags), climb),
+        (x, embed, radial_weight, mix_weight, update_weight, readout),
+        flops=10000000,
+    )
+    before, after = ring(x_copy, "img", 1), ring(x_copy, "img", -1)
+    force, left, right = call(
+        first_kernel,
+        (shape((3, atoms), F32), shape(pack.shape, F32), shape(pack.shape, F32)),
         (),
-        (embed, radial_weight, mix_weight, update_weight, readout),
-        flops=10000000,
-    )
-    force = call(
-        first_kernel, shape((3, atoms), F32), (), (left, pack, right, *weights), scratch(), flops=1000000000
-    )
-    message = call(
-        blend_kernel, shape((8, atoms), F32), (), (force, pack, before, after)
-    )
-    heard = around(message, "dom")
-    state, record = call(
-        functools.partial(second_kernel, images, len(heard)),
-        (shape((40, LANES), F32), shape((2, LANES), F32)),
-        (time_step, jnp.transpose(reset_flags), climb),
-        (left, pack, right, message, *heard, *weights),
+        (sibling, pack, across, *weights),
         scratch(),
         flops=1000000000,
     )
-    band = around(state, "img")
+    message = call(
+        functools.partial(blend_kernel, images), shape((8, atoms), F32), (), (force, pack, before, after)
+    )
+    paired = domains == 4
+    if paired:
+        near = swap(message, "dom", lambda i: i ^ 1)
+        both = call(forward_kernel, shape((8, atoms), F32), (), (message, near))
+        heard = [near, both, swap(both, "dom", lambda i: i ^ 2)]
+    else:
+        heard = around(message, "dom")
+    state, record = call(
+        functools.partial(second_kernel, images, len(heard), paired),
+        (shape((1, 40, LANES), F32), shape((2, LANES), F32)),
+        (),
+        (numbers, left, pack, right, message, *heard, *weights),
+        scratch(),
+        flops=1000000000,
+    )
+    gathered, distance = state, 1
+    while distance < images:
+        more = swap(gathered, "img", lambda i, distance=distance: i ^ distance)
+        gathered = call(join_kernel, shape((2 * distance, 40, LANES), F32), (), (gathered, more))
+        distance *= 2
     rows = 8 * ((images + 7) // 8)
     sums, extra = call(
         functools.partial(gram_kernel, images),
         (shape((rows, LANES), F32), shape((16 + 3 * rows, LANES), F32)),
         (),
-        (state, *band),
-    )
-    others = around(sums, "dom")
+        (gathered,),
+    )
+    distance = 1
+    while True:
+        more = swap(sums, "dom", lambda i, distance=distance: i ^ distance)
+        distance *= 2
+        if distance == domains:
+            break
+        sums = call(add_kernel, shape((rows, LANES), F32), (), (sums, more))
     new_x, new_v, records, path = call(
-        functools.partial(final_kernel, images, len(others), atoms * domains),
+        functools.partial(final_kernel, images, atoms * domains),
         (shape(x.shape, F32), shape(x.shape, F32), shape((2, 1, 2), F32), shape((1, 1), F32)),
-        (climb,),
-        (state, record, extra, sums, *others),
+        (),
+        (numbers, state, record, extra, sums, more),
     )
     return (
         jnp.transpose(new_x, (1, 0, 2)),

time: 44.1 us -> 44.1 us (level)
  waiting for transfers between devices: 8.85 us -> 14.9 us
  starting transfers between devices: 16.3 us -> 10.3 us
    ppermute x11 -> x8, starting transfers between devices: 13.9 us -> 6.68 us  [swap(): lax.ppermute(array, axis, [(i, partner(i)) for i in range(lax.axis_size(a...]
    ppermute x11 -> x8, waiting for transfers between devices: 8.84 us -> 14.9 us  [swap(): lax.ppermute(array, axis, [(i, partner(i)) for i in range(lax.axis_size(a...]
    ppermute x2, starting transfers between devices: 2.43 us -> 3.66 us  [ring(): lax.ppermute(array, axis, [(i, (i + by) % count) for i in range(count)])]
    pallas_call x7 -> x11, Pallas kernels: 16.5 us -> 16.3 us  [call(): pl.pallas_call(body, out_shape=outs, in_specs=[SMEM_SPEC] * len(scalars)...]
  transfers between devices with their start and end apart: 13 -> 10, of which waited for: 5 -> 6; matrix products, arithmetic and copies ran while one was open for 0% -> 0% of each run, Pallas kernels for 16% -> 17%
where the time goes in v5:
time: 44.1 us; the launch traced here: 43.8 us
  Pallas kernels  16.3 us (37%)
  waiting for transfers between devices  14.9 us (34%)
  starting transfers between devices  10.3 us (23%)
  between operations  2.16 us (5%)
    pallas_call x11, Pallas kernels, call(): pl.pallas_call(body, out_shape=outs, in_specs=[SMEM_SPEC] * len(scalars)...  16.3 us
    ppermute x8, waiting for transfers between devices, swap(): lax.ppermute(array, axis, [(i, partner(i)) for i in range(lax.axis_size(a...  14.9 us
    ppermute x8, starting transfers between devices, swap(): lax.ppermute(array, axis, [(i, partner(i)) for i in range(lax.axis_size(a...  6.68 us
    ppermute x2, starting transfers between devices, ring(): lax.ppermute(array, axis, [(i, (i + by) % count) for i in range(count)])  3.66 us
  transfers between devices with their start and end apart: 10, of which 6 were waited for; matrix products, arithmetic and copies ran while one was open for 0% of the time, Pallas kernels for 17%

profile of v5, /device:TPU:0, one launch (start us, length us, event | category | flops | bytes accessed | tf_op | source)
XLA Modules:
  0.0 43.8 jit_solution(6498735232651132407)
XLA Ops:
  0.6 0.0 copy-start.1
  0.6 0.0 copy-start.2
  0.7 0.0 copy-start.3
  0.7 0.0 copy-start.4
  0.7 1.6 %shard_map.166.po_ref = f32[40,512]{1,0:T(8,128)} custom-call(f32[3,1,512]{2,1,0:T(1,128)} %bitcast.10, f32[3,1,512]{2,1,0:T(1,128)} %bitcast.14, s32[512]{0:T(512)} %species_ref.1, s32[8,512]{1,0:T(8,128)} %nbr_ref.1, s32[512]{0:T(512)} %counts_ref.1, f32[3,8,512]{2,1,0:T(8,128)} %bitcast.13), custom_call_target="tpu_custom_call" | custom-call | bytes 262144 | tf_op jit(solution)/shard_map/pallas_call | solution.py:623
  2.2 2.4 %collective-permute-start.1 = (f32[40,512]{1,0:T(8,128)}, f32[40,512]{1,0:T(8,128)S(1)}, u32[]{:S(2)}, u32[]{:S(2)}) collective-permute-start(f32[40,512]{1,0:T(8,128)} %shard_map.166.po_ref), channel_id=1, source_target_pairs={{0,12},{4,8},{8,4},{12,0},{1,13},{5,9},{9,5},{13,1},{2,14},{6,10},... | collective-permute-start | bytes 245768 | tf_op jit(solution)/shard_map/ppermute | solution.py:645
  4.7 0.7 %collective-permute-start = (f32[40,512]{1,0:T(8,128)}, f32[40,512]{1,0:T(8,128)S(1)}, u32[]{:S(2)}, u32[]{:S(2)}) collective-permute-start(f32[40,512]{1,0:T(8,128)} %shard_map.166.po_ref), channel_id=1, source_target_pairs={{0,4},{4,0},{8,12},{12,8},{1,5},{5,1},{9,13},{13,9},{2,6},{6,2},{1... | collective-permute-start | bytes 245768 | tf_op jit(solution)/shard_map/ppermute | solution.py:645
  6.0 0.0 copy-start.5
  6.0 0.0 copy-start.6
  6.0 0.0 copy-start.7
  6.7 0.0 copy-start
  6.7 0.0 copy-done.1
  6.7 0.0 copy-done.2
  6.7 0.0 copy-done.3
  6.8 0.0 copy-done.4
  6.8 0.0 copy-done.5
  6.8 0.0 copy-done.6
  6.8 0.0 copy-done.7
  6.8 1.1 %shard_map.165 = (bf16[64,48]{1,0:T(8,128)(2,1)S(1)}, bf16[64,192]{1,0:T(8,128)(2,1)S(1)}, bf16[64,32]{1,0:T(8,128)(2,1)S(1)}, bf16[64,192]{1,0:T(8,128)(2,1)S(1...) custom-call(f32[1]{0:T(128)S(6)} %copy.19.dt_ref, ...), custom_call_target="tpu_custom_call" | custom-call | flops 10000000 | bytes 262144 | tf_op jit(solution)/shard_map/pallas_call | solution.py:623
  7.9 3.7 %collective-permute-start.3 = (f32[3,1,512]{2,1,0:T(1,128)S(1)}, f32[3,1,512]{2,1,0:T(1,128)S(1)}, u32[]{:S(2)}, u32[]{:S(2)}) collective-permute-start(f32[3,1,512]{2,1,0:T(1,128)S(1)} %get-tuple-element.33), channel_id=1, source_target_pairs={{0,3},{1,0},{2,1},{3,2},{4,7},{5,4},{6,5},{7,6},{8,11},{9,8},{10,9... | collective-permute-start | bytes 18440 | tf_op jit(solution)/shard_map/ppermute | solution.py:641
  11.5 0.0 collective-permute-start.2
  11.5 0.0 collective-permute-done.1.across_ref
  11.5 0.0 collective-permute-done.sibling_ref
  11.5 0.0 copy-done
  11.5 6.3 %shard_map.167 = (f32[3,512]{1,0:T(4,128)S(1)}, f32[40,512]{1,0:T(8,128)S(1)}, f32[40,512]{1,0:T(8,128)S(1)}) custom-call(f32[40,512]{1,0:T(8,128)S(1)} %collective-permute-done.sibling_ref, f32[40,512]{1,0:T(8,128)S(1)} %copy-done, f32[40,512]{1,0:T(8,128)S(1)} %collective-permute-done.1.across_ref, bf16[64,48]{1,0:T(8,128)(2,1)S(1)} %get-tuple-element.24.rest_0_.rest_3_, ...), custom_call_target="tpu_custom_call" | custom-call | flops 1000000000 | bytes 262144 | tf_op jit(solution)/shard_map/pallas_call | solution.py:623
  17.8 0.0 collective-permute-done.3.after_ref
  17.9 0.0 collective-permute-done.2.before_ref
  17.9 0.1 shard_map.168.own_ref
  18.0 0.0 collective-permute-start.4
  18.0 1.2 %collective-permute-done.4.sibling_ref.rest_0_ = f32[8,512]{1,0:T(8,128)S(1)} collective-permute-done((f32[8,512]{1,0:T(8,128)S(1)}, f32[8,512]{1,0:T(8,128)S(1)}, u32[]{:S(2)}, u32[]{:S(2)}) %collective-permute-start.4) | collective-permute-done | bytes 16416 | tf_op jit(solution)/shard_map/ppermute | solution.py:645
  19.2 0.5 %collective-permute-start.5 = (f32[8,512]{1,0:T(8,128)S(1)}, f32[8,512]{1,0:T(8,128)S(1)}, u32[]{:S(2)}, u32[]{:S(2)}) collective-permute-start(f32[8,512]{1,0:T(8,128)S(1)} %shard_map.169.rest_1_), channel_id=1, source_target_pairs={{0,8},{4,12},{8,0},{12,4},{1,9},{5,13},{9,1},{13,5},{2,10},{6,14},... | collective-permute-start | bytes 49160 | tf_op jit(solution)/shard_map/ppermute | solution.py:645
  19.7 3.2 %collective-permute-done.5.rest_2_ = f32[8,512]{1,0:T(8,128)S(1)} collective-permute-done((f32[8,512]{1,0:T(8,128)S(1)}, f32[8,512]{1,0:T(8,128)S(1)}, u32[]{:S(2)}, u32[]{:S(2)}) %collective-permute-start.5) | collective-permute-done | bytes 16416 | tf_op jit(solution)/shard_map/ppermute | solution.py:645
  22.9 6.3 %shard_map.170 = (f32[1,40,128]{2,1,0:T(8,128)S(1)}, f32[2,128]{1,0:T(2,128)S(1)}) custom-call(f32[8,128]{1,0:T(8,128)S(1)} %get-tuple-element.23.number_ref, f32[40,512]{1,0:T(8,128)S(1)} %get-tuple-element.30.pl_ref, f32[40,512]{1,0:T(8,128)S(1)} %copy-done, f32[40,512]{1,0:T(8,128)S(1)} %get-tuple-element.31.pr_ref, f32[8,512]{1,0:T(8,128)S(1)} %shard_map.168.own_ref, ...), custom_call_target="tpu_custom_call" | custom-call | flops 1000000000 | bytes 262144 | tf_op jit(solution)/shard_map/pallas_call | solution.py:623
  29.2 0.1 collective-permute-start.6
  29.3 3.8 %collective-permute-done.6.b_ref = f32[1,40,128]{2,1,0:T(8,128)S(1)} collective-permute-done((f32[1,40,128]{2,1,0:T(8,128)S(1)}, f32[1,40,128]{2,1,0:T(8,128)S(1)}, u32[]{:S(2)}, u32[]{:S(2)}) %collective-permute-start.6) | collective-permute-done | bytes 20512 | tf_op jit(solution)/shard_map/ppermute | solution.py:645
  33.1 2.4 %collective-permute-start.7 = (f32[2,40,128]{2,1,0:T(8,128)S(1)}, f32[2,40,128]{2,1,0:T(8,128)S(1)}, u32[]{:S(2)}, u32[]{:S(2)}) collective-permute-start(f32[2,40,128]{2,1,0:T(8,128)S(1)} %shard_map.171.a_ref), channel_id=1, source_target_pairs={{0,2},{1,3},{2,0},{3,1},{4,6},{5,7},{6,4},{7,5},{8,10},{9,11},{10,... | collective-permute-start | bytes 122888 | tf_op jit(solution)/shard_map/ppermute | solution.py:645
  35.4 2.5 %collective-permute-done.7.b_ref = f32[2,40,128]{2,1,0:T(8,128)S(1)} collective-permute-done((f32[2,40,128]{2,1,0:T(8,128)S(1)}, f32[2,40,128]{2,1,0:T(8,128)S(1)}, u32[]{:S(2)}, u32[]{:S(2)}) %collective-permute-start.7) | collective-permute-done | bytes 40992 | tf_op jit(solution)/shard_map/ppermute | solution.py:645
  38.0 0.2 shard_map.173
  38.2 0.1 collective-permute-start.8
  38.3 1.2 %collective-permute-done.8.b_ref = f32[8,128]{1,0:T(8,128)S(1)} collective-permute-done((f32[8,128]{1,0:T(8,128)S(1)}, f32[8,128]{1,0:T(8,128)S(1)}, u32[]{:S(2)}, u32[]{:S(2)}) %collective-permute-start.8) | collective-permute-done | bytes 4128 | tf_op jit(solution)/shard_map/ppermute | solution.py:645
  39.4 0.5 %collective-permute-start.9 = (f32[8,128]{1,0:T(8,128)S(1)}, f32[8,128]{1,0:T(8,128)S(1)}, u32[]{:S(2)}, u32[]{:S(2)}) collective-permute-start(f32[8,128]{1,0:T(8,128)S(1)} %shard_map.174.sums_ref), channel_id=1, source_target_pairs={{0,8},{4,12},{8,0},{12,4},{1,9},{5,13},{9,1},{13,5},{2,10},{6,14},... | collective-permute-start | bytes 12296 | tf_op jit(solution)/shard_map/ppermute | solution.py:645
  40.0 3.1 %collective-permute-done.9.more_ref = f32[8,128]{1,0:T(8,128)S(1)} collective-permute-done((f32[8,128]{1,0:T(8,128)S(1)}, f32[8,128]{1,0:T(8,128)S(1)}, u32[]{:S(2)}, u32[]{:S(2)}) %collective-permute-start.9) | collective-permute-done | bytes 4128 | tf_op jit(solution)/shard_map/ppermute | solution.py:645
  43.0 0.7 %shard_map.175 = (f32[3,1,512]{2,1,0:T(1,128)}, f32[3,1,512]{2,1,0:T(1,128)}, f32[2,1,2]{2,1,0:T(1,128)}, f32[1,1]{1,0:T(1,128)}) custom-call(f32[8,128]{1,0:T(8,128)S(1)} %get-tuple-element.23.number_ref, f32[1,40,128]{2,1,0:T(8,128)S(1)} %get-tuple-element.34.a_ref.own_ref, f32[2,128]{1,0:T(2,128)S(1)} %get-tuple-element.35.record_ref, ...), custom_call_target="tpu_custom_call" | custom-call | bytes 262144 | tf_op jit(solution)/shard_map/pallas_call | solution.py:623
  (4 shorter events, 0.0 us)
Async XLA Ops:
  0.6 6.1 %copy-start.1 = (f32[2,64,64]{2,1,0:T(8,128)S(1)}, f32[2,64,64]{2,1,0:T(8,128)}, u32[]{:S(2)}) copy-start(f32[2,64,64]{2,1,0:T(8,128)} %mix_ref.1) | copy-start | bytes 98308
  0.6 6.1 %copy-start.2 = (f32[2,64,64]{2,1,0:T(8,128)S(1)}, f32[2,64,64]{2,1,0:T(8,128)}, u32[]{:S(2)}) copy-start(f32[2,64,64]{2,1,0:T(8,128)} %update_ref.1) | copy-start | bytes 98308
  0.7 6.1 %copy-start.3 = (f32[1,3,512]{2,0,1:T(1,128)S(1)}, f32[1,3,512]{2,0,1:T(1,128)}, u32[]{:S(2)}) copy-start(f32[1,3,512]{2,0,1:T(1,128)} %param.14) | copy-start | bytes 18436
  0.7 6.1 %copy-start.4 = (f32[2,8,64]{2,1,0:T(8,128)S(1)}, f32[2,8,64]{2,1,0:T(8,128)}, u32[]{:S(2)}) copy-start(f32[2,8,64]{2,1,0:T(8,128)} %radial_ref.1) | copy-start | bytes 12292
  2.2 9.3 %collective-permute-start.1 = (f32[40,512]{1,0:T(8,128)}, f32[40,512]{1,0:T(8,128)S(1)}, u32[]{:S(2)}, u32[]{:S(2)}) collective-permute-start(f32[40,512]{1,0:T(8,128)} %shard_map.166.po_ref), channel_id=1, source_target_pairs={{0,12},{4,8},{8,4},{12,0},{1,13},{5,9},{9,5},{13,1},{2,14},{6,10},... | collective-permute-start | bytes 245768 | tf_op jit(solution)/shard_map/ppermute | solution.py:645
  4.7 6.8 %collective-permute-start = (f32[40,512]{1,0:T(8,128)}, f32[40,512]{1,0:T(8,128)S(1)}, u32[]{:S(2)}, u32[]{:S(2)}) collective-permute-start(f32[40,512]{1,0:T(8,128)} %shard_map.166.po_ref), channel_id=1, source_target_pairs={{0,4},{4,0},{8,12},{12,8},{1,5},{5,1},{9,13},{13,9},{2,6},{6,2},{1... | collective-permute-start | bytes 245768 | tf_op jit(solution)/shard_map/ppermute | solution.py:645
  6.0 0.8 %copy-start.5 = (f32[2,64]{1,0:T(2,128)S(1)}, f32[2,64]{1,0:T(2,128)}, u32[]{:S(2)}) copy-start(f32[2,64]{1,0:T(2,128)} %embed_ref.1) | copy-start | bytes 1540
  6.0 0.8 %copy-start.6 = (s32[2,1]{0,1:T(1,128)S(1)}, s32[2,1]{0,1:T(1,128)}, u32[]{:S(2)}) copy-start(s32[2,1]{0,1:T(1,128)} %param.17) | copy-start | bytes 28
  6.0 0.8 %copy-start.7 = (f32[64]{0:T(128)S(1)}, f32[64]{0:T(128)}, u32[]{:S(2)}) copy-start(f32[64]{0:T(128)} %readout_ref.1) | copy-start | bytes 772
  6.7 4.8 %copy-start = (f32[40,512]{1,0:T(8,128)S(1)}, f32[40,512]{1,0:T(8,128)}, u32[]{:S(2)}) copy-start(f32[40,512]{1,0:T(8,128)} %shard_map.166.po_ref) | copy-start | bytes 245764
  7.9 10.0 %collective-permute-start.3 = (f32[3,1,512]{2,1,0:T(1,128)S(1)}, f32[3,1,512]{2,1,0:T(1,128)S(1)}, u32[]{:S(2)}, u32[]{:S(2)}) collective-permute-start(f32[3,1,512]{2,1,0:T(1,128)S(1)} %get-tuple-element.33), channel_id=1, source_target_pairs={{0,3},{1,0},{2,1},{3,2},{4,7},{5,4},{6,5},{7,6},{8,11},{9,8},{10,9... | collective-permute-start | bytes 18440 | tf_op jit(solution)/shard_map/ppermute | solution.py:641
  11.5 6.3 %collective-permute-start.2 = (f32[3,1,512]{2,1,0:T(1,128)S(1)}, f32[3,1,512]{2,1,0:T(1,128)S(1)}, u32[]{:S(2)}, u32[]{:S(2)}) collective-permute-start(f32[3,1,512]{2,1,0:T(1,128)S(1)} %get-tuple-element.33), channel_id=1, source_target_pairs={{0,1},{1,2},{2,3},{3,0},{4,5},{5,6},{6,7},{7,4},{8,9},{9,10},{10,1... | collective-permute-start | bytes 18440 | tf_op jit(solution)/shard_map/ppermute | solution.py:641
  18.0 1.2 %collective-permute-start.4 = (f32[8,512]{1,0:T(8,128)S(1)}, f32[8,512]{1,0:T(8,128)S(1)}, u32[]{:S(2)}, u32[]{:S(2)}) collective-permute-start(f32[8,512]{1,0:T(8,128)S(1)} %shard_map.168.own_ref), channel_id=1, source_target_pairs={{0,4},{4,0},{8,12},{12,8},{1,5},{5,1},{9,13},{13,9},{2,6},{6,2},{1... | collective-permute-start | bytes 49160 | tf_op jit(solution)/shard_map/ppermute | solution.py:645
  19.2 3.7 %collective-permute-start.5 = (f32[8,512]{1,0:T(8,128)S(1)}, f32[8,512]{1,0:T(8,128)S(1)}, u32[]{:S(2)}, u32[]{:S(2)}) collective-permute-start(f32[8,512]{1,0:T(8,128)S(1)} %shard_map.169.rest_1_), channel_id=1, source_target_pairs={{0,8},{4,12},{8,0},{12,4},{1,9},{5,13},{9,1},{13,5},{2,10},{6,14},... | collective-permute-start | bytes 49160 | tf_op jit(solution)/shard_map/ppermute | solution.py:645
  29.2 3.8 %collective-permute-start.6 = (f32[1,40,128]{2,1,0:T(8,128)S(1)}, f32[1,40,128]{2,1,0:T(8,128)S(1)}, u32[]{:S(2)}, u32[]{:S(2)}) collective-permute-start(f32[1,40,128]{2,1,0:T(8,128)S(1)} %get-tuple-element.34.a_ref.own_ref), channel_id=1, source_target_pairs={{0,1},{1,0},{2,3},{3,2},{4,5},{5,4},{6,7},{7,6},{8,9},{9,8},{10,11... | collective-permute-start | bytes 61448 | tf_op jit(solution)/shard_map/ppermute | solution.py:645
  33.1 4.9 %collective-permute-start.7 = (f32[2,40,128]{2,1,0:T(8,128)S(1)}, f32[2,40,128]{2,1,0:T(8,128)S(1)}, u32[]{:S(2)}, u32[]{:S(2)}) collective-permute-start(f32[2,40,128]{2,1,0:T(8,128)S(1)} %shard_map.171.a_ref), channel_id=1, source_target_pairs={{0,2},{1,3},{2,0},{3,1},{4,6},{5,7},{6,4},{7,5},{8,10},{9,11},{10,... | collective-permute-start | bytes 122888 | tf_op jit(solution)/shard_map/ppermute | solution.py:645
  38.2 1.2 %collective-permute-start.8 = (f32[8,128]{1,0:T(8,128)S(1)}, f32[8,128]{1,0:T(8,128)S(1)}, u32[]{:S(2)}, u32[]{:S(2)}) collective-permute-start(f32[8,128]{1,0:T(8,128)S(1)} %get-tuple-element.37.a_ref), channel_id=1, source_target_pairs={{0,4},{4,0},{8,12},{12,8},{1,5},{5,1},{9,13},{13,9},{2,6},{6,2},{1... | collective-permute-start | bytes 12296 | tf_op jit(solution)/shard_map/ppermute | solution.py:645
  39.4 3.6 %collective-permute-start.9 = (f32[8,128]{1,0:T(8,128)S(1)}, f32[8,128]{1,0:T(8,128)S(1)}, u32[]{:S(2)}, u32[]{:S(2)}) collective-permute-start(f32[8,128]{1,0:T(8,128)S(1)} %shard_map.174.sums_ref), channel_id=1, source_target_pairs={{0,8},{4,12},{8,0},{12,4},{1,9},{5,13},{9,1},{13,5},{2,10},{6,14},... | collective-permute-start | bytes 12296 | tf_op jit(solution)/shard_map/ppermute | solution.py:645

commit v6 on v5

--- a/solution.py
+++ b/solution.py
@@ -26,6 +26,12 @@
 ROW_KIND = 36
 ROW_V = 37
 PACK_ROWS = 40
+RAW_MIX = 16
+RAW_UPDATE = 144
+RAW_EMBED = 272
+RAW_READOUT = 280
+RAW_NUMBER = 288
+RAW_ROWS = 296
 NT = (((1,), (1,)), ((), ()))
 
 
@@ -58,33 +64,45 @@
     return lax.dot_general(a, b, NT, preferred_element_type=F32)
 
 
-def pack_kernel(x_ref, v_ref, species_ref, nbr_ref, counts_ref, lattice_ref, out_ref, x, v, species, nbr, counts, sems):
-    copies = [
-        pltpu.make_async_copy(source, target, sems.at[i])
-        for i, (source, target) in enumerate(
-            [(x_ref, x), (v_ref, v), (species_ref, species), (nbr_ref, nbr), (counts_ref, counts)]
-            + [(lattice_ref.at[c], out_ref.at[pl.ds(8 + 8 * c, 8)]) for c in range(3)]
-        )
-    ]
+def pack_kernel(*refs):
+    sources, (out_ref, raw_ref), held, sems = refs[:14], refs[14:16], refs[16:26], refs[26]
+    lattice, radial, mix, update = sources[10:]
+    pairs = list(zip(sources, held))
+    pairs += [(lattice.at[c], out_ref.at[pl.ds(8 + 8 * c, 8)]) for c in range(3)]
+    pairs += [(radial.at[l], raw_ref.at[pl.ds(BASIS * l, BASIS)]) for l in range(2)]
+    pairs += [(mix.at[l], raw_ref.at[pl.ds(RAW_MIX + CHANNELS * l, CHANNELS)]) for l in range(2)]
+    pairs += [(update.at[l], raw_ref.at[pl.ds(RAW_UPDATE + CHANNELS * l, CHANNELS)]) for l in range(2)]
+    copies = [pltpu.make_async_copy(a, b, sems.at[i]) for i, (a, b) in enumerate(pairs)]
     for one in copies:
         one.start()
     for one in copies:
         one.wait()
+    x, v, species, nbr, counts, embed, readout, dt, flags, climb = held
     out_ref[0:8, :] = nbr[...].astype(F32)
     for c in range(3):
         out_ref[ROW_X + c : ROW_X + c + 1, :] = x[c]
         out_ref[ROW_V + c : ROW_V + c + 1, :] = v[c]
     out_ref[ROW_COUNT : ROW_COUNT + 1, :] = counts[...].astype(F32).reshape(1, -1)
     out_ref[ROW_KIND : ROW_KIND + 1, :] = species[...].astype(F32).reshape(1, -1)
-
-
-def weight_kernel(
-    dt_ref, flag_ref, climb_ref, x_ref, embed_ref, radial_ref, mix_ref, update_ref, readout_ref, l1_ref, l2_ref, l3_ref, l5_ref, l6_ref, col_ref, copy_ref, number_ref
-):
-    copy_ref[...] = x_ref[...]
-    flags = [flag_ref[0, s].astype(F32) for s in range(flag_ref.shape[1])]
-    for i, value in enumerate([dt_ref[0], climb_ref[0].astype(F32)] + flags):
-        number_ref[i : i + 1, :] = jnp.full((1, LANES), value, F32)
+    raw_ref[RAW_EMBED : RAW_EMBED + 2, :] = embed[...]
+    raw_ref[RAW_READOUT : RAW_READOUT + 1, :] = readout[...].reshape(1, CHANNELS)
+    numbers = [dt[0, 0], climb[0, 0].astype(F32)] + [flags[0, s].astype(F32) for s in range(flags.shape[1])]
+    for i, value in enumerate(numbers):
+        raw_ref[RAW_NUMBER + i : RAW_NUMBER + i + 1, :] = jnp.full((1, CHANNELS), value, F32)
+
+
+def prepare_kernel(po_ref, raw_ref, *rest):
+    own_hot, l1_ref, l2_ref, l3_ref, l5_ref, l6_ref, col_ref, copy_ref, number_ref = rest
+    for b in range(SLAB_BLOCKS):
+        mark(window_index(po_ref, b), [0, 1, 2], own_hot.at[b])
+    for c in range(3):
+        copy_ref[c] = po_ref[ROW_X + c : ROW_X + c + 1, :]
+    number_ref[...] = jnp.broadcast_to(raw_ref[RAW_NUMBER : RAW_NUMBER + 8, 0:1], (8, LANES))
+    radial_ref = [raw_ref[BASIS * l : BASIS * (l + 1), :] for l in range(2)]
+    mix_ref = [raw_ref[RAW_MIX + CHANNELS * l : RAW_MIX + CHANNELS * (l + 1), :] for l in range(2)]
+    update_ref = [raw_ref[RAW_UPDATE + CHANNELS * l : RAW_UPDATE + CHANNELS * (l + 1), :] for l in range(2)]
+    embed_ref = raw_ref[RAW_EMBED : RAW_EMBED + 2, :]
+    readout = raw_ref[RAW_READOUT : RAW_READOUT + 1, :]
     eye = (
         lax.broadcasted_iota(jnp.int32, (CHANNELS, CHANNELS), 0)
         == lax.broadcasted_iota(jnp.int32, (CHANNELS, CHANNELS), 1)
@@ -108,7 +126,6 @@
     l3_ref[...] = jnp.concatenate([high, high, low, jnp.zeros_like(high)], axis=1).astype(BF16)
     l5_ref[...] = left_stack(folded).astype(BF16)
     l6_ref[...] = left_stack(first).astype(BF16)
-    readout = readout_ref[...].reshape(1, CHANNELS)
     wide = (CHANNELS, LANES)
     col_ref[0] = jnp.broadcast_to(jnp.sum(mix_t * base0, axis=1, keepdims=True), wide)
     col_ref[1] = jnp.broadcast_to(jnp.sum(mix_t * base1, axis=1, keepdims=True), wide)
@@ -136,12 +153,38 @@
     return m * sig, sig * (1.0 + m * (1.0 - sig))
 
 
-def force_parts(packs, weights, scr):
+def reach(b, first, last):
+    return [w for w in range(3) if first <= b - 1 + w <= last]
+
+
+SIDE_START = {2: 0, 3: LANES, 8: 3 * LANES, 9: 5 * LANES}
+SIDE_ROWS = 6 * LANES
+
+
+def mark(index, ws, target):
+    count = len(ws) * LANES
+    row_id = lax.broadcasted_iota(jnp.int32, (count, LANES), 0) + ws[0] * LANES
+    for k in range(SLOTS):
+        same = row_id == jnp.broadcast_to(index[k : k + 1, :], (count, LANES))
+        target[:, k * LANES : (k + 1) * LANES] = jnp.where(same, 1.0, 0.0).astype(BF16)
+
+
+def window_index(pack, b):
+    lanes = slice((b % 4) * LANES, (b % 4 + 1) * LANES)
+    return pack[0:8, lanes].astype(jnp.int32) - LANES * (b % 4)
+
+
+def mark_sides(packs, side):
+    for b, start in SIDE_START.items():
+        ws = reach(b, 3, 8)
+        mark(window_index(packs[b // 4], b), ws, side.at[start : start + len(ws) * LANES])
+
+
+def force_parts(packs, weights, own_hot, side_hot, scr):
     l1, l2, l3, l5, l6, col = weights
-    (xs, widx, kinds, geo, bst, bps, bpr, sst, sent_all, slope, hot, dg, pulls, acc) = scr
+    (xs, widx, kinds, geo, bst, bps, bpr, sst, sent_all, slope, dg, pulls, acc) = scr
     centre = 2.0 + 0.5 * lax.broadcasted_iota(jnp.int32, (BASIS, LANES), 0).astype(F32)
     slot = lax.broadcasted_iota(jnp.int32, (SLOTS, LANES), 0)
-    row_id = lax.broadcasted_iota(jnp.int32, (3 * LANES, LANES), 0)
 
     def part_rows(value):
         high, low = split(value)
@@ -150,7 +193,7 @@
     def pairs(b):
         pack = packs[b // 4]
         lanes = slice((b % 4) * LANES, (b % 4 + 1) * LANES)
-        index = pack[0:8, lanes].astype(jnp.int32) - LANES * (b % 4)
+        index = window_index(pack, b)
         widx[b] = index
         inner = index & (LANES - 1)
         part = index >> 7
@@ -211,20 +254,12 @@
             sent_all[:, (b + i) * LANES : (b + i + 1) * LANES] = one
         slope[:, cols] = steep
 
-    def reach(b, first, last):
-        return [w for w in range(3) if first <= b - 1 + w <= last]
-
-    def mark(b):
-        index = widx[b]
-        ws = reach(b, 3, 8)
-        rows = slice(ws[0] * LANES, (ws[-1] + 1) * LANES)
-        for k in range(SLOTS):
-            same = row_id[rows] == jnp.broadcast_to(index[k : k + 1, :], (rows.stop - rows.start, LANES))
-            hot[b, rows, k * LANES : (k + 1) * LANES] = jnp.where(same, 1.0, 0.0).astype(BF16)
-
     def spread(left, b, first, last):
         ws = reach(b, first, last)
-        return ws, mm_nt(left, hot[b, ws[0] * LANES : (ws[-1] + 1) * LANES, :])
+        if b in SIDE_START:
+            start = SIDE_START[b] + (ws[0] - reach(b, 3, 8)[0]) * LANES
+            return ws, mm_nt(left, side_hot[start : start + len(ws) * LANES, :])
+        return ws, mm_nt(left, own_hot[b - 4, ws[0] * LANES : (ws[-1] + 1) * LANES, :])
 
     started = set()
 
@@ -239,7 +274,6 @@
             pick = [jnp.take_along_axis(window, lane, axis=1) for window in windows]
             got.append(jnp.where(which == 0, pick[0], jnp.where(which == 1, pick[1], pick[2])))
         got = jnp.concatenate(got, axis=1)
-        mark(b)
         basis = bst[b]
         radial = mm(l3[...], jnp.concatenate([basis, basis], axis=0))
         message = jnp.zeros((CHANNELS, LANES), F32)
@@ -349,7 +383,6 @@
         pltpu.VMEM((48, wide), BF16),
         pltpu.VMEM((CHANNELS, wide), F32),
         pltpu.VMEM((CHANNELS, wide), F32),
-        pltpu.VMEM((12, 3 * LANES, SLOTS * LANES), BF16),
         pltpu.VMEM((CHANNELS, wide), F32),
         pltpu.VMEM((12, 8, SLOTS * LANES), F32),
         pltpu.VMEM((12, 3, 8, LANES), F32),
@@ -361,12 +394,13 @@
     return jnp.where(even, across, sibling), jnp.where(even, sibling, across)
 
 
-def first_kernel(sibling_ref, po_ref, across_ref, *rest):
-    weights, (out_ref, pl_ref, pr_ref), scr = rest[:6], rest[6:9], rest[9:]
+def first_kernel(sibling_ref, po_ref, across_ref, own_hot, *rest):
+    weights, (out_ref, pl_ref, pr_ref, side_hot), scr = rest[:6], rest[6:10], rest[10:]
     pl_ref[...], pr_ref[...] = by_parity(sibling_ref[...], across_ref[...])
     packs = [pl_ref, po_ref, pr_ref]
+    mark_sides(packs, side_hot)
     fill_region(scr[0], packs, lambda s: packs[s][ROW_X : ROW_X + 3, :])
-    force_parts(packs, weights, scr)
+    force_parts(packs, weights, own_hot, side_hot, scr)
     for c in range(3):
         out_ref[c : c + 1, :] = own_force(scr[-1], c)
 
@@ -380,13 +414,15 @@
     return jnp.concatenate(values, axis=1)
 
 
-def blend_kernel(images, force_ref, po_ref, before_ref, after_ref, out_ref):
+def blend_kernel(images, force_ref, po_ref, pair_ref, other_ref, out_ref, sums_ref):
     x = po_ref[ROW_X : ROW_X + 3, :]
     v = po_ref[ROW_V : ROW_V + 3, :]
     force = force_ref[...]
     here = lax.axis_index("img")
-    before = jnp.where(here > 0, rows_of(before_ref), 0.0)
-    after = jnp.where(here < images - 1, rows_of(after_ref), 0.0)
+    pair, other = rows_of(pair_ref), rows_of(other_ref)
+    even = here % 2 == 0
+    before = jnp.where(here > 0, jnp.where(even, other, pair), 0.0)
+    after = jnp.where(here < images - 1, jnp.where(even, pair, other), 0.0)
     tangent = after - before
     plus = after - x
     minus = x - before
@@ -403,6 +439,7 @@
         axis=0,
     )
     sums = jnp.broadcast_to(lane_total(sums), (8, LANES))
+    sums_ref[...] = sums
     out_ref[0:3, :] = force
     out_ref[3:6, :] = tangent
     out_ref[6:7, :] = block_row(*[sums[i : i + 1] for i in range(4)])
@@ -432,11 +469,6 @@
     )
 
 
-def forward_kernel(own_ref, sibling_ref, out_ref):
-    out_ref[0:6, :] = sibling_ref[0:6, :]
-    out_ref[6:8, :] = own_ref[6:8, :] + sibling_ref[6:8, :]
-
-
 def add_kernel(a_ref, b_ref, out_ref):
     out_ref[...] = a_ref[...] + b_ref[...]
 
@@ -447,22 +479,22 @@
     out_ref[count : 2 * count] = b_ref[...]
 
 
-def second_kernel(images, others, paired, number_ref, pl_ref, po_ref, pr_ref, own_ref, *rest):
-    heard, rest = rest[:others], rest[others:]
-    weights, out_ref, record_ref, scr = rest[:6], rest[6], rest[7], rest[8:]
+def second_kernel(images, domains, number_ref, pl_ref, po_ref, pr_ref, own_ref, near_ref, far_ref, *rest):
+    count = 2 if domains == 4 else 1
+    parts, rest = rest[:count], rest[count:]
+    (own_hot, side_hot), weights, (out_ref, record_ref), scr = rest[:2], rest[2:8], rest[8:10], rest[10:]
     packs = [pl_ref, po_ref, pr_ref]
     here = lax.axis_index("img")
-    if others == 3 and paired:
-        sibling, both, far = heard
-        sums = both[6:8, :] + far[6:8, :]
-        beside = by_parity(sibling[0:6, :], far[0:6, :])
-    else:
-        sums = own_ref[6:8, :]
-        for one in heard:
-            sums = sums + one[6:8, :]
-        beside = heard[0][0:6, :], heard[others - 1][0:6, :]
-    ft, ff, tt, pp = (sums[0:1, i * LANES : (i + 1) * LANES] for i in range(4))
-    mn, vv = (sums[1:2, i * LANES : (i + 1) * LANES] for i in range(2))
+    sums = parts[0][...]
+    if domains == 4:
+        sums = sums + parts[1][...]
+    got = [sums[i : i + 1, :] for i in range(6)]
+    if domains == 4:
+        for one in (near_ref, far_ref):
+            for i in range(6):
+                got[i] = got[i] + one[6 + i // 4 : 7 + i // 4, (i % 4) * LANES : (i % 4 + 1) * LANES]
+    ft, ff, tt, pp, mn, vv = got
+    beside = by_parity(near_ref[0:6, :], far_ref[0:6, :])
     shape = (1, LANES)
     along, spring, keep, pull, side, dt, alpha = step_numbers(
         ft,
@@ -488,7 +520,7 @@
     ]
     moved = [p[ROW_X : ROW_X + 3, :] + wide(dt) * s for p, s in zip(packs, speeds)]
     fill_region(scr[0], packs, lambda s: moved[s])
-    force_parts(packs, weights, scr)
+    force_parts(packs, weights, own_hot, side_hot, scr)
     for c in range(3):
         force = own_force(scr[-1], c)
         for i in range(SLAB_BLOCKS):
@@ -511,8 +543,13 @@
 )
 
 
-def gram_kernel(images, messages_ref, out_ref, state_ref):
+def gram_kernel(images, *refs):
+    parts, (out_ref, state_ref, messages_ref) = refs[:-3], refs[-3:]
     rows = out_ref.shape[0]
+    place = 0
+    for part in parts:
+        messages_ref[place : place + part.shape[0]] = part[...]
+        place += part.shape[0]
     here = lax.axis_index("img")
     blank = [jnp.zeros((rows - images, LANES), F32)] if rows > images else []
     zero = jnp.zeros((1, LANES), F32)
@@ -548,11 +585,13 @@
         state_ref[16 + rows * i : 16 + rows * (i + 1), :] = gathered(36 + i)
 
 
-def final_kernel(images, atoms, number_ref, own_ref, record_ref, state_ref, sums_ref, more_ref, *rest):
-    x_ref, v_ref, band_ref, path_ref = rest
-    rows = sums_ref.shape[0]
+def final_kernel(images, atoms, number_ref, own_ref, record_ref, state_ref, *rest):
+    parts, (x_ref, v_ref, band_ref, path_ref) = rest[:-4], rest[-4:]
+    rows = parts[0].shape[0]
     here = lax.axis_index("img")
-    sums = sums_ref[...] + more_ref[...]
+    sums = parts[0][...]
+    for one in parts[1:]:
+        sums = sums + one[...]
     got = {
         pair: jnp.broadcast_to(sums[:, q : q + 1], (rows, LANES)) for q, pair in enumerate(PRODUCTS)
     }
@@ -631,18 +670,34 @@
     )(*scalars, *arrays)
 
 
-def around(array, axis):
-    count = lax.axis_size(axis)
-    return [lax.ppermute(array, axis, [(i, (i + s) % count) for i in range(count)]) for s in range(1, count)]
-
-
-def ring(array, axis, by):
-    count = lax.axis_size(axis)
-    return lax.ppermute(array, axis, [(i, (i + by) % count) for i in range(count)])
-
-
 def swap(array, axis, partner):
     return lax.ppermute(array, axis, [(i, partner(i)) for i in range(lax.axis_size(axis))])
+
+
+def exchanged(sums, axis):
+    count = lax.axis_size(axis)
+    if count == 4:
+        return [sums] + [swap(sums, axis, lambda i, by=by: i ^ by) for by in (2, 3, 1)]
+    distance = 1
+    while distance < count:
+        more = swap(sums, axis, lambda i, by=distance: i ^ by)
+        sums = call(add_kernel, jax.ShapeDtypeStruct(sums.shape, F32), (), (sums, more))
+        distance *= 2
+    return [sums]
+
+
+def collected(array, axis):
+    count = lax.axis_size(axis)
+    if count == 4:
+        far = [swap(array, axis, lambda i, by=by: i ^ by) for by in (3, 2, 1)]
+        return [array] + far[::-1]
+    distance = 1
+    while distance < count:
+        more = swap(array, axis, lambda i, by=distance: i ^ by)
+        shape = jax.ShapeDtypeStruct((2 * distance,) + array.shape[1:], F32)
+        array = call(join_kernel, shape, (), (array, more))
+        distance *= 2
+    return [array]
 
 
 def local(
@@ -669,20 +724,25 @@
     shape = jax.ShapeDtypeStruct
     x = jnp.transpose(disp, (1, 0, 2))
     v = jnp.transpose(veloc, (1, 0, 2))
-    pack = call(
+    small = (x, v, species, neighbours, counts, embed, readout)
+    numbers = (time_step.reshape(1, 1), jnp.transpose(reset_flags), climb.reshape(1, 1))
+    pack, raw = call(
         pack_kernel,
-        shape((PACK_ROWS, atoms), F32),
+        (shape((PACK_ROWS, atoms), F32), shape((RAW_ROWS, CHANNELS), F32)),
         (),
-        (x, v, species, neighbours, counts, jnp.transpose(lattice, (1, 0, 2))),
-        [pltpu.VMEM(a.shape, a.dtype) for a in (x, v, species, neighbours, counts)] + [pltpu.SemaphoreType.DMA((8,))],
+        (*small, *numbers, jnp.transpose(lattice, (1, 0, 2)), radial_weight, mix_weight, update_weight),
+        [pltpu.VMEM(a.shape, a.dtype) for a in small]
+        + [pltpu.SMEM(a.shape, a.dtype) for a in numbers]
+        + [pltpu.SemaphoreType.DMA((19,))],
         spec=HBM_SPEC,
         vmem=63,
     )
     sibling = swap(pack, "dom", lambda i: i ^ 1)
     across = swap(pack, "dom", lambda i: (i + 2 * (i % 2) - 1) % domains)
-    *weights, x_copy, numbers = call(
-        weight_kernel,
+    own_hot, *weights, x_copy, numbers = call(
+        prepare_kernel,
         (
+            shape((SLAB_BLOCKS, 3 * LANES, SLOTS * LANES), BF16),
             shape((CHANNELS, 48), BF16),
             shape((CHANNELS, 192), BF16),
             shape((CHANNELS, 32), BF16),
@@ -692,61 +752,58 @@
             shape(x.shape, F32),
             shape((8, LANES), F32),
         ),
-        (time_step, jnp.transpose(reset_flags), climb),
-        (x, embed, radial_weight, mix_weight, update_weight, readout),
-        flops=10000000,
-    )
-    before, after = ring(x_copy, "img", 1), ring(x_copy, "img", -1)
-    force, left, right = call(
+        (),
+        (pack, raw),
+        flops=100000000,
+    )
+    pair = swap(x_copy, "img", lambda i: i ^ 1)
+    other = swap(x_copy, "img", lambda i: i if i in (0, images - 1) else i + 2 * (i % 2) - 1)
+    force, left, right, side_hot = call(
         first_kernel,
-        (shape((3, atoms), F32), shape(pack.shape, F32), shape(pack.shape, F32)),
+        (
+            shape((3, atoms), F32),
+            shape(pack.shape, F32),
+            shape(pack.shape, F32),
+            shape((SIDE_ROWS, SLOTS * LANES), BF16),
+        ),
         (),
-        (sibling, pack, across, *weights),
+        (sibling, pack, across, own_hot, *weights),
         scratch(),
         flops=1000000000,
     )
-    message = call(
-        functools.partial(blend_kernel, images), shape((8, atoms), F32), (), (force, pack, before, after)
-    )
-    paired = domains == 4
-    if paired:
-        near = swap(message, "dom", lambda i: i ^ 1)
-        both = call(forward_kernel, shape((8, atoms), F32), (), (message, near))
-        heard = [near, both, swap(both, "dom", lambda i: i ^ 2)]
+    message, sums = call(
+        functools.partial(blend_kernel, images),
+        (shape((8, atoms), F32), shape((8, LANES), F32)),
+        (),
+        (force, pack, pair, other),
+    )
+    far = swap(message, "dom", lambda i: (i + 2 * (i % 2) - 1) % domains)
+    if domains == 4:
+        parts = [sums, swap(sums, "dom", lambda i: i ^ 2)]
     else:
-        heard = around(message, "dom")
+        parts = exchanged(sums, "dom")
+    near = swap(message, "dom", lambda i: i ^ 1)
     state, record = call(
-        functools.partial(second_kernel, images, len(heard), paired),
+        functools.partial(second_kernel, images, domains),
         (shape((1, 40, LANES), F32), shape((2, LANES), F32)),
         (),
-        (numbers, left, pack, right, message, *heard, *weights),
+        (numbers, left, pack, right, message, near, far, *parts, own_hot, side_hot, *weights),
         scratch(),
         flops=1000000000,
     )
-    gathered, distance = state, 1
-    while distance < images:
-        more = swap(gathered, "img", lambda i, distance=distance: i ^ distance)
-        gathered = call(join_kernel, shape((2 * distance, 40, LANES), F32), (), (gathered, more))
-        distance *= 2
     rows = 8 * ((images + 7) // 8)
     sums, extra = call(
         functools.partial(gram_kernel, images),
         (shape((rows, LANES), F32), shape((16 + 3 * rows, LANES), F32)),
         (),
-        (gathered,),
-    )
-    distance = 1
-    while True:
-        more = swap(sums, "dom", lambda i, distance=distance: i ^ distance)
-        distance *= 2
-        if distance == domains:
-            break
-        sums = call(add_kernel, shape((rows, LANES), F32), (), (sums, more))
+        collected(state, "img"),
+        [pltpu.VMEM((images, 40, LANES), F32)],
+    )
     new_x, new_v, records, path = call(
         functools.partial(final_kernel, images, atoms * domains),
         (shape(x.shape, F32), shape(x.shape, F32), shape((2, 1, 2), F32), shape((1, 1), F32)),
         (),
-        (numbers, state, record, extra, sums, more),
+        (numbers, state, record, extra, *exchanged(sums, "dom")),
     )
     return (
         jnp.transpose(new_x, (1, 0, 2)),

time: 44.1 us -> 44.7 us (1.014)
  waiting for transfers between devices: 14.9 us -> 7.66 us
  starting transfers between devices: 10.3 us -> 16.7 us
  local copies, waits for them, and re-layouts: 0.04 us -> 1.83 us
    ppermute x8 -> x13, starting transfers between devices: 6.68 us -> 16.7 us  [swap(): lax.ppermute(array, axis, [(i, partner(i)) for i in range(lax.axis_size(a...]
    ppermute x8 -> x13, waiting for transfers between devices: 14.9 us -> 7.66 us  [swap(): lax.ppermute(array, axis, [(i, partner(i)) for i in range(lax.axis_size(a...]
    ppermute x2 -> x0, starting transfers between devices: 3.66 us -> none  [ring(): lax.ppermute(array, axis, [(i, (i + by) % count) for i in range(count)])]
    unnamed x16 -> x4, local copies, waits for them, and re-layouts: 0.04 us -> 1.83 us
    pallas_call x11 -> x7, Pallas kernels: 16.3 us -> 16.2 us  [call(): pl.pallas_call(body, out_shape=outs, in_specs=[SMEM_SPEC] * len(scalars)...]
  transfers between devices with their start and end apart: 10 -> 13, of which waited for: 6 -> 5; matrix products, arithmetic and copies ran while one was open for 0% -> 0% of each run, Pallas kernels for 17% -> 17%
where the time goes in v6:
time: 44.7 us; the launch traced here: 44.4 us
  starting transfers between devices  16.7 us (37%)
  Pallas kernels  16.2 us (36%)
  waiting for transfers between devices  7.66 us (17%)
  between operations  2.02 us (5%)
  local copies, waits for them, and re-layouts  1.83 us (4%)
    ppermute x13, starting transfers between devices, swap(): lax.ppermute(array, axis, [(i, partner(i)) for i in range(lax.axis_size(a...  16.7 us
    pallas_call x7, Pallas kernels, call(): pl.pallas_call(body, out_shape=outs, in_specs=[SMEM_SPEC] * len(scalars)...  16.2 us
    ppermute x13, waiting for transfers between devices, swap(): lax.ppermute(array, axis, [(i, partner(i)) for i in range(lax.axis_size(a...  7.66 us
    unnamed x4, local copies, waits for them, and re-layouts  1.83 us
  transfers between devices with their start and end apart: 13, of which 5 were waited for; matrix products, arithmetic and copies ran while one was open for 0% of the time, Pallas kernels for 17%

profile of v6, /device:TPU:0, one launch (start us, length us, event | category | flops | bytes accessed | tf_op | source)
XLA Modules:
  0.0 44.4 jit_solution(1284648622082157819)
XLA Ops:
  1.9 1.8 %shard_map.165 = (f32[40,512]{1,0:T(8,128)}, f32[296,64]{1,0:T(8,128)}) custom-call(f32[3,1,512]{2,1,0:T(1,128)} %bitcast.15, f32[3,1,512]{2,1,0:T(1,128)} %bitcast.16, s32[512]{0:T(512)} %refs_2_.1, s32[8,512]{1,0:T(8,128)} %refs_3_.1, s32[512]{0:T(512)} %refs_4_.1, f32[2,64]{1,0:T(2,128)} %refs_5_.1, f32[64]{0:T(128)} %refs_6_.1, f32[1,1]{1,0:T(1,128)} %bitcast.12.refs_7_, ...), custom_call_target="tpu_custom_call" | custom-call | bytes 262144 | tf_op jit(solution)/shard_map/pallas_call | solution.py:662
  3.8 0.5 %collective-permute-start = (f32[40,512]{1,0:T(8,128)}, f32[40,512]{1,0:T(8,128)S(1)}, u32[]{:S(2)}, u32[]{:S(2)}) collective-permute-start(f32[40,512]{1,0:T(8,128)} %get-tuple-element.29.po_ref), channel_id=1, source_target_pairs={{0,4},{4,0},{8,12},{12,8},{1,5},{5,1},{9,13},{13,9},{2,6},{6,2},{1... | collective-permute-start | bytes 245768 | tf_op jit(solution)/shard_map/ppermute | solution.py:674
  4.3 2.6 %collective-permute-start.1 = (f32[40,512]{1,0:T(8,128)}, f32[40,512]{1,0:T(8,128)S(1)}, u32[]{:S(2)}, u32[]{:S(2)}) collective-permute-start(f32[40,512]{1,0:T(8,128)} %get-tuple-element.29.po_ref), channel_id=1, source_target_pairs={{0,12},{4,8},{8,4},{12,0},{1,13},{5,9},{9,5},{13,1},{2,14},{6,10},... | collective-permute-start | bytes 245768 | tf_op jit(solution)/shard_map/ppermute | solution.py:674
  6.9 0.0 copy-start
  6.9 0.9 %copy-done = f32[40,512]{1,0:T(8,128)S(1)} copy-done((f32[40,512]{1,0:T(8,128)S(1)}, f32[40,512]{1,0:T(8,128)}, u32[]{:S(2)}) %copy-start) | copy-done | bytes 81944
  7.8 0.0 copy-start.1
  7.8 0.9 %copy-done.1 = f32[296,64]{1,0:T(8,128)S(1)} copy-done((f32[296,64]{1,0:T(8,128)S(1)}, f32[296,64]{1,0:T(8,128)}, u32[]{:S(2)}) %copy-start.1) | copy-done | bytes 75800
  8.7 1.9 %shard_map.166 = (bf16[4,384,1024]{2,1,0:T(8,128)(2,1)S(1)}, bf16[64,48]{1,0:T(8,128)(2,1)S(1)}, bf16[64,192]{1,0:T(8,128)(2,1)S(1)}, bf16[64,32]{1,0:T(8,128)(2...) custom-call(f32[40,512]{1,0:T(8,128)S(1)} %copy-done, ...), custom_call_target="tpu_custom_call" | custom-call | flops 100000000 | bytes 262144 | tf_op jit(solution)/shard_map/pallas_call | solution.py:662
  10.6 1.6 %collective-permute-start.2 = (f32[3,1,512]{2,1,0:T(1,128)S(1)}, f32[3,1,512]{2,1,0:T(1,128)S(1)}, u32[]{:S(2)}, u32[]{:S(2)}) collective-permute-start(f32[3,1,512]{2,1,0:T(1,128)S(1)} %get-tuple-element.42), channel_id=1, source_target_pairs={{0,1},{1,0},{2,3},{3,2},{4,5},{5,4},{6,7},{7,6},{8,9},{9,8},{10,11... | collective-permute-start | bytes 18440 | tf_op jit(solution)/shard_map/ppermute | solution.py:674
  12.2 0.6 %collective-permute-start.3 = (f32[3,1,512]{2,1,0:T(1,128)S(1)}, f32[3,1,512]{2,1,0:T(1,128)S(1)}, u32[]{:S(2)}, u32[]{:S(2)}) collective-permute-start(f32[3,1,512]{2,1,0:T(1,128)S(1)} %get-tuple-element.42), channel_id=1, source_target_pairs={{0,0},{1,2},{2,1},{3,3},{4,4},{5,6},{6,5},{7,7},{8,8},{9,10},{10,9... | collective-permute-start | bytes 18440 | tf_op jit(solution)/shard_map/ppermute | solution.py:674
  12.9 0.0 collective-permute-done.sibling_ref
  12.9 0.0 collective-permute-done.1.across_ref
  12.9 5.8 %shard_map.167 = (f32[3,512]{1,0:T(4,128)S(1)}, f32[40,512]{1,0:T(8,128)S(1)}, f32[40,512]{1,0:T(8,128)S(1)}, bf16[768,1024]{1,0:T(8,128)(2,1)S(1)}) custom-call(f32[40,512]{1,0:T(8,128)S(1)} %collective-permute-done.sibling_ref, f32[40,512]{1,0:T(8,128)S(1)} %copy-done, f32[40,512]{1,0:T(8,128)S(1)} %collective-permute-done.1.across_ref, ...), custom_call_target="tpu_custom_call" | custom-call | flops 1000000000 | bytes 262144 | tf_op jit(solution)/shard_map/pallas_call | solution.py:662
  18.7 0.0 collective-permute-done.2.pair_ref
  18.7 0.0 collective-permute-done.3.other_ref
  18.7 0.1 shard_map.168
  18.8 0.0 collective-permute-start.4
  18.9 0.7 %collective-permute-start.5 = (f32[8,512]{1,0:T(8,128)S(1)}, f32[8,512]{1,0:T(8,128)S(1)}, u32[]{:S(2)}, u32[]{:S(2)}) collective-permute-start(f32[8,512]{1,0:T(8,128)S(1)} %get-tuple-element.43.own_ref), channel_id=1, source_target_pairs={{0,12},{4,8},{8,4},{12,0},{1,13},{5,9},{9,5},{13,1},{2,14},{6,10},... | collective-permute-start | bytes 49160 | tf_op jit(solution)/shard_map/ppermute | solution.py:674
  19.5 1.5 %collective-permute-start.6 = (f32[8,128]{1,0:T(8,128)S(1)}, f32[8,128]{1,0:T(8,128)S(1)}, u32[]{:S(2)}, u32[]{:S(2)}) collective-permute-start(f32[8,128]{1,0:T(8,128)S(1)} %get-tuple-element.44.rest_0_), channel_id=1, source_target_pairs={{0,8},{4,12},{8,0},{12,4},{1,9},{5,13},{9,1},{13,5},{2,10},{6,14},... | collective-permute-start | bytes 12296 | tf_op jit(solution)/shard_map/ppermute | solution.py:674
  21.0 2.1 %collective-permute-done.6.rest_1_ = f32[8,128]{1,0:T(8,128)S(1)} collective-permute-done((f32[8,128]{1,0:T(8,128)S(1)}, f32[8,128]{1,0:T(8,128)S(1)}, u32[]{:S(2)}, u32[]{:S(2)}) %collective-permute-start.6) | collective-permute-done | bytes 4128 | tf_op jit(solution)/shard_map/ppermute | solution.py:674
  23.1 0.0 collective-permute-done.4.near_ref
  23.1 0.0 collective-permute-done.5.far_ref
  23.1 5.7 %shard_map.169 = (f32[1,40,128]{2,1,0:T(8,128)S(1)}, f32[2,128]{1,0:T(2,128)S(1)}) custom-call(f32[8,128]{1,0:T(8,128)S(1)} %get-tuple-element.31.number_ref, f32[40,512]{1,0:T(8,128)S(1)} %get-tuple-element.39.pl_ref, f32[40,512]{1,0:T(8,128)S(1)} %copy-done, f32[40,512]{1,0:T(8,128)S(1)} %get-tuple-element.40.pr_ref, ...), custom_call_target="tpu_custom_call" | custom-call | flops 1000000000 | bytes 262144 | tf_op jit(solution)/shard_map/pallas_call | solution.py:662
  28.8 4.5 %collective-permute-start.7 = (f32[1,40,128]{2,1,0:T(8,128)S(1)}, f32[1,40,128]{2,1,0:T(8,128)S(1)}, u32[]{:S(2)}, u32[]{:S(2)}) collective-permute-start(f32[1,40,128]{2,1,0:T(8,128)S(1)} %get-tuple-element.46.refs_0_.own_ref), channel_id=1, source_target_pairs={{0,1},{1,0},{2,3},{3,2},{4,5},{5,4},{6,7},{7,6},{8,9},{9,8},{10,11... | collective-permute-start | bytes 61448 | tf_op jit(solution)/shard_map/ppermute | solution.py:674
  33.3 0.0 collective-permute-start.8
  33.3 2.4 %collective-permute-start.9 = (f32[1,40,128]{2,1,0:T(8,128)S(1)}, f32[1,40,128]{2,1,0:T(8,128)S(1)}, u32[]{:S(2)}, u32[]{:S(2)}) collective-permute-start(f32[1,40,128]{2,1,0:T(8,128)S(1)} %get-tuple-element.46.refs_0_.own_ref), channel_id=1, source_target_pairs={{0,3},{1,2},{2,1},{3,0},{4,7},{5,6},{6,5},{7,4},{8,11},{9,10},{10,... | collective-permute-start | bytes 61448 | tf_op jit(solution)/shard_map/ppermute | solution.py:674
  35.7 0.0 collective-permute-done.7.refs_1_
  35.7 2.2 %collective-permute-done.8.refs_2_ = f32[1,40,128]{2,1,0:T(8,128)S(1)} collective-permute-done((f32[1,40,128]{2,1,0:T(8,128)S(1)}, f32[1,40,128]{2,1,0:T(8,128)S(1)}, u32[]{:S(2)}, u32[]{:S(2)}) %collective-permute-start.8) | collective-permute-done | bytes 20512 | tf_op jit(solution)/shard_map/ppermute | solution.py:674
  37.9 0.9 %collective-permute-done.9.refs_3_ = f32[1,40,128]{2,1,0:T(8,128)S(1)} collective-permute-done((f32[1,40,128]{2,1,0:T(8,128)S(1)}, f32[1,40,128]{2,1,0:T(8,128)S(1)}, u32[]{:S(2)}, u32[]{:S(2)}) %collective-permute-start.9) | collective-permute-done | bytes 20512 | tf_op jit(solution)/shard_map/ppermute | solution.py:674
  38.8 0.2 shard_map.170
  39.1 1.6 %collective-permute-start.10 = (f32[8,128]{1,0:T(8,128)S(1)}, f32[8,128]{1,0:T(8,128)S(1)}, u32[]{:S(2)}, u32[]{:S(2)}) collective-permute-start(f32[8,128]{1,0:T(8,128)S(1)} %get-tuple-element.49.rest_0_), channel_id=1, source_target_pairs={{0,8},{4,12},{8,0},{12,4},{1,9},{5,13},{9,1},{13,5},{2,10},{6,14},... | collective-permute-start | bytes 12296 | tf_op jit(solution)/shard_map/ppermute | solution.py:674
  40.6 0.0 collective-permute-start.11
  40.6 0.6 %collective-permute-start.12 = (f32[8,128]{1,0:T(8,128)S(1)}, f32[8,128]{1,0:T(8,128)S(1)}, u32[]{:S(2)}, u32[]{:S(2)}) collective-permute-start(f32[8,128]{1,0:T(8,128)S(1)} %get-tuple-element.49.rest_0_), channel_id=1, source_target_pairs={{0,4},{4,0},{8,12},{12,8},{1,5},{5,1},{9,13},{13,9},{2,6},{6,2},{1... | collective-permute-start | bytes 12296 | tf_op jit(solution)/shard_map/ppermute | solution.py:674
  41.3 1.5 %collective-permute-done.10.rest_1_ = f32[8,128]{1,0:T(8,128)S(1)} collective-permute-done((f32[8,128]{1,0:T(8,128)S(1)}, f32[8,128]{1,0:T(8,128)S(1)}, u32[]{:S(2)}, u32[]{:S(2)}) %collective-permute-start.10) | collective-permute-done | bytes 4128 | tf_op jit(solution)/shard_map/ppermute | solution.py:674
  42.7 0.9 %collective-permute-done.11.rest_2_ = f32[8,128]{1,0:T(8,128)S(1)} collective-permute-done((f32[8,128]{1,0:T(8,128)S(1)}, f32[8,128]{1,0:T(8,128)S(1)}, u32[]{:S(2)}, u32[]{:S(2)}) %collective-permute-start.11) | collective-permute-done | bytes 4128 | tf_op jit(solution)/shard_map/ppermute | solution.py:674
  43.6 0.0 collective-permute-done.12.rest_3_
  43.7 0.7 %shard_map.171 = (f32[3,1,512]{2,1,0:T(1,128)}, f32[3,1,512]{2,1,0:T(1,128)}, f32[2,1,2]{2,1,0:T(1,128)}, f32[1,1]{1,0:T(1,128)}) custom-call(f32[8,128]{1,0:T(8,128)S(1)} %get-tuple-element.31.number_ref, f32[1,40,128]{2,1,0:T(8,128)S(1)} %get-tuple-element.46.refs_0_.own_ref, f32[2,128]{1,0:T(2,128)S(1)} %get-tuple-element.47.record_ref, ...), custom_call_target="tpu_custom_call" | custom-call | bytes 262144 | tf_op jit(solution)/shard_map/pallas_call | solution.py:662
Async XLA Ops:
  3.8 9.1 %collective-permute-start = (f32[40,512]{1,0:T(8,128)}, f32[40,512]{1,0:T(8,128)S(1)}, u32[]{:S(2)}, u32[]{:S(2)}) collective-permute-start(f32[40,512]{1,0:T(8,128)} %get-tuple-element.29.po_ref), channel_id=1, source_target_pairs={{0,4},{4,0},{8,12},{12,8},{1,5},{5,1},{9,13},{13,9},{2,6},{6,2},{1... | collective-permute-start | bytes 245768 | tf_op jit(solution)/shard_map/ppermute | solution.py:674
  4.3 8.6 %collective-permute-start.1 = (f32[40,512]{1,0:T(8,128)}, f32[40,512]{1,0:T(8,128)S(1)}, u32[]{:S(2)}, u32[]{:S(2)}) collective-permute-start(f32[40,512]{1,0:T(8,128)} %get-tuple-element.29.po_ref), channel_id=1, source_target_pairs={{0,12},{4,8},{8,4},{12,0},{1,13},{5,9},{9,5},{13,1},{2,14},{6,10},... | collective-permute-start | bytes 245768 | tf_op jit(solution)/shard_map/ppermute | solution.py:674
  6.9 0.9 %copy-start = (f32[40,512]{1,0:T(8,128)S(1)}, f32[40,512]{1,0:T(8,128)}, u32[]{:S(2)}) copy-start(f32[40,512]{1,0:T(8,128)} %get-tuple-element.29.po_ref) | copy-start | bytes 245764
  7.8 0.9 %copy-start.1 = (f32[296,64]{1,0:T(8,128)S(1)}, f32[296,64]{1,0:T(8,128)}, u32[]{:S(2)}) copy-start(f32[296,64]{1,0:T(8,128)} %get-tuple-element.30.raw_ref) | copy-start | bytes 227332
  10.6 8.1 %collective-permute-start.2 = (f32[3,1,512]{2,1,0:T(1,128)S(1)}, f32[3,1,512]{2,1,0:T(1,128)S(1)}, u32[]{:S(2)}, u32[]{:S(2)}) collective-permute-start(f32[3,1,512]{2,1,0:T(1,128)S(1)} %get-tuple-element.42), channel_id=1, source_target_pairs={{0,1},{1,0},{2,3},{3,2},{4,5},{5,4},{6,7},{7,6},{8,9},{9,8},{10,11... | collective-permute-start | bytes 18440 | tf_op jit(solution)/shard_map/ppermute | solution.py:674
  12.2 6.5 %collective-permute-start.3 = (f32[3,1,512]{2,1,0:T(1,128)S(1)}, f32[3,1,512]{2,1,0:T(1,128)S(1)}, u32[]{:S(2)}, u32[]{:S(2)}) collective-permute-start(f32[3,1,512]{2,1,0:T(1,128)S(1)} %get-tuple-element.42), channel_id=1, source_target_pairs={{0,0},{1,2},{2,1},{3,3},{4,4},{5,6},{6,5},{7,7},{8,8},{9,10},{10,9... | collective-permute-start | bytes 18440 | tf_op jit(solution)/shard_map/ppermute | solution.py:674
  18.8 4.3 %collective-permute-start.4 = (f32[8,512]{1,0:T(8,128)S(1)}, f32[8,512]{1,0:T(8,128)S(1)}, u32[]{:S(2)}, u32[]{:S(2)}) collective-permute-start(f32[8,512]{1,0:T(8,128)S(1)} %get-tuple-element.43.own_ref), channel_id=1, source_target_pairs={{0,4},{4,0},{8,12},{12,8},{1,5},{5,1},{9,13},{13,9},{2,6},{6,2},{1... | collective-permute-start | bytes 49160 | tf_op jit(solution)/shard_map/ppermute | solution.py:674
  18.9 4.3 %collective-permute-start.5 = (f32[8,512]{1,0:T(8,128)S(1)}, f32[8,512]{1,0:T(8,128)S(1)}, u32[]{:S(2)}, u32[]{:S(2)}) collective-permute-start(f32[8,512]{1,0:T(8,128)S(1)} %get-tuple-element.43.own_ref), channel_id=1, source_target_pairs={{0,12},{4,8},{8,4},{12,0},{1,13},{5,9},{9,5},{13,1},{2,14},{6,10},... | collective-permute-start | bytes 49160 | tf_op jit(solution)/shard_map/ppermute | solution.py:674
  19.5 3.6 %collective-permute-start.6 = (f32[8,128]{1,0:T(8,128)S(1)}, f32[8,128]{1,0:T(8,128)S(1)}, u32[]{:S(2)}, u32[]{:S(2)}) collective-permute-start(f32[8,128]{1,0:T(8,128)S(1)} %get-tuple-element.44.rest_0_), channel_id=1, source_target_pairs={{0,8},{4,12},{8,0},{12,4},{1,9},{5,13},{9,1},{13,5},{2,10},{6,14},... | collective-permute-start | bytes 12296 | tf_op jit(solution)/shard_map/ppermute | solution.py:674
  28.8 6.9 %collective-permute-start.7 = (f32[1,40,128]{2,1,0:T(8,128)S(1)}, f32[1,40,128]{2,1,0:T(8,128)S(1)}, u32[]{:S(2)}, u32[]{:S(2)}) collective-permute-start(f32[1,40,128]{2,1,0:T(8,128)S(1)} %get-tuple-element.46.refs_0_.own_ref), channel_id=1, source_target_pairs={{0,1},{1,0},{2,3},{3,2},{4,5},{5,4},{6,7},{7,6},{8,9},{9,8},{10,11... | collective-permute-start | bytes 61448 | tf_op jit(solution)/shard_map/ppermute | solution.py:674
  33.3 4.7 %collective-permute-start.8 = (f32[1,40,128]{2,1,0:T(8,128)S(1)}, f32[1,40,128]{2,1,0:T(8,128)S(1)}, u32[]{:S(2)}, u32[]{:S(2)}) collective-permute-start(f32[1,40,128]{2,1,0:T(8,128)S(1)} %get-tuple-element.46.refs_0_.own_ref), channel_id=1, source_target_pairs={{0,2},{1,3},{2,0},{3,1},{4,6},{5,7},{6,4},{7,5},{8,10},{9,11},{10,... | collective-permute-start | bytes 61448 | tf_op jit(solution)/shard_map/ppermute | solution.py:674
  33.3 5.6 %collective-permute-start.9 = (f32[1,40,128]{2,1,0:T(8,128)S(1)}, f32[1,40,128]{2,1,0:T(8,128)S(1)}, u32[]{:S(2)}, u32[]{:S(2)}) collective-permute-start(f32[1,40,128]{2,1,0:T(8,128)S(1)} %get-tuple-element.46.refs_0_.own_ref), channel_id=1, source_target_pairs={{0,3},{1,2},{2,1},{3,0},{4,7},{5,6},{6,5},{7,4},{8,11},{9,10},{10,... | collective-permute-start | bytes 61448 | tf_op jit(solution)/shard_map/ppermute | solution.py:674
  39.1 3.7 %collective-permute-start.10 = (f32[8,128]{1,0:T(8,128)S(1)}, f32[8,128]{1,0:T(8,128)S(1)}, u32[]{:S(2)}, u32[]{:S(2)}) collective-permute-start(f32[8,128]{1,0:T(8,128)S(1)} %get-tuple-element.49.rest_0_), channel_id=1, source_target_pairs={{0,8},{4,12},{8,0},{12,4},{1,9},{5,13},{9,1},{13,5},{2,10},{6,14},... | collective-permute-start | bytes 12296 | tf_op jit(solution)/shard_map/ppermute | solution.py:674
  40.6 3.0 %collective-permute-start.11 = (f32[8,128]{1,0:T(8,128)S(1)}, f32[8,128]{1,0:T(8,128)S(1)}, u32[]{:S(2)}, u32[]{:S(2)}) collective-permute-start(f32[8,128]{1,0:T(8,128)S(1)} %get-tuple-element.49.rest_0_), channel_id=1, source_target_pairs={{0,12},{4,8},{8,4},{12,0},{1,13},{5,9},{9,5},{13,1},{2,14},{6,10},... | collective-permute-start | bytes 12296 | tf_op jit(solution)/shard_map/ppermute | solution.py:674
  40.6 3.0 %collective-permute-start.12 = (f32[8,128]{1,0:T(8,128)S(1)}, f32[8,128]{1,0:T(8,128)S(1)}, u32[]{:S(2)}, u32[]{:S(2)}) collective-permute-start(f32[8,128]{1,0:T(8,128)S(1)} %get-tuple-element.49.rest_0_), channel_id=1, source_target_pairs={{0,4},{4,0},{8,12},{12,8},{1,5},{5,1},{9,13},{13,9},{2,6},{6,2},{1... | collective-permute-start | bytes 12296 | tf_op jit(solution)/shard_map/ppermute | solution.py:674

commit v7 on v6

--- a/solution.py
+++ b/solution.py
@@ -26,12 +26,7 @@
 ROW_KIND = 36
 ROW_V = 37
 PACK_ROWS = 40
-RAW_MIX = 16
-RAW_UPDATE = 144
-RAW_EMBED = 272
-RAW_READOUT = 280
-RAW_NUMBER = 288
-RAW_ROWS = 296
+OWN_ROWS = PACK_ROWS + CHANNELS + BASIS
 NT = (((1,), (1,)), ((), ()))
 
 
@@ -65,44 +60,47 @@
 
 
 def pack_kernel(*refs):
-    sources, (out_ref, raw_ref), held, sems = refs[:14], refs[14:16], refs[16:26], refs[26]
-    lattice, radial, mix, update = sources[10:]
+    sources, (out_ref, own_ref), held, sems = refs[:11], refs[11:13], refs[13:23], refs[23]
+    lattice = sources[10]
     pairs = list(zip(sources, held))
-    pairs += [(lattice.at[c], out_ref.at[pl.ds(8 + 8 * c, 8)]) for c in range(3)]
-    pairs += [(radial.at[l], raw_ref.at[pl.ds(BASIS * l, BASIS)]) for l in range(2)]
-    pairs += [(mix.at[l], raw_ref.at[pl.ds(RAW_MIX + CHANNELS * l, CHANNELS)]) for l in range(2)]
-    pairs += [(update.at[l], raw_ref.at[pl.ds(RAW_UPDATE + CHANNELS * l, CHANNELS)]) for l in range(2)]
+    for c in range(3):
+        rows = pl.ds(8 + 8 * c, 8)
+        pairs += [(lattice.at[c], out_ref.at[rows]), (lattice.at[c], own_ref.at[rows])]
     copies = [pltpu.make_async_copy(a, b, sems.at[i]) for i, (a, b) in enumerate(pairs)]
     for one in copies:
         one.start()
     for one in copies:
         one.wait()
-    x, v, species, nbr, counts, embed, readout, dt, flags, climb = held
-    out_ref[0:8, :] = nbr[...].astype(F32)
-    for c in range(3):
-        out_ref[ROW_X + c : ROW_X + c + 1, :] = x[c]
-        out_ref[ROW_V + c : ROW_V + c + 1, :] = v[c]
-    out_ref[ROW_COUNT : ROW_COUNT + 1, :] = counts[...].astype(F32).reshape(1, -1)
-    out_ref[ROW_KIND : ROW_KIND + 1, :] = species[...].astype(F32).reshape(1, -1)
-    raw_ref[RAW_EMBED : RAW_EMBED + 2, :] = embed[...]
-    raw_ref[RAW_READOUT : RAW_READOUT + 1, :] = readout[...].reshape(1, CHANNELS)
-    numbers = [dt[0, 0], climb[0, 0].astype(F32)] + [flags[0, s].astype(F32) for s in range(flags.shape[1])]
-    for i, value in enumerate(numbers):
-        raw_ref[RAW_NUMBER + i : RAW_NUMBER + i + 1, :] = jnp.full((1, CHANNELS), value, F32)
-
-
-def prepare_kernel(po_ref, raw_ref, *rest):
-    own_hot, l1_ref, l2_ref, l3_ref, l5_ref, l6_ref, col_ref, copy_ref, number_ref = rest
+    x, v, species, nbr, counts, embed, readout, radial, mix, update = held
+    for ref in (out_ref, own_ref):
+        ref[0:8, :] = nbr[...].astype(F32)
+        for c in range(3):
+            ref[ROW_X + c : ROW_X + c + 1, :] = x[c]
+            ref[ROW_V + c : ROW_V + c + 1, :] = v[c]
+        ref[ROW_COUNT : ROW_COUNT + 1, :] = counts[...].astype(F32).reshape(1, -1)
+        ref[ROW_KIND : ROW_KIND + 1, :] = species[...].astype(F32).reshape(1, -1)
+    top, low = PACK_ROWS, PACK_ROWS + CHANNELS
+    for i, value in enumerate([mix[0], mix[1], update[0], update[1]]):
+        own_ref[top:low, i * LANES : i * LANES + CHANNELS] = value
+    for i, value in enumerate([radial[0], radial[1], embed[...], readout[...].reshape(1, CHANNELS)]):
+        own_ref[low : low + value.shape[0], i * LANES : i * LANES + CHANNELS] = value
+
+
+def prepare_kernel(po_ref, *rest):
+    own_hot, l1_ref, l2_ref, l3_ref, l5_ref, l6_ref, col_ref, copy_ref = rest
     for b in range(SLAB_BLOCKS):
         mark(window_index(po_ref, b), [0, 1, 2], own_hot.at[b])
     for c in range(3):
         copy_ref[c] = po_ref[ROW_X + c : ROW_X + c + 1, :]
-    number_ref[...] = jnp.broadcast_to(raw_ref[RAW_NUMBER : RAW_NUMBER + 8, 0:1], (8, LANES))
-    radial_ref = [raw_ref[BASIS * l : BASIS * (l + 1), :] for l in range(2)]
-    mix_ref = [raw_ref[RAW_MIX + CHANNELS * l : RAW_MIX + CHANNELS * (l + 1), :] for l in range(2)]
-    update_ref = [raw_ref[RAW_UPDATE + CHANNELS * l : RAW_UPDATE + CHANNELS * (l + 1), :] for l in range(2)]
-    embed_ref = raw_ref[RAW_EMBED : RAW_EMBED + 2, :]
-    readout = raw_ref[RAW_READOUT : RAW_READOUT + 1, :]
+
+    def raw(first, count, i):
+        return po_ref[first : first + count, i * LANES : i * LANES + CHANNELS]
+
+    low = PACK_ROWS + CHANNELS
+    mix_ref = [raw(PACK_ROWS, CHANNELS, i) for i in range(2)]
+    update_ref = [raw(PACK_ROWS, CHANNELS, 2 + i) for i in range(2)]
+    radial_ref = [raw(low, BASIS, i) for i in range(2)]
+    embed_ref, readout = raw(low, 2, 2), raw(low, 1, 3)
     eye = (
         lax.broadcasted_iota(jnp.int32, (CHANNELS, CHANNELS), 0)
         == lax.broadcasted_iota(jnp.int32, (CHANNELS, CHANNELS), 1)
@@ -180,9 +178,9 @@
         mark(window_index(packs[b // 4], b), ws, side.at[start : start + len(ws) * LANES])
 
 
-def force_parts(packs, weights, own_hot, side_hot, scr):
+def forward_parts(packs, weights, xs, sst, kept):
     l1, l2, l3, l5, l6, col = weights
-    (xs, widx, kinds, geo, bst, bps, bpr, sst, sent_all, slope, dg, pulls, acc) = scr
+    (widx, kinds, geo, bst, bps, bpr, sent_all, slope) = kept
     centre = 2.0 + 0.5 * lax.broadcasted_iota(jnp.int32, (BASIS, LANES), 0).astype(F32)
     slot = lax.broadcasted_iota(jnp.int32, (SLOTS, LANES), 0)
 
@@ -253,6 +251,12 @@
             one = one + col[0] + col[1] * jnp.broadcast_to(xs[b + i, 3:4, :], (CHANNELS, LANES))
             sent_all[:, (b + i) * LANES : (b + i + 1) * LANES] = one
         slope[:, cols] = steep
+
+
+def force_parts(weights, own_hot, side_hot, kept, dg, pulls, acc):
+    l1, l2, l3, l5, l6, col = weights
+    (widx, kinds, geo, bst, bps, bpr, sent_all, slope) = kept
+    slot = lax.broadcasted_iota(jnp.int32, (SLOTS, LANES), 0)
 
     def spread(left, b, first, last):
         ws = reach(b, first, last)
@@ -370,20 +374,27 @@
     return jnp.sum(a * b, axis=0, keepdims=True)
 
 
-def scratch():
+def kept_shapes():
     wide = 12 * LANES
     return [
-        pltpu.VMEM((12, 8, LANES), F32),
-        pltpu.VMEM((12, 8, LANES), jnp.int32),
-        pltpu.VMEM((12, 8, LANES), F32),
-        pltpu.VMEM((12, 4, 8, LANES), F32),
-        pltpu.VMEM((12, 16, SLOTS * LANES), BF16),
-        pltpu.VMEM((12, 16, SLOTS * LANES), BF16),
-        pltpu.VMEM((12, 8, SLOTS * LANES), F32),
-        pltpu.VMEM((48, wide), BF16),
-        pltpu.VMEM((CHANNELS, wide), F32),
-        pltpu.VMEM((CHANNELS, wide), F32),
-        pltpu.VMEM((CHANNELS, wide), F32),
+        ((12, 8, LANES), jnp.int32),
+        ((12, 8, LANES), F32),
+        ((12, 4, 8, LANES), F32),
+        ((12, 16, SLOTS * LANES), BF16),
+        ((12, 16, SLOTS * LANES), BF16),
+        ((12, 8, SLOTS * LANES), F32),
+        ((CHANNELS, wide), F32),
+        ((CHANNELS, wide), F32),
+    ]
+
+
+def forward_scratch():
+    return [pltpu.VMEM((12, 8, LANES), F32), pltpu.VMEM((48, 12 * LANES), BF16)]
+
+
+def back_scratch():
+    return [
+        pltpu.VMEM((CHANNELS, 12 * LANES), F32),
         pltpu.VMEM((12, 8, SLOTS * LANES), F32),
         pltpu.VMEM((12, 3, 8, LANES), F32),
     ]
@@ -394,13 +405,19 @@
     return jnp.where(even, across, sibling), jnp.where(even, sibling, across)
 
 
-def first_kernel(sibling_ref, po_ref, across_ref, own_hot, *rest):
-    weights, (out_ref, pl_ref, pr_ref, side_hot), scr = rest[:6], rest[6:10], rest[10:]
+def first_kernel(x_ref, sibling_ref, po_ref, across_ref, *rest):
+    weights, (pl_ref, pr_ref, side_hot, copy_ref), kept, (xs, sst) = rest[:6], rest[6:10], rest[10:18], rest[18:]
+    copy_ref[...] = x_ref[...]
     pl_ref[...], pr_ref[...] = by_parity(sibling_ref[...], across_ref[...])
     packs = [pl_ref, po_ref, pr_ref]
     mark_sides(packs, side_hot)
-    fill_region(scr[0], packs, lambda s: packs[s][ROW_X : ROW_X + 3, :])
-    force_parts(packs, weights, own_hot, side_hot, scr)
+    fill_region(xs, packs, lambda s: packs[s][ROW_X : ROW_X + 3, :])
+    forward_parts(packs, weights, xs, sst, kept)
+
+
+def first_back_kernel(own_hot, side_hot, *rest):
+    weights, kept, out_ref, scr = rest[:6], rest[6:14], rest[14], rest[15:]
+    force_parts(weights, own_hot, side_hot, kept, *scr)
     for c in range(3):
         out_ref[c : c + 1, :] = own_force(scr[-1], c)
 
@@ -479,7 +496,7 @@
     out_ref[count : 2 * count] = b_ref[...]
 
 
-def second_kernel(images, domains, number_ref, pl_ref, po_ref, pr_ref, own_ref, near_ref, far_ref, *rest):
+def second_kernel(images, domains, dt_ref, flag_ref, climb_ref, pl_ref, po_ref, pr_ref, own_ref, near_ref, far_ref, *rest):
     count = 2 if domains == 4 else 1
     parts, rest = rest[:count], rest[count:]
     (own_hot, side_hot), weights, (out_ref, record_ref), scr = rest[:2], rest[2:8], rest[8:10], rest[10:]
@@ -503,10 +520,10 @@
         pp,
         mn,
         vv,
-        number_ref[0:1, :],
+        jnp.full(shape, dt_ref[0], F32),
         jnp.full(shape, ALPHA_START, F32),
-        number_ref[2:3, :] == 1.0,
-        number_ref[1:2, :] == jnp.full(shape, here, jnp.int32).astype(F32),
+        jnp.full(shape, flag_ref[0, 0], jnp.int32) == 1,
+        jnp.full(shape, here - climb_ref[0], jnp.int32) == 0,
         jnp.full(shape, jnp.where((here >= 1) & (here <= images - 2), 1, 0), jnp.int32) == 1,
     )
     messages = [beside[0], own_ref[0:6, :], beside[1]]
@@ -519,8 +536,10 @@
         for p, m in zip(packs, messages)
     ]
     moved = [p[ROW_X : ROW_X + 3, :] + wide(dt) * s for p, s in zip(packs, speeds)]
-    fill_region(scr[0], packs, lambda s: moved[s])
-    force_parts(packs, weights, own_hot, side_hot, scr)
+    xs, sst, kept = scr[0], scr[1], scr[2:10]
+    fill_region(xs, packs, lambda s: moved[s])
+    forward_parts(packs, weights, xs, sst, kept)
+    force_parts(weights, own_hot, side_hot, kept, *scr[10:])
     for c in range(3):
         force = own_force(scr[-1], c)
         for i in range(SLAB_BLOCKS):
@@ -531,9 +550,10 @@
             out_ref[0, 24 + row : 25 + row, :] = moved[1][c : c + 1, lanes]
     out_ref[0, 36:37, :] = dt
     out_ref[0, 37:38, :] = alpha
-    out_ref[0, 38:40, :] = jnp.broadcast_to(number_ref[3:4, :], (2, LANES))
+    out_ref[0, 38:40, :] = jnp.full((2, LANES), flag_ref[0, 1], jnp.int32).astype(F32)
     record_ref[0:1, :] = along
     record_ref[1:2, :] = spring
+    record_ref[2:3, :] = jnp.full(shape, climb_ref[0], jnp.int32).astype(F32)
 
 
 PRODUCTS = (
@@ -585,7 +605,7 @@
         state_ref[16 + rows * i : 16 + rows * (i + 1), :] = gathered(36 + i)
 
 
-def final_kernel(images, atoms, number_ref, own_ref, record_ref, state_ref, *rest):
+def final_kernel(images, atoms, own_ref, record_ref, state_ref, *rest):
     parts, (x_ref, v_ref, band_ref, path_ref) = rest[:-4], rest[-4:]
     rows = parts[0].shape[0]
     here = lax.axis_index("img")
@@ -597,7 +617,7 @@
     }
     number = lax.broadcasted_iota(jnp.int32, (rows, LANES), 0)
     inside = (number >= 1) & (number <= images - 2)
-    climb = jnp.broadcast_to(number_ref[1:2, :], (rows, LANES))
+    climb = jnp.broadcast_to(record_ref[2:3, :], (rows, LANES))
     dt0, alpha0, flag = (state_ref[16 + rows * i : 16 + rows * (i + 1), :] for i in range(3))
     along, spring, keep, pull, side, dt, _ = step_numbers(
         got["f", "t"],
@@ -724,22 +744,19 @@
     shape = jax.ShapeDtypeStruct
     x = jnp.transpose(disp, (1, 0, 2))
     v = jnp.transpose(veloc, (1, 0, 2))
-    small = (x, v, species, neighbours, counts, embed, readout)
-    numbers = (time_step.reshape(1, 1), jnp.transpose(reset_flags), climb.reshape(1, 1))
-    pack, raw = call(
+    small = (x, v, species, neighbours, counts, embed, readout, radial_weight, mix_weight, update_weight)
+    sent, pack = call(
         pack_kernel,
-        (shape((PACK_ROWS, atoms), F32), shape((RAW_ROWS, CHANNELS), F32)),
+        (shape((PACK_ROWS, atoms), F32), shape((OWN_ROWS, atoms), F32)),
         (),
-        (*small, *numbers, jnp.transpose(lattice, (1, 0, 2)), radial_weight, mix_weight, update_weight),
-        [pltpu.VMEM(a.shape, a.dtype) for a in small]
-        + [pltpu.SMEM(a.shape, a.dtype) for a in numbers]
-        + [pltpu.SemaphoreType.DMA((19,))],
+        (*small, jnp.transpose(lattice, (1, 0, 2))),
+        [pltpu.VMEM(a.shape, a.dtype) for a in small] + [pltpu.SemaphoreType.DMA((16,))],
         spec=HBM_SPEC,
         vmem=63,
     )
-    sibling = swap(pack, "dom", lambda i: i ^ 1)
-    across = swap(pack, "dom", lambda i: (i + 2 * (i % 2) - 1) % domains)
-    own_hot, *weights, x_copy, numbers = call(
+    sibling = swap(sent, "dom", lambda i: i ^ 1)
+    across = swap(sent, "dom", lambda i: (i + 2 * (i % 2) - 1) % domains)
+    own_hot, *weights, x_copy = call(
         prepare_kernel,
         (
             shape((SLAB_BLOCKS, 3 * LANES, SLOTS * LANES), BF16),
@@ -750,25 +767,33 @@
             shape((16, 192), BF16),
             shape((4, CHANNELS, LANES), F32),
             shape(x.shape, F32),
-            shape((8, LANES), F32),
         ),
         (),
-        (pack, raw),
+        (pack,),
         flops=100000000,
     )
     pair = swap(x_copy, "img", lambda i: i ^ 1)
-    other = swap(x_copy, "img", lambda i: i if i in (0, images - 1) else i + 2 * (i % 2) - 1)
-    force, left, right, side_hot = call(
+    left, right, side_hot, x_copy, *kept = call(
         first_kernel,
         (
-            shape((3, atoms), F32),
-            shape(pack.shape, F32),
-            shape(pack.shape, F32),
+            shape(sent.shape, F32),
+            shape(sent.shape, F32),
             shape((SIDE_ROWS, SLOTS * LANES), BF16),
+            shape(x.shape, F32),
+            *[shape(*one) for one in kept_shapes()],
         ),
         (),
-        (sibling, pack, across, own_hot, *weights),
-        scratch(),
+        (x_copy, sibling, pack, across, *weights),
+        forward_scratch(),
+        flops=1000000000,
+    )
+    other = swap(x_copy, "img", lambda i: i if i in (0, images - 1) else i + 2 * (i % 2) - 1)
+    force = call(
+        first_back_kernel,
+        shape((3, atoms), F32),
+        (),
+        (own_hot, side_hot, *weights, *kept),
+        back_scratch(),
         flops=1000000000,
     )
     message, sums = call(
@@ -785,10 +810,10 @@
     near = swap(message, "dom", lambda i: i ^ 1)
     state, record = call(
         functools.partial(second_kernel, images, domains),
-        (shape((1, 40, LANES), F32), shape((2, LANES), F32)),
-        (),
-        (numbers, left, pack, right, message, near, far, *parts, own_hot, side_hot, *weights),
-        scratch(),
+        (shape((1, 40, LANES), F32), shape((3, LANES), F32)),
+        (time_step, jnp.transpose(reset_flags), climb),
+        (left, pack, right, message, near, far, *parts, own_hot, side_hot, *weights),
+        forward_scratch() + [pltpu.VMEM(*one) for one in kept_shapes()] + back_scratch(),
         flops=1000000000,
     )
     rows = 8 * ((images + 7) // 8)
@@ -803,7 +828,7 @@
         functools.partial(final_kernel, images, atoms * domains),
         (shape(x.shape, F32), shape(x.shape, F32), shape((2, 1, 2), F32), shape((1, 1), F32)),
         (),
-        (numbers, state, record, extra, *exchanged(sums, "dom")),
+        (state, record, extra, *exchanged(sums, "dom")),
     )
     return (
         jnp.transpose(new_x, (1, 0, 2)),

time: 44.7 us -> 44 us (0.984)
  Pallas kernels: 16.2 us -> 17.6 us
  waiting for transfers between devices: 7.66 us -> 6.36 us
  local copies, waits for them, and re-layouts: 1.83 us -> 0.94 us
    pallas_call x7 -> x8, Pallas kernels: 16.2 us -> 17.6 us  [call(): pl.pallas_call(body, out_shape=outs, in_specs=[SMEM_SPEC] * len(scalars)...]
    ppermute x13, waiting for transfers between devices: 7.66 us -> 6.36 us  [swap(): lax.ppermute(array, axis, [(i, partner(i)) for i in range(lax.axis_size(a...]
    unnamed x4, local copies, waits for them, and re-layouts: 1.83 us -> 0.94 us
  transfers between devices with their start and end apart: 13 -> 13, of which waited for: 5 -> 5; matrix products, arithmetic and copies ran while one was open for 0% -> 0% of each run, Pallas kernels for 17% -> 19%
where the time goes in v7:
time: 44 us; the launch traced here: 43.7 us
  Pallas kernels  17.6 us (40%)
  starting transfers between devices  16.8 us (38%)
  waiting for transfers between devices  6.36 us (14%)
  between operations  2.03 us (5%)
  local copies, waits for them, and re-layouts  0.94 us (2%)
    pallas_call x8, Pallas kernels, call(): pl.pallas_call(body, out_shape=outs, in_specs=[SMEM_SPEC] * len(scalars)...  17.6 us
    ppermute x13, starting transfers between devices, swap(): lax.ppermute(array, axis, [(i, partner(i)) for i in range(lax.axis_size(a...  16.8 us
    ppermute x13, waiting for transfers between devices, swap(): lax.ppermute(array, axis, [(i, partner(i)) for i in range(lax.axis_size(a...  6.36 us
    unnamed x4, local copies, waits for them, and re-layouts  0.94 us
  transfers between devices with their start and end apart: 13, of which 5 were waited for; matrix products, arithmetic and copies ran while one was open for 0% of the time, Pallas kernels for 19%

profile of v7, /device:TPU:0, one launch (start us, length us, event | category | flops | bytes accessed | tf_op | source)
XLA Modules:
  0.0 43.7 jit_solution(9223560191081682120)
XLA Ops:
  0.6 1.9 %shard_map.165 = (f32[40,512]{1,0:T(8,128)}, f32[112,512]{1,0:T(8,128)}) custom-call(f32[3,1,512]{2,1,0:T(1,128)} %bitcast.12, f32[3,1,512]{2,1,0:T(1,128)} %bitcast.13, s32[512]{0:T(512)} %refs_2_.1, s32[8,512]{1,0:T(8,128)} %refs_3_.1, s32[512]{0:T(512)} %refs_4_.1, f32[2,64]{1,0:T(2,128)} %refs_5_.1, f32[64]{0:T(128)} %refs_6_.1, f32[2,8,64]{2,1,0:T(8,128)} %refs_7_.1, ...), custom_call_target="tpu_custom_call" | custom-call | bytes 262144 | tf_op jit(solution)/shard_map/pallas_call | solution.py:682
  2.5 0.5 %collective-permute-start = (f32[40,512]{1,0:T(8,128)}, f32[40,512]{1,0:T(8,128)S(1)}, u32[]{:S(2)}, u32[]{:S(2)}) collective-permute-start(f32[40,512]{1,0:T(8,128)} %get-tuple-element.38), channel_id=1, source_target_pairs={{0,4},{4,0},{8,12},{12,8},{1,5},{5,1},{9,13},{13,9},{2,6},{6,2},{1... | collective-permute-start | bytes 245768 | tf_op jit(solution)/shard_map/ppermute | solution.py:694
  3.0 2.6 %collective-permute-start.1 = (f32[40,512]{1,0:T(8,128)}, f32[40,512]{1,0:T(8,128)S(1)}, u32[]{:S(2)}, u32[]{:S(2)}) collective-permute-start(f32[40,512]{1,0:T(8,128)} %get-tuple-element.38), channel_id=1, source_target_pairs={{0,12},{4,8},{8,4},{12,0},{1,13},{5,9},{9,5},{13,1},{2,14},{6,10},... | collective-permute-start | bytes 245768 | tf_op jit(solution)/shard_map/ppermute | solution.py:694
  5.7 0.0 copy-start
  5.7 0.9 %copy-done = f32[112,512]{1,0:T(8,128)S(1)} copy-done((f32[112,512]{1,0:T(8,128)S(1)}, f32[112,512]{1,0:T(8,128)}, u32[]{:S(2)}) %copy-start) | copy-done | bytes 229400
  6.6 1.9 %shard_map.166 = (bf16[4,384,1024]{2,1,0:T(8,128)(2,1)S(1)}, bf16[64,48]{1,0:T(8,128)(2,1)S(1)}, bf16[64,192]{1,0:T(8,128)(2,1)S(1)}, bf16[64,32]{1,0:T(8,128)(2...) custom-call(f32[112,512]{1,0:T(8,128)S(1)} %copy-done), custom_call_target="tpu_custom_call" | custom-call | flops 100000000 | bytes 262144 | tf_op jit(solution)/shard_map/pallas_call | solution.py:682
  8.5 1.6 %collective-permute-start.2 = (f32[3,1,512]{2,1,0:T(1,128)S(1)}, f32[3,1,512]{2,1,0:T(1,128)S(1)}, u32[]{:S(2)}, u32[]{:S(2)}) collective-permute-start(f32[3,1,512]{2,1,0:T(1,128)S(1)} %get-tuple-element.37.x_ref), channel_id=1, source_target_pairs={{0,1},{1,0},{2,3},{3,2},{4,5},{5,4},{6,7},{7,6},{8,9},{9,8},{10,11... | collective-permute-start | bytes 18440 | tf_op jit(solution)/shard_map/ppermute | solution.py:694
  10.1 0.0 collective-permute-done.sibling_ref
  10.1 0.0 collective-permute-done.1.across_ref
  10.1 1.5 %shard_map.167 = (f32[40,512]{1,0:T(8,128)S(1)}, f32[40,512]{1,0:T(8,128)S(1)}, bf16[768,1024]{1,0:T(8,128)(2,1)S(1)}, f32[3,1,512]{2,1,0:T(1,128)S(1)}, s32[12,...) custom-call(f32[3,1,512]{2,1,0:T(1,128)S(1)} %get-tuple-element.37.x, ...), custom_call_target="tpu_custom_call" | custom-call | flops 1000000000 | bytes 262144 | tf_op jit(solution)/shard_map/pallas_call | solution.py:682
  11.6 0.8 %collective-permute-start.3 = (f32[3,1,512]{2,1,0:T(1,128)S(1)}, f32[3,1,512]{2,1,0:T(1,128)S(1)}, u32[]{:S(2)}, u32[]{:S(2)}) collective-permute-start(f32[3,1,512]{2,1,0:T(1,128)S(1)} %get-tuple-element.57), channel_id=1, source_target_pairs={{0,0},{1,2},{2,1},{3,3},{4,4},{5,6},{6,5},{7,7},{8,8},{9,10},{10,9... | collective-permute-start | bytes 18440 | tf_op jit(solution)/shard_map/ppermute | solution.py:694
  12.5 0.0 copy-start.1
  12.5 5.1 %shard_map.168.force_ref = f32[3,512]{1,0:T(4,128)S(1)} custom-call(bf16[4,384,1024]{2,1,0:T(8,128)(2,1)S(1)} %get-tuple-element.47.own_hot.rest_2_, bf16[768,1024]{1,0:T(8,128)(2,1)S(1)} %get-tuple-element.48.side_hot.rest_3_, bf16[64,48]{1,0:T(8,128)(2,1)S(1)} %get-tuple-element.39.rest_0_.rest_4_, bf16[64,192]{1,0:T(8,128)(2,1)S(1)} %get-tuple-element.40.rest_1_.rest_5_, ...), custom_call_target="tpu_custom_call" | custom-call | flops 1000000000 | bytes 262144 | tf_op jit(solution)/shard_map/pallas_call | solution.py:682
  17.5 0.0 collective-permute-done.2.pair_ref
  17.5 0.0 collective-permute-done.3.other_ref
  17.5 0.1 shard_map.169
  17.7 0.0 collective-permute-start.4
  17.7 0.6 %collective-permute-start.5 = (f32[8,512]{1,0:T(8,128)S(1)}, f32[8,512]{1,0:T(8,128)S(1)}, u32[]{:S(2)}, u32[]{:S(2)}) collective-permute-start(f32[8,512]{1,0:T(8,128)S(1)} %get-tuple-element.58.own_ref), channel_id=1, source_target_pairs={{0,12},{4,8},{8,4},{12,0},{1,13},{5,9},{9,5},{13,1},{2,14},{6,10},... | collective-permute-start | bytes 49160 | tf_op jit(solution)/shard_map/ppermute | solution.py:694
  18.3 1.5 %collective-permute-start.6 = (f32[8,128]{1,0:T(8,128)S(1)}, f32[8,128]{1,0:T(8,128)S(1)}, u32[]{:S(2)}, u32[]{:S(2)}) collective-permute-start(f32[8,128]{1,0:T(8,128)S(1)} %get-tuple-element.59.rest_0_), channel_id=1, source_target_pairs={{0,8},{4,12},{8,0},{12,4},{1,9},{5,13},{9,1},{13,5},{2,10},{6,14},... | collective-permute-start | bytes 12296 | tf_op jit(solution)/shard_map/ppermute | solution.py:694
  21.1 0.8 %collective-permute-done.6.rest_1_ = f32[8,128]{1,0:T(8,128)S(1)} collective-permute-done((f32[8,128]{1,0:T(8,128)S(1)}, f32[8,128]{1,0:T(8,128)S(1)}, u32[]{:S(2)}, u32[]{:S(2)}) %collective-permute-start.6) | collective-permute-done | bytes 4128 | tf_op jit(solution)/shard_map/ppermute | solution.py:694
  21.9 0.0 collective-permute-done.4.near_ref
  21.9 0.0 collective-permute-done.5.far_ref
  21.9 0.0 copy-done.1
  21.9 6.2 %shard_map.170 = (f32[1,40,128]{2,1,0:T(8,128)S(1)}, f32[3,128]{1,0:T(4,128)S(1)}) custom-call(f32[1]{0:T(128)S(6)} %copy.19.dt_ref, s32[1,2]{1,0:T(1,128)S(1)} %bitcast.10, s32[1]{0:T(128)S(6)} %copy.20.climb_ref, f32[40,512]{1,0:T(8,128)S(1)} %get-tuple-element.45.pl_ref, f32[112,512]{1,0:T(8,128)S(1)} %copy-done, f32[40,512]{1,0:T(8,128)S(1)} %get-tuple-element.46.pr_ref, ...), custom_call_target="tpu_custom_call" | custom-call | flops 1000000000 | bytes 262144 | tf_op jit(solution)/shard_map/pallas_call | solution.py:682
  28.1 4.5 %collective-permute-start.7 = (f32[1,40,128]{2,1,0:T(8,128)S(1)}, f32[1,40,128]{2,1,0:T(8,128)S(1)}, u32[]{:S(2)}, u32[]{:S(2)}) collective-permute-start(f32[1,40,128]{2,1,0:T(8,128)S(1)} %get-tuple-element.60.refs_0_.own_ref), channel_id=1, source_target_pairs={{0,1},{1,0},{2,3},{3,2},{4,5},{5,4},{6,7},{7,6},{8,9},{9,8},{10,11... | collective-permute-start | bytes 61448 | tf_op jit(solution)/shard_map/ppermute | solution.py:694
  32.6 0.0 collective-permute-start.8
  32.6 2.4 %collective-permute-start.9 = (f32[1,40,128]{2,1,0:T(8,128)S(1)}, f32[1,40,128]{2,1,0:T(8,128)S(1)}, u32[]{:S(2)}, u32[]{:S(2)}) collective-permute-start(f32[1,40,128]{2,1,0:T(8,128)S(1)} %get-tuple-element.60.refs_0_.own_ref), channel_id=1, source_target_pairs={{0,3},{1,2},{2,1},{3,0},{4,7},{5,6},{6,5},{7,4},{8,11},{9,10},{10,... | collective-permute-start | bytes 61448 | tf_op jit(solution)/shard_map/ppermute | solution.py:694
  35.0 0.0 collective-permute-done.7.refs_1_
  35.0 2.2 %collective-permute-done.8.refs_2_ = f32[1,40,128]{2,1,0:T(8,128)S(1)} collective-permute-done((f32[1,40,128]{2,1,0:T(8,128)S(1)}, f32[1,40,128]{2,1,0:T(8,128)S(1)}, u32[]{:S(2)}, u32[]{:S(2)}) %collective-permute-start.8) | collective-permute-done | bytes 20512 | tf_op jit(solution)/shard_map/ppermute | solution.py:694
  37.3 0.9 %collective-permute-done.9.refs_3_ = f32[1,40,128]{2,1,0:T(8,128)S(1)} collective-permute-done((f32[1,40,128]{2,1,0:T(8,128)S(1)}, f32[1,40,128]{2,1,0:T(8,128)S(1)}, u32[]{:S(2)}, u32[]{:S(2)}) %collective-permute-start.9) | collective-permute-done | bytes 20512 | tf_op jit(solution)/shard_map/ppermute | solution.py:694
  38.2 0.2 shard_map.171
  38.4 1.6 %collective-permute-start.10 = (f32[8,128]{1,0:T(8,128)S(1)}, f32[8,128]{1,0:T(8,128)S(1)}, u32[]{:S(2)}, u32[]{:S(2)}) collective-permute-start(f32[8,128]{1,0:T(8,128)S(1)} %get-tuple-element.63.rest_0_), channel_id=1, source_target_pairs={{0,8},{4,12},{8,0},{12,4},{1,9},{5,13},{9,1},{13,5},{2,10},{6,14},... | collective-permute-start | bytes 12296 | tf_op jit(solution)/shard_map/ppermute | solution.py:694
  40.0 0.0 collective-permute-start.11
  40.0 0.6 %collective-permute-start.12 = (f32[8,128]{1,0:T(8,128)S(1)}, f32[8,128]{1,0:T(8,128)S(1)}, u32[]{:S(2)}, u32[]{:S(2)}) collective-permute-start(f32[8,128]{1,0:T(8,128)S(1)} %get-tuple-element.63.rest_0_), channel_id=1, source_target_pairs={{0,4},{4,0},{8,12},{12,8},{1,5},{5,1},{9,13},{13,9},{2,6},{6,2},{1... | collective-permute-start | bytes 12296 | tf_op jit(solution)/shard_map/ppermute | solution.py:694
  40.6 1.5 %collective-permute-done.10.rest_1_ = f32[8,128]{1,0:T(8,128)S(1)} collective-permute-done((f32[8,128]{1,0:T(8,128)S(1)}, f32[8,128]{1,0:T(8,128)S(1)}, u32[]{:S(2)}, u32[]{:S(2)}) %collective-permute-start.10) | collective-permute-done | bytes 4128 | tf_op jit(solution)/shard_map/ppermute | solution.py:694
  42.1 0.9 %collective-permute-done.11.rest_2_ = f32[8,128]{1,0:T(8,128)S(1)} collective-permute-done((f32[8,128]{1,0:T(8,128)S(1)}, f32[8,128]{1,0:T(8,128)S(1)}, u32[]{:S(2)}, u32[]{:S(2)}) %collective-permute-start.11) | collective-permute-done | bytes 4128 | tf_op jit(solution)/shard_map/ppermute | solution.py:694
  43.0 0.0 collective-permute-done.12.rest_3_
  43.0 0.7 %shard_map.172 = (f32[3,1,512]{2,1,0:T(1,128)}, f32[3,1,512]{2,1,0:T(1,128)}, f32[2,1,2]{2,1,0:T(1,128)}, f32[1,1]{1,0:T(1,128)}) custom-call(f32[1,40,128]{2,1,0:T(8,128)S(1)} %get-tuple-element.60.refs_0_.own_ref, f32[3,128]{1,0:T(4,128)S(1)} %get-tuple-element.61.record_ref, f32[40,128]{1,0:T(8,128)S(1)} %get-tuple-element.62.state_ref, ...), custom_call_target="tpu_custom_call" | custom-call | bytes 262144 | tf_op jit(solution)/shard_map/pallas_call | solution.py:682
Async XLA Ops:
  2.5 7.6 %collective-permute-start = (f32[40,512]{1,0:T(8,128)}, f32[40,512]{1,0:T(8,128)S(1)}, u32[]{:S(2)}, u32[]{:S(2)}) collective-permute-start(f32[40,512]{1,0:T(8,128)} %get-tuple-element.38), channel_id=1, source_target_pairs={{0,4},{4,0},{8,12},{12,8},{1,5},{5,1},{9,13},{13,9},{2,6},{6,2},{1... | collective-permute-start | bytes 245768 | tf_op jit(solution)/shard_map/ppermute | solution.py:694
  3.0 7.1 %collective-permute-start.1 = (f32[40,512]{1,0:T(8,128)}, f32[40,512]{1,0:T(8,128)S(1)}, u32[]{:S(2)}, u32[]{:S(2)}) collective-permute-start(f32[40,512]{1,0:T(8,128)} %get-tuple-element.38), channel_id=1, source_target_pairs={{0,12},{4,8},{8,4},{12,0},{1,13},{5,9},{9,5},{13,1},{2,14},{6,10},... | collective-permute-start | bytes 245768 | tf_op jit(solution)/shard_map/ppermute | solution.py:694
  5.7 0.9 %copy-start = (f32[112,512]{1,0:T(8,128)S(1)}, f32[112,512]{1,0:T(8,128)}, u32[]{:S(2)}) copy-start(f32[112,512]{1,0:T(8,128)} %get-tuple-element.36.po_ref) | copy-start | bytes 688132
  8.5 9.0 %collective-permute-start.2 = (f32[3,1,512]{2,1,0:T(1,128)S(1)}, f32[3,1,512]{2,1,0:T(1,128)S(1)}, u32[]{:S(2)}, u32[]{:S(2)}) collective-permute-start(f32[3,1,512]{2,1,0:T(1,128)S(1)} %get-tuple-element.37.x_ref), channel_id=1, source_target_pairs={{0,1},{1,0},{2,3},{3,2},{4,5},{5,4},{6,7},{7,6},{8,9},{9,8},{10,11... | collective-permute-start | bytes 18440 | tf_op jit(solution)/shard_map/ppermute | solution.py:694
  11.6 5.9 %collective-permute-start.3 = (f32[3,1,512]{2,1,0:T(1,128)S(1)}, f32[3,1,512]{2,1,0:T(1,128)S(1)}, u32[]{:S(2)}, u32[]{:S(2)}) collective-permute-start(f32[3,1,512]{2,1,0:T(1,128)S(1)} %get-tuple-element.57), channel_id=1, source_target_pairs={{0,0},{1,2},{2,1},{3,3},{4,4},{5,6},{6,5},{7,7},{8,8},{9,10},{10,9... | collective-permute-start | bytes 18440 | tf_op jit(solution)/shard_map/ppermute | solution.py:694
  12.5 9.5 %copy-start.1 = (s32[2,1]{0,1:T(1,128)S(1)}, s32[2,1]{0,1:T(1,128)}, u32[]{:S(2)}) copy-start(s32[2,1]{0,1:T(1,128)} %param.17) | copy-start | bytes 28
  17.7 4.3 %collective-permute-start.4 = (f32[8,512]{1,0:T(8,128)S(1)}, f32[8,512]{1,0:T(8,128)S(1)}, u32[]{:S(2)}, u32[]{:S(2)}) collective-permute-start(f32[8,512]{1,0:T(8,128)S(1)} %get-tuple-element.58.own_ref), channel_id=1, source_target_pairs={{0,4},{4,0},{8,12},{12,8},{1,5},{5,1},{9,13},{13,9},{2,6},{6,2},{1... | collective-permute-start | bytes 49160 | tf_op jit(solution)/shard_map/ppermute | solution.py:694
  17.7 4.3 %collective-permute-start.5 = (f32[8,512]{1,0:T(8,128)S(1)}, f32[8,512]{1,0:T(8,128)S(1)}, u32[]{:S(2)}, u32[]{:S(2)}) collective-permute-start(f32[8,512]{1,0:T(8,128)S(1)} %get-tuple-element.58.own_ref), channel_id=1, source_target_pairs={{0,12},{4,8},{8,4},{12,0},{1,13},{5,9},{9,5},{13,1},{2,14},{6,10},... | collective-permute-start | bytes 49160 | tf_op jit(solution)/shard_map/ppermute | solution.py:694
  18.3 3.6 %collective-permute-start.6 = (f32[8,128]{1,0:T(8,128)S(1)}, f32[8,128]{1,0:T(8,128)S(1)}, u32[]{:S(2)}, u32[]{:S(2)}) collective-permute-start(f32[8,128]{1,0:T(8,128)S(1)} %get-tuple-element.59.rest_0_), channel_id=1, source_target_pairs={{0,8},{4,12},{8,0},{12,4},{1,9},{5,13},{9,1},{13,5},{2,10},{6,14},... | collective-permute-start | bytes 12296 | tf_op jit(solution)/shard_map/ppermute | solution.py:694
  28.1 6.9 %collective-permute-start.7 = (f32[1,40,128]{2,1,0:T(8,128)S(1)}, f32[1,40,128]{2,1,0:T(8,128)S(1)}, u32[]{:S(2)}, u32[]{:S(2)}) collective-permute-start(f32[1,40,128]{2,1,0:T(8,128)S(1)} %get-tuple-element.60.refs_0_.own_ref), channel_id=1, source_target_pairs={{0,1},{1,0},{2,3},{3,2},{4,5},{5,4},{6,7},{7,6},{8,9},{9,8},{10,11... | collective-permute-start | bytes 61448 | tf_op jit(solution)/shard_map/ppermute | solution.py:694
  32.6 4.7 %collective-permute-start.8 = (f32[1,40,128]{2,1,0:T(8,128)S(1)}, f32[1,40,128]{2,1,0:T(8,128)S(1)}, u32[]{:S(2)}, u32[]{:S(2)}) collective-permute-start(f32[1,40,128]{2,1,0:T(8,128)S(1)} %get-tuple-element.60.refs_0_.own_ref), channel_id=1, source_target_pairs={{0,2},{1,3},{2,0},{3,1},{4,6},{5,7},{6,4},{7,5},{8,10},{9,11},{10,... | collective-permute-start | bytes 61448 | tf_op jit(solution)/shard_map/ppermute | solution.py:694
  32.6 5.6 %collective-permute-start.9 = (f32[1,40,128]{2,1,0:T(8,128)S(1)}, f32[1,40,128]{2,1,0:T(8,128)S(1)}, u32[]{:S(2)}, u32[]{:S(2)}) collective-permute-start(f32[1,40,128]{2,1,0:T(8,128)S(1)} %get-tuple-element.60.refs_0_.own_ref), channel_id=1, source_target_pairs={{0,3},{1,2},{2,1},{3,0},{4,7},{5,6},{6,5},{7,4},{8,11},{9,10},{10,... | collective-permute-start | bytes 61448 | tf_op jit(solution)/shard_map/ppermute | solution.py:694
  38.4 3.7 %collective-permute-start.10 = (f32[8,128]{1,0:T(8,128)S(1)}, f32[8,128]{1,0:T(8,128)S(1)}, u32[]{:S(2)}, u32[]{:S(2)}) collective-permute-start(f32[8,128]{1,0:T(8,128)S(1)} %get-tuple-element.63.rest_0_), channel_id=1, source_target_pairs={{0,8},{4,12},{8,0},{12,4},{1,9},{5,13},{9,1},{13,5},{2,10},{6,14},... | collective-permute-start | bytes 12296 | tf_op jit(solution)/shard_map/ppermute | solution.py:694
  40.0 3.0 %collective-permute-start.11 = (f32[8,128]{1,0:T(8,128)S(1)}, f32[8,128]{1,0:T(8,128)S(1)}, u32[]{:S(2)}, u32[]{:S(2)}) collective-permute-start(f32[8,128]{1,0:T(8,128)S(1)} %get-tuple-element.63.rest_0_), channel_id=1, source_target_pairs={{0,12},{4,8},{8,4},{12,0},{1,13},{5,9},{9,5},{13,1},{2,14},{6,10},... | collective-permute-start | bytes 12296 | tf_op jit(solution)/shard_map/ppermute | solution.py:694
  40.0 3.0 %collective-permute-start.12 = (f32[8,128]{1,0:T(8,128)S(1)}, f32[8,128]{1,0:T(8,128)S(1)}, u32[]{:S(2)}, u32[]{:S(2)}) collective-permute-start(f32[8,128]{1,0:T(8,128)S(1)} %get-tuple-element.63.rest_0_), channel_id=1, source_target_pairs={{0,4},{4,0},{8,12},{12,8},{1,5},{5,1},{9,13},{13,9},{2,6},{6,2},{1... | collective-permute-start | bytes 12296 | tf_op jit(solution)/shard_map/ppermute | solution.py:694

commit v8 on v7

--- a/solution.py
+++ b/solution.py
@@ -122,7 +122,8 @@
     l2_ref[...] = left_stack(turned(folded)).astype(BF16)
     high, low = split(turned(second))
     l3_ref[...] = jnp.concatenate([high, high, low, jnp.zeros_like(high)], axis=1).astype(BF16)
-    l5_ref[...] = left_stack(folded).astype(BF16)
+    high, low = split(folded)
+    l5_ref[...] = jnp.concatenate([high, high, high, high, low, low], axis=1).astype(BF16)
     l6_ref[...] = left_stack(first).astype(BF16)
     wide = (CHANNELS, LANES)
     col_ref[0] = jnp.broadcast_to(jnp.sum(mix_t * base0, axis=1, keepdims=True), wide)
@@ -253,17 +254,28 @@
         slope[:, cols] = steep
 
 
-def force_parts(weights, own_hot, side_hot, kept, dg, pulls, acc):
+def force_parts(weights, own_hot, side_hot, kept, dg, pulls, met, acc):
     l1, l2, l3, l5, l6, col = weights
     (widx, kinds, geo, bst, bps, bpr, sent_all, slope) = kept
     slot = lax.broadcasted_iota(jnp.int32, (SLOTS, LANES), 0)
 
-    def spread(left, b, first, last):
+    def spread(left, b, first, last, held):
         ws = reach(b, first, last)
         if b in SIDE_START:
             start = SIDE_START[b] + (ws[0] - reach(b, 3, 8)[0]) * LANES
-            return ws, mm_nt(left, side_hot[start : start + len(ws) * LANES, :])
-        return ws, mm_nt(left, own_hot[b - 4, ws[0] * LANES : (ws[-1] + 1) * LANES, :])
+            picked = side_hot[start : start + len(ws) * LANES, :]
+        else:
+            picked = own_hot[b - 4, ws[0] * LANES : (ws[-1] + 1) * LANES, :]
+        out = mm_nt(picked, left)
+        for i, w in enumerate(ws):
+            target = b - 1 + w
+            piece = out[i * LANES : (i + 1) * LANES]
+            rows = slice((target - first) * LANES, (target - first + 1) * LANES)
+            if (id(held), target) in started:
+                held[rows, :] += piece
+            else:
+                held[rows, :] = piece
+                started.add((id(held), target))
 
     started = set()
 
@@ -286,17 +298,7 @@
             message = message + radial[:, cols] * got[:, cols]
         _, steep = silu_parts(message)
         back = jnp.concatenate([col[3] * steep] * SLOTS, axis=1)
-        ws, out = spread(pair_stack(radial * back), b, 3, 8)
-        out = out[:CHANNELS] + out[CHANNELS:]
-        for i, w in enumerate(ws):
-            target = b - 1 + w
-            piece = out[:, i * LANES : (i + 1) * LANES]
-            where = slice(target * LANES, (target + 1) * LANES)
-            if target in started:
-                dg[:, where] += piece
-            else:
-                dg[:, where] = piece
-                started.add(target)
+        spread(pair_stack(radial * back), b, 3, 8, dg)
         if 3 <= b <= 8:
             basis = bps[b]
             steepness = mm(l3[...], jnp.concatenate([basis, basis], axis=0))
@@ -308,15 +310,6 @@
 
     for b in range(2, 10):
         gather_and_return(b)
-
-    begun = set()
-
-    def put(b, c, value):
-        if (b, c) in begun:
-            acc[b, c] += value
-        else:
-            acc[b, c] = value
-            begun.add((b, c))
 
     def finish(b, sums):
         kind = kinds[b]
@@ -330,31 +323,31 @@
         for c in range(3):
             value = pull * geo[b, c]
             if 4 <= b <= 7:
-                put(b, c, -value)
+                acc[b - 4, c] = jnp.sum(value, axis=0, keepdims=True)
             pieces.append(split(value))
         lines = []
         for h in range(2):
             for c in range(3):
                 lines.append(jnp.concatenate([jnp.where(slot == k, pieces[c][h], 0.0) for k in range(SLOTS)], axis=1))
-        ws, out = spread(jnp.concatenate(lines, axis=0).astype(BF16), b, 4, 7)
-        for c in range(3):
-            both = out[8 * c : 8 * c + 8] + out[24 + 8 * c : 32 + 8 * c]
-            for i, w in enumerate(ws):
-                put(b - 1 + w, c, both[:, i * LANES : (i + 1) * LANES])
+        spread(jnp.concatenate(lines, axis=0).astype(BF16), b, 4, 7, met)
 
     for b in range(3, 9, 2):
         cols = slice(b * LANES, (b + 2) * LANES)
-        steep = mm(l5[...], right_stack(dg[:, cols]))
+        high, low = split(dg[(b - 3) * LANES : (b - 1) * LANES, :])
+        steep = mm_nt(l5[...], jnp.concatenate([high, low, high], axis=1).astype(BF16))
         steep = steep + jnp.concatenate([col[2], col[2]], axis=1)
         sums = mm(l6[...], right_stack(steep * slope[:, cols]))
         for i in range(2):
             finish(b + i, sums[:, i * LANES : (i + 1) * LANES])
 
-
-def own_force(acc, c):
-    return jnp.concatenate(
-        [-jnp.sum(acc[4 + i, c], axis=0, keepdims=True) for i in range(SLAB_BLOCKS)], axis=1
-    )
+    high, low = split(met[...])
+    column = lax.broadcasted_iota(jnp.int32, (16, 6 * SLOTS), 1)
+    column = jnp.where(column < 3 * SLOTS, column, column - 3 * SLOTS)
+    first = SLOTS * lax.broadcasted_iota(jnp.int32, (16, 6 * SLOTS), 0)
+    choose = jnp.where((column >= first) & (column < first + SLOTS), 1.0, 0.0).astype(BF16)
+    back = mm_nt(choose, high.astype(BF16)) + mm_nt(choose, low.astype(BF16))
+    away = [jnp.concatenate([acc[i, c] for i in range(SLAB_BLOCKS)], axis=1) for c in range(3)]
+    return jnp.concatenate(away, axis=0) - back[0:3]
 
 
 def fill_region(xs, packs, rows_of):
@@ -394,9 +387,10 @@
 
 def back_scratch():
     return [
-        pltpu.VMEM((CHANNELS, 12 * LANES), F32),
+        pltpu.VMEM((6 * LANES, 2 * CHANNELS), F32),
         pltpu.VMEM((12, 8, SLOTS * LANES), F32),
-        pltpu.VMEM((12, 3, 8, LANES), F32),
+        pltpu.VMEM((SLAB_BLOCKS * LANES, 6 * SLOTS), F32),
+        pltpu.VMEM((SLAB_BLOCKS, 3, 1, LANES), F32),
     ]
 
 
@@ -417,9 +411,7 @@
 
 def first_back_kernel(own_hot, side_hot, *rest):
     weights, kept, out_ref, scr = rest[:6], rest[6:14], rest[14], rest[15:]
-    force_parts(weights, own_hot, side_hot, kept, *scr)
-    for c in range(3):
-        out_ref[c : c + 1, :] = own_force(scr[-1], c)
+    out_ref[...] = force_parts(weights, own_hot, side_hot, kept, *scr)
 
 
 def rows_of(ref):
@@ -431,15 +423,13 @@
     return jnp.concatenate(values, axis=1)
 
 
-def blend_kernel(images, force_ref, po_ref, pair_ref, other_ref, out_ref, sums_ref):
+def blend_kernel(images, force_ref, po_ref, before_ref, after_ref, out_ref, sums_ref):
     x = po_ref[ROW_X : ROW_X + 3, :]
     v = po_ref[ROW_V : ROW_V + 3, :]
     force = force_ref[...]
     here = lax.axis_index("img")
-    pair, other = rows_of(pair_ref), rows_of(other_ref)
-    even = here % 2 == 0
-    before = jnp.where(here > 0, jnp.where(even, other, pair), 0.0)
-    after = jnp.where(here < images - 1, jnp.where(even, pair, other), 0.0)
+    before = jnp.where(here > 0, rows_of(before_ref), 0.0)
+    after = jnp.where(here < images - 1, rows_of(after_ref), 0.0)
     tangent = after - before
     plus = after - x
     minus = x - before
@@ -496,7 +486,13 @@
     out_ref[count : 2 * count] = b_ref[...]
 
 
-def second_kernel(images, domains, dt_ref, flag_ref, climb_ref, pl_ref, po_ref, pr_ref, own_ref, near_ref, far_ref, *rest):
+def number_kernel(dt_ref, flag_ref, climb_ref, out_ref):
+    flags = [flag_ref[0, s].astype(F32) for s in range(flag_ref.shape[1])]
+    for i, value in enumerate([dt_ref[0], climb_ref[0].astype(F32)] + flags):
+        out_ref[i : i + 1, :] = jnp.full((1, LANES), value, F32)
+
+
+def second_kernel(images, domains, number_ref, pl_ref, po_ref, pr_ref, own_ref, near_ref, far_ref, *rest):
     count = 2 if domains == 4 else 1
     parts, rest = rest[:count], rest[count:]
     (own_hot, side_hot), weights, (out_ref, record_ref), scr = rest[:2], rest[2:8], rest[8:10], rest[10:]
@@ -520,10 +516,10 @@
         pp,
         mn,
         vv,
-        jnp.full(shape, dt_ref[0], F32),
+        number_ref[0:1, :],
         jnp.full(shape, ALPHA_START, F32),
-        jnp.full(shape, flag_ref[0, 0], jnp.int32) == 1,
-        jnp.full(shape, here - climb_ref[0], jnp.int32) == 0,
+        number_ref[2:3, :] == 1.0,
+        number_ref[1:2, :] == jnp.full(shape, here, jnp.int32).astype(F32),
         jnp.full(shape, jnp.where((here >= 1) & (here <= images - 2), 1, 0), jnp.int32) == 1,
     )
     messages = [beside[0], own_ref[0:6, :], beside[1]]
@@ -539,21 +535,20 @@
     xs, sst, kept = scr[0], scr[1], scr[2:10]
     fill_region(xs, packs, lambda s: moved[s])
     forward_parts(packs, weights, xs, sst, kept)
-    force_parts(weights, own_hot, side_hot, kept, *scr[10:])
+    force = force_parts(weights, own_hot, side_hot, kept, *scr[10:])
     for c in range(3):
-        force = own_force(scr[-1], c)
         for i in range(SLAB_BLOCKS):
             lanes = slice(i * LANES, (i + 1) * LANES)
             row = 4 * c + i
             out_ref[0, row : row + 1, :] = speeds[1][c : c + 1, lanes]
-            out_ref[0, 12 + row : 13 + row, :] = force[:, lanes]
+            out_ref[0, 12 + row : 13 + row, :] = force[c : c + 1, lanes]
             out_ref[0, 24 + row : 25 + row, :] = moved[1][c : c + 1, lanes]
     out_ref[0, 36:37, :] = dt
     out_ref[0, 37:38, :] = alpha
-    out_ref[0, 38:40, :] = jnp.full((2, LANES), flag_ref[0, 1], jnp.int32).astype(F32)
+    out_ref[0, 38:40, :] = jnp.broadcast_to(number_ref[3:4, :], (2, LANES))
     record_ref[0:1, :] = along
     record_ref[1:2, :] = spring
-    record_ref[2:3, :] = jnp.full(shape, climb_ref[0], jnp.int32).astype(F32)
+    record_ref[2:3, :] = number_ref[1:2, :]
 
 
 PRODUCTS = (
@@ -763,7 +758,7 @@
             shape((CHANNELS, 48), BF16),
             shape((CHANNELS, 192), BF16),
             shape((CHANNELS, 32), BF16),
-            shape((CHANNELS, 192), BF16),
+            shape((CHANNELS, 3 * LANES), BF16),
             shape((16, 192), BF16),
             shape((4, CHANNELS, LANES), F32),
             shape(x.shape, F32),
@@ -772,7 +767,7 @@
         (pack,),
         flops=100000000,
     )
-    pair = swap(x_copy, "img", lambda i: i ^ 1)
+    before = swap(x_copy, "img", lambda i: (i + 1) % images)
     left, right, side_hot, x_copy, *kept = call(
         first_kernel,
         (
@@ -787,7 +782,7 @@
         forward_scratch(),
         flops=1000000000,
     )
-    other = swap(x_copy, "img", lambda i: i if i in (0, images - 1) else i + 2 * (i % 2) - 1)
+    after = swap(x_copy, "img", lambda i: (i - 1) % images)
     force = call(
         first_back_kernel,
         shape((3, atoms), F32),
@@ -800,7 +795,7 @@
         functools.partial(blend_kernel, images),
         (shape((8, atoms), F32), shape((8, LANES), F32)),
         (),
-        (force, pack, pair, other),
+        (force, pack, before, after),
     )
     far = swap(message, "dom", lambda i: (i + 2 * (i % 2) - 1) % domains)
     if domains == 4:
@@ -808,11 +803,12 @@
     else:
         parts = exchanged(sums, "dom")
     near = swap(message, "dom", lambda i: i ^ 1)
+    numbers = call(number_kernel, shape((8, LANES), F32), (time_step, jnp.transpose(reset_flags), climb), ())
     state, record = call(
         functools.partial(second_kernel, images, domains),
         (shape((1, 40, LANES), F32), shape((3, LANES), F32)),
-        (time_step, jnp.transpose(reset_flags), climb),
-        (left, pack, right, message, near, far, *parts, own_hot, side_hot, *weights),
+        (),
+        (numbers, left, pack, right, message, near, far, *parts, own_hot, side_hot, *weights),
         forward_scratch() + [pltpu.VMEM(*one) for one in kept_shapes()] + back_scratch(),
         flops=1000000000,
     )

time: 44 us -> 43.2 us (0.982)
  starting transfers between devices: 16.8 us -> 16 us
    ppermute x13, starting transfers between devices: 16.8 us -> 16 us  [swap(): lax.ppermute(array, axis, [(i, partner(i)) for i in range(lax.axis_size(a...]
    pallas_call x8 -> x9, Pallas kernels: 17.6 us -> 17.8 us  [call(): pl.pallas_call(body, out_shape=outs, in_specs=[SMEM_SPEC] * len(scalars)...]
    unnamed x4 -> x6, local copies, waits for them, and re-layouts: 0.94 us -> 0.95 us
  transfers between devices with their start and end apart: 13 -> 13, of which waited for: 5 -> 5; matrix products, arithmetic and copies ran while one was open for 0% -> 0% of each run, Pallas kernels for 19% -> 21%
where the time goes in v8:
time: 43.2 us; the launch traced here: 42.9 us
  Pallas kernels  17.8 us (41%)
  starting transfers between devices  16 us (37%)
  waiting for transfers between devices  6.21 us (14%)
  between operations  2.02 us (5%)
  local copies, waits for them, and re-layouts  0.95 us (2%)
    pallas_call x9, Pallas kernels, call(): pl.pallas_call(body, out_shape=outs, in_specs=[SMEM_SPEC] * len(scalars)...  17.8 us
    ppermute x13, starting transfers between devices, swap(): lax.ppermute(array, axis, [(i, partner(i)) for i in range(lax.axis_size(a...  16 us
    ppermute x13, waiting for transfers between devices, swap(): lax.ppermute(array, axis, [(i, partner(i)) for i in range(lax.axis_size(a...  6.21 us
    unnamed x6, local copies, waits for them, and re-layouts  0.95 us
  transfers between devices with their start and end apart: 13, of which 5 were waited for; matrix products, arithmetic and copies ran while one was open for 0% of the time, Pallas kernels for 21%

profile of v8, /device:TPU:0, one launch (start us, length us, event | category | flops | bytes accessed | tf_op | source)
XLA Modules:
  0.0 42.9 jit_solution(13234140134883330542)
XLA Ops:
  0.6 1.9 %shard_map.166 = (f32[40,512]{1,0:T(8,128)}, f32[112,512]{1,0:T(8,128)}) custom-call(f32[3,1,512]{2,1,0:T(1,128)} %bitcast.12, f32[3,1,512]{2,1,0:T(1,128)} %bitcast.13, s32[512]{0:T(512)} %refs_2_.1, s32[8,512]{1,0:T(8,128)} %refs_3_.1, s32[512]{0:T(512)} %refs_4_.1, f32[2,64]{1,0:T(2,128)} %refs_5_.1, f32[64]{0:T(128)} %refs_6_.1, f32[2,8,64]{2,1,0:T(8,128)} %refs_7_.1, ...), custom_call_target="tpu_custom_call" | custom-call | bytes 262144 | tf_op jit(solution)/shard_map/pallas_call | solution.py:677
  2.5 0.5 %collective-permute-start = (f32[40,512]{1,0:T(8,128)}, f32[40,512]{1,0:T(8,128)S(1)}, u32[]{:S(2)}, u32[]{:S(2)}) collective-permute-start(f32[40,512]{1,0:T(8,128)} %get-tuple-element.38), channel_id=1, source_target_pairs={{0,4},{4,0},{8,12},{12,8},{1,5},{5,1},{9,13},{13,9},{2,6},{6,2},{1... | collective-permute-start | bytes 245768 | tf_op jit(solution)/shard_map/ppermute | solution.py:689
  3.0 2.6 %collective-permute-start.1 = (f32[40,512]{1,0:T(8,128)}, f32[40,512]{1,0:T(8,128)S(1)}, u32[]{:S(2)}, u32[]{:S(2)}) collective-permute-start(f32[40,512]{1,0:T(8,128)} %get-tuple-element.38), channel_id=1, source_target_pairs={{0,12},{4,8},{8,4},{12,0},{1,13},{5,9},{9,5},{13,1},{2,14},{6,10},... | collective-permute-start | bytes 245768 | tf_op jit(solution)/shard_map/ppermute | solution.py:689
  5.7 0.0 copy-start
  5.7 0.9 %copy-done = f32[112,512]{1,0:T(8,128)S(1)} copy-done((f32[112,512]{1,0:T(8,128)S(1)}, f32[112,512]{1,0:T(8,128)}, u32[]{:S(2)}) %copy-start) | copy-done | bytes 229400
  6.6 1.9 %shard_map.167 = (bf16[4,384,1024]{2,1,0:T(8,128)(2,1)S(1)}, bf16[64,48]{1,0:T(8,128)(2,1)S(1)}, bf16[64,192]{1,0:T(8,128)(2,1)S(1)}, bf16[64,32]{1,0:T(8,128)(2...) custom-call(f32[112,512]{1,0:T(8,128)S(1)} %copy-done), custom_call_target="tpu_custom_call" | custom-call | flops 100000000 | bytes 262144 | tf_op jit(solution)/shard_map/pallas_call | solution.py:677
  8.5 1.6 %collective-permute-start.2 = (f32[3,1,512]{2,1,0:T(1,128)S(1)}, f32[3,1,512]{2,1,0:T(1,128)S(1)}, u32[]{:S(2)}, u32[]{:S(2)}) collective-permute-start(f32[3,1,512]{2,1,0:T(1,128)S(1)} %get-tuple-element.37.x_ref), channel_id=1, source_target_pairs={{0,1},{1,2},{2,3},{3,0},{4,5},{5,6},{6,7},{7,4},{8,9},{9,10},{10,1... | collective-permute-start | bytes 18440 | tf_op jit(solution)/shard_map/ppermute | solution.py:689
  10.1 0.0 collective-permute-done.sibling_ref
  10.1 0.0 collective-permute-done.1.across_ref
  10.1 1.5 %shard_map.168 = (f32[40,512]{1,0:T(8,128)S(1)}, f32[40,512]{1,0:T(8,128)S(1)}, bf16[768,1024]{1,0:T(8,128)(2,1)S(1)}, f32[3,1,512]{2,1,0:T(1,128)S(1)}, s32[12,...) custom-call(f32[3,1,512]{2,1,0:T(1,128)S(1)} %get-tuple-element.37.x, ...), custom_call_target="tpu_custom_call" | custom-call | flops 1000000000 | bytes 262144 | tf_op jit(solution)/shard_map/pallas_call | solution.py:677
  11.6 2.5 %collective-permute-start.3 = (f32[3,1,512]{2,1,0:T(1,128)S(1)}, f32[3,1,512]{2,1,0:T(1,128)S(1)}, u32[]{:S(2)}, u32[]{:S(2)}) collective-permute-start(f32[3,1,512]{2,1,0:T(1,128)S(1)} %get-tuple-element.57), channel_id=1, source_target_pairs={{0,3},{1,0},{2,1},{3,2},{4,7},{5,4},{6,5},{7,6},{8,11},{9,8},{10,9... | collective-permute-start | bytes 18440 | tf_op jit(solution)/shard_map/ppermute | solution.py:689
  14.1 0.0 copy-start.2
  14.1 0.0 copy-start.1
  14.1 5.1 %shard_map.169.force_ref = f32[3,512]{1,0:T(4,128)S(1)} custom-call(bf16[4,384,1024]{2,1,0:T(8,128)(2,1)S(1)} %get-tuple-element.47.own_hot.rest_2_, bf16[768,1024]{1,0:T(8,128)(2,1)S(1)} %get-tuple-element.48.side_hot.rest_3_, bf16[64,48]{1,0:T(8,128)(2,1)S(1)} %get-tuple-element.39.rest_0_.rest_4_, bf16[64,192]{1,0:T(8,128)(2,1)S(1)} %get-tuple-element.40.rest_1_.rest_5_, ...), custom_call_target="tpu_custom_call" | custom-call | flops 1000000000 | bytes 262144 | tf_op jit(solution)/shard_map/pallas_call | solution.py:677
  19.2 0.0 collective-permute-done.2.before_ref
  19.2 0.0 collective-permute-done.3.after_ref
  19.2 0.1 shard_map.170
  19.4 0.0 collective-permute-start.4
  19.4 1.3 %collective-permute-start.5 = (f32[8,512]{1,0:T(8,128)S(1)}, f32[8,512]{1,0:T(8,128)S(1)}, u32[]{:S(2)}, u32[]{:S(2)}) collective-permute-start(f32[8,512]{1,0:T(8,128)S(1)} %get-tuple-element.58.own_ref), channel_id=1, source_target_pairs={{0,12},{4,8},{8,4},{12,0},{1,13},{5,9},{9,5},{13,1},{2,14},{6,10},... | collective-permute-start | bytes 49160 | tf_op jit(solution)/shard_map/ppermute | solution.py:689
  20.7 0.8 %collective-permute-start.6 = (f32[8,128]{1,0:T(8,128)S(1)}, f32[8,128]{1,0:T(8,128)S(1)}, u32[]{:S(2)}, u32[]{:S(2)}) collective-permute-start(f32[8,128]{1,0:T(8,128)S(1)} %get-tuple-element.59.rest_0_), channel_id=1, source_target_pairs={{0,8},{4,12},{8,0},{12,4},{1,9},{5,13},{9,1},{13,5},{2,10},{6,14},... | collective-permute-start | bytes 12296 | tf_op jit(solution)/shard_map/ppermute | solution.py:689
  22.8 0.0 copy-done.2
  22.8 0.5 %shard_map.165.number_ref = f32[8,128]{1,0:T(8,128)S(1)} custom-call(f32[1]{0:T(128)S(6)} %copy.19.dt_ref, s32[1,2]{1,0:T(1,128)S(1)} %bitcast.10, s32[1]{0:T(128)S(6)} %copy.20.climb_ref), custom_call_target="tpu_custom_call" | custom-call | bytes 262144 | tf_op jit(solution)/shard_map/pallas_call | solution.py:677
  23.4 0.9 %collective-permute-done.6.rest_1_ = f32[8,128]{1,0:T(8,128)S(1)} collective-permute-done((f32[8,128]{1,0:T(8,128)S(1)}, f32[8,128]{1,0:T(8,128)S(1)}, u32[]{:S(2)}, u32[]{:S(2)}) %collective-permute-start.6) | collective-permute-done | bytes 4128 | tf_op jit(solution)/shard_map/ppermute | solution.py:689
  24.3 0.0 collective-permute-done.4.near_ref
  24.3 0.0 collective-permute-done.5.far_ref
  24.3 0.0 copy-done.1
  24.3 5.8 %shard_map.171 = (f32[1,40,128]{2,1,0:T(8,128)S(1)}, f32[3,128]{1,0:T(4,128)S(1)}) custom-call(f32[8,128]{1,0:T(8,128)S(1)} %shard_map.165.number_ref, f32[40,512]{1,0:T(8,128)S(1)} %get-tuple-element.45.pl_ref, f32[112,512]{1,0:T(8,128)S(1)} %copy-done.1, f32[40,512]{1,0:T(8,128)S(1)} %get-tuple-element.46.pr_ref, f32[8,512]{1,0:T(8,128)S(1)} %get-tuple-element.58.own_ref, ...), custom_call_target="tpu_custom_call" | custom-call | flops 1000000000 | bytes 262144 | tf_op jit(solution)/shard_map/pallas_call | solution.py:677
  30.1 0.0 collective-permute-start.7
  30.1 1.7 %collective-permute-start.8 = (f32[1,40,128]{2,1,0:T(8,128)S(1)}, f32[1,40,128]{2,1,0:T(8,128)S(1)}, u32[]{:S(2)}, u32[]{:S(2)}) collective-permute-start(f32[1,40,128]{2,1,0:T(8,128)S(1)} %get-tuple-element.60.refs_0_.own_ref), channel_id=1, source_target_pairs={{0,2},{1,3},{2,0},{3,1},{4,6},{5,7},{6,4},{7,5},{8,10},{9,11},{10,... | collective-permute-start | bytes 61448 | tf_op jit(solution)/shard_map/ppermute | solution.py:689
  31.8 2.7 %collective-permute-start.9 = (f32[1,40,128]{2,1,0:T(8,128)S(1)}, f32[1,40,128]{2,1,0:T(8,128)S(1)}, u32[]{:S(2)}, u32[]{:S(2)}) collective-permute-start(f32[1,40,128]{2,1,0:T(8,128)S(1)} %get-tuple-element.60.refs_0_.own_ref), channel_id=1, source_target_pairs={{0,3},{1,2},{2,1},{3,0},{4,7},{5,6},{6,5},{7,4},{8,11},{9,10},{10,... | collective-permute-start | bytes 61448 | tf_op jit(solution)/shard_map/ppermute | solution.py:689
  34.5 0.0 collective-permute-done.7.refs_1_
  34.5 0.3 collective-permute-done.8.refs_2_
  34.8 2.6 %collective-permute-done.9.refs_3_ = f32[1,40,128]{2,1,0:T(8,128)S(1)} collective-permute-done((f32[1,40,128]{2,1,0:T(8,128)S(1)}, f32[1,40,128]{2,1,0:T(8,128)S(1)}, u32[]{:S(2)}, u32[]{:S(2)}) %collective-permute-start.9) | collective-permute-done | bytes 20512 | tf_op jit(solution)/shard_map/ppermute | solution.py:689
  37.4 0.2 shard_map.172
  37.6 1.6 %collective-permute-start.10 = (f32[8,128]{1,0:T(8,128)S(1)}, f32[8,128]{1,0:T(8,128)S(1)}, u32[]{:S(2)}, u32[]{:S(2)}) collective-permute-start(f32[8,128]{1,0:T(8,128)S(1)} %get-tuple-element.63.rest_0_), channel_id=1, source_target_pairs={{0,8},{4,12},{8,0},{12,4},{1,9},{5,13},{9,1},{13,5},{2,10},{6,14},... | collective-permute-start | bytes 12296 | tf_op jit(solution)/shard_map/ppermute | solution.py:689
  39.2 0.0 collective-permute-start.11
  39.2 0.6 %collective-permute-start.12 = (f32[8,128]{1,0:T(8,128)S(1)}, f32[8,128]{1,0:T(8,128)S(1)}, u32[]{:S(2)}, u32[]{:S(2)}) collective-permute-start(f32[8,128]{1,0:T(8,128)S(1)} %get-tuple-element.63.rest_0_), channel_id=1, source_target_pairs={{0,4},{4,0},{8,12},{12,8},{1,5},{5,1},{9,13},{13,9},{2,6},{6,2},{1... | collective-permute-start | bytes 12296 | tf_op jit(solution)/shard_map/ppermute | solution.py:689
  39.8 1.5 %collective-permute-done.10.rest_1_ = f32[8,128]{1,0:T(8,128)S(1)} collective-permute-done((f32[8,128]{1,0:T(8,128)S(1)}, f32[8,128]{1,0:T(8,128)S(1)}, u32[]{:S(2)}, u32[]{:S(2)}) %collective-permute-start.10) | collective-permute-done | bytes 4128 | tf_op jit(solution)/shard_map/ppermute | solution.py:689
  41.3 0.9 %collective-permute-done.11.rest_2_ = f32[8,128]{1,0:T(8,128)S(1)} collective-permute-done((f32[8,128]{1,0:T(8,128)S(1)}, f32[8,128]{1,0:T(8,128)S(1)}, u32[]{:S(2)}, u32[]{:S(2)}) %collective-permute-start.11) | collective-permute-done | bytes 4128 | tf_op jit(solution)/shard_map/ppermute | solution.py:689
  42.2 0.0 collective-permute-done.12.rest_3_
  42.2 0.7 %shard_map.173 = (f32[3,1,512]{2,1,0:T(1,128)}, f32[3,1,512]{2,1,0:T(1,128)}, f32[2,1,2]{2,1,0:T(1,128)}, f32[1,1]{1,0:T(1,128)}) custom-call(f32[1,40,128]{2,1,0:T(8,128)S(1)} %get-tuple-element.60.refs_0_.own_ref, f32[3,128]{1,0:T(4,128)S(1)} %get-tuple-element.61.record_ref, f32[40,128]{1,0:T(8,128)S(1)} %get-tuple-element.62.state_ref, ...), custom_call_target="tpu_custom_call" | custom-call | bytes 262144 | tf_op jit(solution)/shard_map/pallas_call | solution.py:677
Async XLA Ops:
  2.5 7.6 %collective-permute-start = (f32[40,512]{1,0:T(8,128)}, f32[40,512]{1,0:T(8,128)S(1)}, u32[]{:S(2)}, u32[]{:S(2)}) collective-permute-start(f32[40,512]{1,0:T(8,128)} %get-tuple-element.38), channel_id=1, source_target_pairs={{0,4},{4,0},{8,12},{12,8},{1,5},{5,1},{9,13},{13,9},{2,6},{6,2},{1... | collective-permute-start | bytes 245768 | tf_op jit(solution)/shard_map/ppermute | solution.py:689
  3.0 7.1 %collective-permute-start.1 = (f32[40,512]{1,0:T(8,128)}, f32[40,512]{1,0:T(8,128)S(1)}, u32[]{:S(2)}, u32[]{:S(2)}) collective-permute-start(f32[40,512]{1,0:T(8,128)} %get-tuple-element.38), channel_id=1, source_target_pairs={{0,12},{4,8},{8,4},{12,0},{1,13},{5,9},{9,5},{13,1},{2,14},{6,10},... | collective-permute-start | bytes 245768 | tf_op jit(solution)/shard_map/ppermute | solution.py:689
  5.7 0.9 %copy-start = (f32[112,512]{1,0:T(8,128)S(1)}, f32[112,512]{1,0:T(8,128)}, u32[]{:S(2)}) copy-start(f32[112,512]{1,0:T(8,128)} %get-tuple-element.36.po_ref) | copy-start | bytes 688132
  8.5 10.7 %collective-permute-start.2 = (f32[3,1,512]{2,1,0:T(1,128)S(1)}, f32[3,1,512]{2,1,0:T(1,128)S(1)}, u32[]{:S(2)}, u32[]{:S(2)}) collective-permute-start(f32[3,1,512]{2,1,0:T(1,128)S(1)} %get-tuple-element.37.x_ref), channel_id=1, source_target_pairs={{0,1},{1,2},{2,3},{3,0},{4,5},{5,6},{6,7},{7,4},{8,9},{9,10},{10,1... | collective-permute-start | bytes 18440 | tf_op jit(solution)/shard_map/ppermute | solution.py:689
  11.6 7.6 %collective-permute-start.3 = (f32[3,1,512]{2,1,0:T(1,128)S(1)}, f32[3,1,512]{2,1,0:T(1,128)S(1)}, u32[]{:S(2)}, u32[]{:S(2)}) collective-permute-start(f32[3,1,512]{2,1,0:T(1,128)S(1)} %get-tuple-element.57), channel_id=1, source_target_pairs={{0,3},{1,0},{2,1},{3,2},{4,7},{5,4},{6,5},{7,6},{8,11},{9,8},{10,9... | collective-permute-start | bytes 18440 | tf_op jit(solution)/shard_map/ppermute | solution.py:689
  14.1 8.7 %copy-start.2 = (s32[2,1]{0,1:T(1,128)S(1)}, s32[2,1]{0,1:T(1,128)}, u32[]{:S(2)}) copy-start(s32[2,1]{0,1:T(1,128)} %param.17) | copy-start | bytes 28
  14.1 10.3 %copy-start.1 = (f32[112,512]{1,0:T(8,128)S(1)}, f32[112,512]{1,0:T(8,128)}, u32[]{:S(2)}) copy-start(f32[112,512]{1,0:T(8,128)} %get-tuple-element.36.po_ref) | copy-start | bytes 688132
  19.4 5.0 %collective-permute-start.4 = (f32[8,512]{1,0:T(8,128)S(1)}, f32[8,512]{1,0:T(8,128)S(1)}, u32[]{:S(2)}, u32[]{:S(2)}) collective-permute-start(f32[8,512]{1,0:T(8,128)S(1)} %get-tuple-element.58.own_ref), channel_id=1, source_target_pairs={{0,4},{4,0},{8,12},{12,8},{1,5},{5,1},{9,13},{13,9},{2,6},{6,2},{1... | collective-permute-start | bytes 49160 | tf_op jit(solution)/shard_map/ppermute | solution.py:689
  19.4 5.0 %collective-permute-start.5 = (f32[8,512]{1,0:T(8,128)S(1)}, f32[8,512]{1,0:T(8,128)S(1)}, u32[]{:S(2)}, u32[]{:S(2)}) collective-permute-start(f32[8,512]{1,0:T(8,128)S(1)} %get-tuple-element.58.own_ref), channel_id=1, source_target_pairs={{0,12},{4,8},{8,4},{12,0},{1,13},{5,9},{9,5},{13,1},{2,14},{6,10},... | collective-permute-start | bytes 49160 | tf_op jit(solution)/shard_map/ppermute | solution.py:689
  20.7 3.6 %collective-permute-start.6 = (f32[8,128]{1,0:T(8,128)S(1)}, f32[8,128]{1,0:T(8,128)S(1)}, u32[]{:S(2)}, u32[]{:S(2)}) collective-permute-start(f32[8,128]{1,0:T(8,128)S(1)} %get-tuple-element.59.rest_0_), channel_id=1, source_target_pairs={{0,8},{4,12},{8,0},{12,4},{1,9},{5,13},{9,1},{13,5},{2,10},{6,14},... | collective-permute-start | bytes 12296 | tf_op jit(solution)/shard_map/ppermute | solution.py:689
  30.1 4.4 %collective-permute-start.7 = (f32[1,40,128]{2,1,0:T(8,128)S(1)}, f32[1,40,128]{2,1,0:T(8,128)S(1)}, u32[]{:S(2)}, u32[]{:S(2)}) collective-permute-start(f32[1,40,128]{2,1,0:T(8,128)S(1)} %get-tuple-element.60.refs_0_.own_ref), channel_id=1, source_target_pairs={{0,1},{1,0},{2,3},{3,2},{4,5},{5,4},{6,7},{7,6},{8,9},{9,8},{10,11... | collective-permute-start | bytes 61448 | tf_op jit(solution)/shard_map/ppermute | solution.py:689
  30.1 4.7 %collective-permute-start.8 = (f32[1,40,128]{2,1,0:T(8,128)S(1)}, f32[1,40,128]{2,1,0:T(8,128)S(1)}, u32[]{:S(2)}, u32[]{:S(2)}) collective-permute-start(f32[1,40,128]{2,1,0:T(8,128)S(1)} %get-tuple-element.60.refs_0_.own_ref), channel_id=1, source_target_pairs={{0,2},{1,3},{2,0},{3,1},{4,6},{5,7},{6,4},{7,5},{8,10},{9,11},{10,... | collective-permute-start | bytes 61448 | tf_op jit(solution)/shard_map/ppermute | solution.py:689
  31.8 5.6 %collective-permute-start.9 = (f32[1,40,128]{2,1,0:T(8,128)S(1)}, f32[1,40,128]{2,1,0:T(8,128)S(1)}, u32[]{:S(2)}, u32[]{:S(2)}) collective-permute-start(f32[1,40,128]{2,1,0:T(8,128)S(1)} %get-tuple-element.60.refs_0_.own_ref), channel_id=1, source_target_pairs={{0,3},{1,2},{2,1},{3,0},{4,7},{5,6},{6,5},{7,4},{8,11},{9,10},{10,... | collective-permute-start | bytes 61448 | tf_op jit(solution)/shard_map/ppermute | solution.py:689
  37.6 3.7 %collective-permute-start.10 = (f32[8,128]{1,0:T(8,128)S(1)}, f32[8,128]{1,0:T(8,128)S(1)}, u32[]{:S(2)}, u32[]{:S(2)}) collective-permute-start(f32[8,128]{1,0:T(8,128)S(1)} %get-tuple-element.63.rest_0_), channel_id=1, source_target_pairs={{0,8},{4,12},{8,0},{12,4},{1,9},{5,13},{9,1},{13,5},{2,10},{6,14},... | collective-permute-start | bytes 12296 | tf_op jit(solution)/shard_map/ppermute | solution.py:689
  39.2 3.0 %collective-permute-start.11 = (f32[8,128]{1,0:T(8,128)S(1)}, f32[8,128]{1,0:T(8,128)S(1)}, u32[]{:S(2)}, u32[]{:S(2)}) collective-permute-start(f32[8,128]{1,0:T(8,128)S(1)} %get-tuple-element.63.rest_0_), channel_id=1, source_target_pairs={{0,12},{4,8},{8,4},{12,0},{1,13},{5,9},{9,5},{13,1},{2,14},{6,10},... | collective-permute-start | bytes 12296 | tf_op jit(solution)/shard_map/ppermute | solution.py:689
  39.2 3.0 %collective-permute-start.12 = (f32[8,128]{1,0:T(8,128)S(1)}, f32[8,128]{1,0:T(8,128)S(1)}, u32[]{:S(2)}, u32[]{:S(2)}) collective-permute-start(f32[8,128]{1,0:T(8,128)S(1)} %get-tuple-element.63.rest_0_), channel_id=1, source_target_pairs={{0,4},{4,0},{8,12},{12,8},{1,5},{5,1},{9,13},{13,9},{2,6},{6,2},{1... | collective-permute-start | bytes 12296 | tf_op jit(solution)/shard_map/ppermute | solution.py:689

commit v9 on v8

--- a/solution.py
+++ b/solution.py
@@ -152,6 +152,10 @@
     return m * sig, sig * (1.0 + m * (1.0 - sig))
 
 
+def pick(values, lanes):
+    return jnp.take_along_axis(values, lanes, axis=1, mode="promise_in_bounds")
+
+
 def reach(b, first, last):
     return [w for w in range(3) if first <= b - 1 + w <= last]
 
@@ -162,10 +166,12 @@
 
 def mark(index, ws, target):
     count = len(ws) * LANES
-    row_id = lax.broadcasted_iota(jnp.int32, (count, LANES), 0) + ws[0] * LANES
+    row_id = (lax.broadcasted_iota(jnp.int32, (count, LANES), 0) + ws[0] * LANES).astype(jnp.int16)
+    one, zero = jnp.ones((count, LANES), BF16), jnp.zeros((count, LANES), BF16)
     for k in range(SLOTS):
-        same = row_id == jnp.broadcast_to(index[k : k + 1, :], (count, LANES))
-        target[:, k * LANES : (k + 1) * LANES] = jnp.where(same, 1.0, 0.0).astype(BF16)
+        wanted = jnp.broadcast_to(index[k : k + 1, :], (16, LANES)).astype(jnp.int16)
+        wanted = jnp.concatenate([wanted] * (count // 16), axis=0)
+        target[:, k * LANES : (k + 1) * LANES] = jnp.where(row_id == wanted, one, zero)
 
 
 def window_index(pack, b):
@@ -199,7 +205,7 @@
 
         def taken(row):
             got = [
-                jnp.take_along_axis(jnp.broadcast_to(xs[b - 1 + w, row : row + 1, :], (SLOTS, LANES)), inner, axis=1)
+                pick(jnp.broadcast_to(xs[b - 1 + w, row : row + 1, :], (SLOTS, LANES)), inner)
                 for w in range(3)
             ]
             return jnp.where(part == 0, got[0], jnp.where(part == 1, got[1], got[2]))
@@ -254,12 +260,12 @@
         slope[:, cols] = steep
 
 
-def force_parts(weights, own_hot, side_hot, kept, dg, pulls, met, acc):
+def force_parts(weights, own_hot, side_hot, kept, dg, pulls, met, acc, held):
     l1, l2, l3, l5, l6, col = weights
     (widx, kinds, geo, bst, bps, bpr, sent_all, slope) = kept
     slot = lax.broadcasted_iota(jnp.int32, (SLOTS, LANES), 0)
 
-    def spread(left, b, first, last, held):
+    def spread(left, b, first, last, sums):
         ws = reach(b, first, last)
         if b in SIDE_START:
             start = SIDE_START[b] + (ws[0] - reach(b, 3, 8)[0]) * LANES
@@ -271,42 +277,51 @@
             target = b - 1 + w
             piece = out[i * LANES : (i + 1) * LANES]
             rows = slice((target - first) * LANES, (target - first + 1) * LANES)
-            if (id(held), target) in started:
-                held[rows, :] += piece
+            if (first, target) in started:
+                sums[rows, :] += piece
             else:
-                held[rows, :] = piece
-                started.add((id(held), target))
+                sums[rows, :] = piece
+                started.add((first, target))
 
     started = set()
 
     def gather_and_return(b):
         index = widx[b]
         inner, part = index & (LANES - 1), index >> 7
-        windows = [sent_all[:, (b - 1 + w) * LANES : (b + w) * LANES] for w in range(3)]
-        got = []
-        for k in range(SLOTS):
-            lane = jnp.broadcast_to(inner[k : k + 1, :], (CHANNELS, LANES))
-            which = jnp.broadcast_to(part[k : k + 1, :], (CHANNELS, LANES))
-            pick = [jnp.take_along_axis(window, lane, axis=1) for window in windows]
-            got.append(jnp.where(which == 0, pick[0], jnp.where(which == 1, pick[1], pick[2])))
-        got = jnp.concatenate(got, axis=1)
         basis = bst[b]
         radial = mm(l3[...], jnp.concatenate([basis, basis], axis=0))
-        message = jnp.zeros((CHANNELS, LANES), F32)
-        for k in range(SLOTS):
-            cols = slice(k * LANES, (k + 1) * LANES)
-            message = message + radial[:, cols] * got[:, cols]
-        _, steep = silu_parts(message)
-        back = jnp.concatenate([col[3] * steep] * SLOTS, axis=1)
-        spread(pair_stack(radial * back), b, 3, 8, dg)
         if 3 <= b <= 8:
             basis = bps[b]
             steepness = mm(l3[...], jnp.concatenate([basis, basis], axis=0))
-            pull = got * back * steepness
-            total = pull[0:8]
-            for i in range(1, CHANNELS // 8):
-                total = total + pull[8 * i : 8 * i + 8]
-            pulls[b] = total
+        lanes = [jnp.broadcast_to(inner[k : k + 1, :], (16, LANES)) for k in range(SLOTS)]
+        parts = [jnp.broadcast_to(part[k : k + 1, :], (16, LANES)) for k in range(SLOTS)]
+        value = held.at[b % 2]
+        total = [jnp.zeros((8, LANES), F32)] * SLOTS
+        for u in range(CHANNELS // 16):
+            rows = slice(16 * u, 16 * u + 16)
+            low_rows = slice(CHANNELS + 16 * u, CHANNELS + 16 * u + 16)
+            windows = [sent_all[rows, (b - 1 + w) * LANES : (b + w) * LANES] for w in range(3)]
+            got = []
+            message = jnp.zeros((16, LANES), F32)
+            for k in range(SLOTS):
+                cols = slice(k * LANES, (k + 1) * LANES)
+                found = [pick(window, lanes[k]) for window in windows]
+                got.append(jnp.where(parts[k] == 0, found[0], jnp.where(parts[k] == 1, found[1], found[2])))
+                message = message + radial[rows, cols] * got[k]
+            _, steep = silu_parts(message)
+            back = col[3, rows] * steep
+            for k in range(SLOTS):
+                cols = slice(k * LANES, (k + 1) * LANES)
+                high, low = split(radial[rows, cols] * back)
+                value[rows, cols] = high.astype(BF16)
+                value[low_rows, cols] = low.astype(BF16)
+                if 3 <= b <= 8:
+                    pull = got[k] * back * steepness[rows, cols]
+                    total[k] = total[k] + pull[0:8] + pull[8:16]
+        spread(value[...], b, 3, 8, dg)
+        if 3 <= b <= 8:
+            for k in range(SLOTS):
+                pulls[b, :, k * LANES : (k + 1) * LANES] = total[k]
 
     for b in range(2, 10):
         gather_and_return(b)
@@ -391,6 +406,7 @@
         pltpu.VMEM((12, 8, SLOTS * LANES), F32),
         pltpu.VMEM((SLAB_BLOCKS * LANES, 6 * SLOTS), F32),
         pltpu.VMEM((SLAB_BLOCKS, 3, 1, LANES), F32),
+        pltpu.VMEM((2, 2 * CHANNELS, SLOTS * LANES), BF16),
     ]
 
 

time: 43.2 us -> 42.2 us (0.977)
  Pallas kernels: 17.8 us -> 17 us
    pallas_call x9, Pallas kernels: 17.8 us -> 17 us  [call(): pl.pallas_call(body, out_shape=outs, in_specs=[SMEM_SPEC] * len(scalars)...]
  transfers between devices with their start and end apart: 13 -> 13, of which waited for: 5 -> 5; matrix products, arithmetic and copies ran while one was open for 0% -> 0% of each run, Pallas kernels for 21% -> 19%
where the time goes in v9:
time: 42.2 us; the launch traced here: 41.9 us
  Pallas kernels  17 us (40%)
  starting transfers between devices  16.2 us (38%)
  waiting for transfers between devices  5.78 us (14%)
  between operations  2.01 us (5%)
  local copies, waits for them, and re-layouts  0.95 us (2%)
    pallas_call x9, Pallas kernels, call(): pl.pallas_call(body, out_shape=outs, in_specs=[SMEM_SPEC] * len(scalars)...  17 us
    ppermute x13, starting transfers between devices, swap(): lax.ppermute(array, axis, [(i, partner(i)) for i in range(lax.axis_size(a...  16.2 us
    ppermute x13, waiting for transfers between devices, swap(): lax.ppermute(array, axis, [(i, partner(i)) for i in range(lax.axis_size(a...  5.78 us
    unnamed x6, local copies, waits for them, and re-layouts  0.95 us
  transfers between devices with their start and end apart: 13, of which 5 were waited for; matrix products, arithmetic and copies ran while one was open for 0% of the time, Pallas kernels for 19%

profile of v9, /device:TPU:0, one launch (start us, length us, event | category | flops | bytes accessed | tf_op | source)
XLA Modules:
  0.0 41.9 jit_solution(14981584982258551941)
XLA Ops:
  0.6 1.9 %shard_map.166 = (f32[40,512]{1,0:T(8,128)}, f32[112,512]{1,0:T(8,128)}) custom-call(f32[3,1,512]{2,1,0:T(1,128)} %bitcast.12, f32[3,1,512]{2,1,0:T(1,128)} %bitcast.13, s32[512]{0:T(512)} %refs_2_.1, s32[8,512]{1,0:T(8,128)} %refs_3_.1, s32[512]{0:T(512)} %refs_4_.1, f32[2,64]{1,0:T(2,128)} %refs_5_.1, f32[64]{0:T(128)} %refs_6_.1, f32[2,8,64]{2,1,0:T(8,128)} %refs_7_.1, ...), custom_call_target="tpu_custom_call" | custom-call | bytes 262144 | tf_op jit(solution)/shard_map/pallas_call | solution.py:693
  2.5 0.5 %collective-permute-start = (f32[40,512]{1,0:T(8,128)}, f32[40,512]{1,0:T(8,128)S(1)}, u32[]{:S(2)}, u32[]{:S(2)}) collective-permute-start(f32[40,512]{1,0:T(8,128)} %get-tuple-element.38), channel_id=1, source_target_pairs={{0,4},{4,0},{8,12},{12,8},{1,5},{5,1},{9,13},{13,9},{2,6},{6,2},{1... | collective-permute-start | bytes 245768 | tf_op jit(solution)/shard_map/ppermute | solution.py:705
  3.0 2.6 %collective-permute-start.1 = (f32[40,512]{1,0:T(8,128)}, f32[40,512]{1,0:T(8,128)S(1)}, u32[]{:S(2)}, u32[]{:S(2)}) collective-permute-start(f32[40,512]{1,0:T(8,128)} %get-tuple-element.38), channel_id=1, source_target_pairs={{0,12},{4,8},{8,4},{12,0},{1,13},{5,9},{9,5},{13,1},{2,14},{6,10},... | collective-permute-start | bytes 245768 | tf_op jit(solution)/shard_map/ppermute | solution.py:705
  5.7 0.0 copy-start
  5.7 0.9 %copy-done = f32[112,512]{1,0:T(8,128)S(1)} copy-done((f32[112,512]{1,0:T(8,128)S(1)}, f32[112,512]{1,0:T(8,128)}, u32[]{:S(2)}) %copy-start) | copy-done | bytes 229400
  6.6 1.2 %shard_map.167 = (bf16[4,384,1024]{2,1,0:T(8,128)(2,1)S(1)}, bf16[64,48]{1,0:T(8,128)(2,1)S(1)}, bf16[64,192]{1,0:T(8,128)(2,1)S(1)}, bf16[64,32]{1,0:T(8,128)(2...) custom-call(f32[112,512]{1,0:T(8,128)S(1)} %copy-done), custom_call_target="tpu_custom_call" | custom-call | flops 100000000 | bytes 262144 | tf_op jit(solution)/shard_map/pallas_call | solution.py:693
  7.8 1.6 %collective-permute-start.2 = (f32[3,1,512]{2,1,0:T(1,128)S(1)}, f32[3,1,512]{2,1,0:T(1,128)S(1)}, u32[]{:S(2)}, u32[]{:S(2)}) collective-permute-start(f32[3,1,512]{2,1,0:T(1,128)S(1)} %get-tuple-element.37.x_ref), channel_id=1, source_target_pairs={{0,1},{1,2},{2,3},{3,0},{4,5},{5,6},{6,7},{7,4},{8,9},{9,10},{10,1... | collective-permute-start | bytes 18440 | tf_op jit(solution)/shard_map/ppermute | solution.py:705
  9.4 0.0 collective-permute-done.sibling_ref
  9.4 0.0 collective-permute-done.1.across_ref
  9.4 1.3 %shard_map.168 = (f32[40,512]{1,0:T(8,128)S(1)}, f32[40,512]{1,0:T(8,128)S(1)}, bf16[768,1024]{1,0:T(8,128)(2,1)S(1)}, f32[3,1,512]{2,1,0:T(1,128)S(1)}, s32[12,...) custom-call(f32[3,1,512]{2,1,0:T(1,128)S(1)} %get-tuple-element.37.x, ...), custom_call_target="tpu_custom_call" | custom-call | flops 1000000000 | bytes 262144 | tf_op jit(solution)/shard_map/pallas_call | solution.py:693
  10.7 2.7 %collective-permute-start.3 = (f32[3,1,512]{2,1,0:T(1,128)S(1)}, f32[3,1,512]{2,1,0:T(1,128)S(1)}, u32[]{:S(2)}, u32[]{:S(2)}) collective-permute-start(f32[3,1,512]{2,1,0:T(1,128)S(1)} %get-tuple-element.57), channel_id=1, source_target_pairs={{0,3},{1,0},{2,1},{3,2},{4,7},{5,4},{6,5},{7,6},{8,11},{9,8},{10,9... | collective-permute-start | bytes 18440 | tf_op jit(solution)/shard_map/ppermute | solution.py:705
  13.4 0.0 copy-start.2
  13.4 0.0 copy-start.1
  13.4 5.2 %shard_map.169.force_ref = f32[3,512]{1,0:T(4,128)S(1)} custom-call(bf16[4,384,1024]{2,1,0:T(8,128)(2,1)S(1)} %get-tuple-element.47.own_hot.rest_2_, bf16[768,1024]{1,0:T(8,128)(2,1)S(1)} %get-tuple-element.48.side_hot.rest_3_, bf16[64,48]{1,0:T(8,128)(2,1)S(1)} %get-tuple-element.39.rest_0_.rest_4_, bf16[64,192]{1,0:T(8,128)(2,1)S(1)} %get-tuple-element.40.rest_1_.rest_5_, ...), custom_call_target="tpu_custom_call" | custom-call | flops 1000000000 | bytes 262144 | tf_op jit(solution)/shard_map/pallas_call | solution.py:693
  18.6 0.0 collective-permute-done.2.before_ref
  18.6 0.0 collective-permute-done.3.after_ref
  18.6 0.1 shard_map.170
  18.7 0.2 collective-permute-start.4
  18.9 1.5 %collective-permute-start.5 = (f32[8,512]{1,0:T(8,128)S(1)}, f32[8,512]{1,0:T(8,128)S(1)}, u32[]{:S(2)}, u32[]{:S(2)}) collective-permute-start(f32[8,512]{1,0:T(8,128)S(1)} %get-tuple-element.58.own_ref), channel_id=1, source_target_pairs={{0,12},{4,8},{8,4},{12,0},{1,13},{5,9},{9,5},{13,1},{2,14},{6,10},... | collective-permute-start | bytes 49160 | tf_op jit(solution)/shard_map/ppermute | solution.py:705
  20.3 0.5 %collective-permute-start.6 = (f32[8,128]{1,0:T(8,128)S(1)}, f32[8,128]{1,0:T(8,128)S(1)}, u32[]{:S(2)}, u32[]{:S(2)}) collective-permute-start(f32[8,128]{1,0:T(8,128)S(1)} %get-tuple-element.59.rest_0_), channel_id=1, source_target_pairs={{0,8},{4,12},{8,0},{12,4},{1,9},{5,13},{9,1},{13,5},{2,10},{6,14},... | collective-permute-start | bytes 12296 | tf_op jit(solution)/shard_map/ppermute | solution.py:705
  22.2 0.0 copy-done.2
  22.2 0.5 %shard_map.165.number_ref = f32[8,128]{1,0:T(8,128)S(1)} custom-call(f32[1]{0:T(128)S(6)} %copy.19.dt_ref, s32[1,2]{1,0:T(1,128)S(1)} %bitcast.10, s32[1]{0:T(128)S(6)} %copy.20.climb_ref), custom_call_target="tpu_custom_call" | custom-call | bytes 262144 | tf_op jit(solution)/shard_map/pallas_call | solution.py:693
  22.7 1.2 %collective-permute-done.6.rest_1_ = f32[8,128]{1,0:T(8,128)S(1)} collective-permute-done((f32[8,128]{1,0:T(8,128)S(1)}, f32[8,128]{1,0:T(8,128)S(1)}, u32[]{:S(2)}, u32[]{:S(2)}) %collective-permute-start.6) | collective-permute-done | bytes 4128 | tf_op jit(solution)/shard_map/ppermute | solution.py:705
  23.9 0.0 collective-permute-done.4.near_ref
  23.9 0.0 collective-permute-done.5.far_ref
  23.9 0.0 copy-done.1
  23.9 5.8 %shard_map.171 = (f32[1,40,128]{2,1,0:T(8,128)S(1)}, f32[3,128]{1,0:T(4,128)S(1)}) custom-call(f32[8,128]{1,0:T(8,128)S(1)} %shard_map.165.number_ref, f32[40,512]{1,0:T(8,128)S(1)} %get-tuple-element.45.pl_ref, f32[112,512]{1,0:T(8,128)S(1)} %copy-done.1, f32[40,512]{1,0:T(8,128)S(1)} %get-tuple-element.46.pr_ref, f32[8,512]{1,0:T(8,128)S(1)} %get-tuple-element.58.own_ref, ...), custom_call_target="tpu_custom_call" | custom-call | flops 1000000000 | bytes 262144 | tf_op jit(solution)/shard_map/pallas_call | solution.py:693
  29.8 0.0 collective-permute-start.7
  29.8 1.0 %collective-permute-start.8 = (f32[1,40,128]{2,1,0:T(8,128)S(1)}, f32[1,40,128]{2,1,0:T(8,128)S(1)}, u32[]{:S(2)}, u32[]{:S(2)}) collective-permute-start(f32[1,40,128]{2,1,0:T(8,128)S(1)} %get-tuple-element.60.refs_0_.own_ref), channel_id=1, source_target_pairs={{0,2},{1,3},{2,0},{3,1},{4,6},{5,7},{6,4},{7,5},{8,10},{9,11},{10,... | collective-permute-start | bytes 61448 | tf_op jit(solution)/shard_map/ppermute | solution.py:705
  30.8 3.4 %collective-permute-start.9 = (f32[1,40,128]{2,1,0:T(8,128)S(1)}, f32[1,40,128]{2,1,0:T(8,128)S(1)}, u32[]{:S(2)}, u32[]{:S(2)}) collective-permute-start(f32[1,40,128]{2,1,0:T(8,128)S(1)} %get-tuple-element.60.refs_0_.own_ref), channel_id=1, source_target_pairs={{0,3},{1,2},{2,1},{3,0},{4,7},{5,6},{6,5},{7,4},{8,11},{9,10},{10,... | collective-permute-start | bytes 61448 | tf_op jit(solution)/shard_map/ppermute | solution.py:705
  34.2 0.0 collective-permute-done.7.refs_1_
  34.2 0.4 %collective-permute-done.8.refs_2_ = f32[1,40,128]{2,1,0:T(8,128)S(1)} collective-permute-done((f32[1,40,128]{2,1,0:T(8,128)S(1)}, f32[1,40,128]{2,1,0:T(8,128)S(1)}, u32[]{:S(2)}, u32[]{:S(2)}) %collective-permute-start.8) | collective-permute-done | bytes 20512 | tf_op jit(solution)/shard_map/ppermute | solution.py:705
  34.6 1.8 %collective-permute-done.9.refs_3_ = f32[1,40,128]{2,1,0:T(8,128)S(1)} collective-permute-done((f32[1,40,128]{2,1,0:T(8,128)S(1)}, f32[1,40,128]{2,1,0:T(8,128)S(1)}, u32[]{:S(2)}, u32[]{:S(2)}) %collective-permute-start.9) | collective-permute-done | bytes 20512 | tf_op jit(solution)/shard_map/ppermute | solution.py:705
  36.4 0.2 shard_map.172
  36.6 1.5 %collective-permute-start.10 = (f32[8,128]{1,0:T(8,128)S(1)}, f32[8,128]{1,0:T(8,128)S(1)}, u32[]{:S(2)}, u32[]{:S(2)}) collective-permute-start(f32[8,128]{1,0:T(8,128)S(1)} %get-tuple-element.63.rest_0_), channel_id=1, source_target_pairs={{0,8},{4,12},{8,0},{12,4},{1,9},{5,13},{9,1},{13,5},{2,10},{6,14},... | collective-permute-start | bytes 12296 | tf_op jit(solution)/shard_map/ppermute | solution.py:705
  38.2 0.0 collective-permute-start.11
  38.2 0.7 %collective-permute-start.12 = (f32[8,128]{1,0:T(8,128)S(1)}, f32[8,128]{1,0:T(8,128)S(1)}, u32[]{:S(2)}, u32[]{:S(2)}) collective-permute-start(f32[8,128]{1,0:T(8,128)S(1)} %get-tuple-element.63.rest_0_), channel_id=1, source_target_pairs={{0,4},{4,0},{8,12},{12,8},{1,5},{5,1},{9,13},{13,9},{2,6},{6,2},{1... | collective-permute-start | bytes 12296 | tf_op jit(solution)/shard_map/ppermute | solution.py:705
  38.8 1.5 %collective-permute-done.10.rest_1_ = f32[8,128]{1,0:T(8,128)S(1)} collective-permute-done((f32[8,128]{1,0:T(8,128)S(1)}, f32[8,128]{1,0:T(8,128)S(1)}, u32[]{:S(2)}, u32[]{:S(2)}) %collective-permute-start.10) | collective-permute-done | bytes 4128 | tf_op jit(solution)/shard_map/ppermute | solution.py:705
  40.3 0.9 %collective-permute-done.11.rest_2_ = f32[8,128]{1,0:T(8,128)S(1)} collective-permute-done((f32[8,128]{1,0:T(8,128)S(1)}, f32[8,128]{1,0:T(8,128)S(1)}, u32[]{:S(2)}, u32[]{:S(2)}) %collective-permute-start.11) | collective-permute-done | bytes 4128 | tf_op jit(solution)/shard_map/ppermute | solution.py:705
  41.2 0.0 collective-permute-done.12.rest_3_
  41.2 0.7 %shard_map.173 = (f32[3,1,512]{2,1,0:T(1,128)}, f32[3,1,512]{2,1,0:T(1,128)}, f32[2,1,2]{2,1,0:T(1,128)}, f32[1,1]{1,0:T(1,128)}) custom-call(f32[1,40,128]{2,1,0:T(8,128)S(1)} %get-tuple-element.60.refs_0_.own_ref, f32[3,128]{1,0:T(4,128)S(1)} %get-tuple-element.61.record_ref, f32[40,128]{1,0:T(8,128)S(1)} %get-tuple-element.62.state_ref, ...), custom_call_target="tpu_custom_call" | custom-call | bytes 262144 | tf_op jit(solution)/shard_map/pallas_call | solution.py:693
Async XLA Ops:
  2.5 6.9 %collective-permute-start = (f32[40,512]{1,0:T(8,128)}, f32[40,512]{1,0:T(8,128)S(1)}, u32[]{:S(2)}, u32[]{:S(2)}) collective-permute-start(f32[40,512]{1,0:T(8,128)} %get-tuple-element.38), channel_id=1, source_target_pairs={{0,4},{4,0},{8,12},{12,8},{1,5},{5,1},{9,13},{13,9},{2,6},{6,2},{1... | collective-permute-start | bytes 245768 | tf_op jit(solution)/shard_map/ppermute | solution.py:705
  3.0 6.4 %collective-permute-start.1 = (f32[40,512]{1,0:T(8,128)}, f32[40,512]{1,0:T(8,128)S(1)}, u32[]{:S(2)}, u32[]{:S(2)}) collective-permute-start(f32[40,512]{1,0:T(8,128)} %get-tuple-element.38), channel_id=1, source_target_pairs={{0,12},{4,8},{8,4},{12,0},{1,13},{5,9},{9,5},{13,1},{2,14},{6,10},... | collective-permute-start | bytes 245768 | tf_op jit(solution)/shard_map/ppermute | solution.py:705
  5.7 0.9 %copy-start = (f32[112,512]{1,0:T(8,128)S(1)}, f32[112,512]{1,0:T(8,128)}, u32[]{:S(2)}) copy-start(f32[112,512]{1,0:T(8,128)} %get-tuple-element.36.po_ref) | copy-start | bytes 688132
  7.8 10.8 %collective-permute-start.2 = (f32[3,1,512]{2,1,0:T(1,128)S(1)}, f32[3,1,512]{2,1,0:T(1,128)S(1)}, u32[]{:S(2)}, u32[]{:S(2)}) collective-permute-start(f32[3,1,512]{2,1,0:T(1,128)S(1)} %get-tuple-element.37.x_ref), channel_id=1, source_target_pairs={{0,1},{1,2},{2,3},{3,0},{4,5},{5,6},{6,7},{7,4},{8,9},{9,10},{10,1... | collective-permute-start | bytes 18440 | tf_op jit(solution)/shard_map/ppermute | solution.py:705
  10.7 7.9 %collective-permute-start.3 = (f32[3,1,512]{2,1,0:T(1,128)S(1)}, f32[3,1,512]{2,1,0:T(1,128)S(1)}, u32[]{:S(2)}, u32[]{:S(2)}) collective-permute-start(f32[3,1,512]{2,1,0:T(1,128)S(1)} %get-tuple-element.57), channel_id=1, source_target_pairs={{0,3},{1,0},{2,1},{3,2},{4,7},{5,4},{6,5},{7,6},{8,11},{9,8},{10,9... | collective-permute-start | bytes 18440 | tf_op jit(solution)/shard_map/ppermute | solution.py:705
  13.4 8.7 %copy-start.2 = (s32[2,1]{0,1:T(1,128)S(1)}, s32[2,1]{0,1:T(1,128)}, u32[]{:S(2)}) copy-start(s32[2,1]{0,1:T(1,128)} %param.17) | copy-start | bytes 28
  13.4 10.5 %copy-start.1 = (f32[112,512]{1,0:T(8,128)S(1)}, f32[112,512]{1,0:T(8,128)}, u32[]{:S(2)}) copy-start(f32[112,512]{1,0:T(8,128)} %get-tuple-element.36.po_ref) | copy-start | bytes 688132
  18.7 5.2 %collective-permute-start.4 = (f32[8,512]{1,0:T(8,128)S(1)}, f32[8,512]{1,0:T(8,128)S(1)}, u32[]{:S(2)}, u32[]{:S(2)}) collective-permute-start(f32[8,512]{1,0:T(8,128)S(1)} %get-tuple-element.58.own_ref), channel_id=1, source_target_pairs={{0,4},{4,0},{8,12},{12,8},{1,5},{5,1},{9,13},{13,9},{2,6},{6,2},{1... | collective-permute-start | bytes 49160 | tf_op jit(solution)/shard_map/ppermute | solution.py:705
  18.9 5.1 %collective-permute-start.5 = (f32[8,512]{1,0:T(8,128)S(1)}, f32[8,512]{1,0:T(8,128)S(1)}, u32[]{:S(2)}, u32[]{:S(2)}) collective-permute-start(f32[8,512]{1,0:T(8,128)S(1)} %get-tuple-element.58.own_ref), channel_id=1, source_target_pairs={{0,12},{4,8},{8,4},{12,0},{1,13},{5,9},{9,5},{13,1},{2,14},{6,10},... | collective-permute-start | bytes 49160 | tf_op jit(solution)/shard_map/ppermute | solution.py:705
  20.3 3.6 %collective-permute-start.6 = (f32[8,128]{1,0:T(8,128)S(1)}, f32[8,128]{1,0:T(8,128)S(1)}, u32[]{:S(2)}, u32[]{:S(2)}) collective-permute-start(f32[8,128]{1,0:T(8,128)S(1)} %get-tuple-element.59.rest_0_), channel_id=1, source_target_pairs={{0,8},{4,12},{8,0},{12,4},{1,9},{5,13},{9,1},{13,5},{2,10},{6,14},... | collective-permute-start | bytes 12296 | tf_op jit(solution)/shard_map/ppermute | solution.py:705
  29.8 4.4 %collective-permute-start.7 = (f32[1,40,128]{2,1,0:T(8,128)S(1)}, f32[1,40,128]{2,1,0:T(8,128)S(1)}, u32[]{:S(2)}, u32[]{:S(2)}) collective-permute-start(f32[1,40,128]{2,1,0:T(8,128)S(1)} %get-tuple-element.60.refs_0_.own_ref), channel_id=1, source_target_pairs={{0,1},{1,0},{2,3},{3,2},{4,5},{5,4},{6,7},{7,6},{8,9},{9,8},{10,11... | collective-permute-start | bytes 61448 | tf_op jit(solution)/shard_map/ppermute | solution.py:705
  29.8 4.8 %collective-permute-start.8 = (f32[1,40,128]{2,1,0:T(8,128)S(1)}, f32[1,40,128]{2,1,0:T(8,128)S(1)}, u32[]{:S(2)}, u32[]{:S(2)}) collective-permute-start(f32[1,40,128]{2,1,0:T(8,128)S(1)} %get-tuple-element.60.refs_0_.own_ref), channel_id=1, source_target_pairs={{0,2},{1,3},{2,0},{3,1},{4,6},{5,7},{6,4},{7,5},{8,10},{9,11},{10,... | collective-permute-start | bytes 61448 | tf_op jit(solution)/shard_map/ppermute | solution.py:705
  30.8 5.6 %collective-permute-start.9 = (f32[1,40,128]{2,1,0:T(8,128)S(1)}, f32[1,40,128]{2,1,0:T(8,128)S(1)}, u32[]{:S(2)}, u32[]{:S(2)}) collective-permute-start(f32[1,40,128]{2,1,0:T(8,128)S(1)} %get-tuple-element.60.refs_0_.own_ref), channel_id=1, source_target_pairs={{0,3},{1,2},{2,1},{3,0},{4,7},{5,6},{6,5},{7,4},{8,11},{9,10},{10,... | collective-permute-start | bytes 61448 | tf_op jit(solution)/shard_map/ppermute | solution.py:705
  36.6 3.7 %collective-permute-start.10 = (f32[8,128]{1,0:T(8,128)S(1)}, f32[8,128]{1,0:T(8,128)S(1)}, u32[]{:S(2)}, u32[]{:S(2)}) collective-permute-start(f32[8,128]{1,0:T(8,128)S(1)} %get-tuple-element.63.rest_0_), channel_id=1, source_target_pairs={{0,8},{4,12},{8,0},{12,4},{1,9},{5,13},{9,1},{13,5},{2,10},{6,14},... | collective-permute-start | bytes 12296 | tf_op jit(solution)/shard_map/ppermute | solution.py:705
  38.2 3.0 %collective-permute-start.11 = (f32[8,128]{1,0:T(8,128)S(1)}, f32[8,128]{1,0:T(8,128)S(1)}, u32[]{:S(2)}, u32[]{:S(2)}) collective-permute-start(f32[8,128]{1,0:T(8,128)S(1)} %get-tuple-element.63.rest_0_), channel_id=1, source_target_pairs={{0,12},{4,8},{8,4},{12,0},{1,13},{5,9},{9,5},{13,1},{2,14},{6,10},... | collective-permute-start | bytes 12296 | tf_op jit(solution)/shard_map/ppermute | solution.py:705
  38.2 3.0 %collective-permute-start.12 = (f32[8,128]{1,0:T(8,128)S(1)}, f32[8,128]{1,0:T(8,128)S(1)}, u32[]{:S(2)}, u32[]{:S(2)}) collective-permute-start(f32[8,128]{1,0:T(8,128)S(1)} %get-tuple-element.63.rest_0_), channel_id=1, source_target_pairs={{0,4},{4,0},{8,12},{12,8},{1,5},{5,1},{9,13},{13,9},{2,6},{6,2},{1... | collective-permute-start | bytes 12296 | tf_op jit(solution)/shard_map/ppermute | solution.py:705

commit v10 on v9

--- a/solution.py
+++ b/solution.py
@@ -260,7 +260,7 @@
         slope[:, cols] = steep
 
 
-def force_parts(weights, own_hot, side_hot, kept, dg, pulls, met, acc, held):
+def force_parts(weights, own_hot, side_hot, kept, dg, pulls, met, acc, held, radial, steepness, got, backs):
     l1, l2, l3, l5, l6, col = weights
     (widx, kinds, geo, bst, bps, bpr, sent_all, slope) = kept
     slot = lax.broadcasted_iota(jnp.int32, (SLOTS, LANES), 0)
@@ -285,53 +285,75 @@
 
     started = set()
 
-    def gather_and_return(b):
+    blocks, inner_blocks = range(2, 10), range(3, 9)
+    for b in blocks:
+        basis = bst[b]
+        radial[b - 2] = mm(l3[...], jnp.concatenate([basis, basis], axis=0))
+    for b in inner_blocks:
+        basis = bps[b]
+        steepness[b - 3] = mm(l3[...], jnp.concatenate([basis, basis], axis=0))
+
+    for b in blocks:
         index = widx[b]
         inner, part = index & (LANES - 1), index >> 7
-        basis = bst[b]
-        radial = mm(l3[...], jnp.concatenate([basis, basis], axis=0))
-        if 3 <= b <= 8:
-            basis = bps[b]
-            steepness = mm(l3[...], jnp.concatenate([basis, basis], axis=0))
         lanes = [jnp.broadcast_to(inner[k : k + 1, :], (16, LANES)) for k in range(SLOTS)]
         parts = [jnp.broadcast_to(part[k : k + 1, :], (16, LANES)) for k in range(SLOTS)]
-        value = held.at[b % 2]
+        for u in range(CHANNELS // 16):
+            rows = slice(16 * u, 16 * u + 16)
+            windows = [sent_all[rows, (b - 1 + w) * LANES : (b + w) * LANES] for w in range(3)]
+            message = jnp.zeros((16, LANES), F32)
+            for k in range(SLOTS):
+                cols = slice(k * LANES, (k + 1) * LANES)
+                found = [pick(window, lanes[k]) for window in windows]
+                one = jnp.where(parts[k] == 0, found[0], jnp.where(parts[k] == 1, found[1], found[2]))
+                if b in inner_blocks:
+                    got[b - 3, rows, cols] = one
+                message = message + radial[b - 2, rows, cols] * one
+            backs[b - 2, rows] = message
+
+    for b in blocks:
+        _, steep = silu_parts(backs[b - 2])
+        backs[b - 2] = col[3] * steep
+
+    for b in blocks:
         total = [jnp.zeros((8, LANES), F32)] * SLOTS
         for u in range(CHANNELS // 16):
             rows = slice(16 * u, 16 * u + 16)
             low_rows = slice(CHANNELS + 16 * u, CHANNELS + 16 * u + 16)
-            windows = [sent_all[rows, (b - 1 + w) * LANES : (b + w) * LANES] for w in range(3)]
-            got = []
-            message = jnp.zeros((16, LANES), F32)
+            back = backs[b - 2, rows]
             for k in range(SLOTS):
                 cols = slice(k * LANES, (k + 1) * LANES)
-                found = [pick(window, lanes[k]) for window in windows]
-                got.append(jnp.where(parts[k] == 0, found[0], jnp.where(parts[k] == 1, found[1], found[2])))
-                message = message + radial[rows, cols] * got[k]
-            _, steep = silu_parts(message)
-            back = col[3, rows] * steep
-            for k in range(SLOTS):
-                cols = slice(k * LANES, (k + 1) * LANES)
-                high, low = split(radial[rows, cols] * back)
-                value[rows, cols] = high.astype(BF16)
-                value[low_rows, cols] = low.astype(BF16)
-                if 3 <= b <= 8:
-                    pull = got[k] * back * steepness[rows, cols]
+                high, low = split(radial[b - 2, rows, cols] * back)
+                held[b - 2, rows, cols] = high.astype(BF16)
+                held[b - 2, low_rows, cols] = low.astype(BF16)
+                if b in inner_blocks:
+                    pull = got[b - 3, rows, cols] * back * steepness[b - 3, rows, cols]
                     total[k] = total[k] + pull[0:8] + pull[8:16]
-        spread(value[...], b, 3, 8, dg)
-        if 3 <= b <= 8:
+        if b in inner_blocks:
             for k in range(SLOTS):
                 pulls[b, :, k * LANES : (k + 1) * LANES] = total[k]
 
-    for b in range(2, 10):
-        gather_and_return(b)
-
-    def finish(b, sums):
+    for b in blocks:
+        spread(held[b - 2], b, 3, 8, dg)
+
+    steeps = []
+    for b in range(3, 9, 2):
+        high, low = split(dg[(b - 3) * LANES : (b - 1) * LANES, :])
+        steeps.append(mm_nt(l5[...], jnp.concatenate([high, low, high], axis=1).astype(BF16)))
+    steeps = [
+        (steep + jnp.concatenate([col[2], col[2]], axis=1)) * slope[:, b * LANES : (b + 2) * LANES]
+        for b, steep in zip(range(3, 9, 2), steeps)
+    ]
+    sums = [mm(l6[...], right_stack(steep)) for steep in steeps]
+
+    lines = []
+    for b in inner_blocks:
+        mine = sums[(b - 3) // 2][:, (b - 3) % 2 * LANES : ((b - 3) % 2 + 1) * LANES]
         kind = kinds[b]
         rows = []
         for k in range(SLOTS):
             cols = slice(k * LANES, (k + 1) * LANES)
-            weight = sums[0:8] + wide_row(kind, k) * sums[8:16]
+            weight = mine[0:8] + wide_row(kind, k) * mine[8:16]
             rows.append(jnp.sum(bpr[b, :, cols] * weight + pulls[b, :, cols], axis=0, keepdims=True))
         pull = jnp.concatenate(rows, axis=0) * geo[b, 3]
         pieces = []
@@ -340,20 +362,13 @@
             if 4 <= b <= 7:
                 acc[b - 4, c] = jnp.sum(value, axis=0, keepdims=True)
             pieces.append(split(value))
-        lines = []
+        parts = []
         for h in range(2):
             for c in range(3):
-                lines.append(jnp.concatenate([jnp.where(slot == k, pieces[c][h], 0.0) for k in range(SLOTS)], axis=1))
-        spread(jnp.concatenate(lines, axis=0).astype(BF16), b, 4, 7, met)
-
-    for b in range(3, 9, 2):
-        cols = slice(b * LANES, (b + 2) * LANES)
-        high, low = split(dg[(b - 3) * LANES : (b - 1) * LANES, :])
-        steep = mm_nt(l5[...], jnp.concatenate([high, low, high], axis=1).astype(BF16))
-        steep = steep + jnp.concatenate([col[2], col[2]], axis=1)
-        sums = mm(l6[...], right_stack(steep * slope[:, cols]))
-        for i in range(2):
-            finish(b + i, sums[:, i * LANES : (i + 1) * LANES])
+                parts.append(jnp.concatenate([jnp.where(slot == k, pieces[c][h], 0.0) for k in range(SLOTS)], axis=1))
+        lines.append(jnp.concatenate(parts, axis=0).astype(BF16))
+    for b in inner_blocks:
+        spread(lines[b - 3], b, 4, 7, met)
 
     high, low = split(met[...])
     column = lax.broadcasted_iota(jnp.int32, (16, 6 * SLOTS), 1)
@@ -406,7 +421,11 @@
         pltpu.VMEM((12, 8, SLOTS * LANES), F32),
         pltpu.VMEM((SLAB_BLOCKS * LANES, 6 * SLOTS), F32),
         pltpu.VMEM((SLAB_BLOCKS, 3, 1, LANES), F32),
-        pltpu.VMEM((2, 2 * CHANNELS, SLOTS * LANES), BF16),
+        pltpu.VMEM((8, 2 * CHANNELS, SLOTS * LANES), BF16),
+        pltpu.VMEM((8, CHANNELS, SLOTS * LANES), F32),
+        pltpu.VMEM((6, CHANNELS, SLOTS * LANES), F32),
+        pltpu.VMEM((6, CHANNELS, SLOTS * LANES), F32),
+        pltpu.VMEM((8, CHANNELS, LANES), F32),
     ]
 
 

time: 42.2 us -> 43.5 us (1.031)
  Pallas kernels: 17 us -> 18.3 us
    pallas_call x9, Pallas kernels: 17 us -> 18.3 us  [call(): pl.pallas_call(body, out_shape=outs, in_specs=[SMEM_SPEC] * len(scalars)...]
  transfers between devices with their start and end apart: 13 -> 13, of which waited for: 5 -> 5; matrix products, arithmetic and copies ran while one was open for 0% -> 0% of each run, Pallas kernels for 19% -> 20%
where the time goes in v10:
time: 43.5 us; the launch traced here: 43.3 us
  Pallas kernels  18.3 us (42%)
  starting transfers between devices  16.2 us (37%)
  waiting for transfers between devices  5.78 us (13%)
  between operations  2.02 us (5%)
  local copies, waits for them, and re-layouts  0.95 us (2%)
    pallas_call x9, Pallas kernels, call(): pl.pallas_call(body, out_shape=outs, in_specs=[SMEM_SPEC] * len(scalars)...  18.3 us
    ppermute x13, starting transfers between devices, swap(): lax.ppermute(array, axis, [(i, partner(i)) for i in range(lax.axis_size(a...  16.2 us
    ppermute x13, waiting for transfers between devices, swap(): lax.ppermute(array, axis, [(i, partner(i)) for i in range(lax.axis_size(a...  5.78 us
    unnamed x6, local copies, waits for them, and re-layouts  0.95 us
  transfers between devices with their start and end apart: 13, of which 5 were waited for; matrix products, arithmetic and copies ran while one was open for 0% of the time, Pallas kernels for 20%

profile of v10, /device:TPU:0, one launch (start us, length us, event | category | flops | bytes accessed | tf_op | source)
XLA Modules:
  0.0 43.3 jit_solution(2957584826188518614)
XLA Ops:
  0.6 1.9 %shard_map.166 = (f32[40,512]{1,0:T(8,128)}, f32[112,512]{1,0:T(8,128)}) custom-call(f32[3,1,512]{2,1,0:T(1,128)} %bitcast.12, f32[3,1,512]{2,1,0:T(1,128)} %bitcast.13, s32[512]{0:T(512)} %refs_2_.1, s32[8,512]{1,0:T(8,128)} %refs_3_.1, s32[512]{0:T(512)} %refs_4_.1, f32[2,64]{1,0:T(2,128)} %refs_5_.1, f32[64]{0:T(128)} %refs_6_.1, f32[2,8,64]{2,1,0:T(8,128)} %refs_7_.1, ...), custom_call_target="tpu_custom_call" | custom-call | bytes 262144 | tf_op jit(solution)/shard_map/pallas_call | solution.py:712
  2.5 0.5 %collective-permute-start = (f32[40,512]{1,0:T(8,128)}, f32[40,512]{1,0:T(8,128)S(1)}, u32[]{:S(2)}, u32[]{:S(2)}) collective-permute-start(f32[40,512]{1,0:T(8,128)} %get-tuple-element.38), channel_id=1, source_target_pairs={{0,4},{4,0},{8,12},{12,8},{1,5},{5,1},{9,13},{13,9},{2,6},{6,2},{1... | collective-permute-start | bytes 245768 | tf_op jit(solution)/shard_map/ppermute | solution.py:724
  3.0 2.6 %collective-permute-start.1 = (f32[40,512]{1,0:T(8,128)}, f32[40,512]{1,0:T(8,128)S(1)}, u32[]{:S(2)}, u32[]{:S(2)}) collective-permute-start(f32[40,512]{1,0:T(8,128)} %get-tuple-element.38), channel_id=1, source_target_pairs={{0,12},{4,8},{8,4},{12,0},{1,13},{5,9},{9,5},{13,1},{2,14},{6,10},... | collective-permute-start | bytes 245768 | tf_op jit(solution)/shard_map/ppermute | solution.py:724
  5.7 0.0 copy-start
  5.7 0.9 %copy-done = f32[112,512]{1,0:T(8,128)S(1)} copy-done((f32[112,512]{1,0:T(8,128)S(1)}, f32[112,512]{1,0:T(8,128)}, u32[]{:S(2)}) %copy-start) | copy-done | bytes 229400
  6.6 1.2 %shard_map.167 = (bf16[4,384,1024]{2,1,0:T(8,128)(2,1)S(1)}, bf16[64,48]{1,0:T(8,128)(2,1)S(1)}, bf16[64,192]{1,0:T(8,128)(2,1)S(1)}, bf16[64,32]{1,0:T(8,128)(2...) custom-call(f32[112,512]{1,0:T(8,128)S(1)} %copy-done), custom_call_target="tpu_custom_call" | custom-call | flops 100000000 | bytes 262144 | tf_op jit(solution)/shard_map/pallas_call | solution.py:712
  7.8 1.6 %collective-permute-start.2 = (f32[3,1,512]{2,1,0:T(1,128)S(1)}, f32[3,1,512]{2,1,0:T(1,128)S(1)}, u32[]{:S(2)}, u32[]{:S(2)}) collective-permute-start(f32[3,1,512]{2,1,0:T(1,128)S(1)} %get-tuple-element.37.x_ref), channel_id=1, source_target_pairs={{0,1},{1,2},{2,3},{3,0},{4,5},{5,6},{6,7},{7,4},{8,9},{9,10},{10,1... | collective-permute-start | bytes 18440 | tf_op jit(solution)/shard_map/ppermute | solution.py:724
  9.4 0.0 collective-permute-done.sibling_ref
  9.4 0.0 collective-permute-done.1.across_ref
  9.4 1.3 %shard_map.168 = (f32[40,512]{1,0:T(8,128)S(1)}, f32[40,512]{1,0:T(8,128)S(1)}, bf16[768,1024]{1,0:T(8,128)(2,1)S(1)}, f32[3,1,512]{2,1,0:T(1,128)S(1)}, s32[12,...) custom-call(f32[3,1,512]{2,1,0:T(1,128)S(1)} %get-tuple-element.37.x, ...), custom_call_target="tpu_custom_call" | custom-call | flops 1000000000 | bytes 262144 | tf_op jit(solution)/shard_map/pallas_call | solution.py:712
  10.7 2.7 %collective-permute-start.3 = (f32[3,1,512]{2,1,0:T(1,128)S(1)}, f32[3,1,512]{2,1,0:T(1,128)S(1)}, u32[]{:S(2)}, u32[]{:S(2)}) collective-permute-start(f32[3,1,512]{2,1,0:T(1,128)S(1)} %get-tuple-element.57), channel_id=1, source_target_pairs={{0,3},{1,0},{2,1},{3,2},{4,7},{5,4},{6,5},{7,6},{8,11},{9,8},{10,9... | collective-permute-start | bytes 18440 | tf_op jit(solution)/shard_map/ppermute | solution.py:724
  13.4 0.0 copy-start.2
  13.4 0.0 copy-start.1
  13.4 5.8 %shard_map.169.force_ref = f32[3,512]{1,0:T(4,128)S(1)} custom-call(bf16[4,384,1024]{2,1,0:T(8,128)(2,1)S(1)} %get-tuple-element.47.own_hot.rest_2_, bf16[768,1024]{1,0:T(8,128)(2,1)S(1)} %get-tuple-element.48.side_hot.rest_3_, bf16[64,48]{1,0:T(8,128)(2,1)S(1)} %get-tuple-element.39.rest_0_.rest_4_, bf16[64,192]{1,0:T(8,128)(2,1)S(1)} %get-tuple-element.40.rest_1_.rest_5_, ...), custom_call_target="tpu_custom_call" | custom-call | flops 1000000000 | bytes 262144 | tf_op jit(solution)/shard_map/pallas_call | solution.py:712
  19.2 0.0 collective-permute-done.2.before_ref
  19.2 0.0 collective-permute-done.3.after_ref
  19.2 0.1 shard_map.170
  19.3 0.2 collective-permute-start.4
  19.5 1.5 %collective-permute-start.5 = (f32[8,512]{1,0:T(8,128)S(1)}, f32[8,512]{1,0:T(8,128)S(1)}, u32[]{:S(2)}, u32[]{:S(2)}) collective-permute-start(f32[8,512]{1,0:T(8,128)S(1)} %get-tuple-element.58.own_ref), channel_id=1, source_target_pairs={{0,12},{4,8},{8,4},{12,0},{1,13},{5,9},{9,5},{13,1},{2,14},{6,10},... | collective-permute-start | bytes 49160 | tf_op jit(solution)/shard_map/ppermute | solution.py:724
  20.9 0.5 %collective-permute-start.6 = (f32[8,128]{1,0:T(8,128)S(1)}, f32[8,128]{1,0:T(8,128)S(1)}, u32[]{:S(2)}, u32[]{:S(2)}) collective-permute-start(f32[8,128]{1,0:T(8,128)S(1)} %get-tuple-element.59.rest_0_), channel_id=1, source_target_pairs={{0,8},{4,12},{8,0},{12,4},{1,9},{5,13},{9,1},{13,5},{2,10},{6,14},... | collective-permute-start | bytes 12296 | tf_op jit(solution)/shard_map/ppermute | solution.py:724
  22.8 0.0 copy-done.2
  22.8 0.5 %shard_map.165.number_ref = f32[8,128]{1,0:T(8,128)S(1)} custom-call(f32[1]{0:T(128)S(6)} %copy.19.dt_ref, s32[1,2]{1,0:T(1,128)S(1)} %bitcast.10, s32[1]{0:T(128)S(6)} %copy.20.climb_ref), custom_call_target="tpu_custom_call" | custom-call | bytes 262144 | tf_op jit(solution)/shard_map/pallas_call | solution.py:712
  23.3 1.2 %collective-permute-done.6.rest_1_ = f32[8,128]{1,0:T(8,128)S(1)} collective-permute-done((f32[8,128]{1,0:T(8,128)S(1)}, f32[8,128]{1,0:T(8,128)S(1)}, u32[]{:S(2)}, u32[]{:S(2)}) %collective-permute-start.6) | collective-permute-done | bytes 4128 | tf_op jit(solution)/shard_map/ppermute | solution.py:724
  24.5 0.0 collective-permute-done.4.near_ref
  24.5 0.0 collective-permute-done.5.far_ref
  24.6 0.0 copy-done.1
  24.6 6.6 %shard_map.171 = (f32[1,40,128]{2,1,0:T(8,128)S(1)}, f32[3,128]{1,0:T(4,128)S(1)}) custom-call(f32[8,128]{1,0:T(8,128)S(1)} %shard_map.165.number_ref, f32[40,512]{1,0:T(8,128)S(1)} %get-tuple-element.45.pl_ref, f32[112,512]{1,0:T(8,128)S(1)} %copy-done.1, f32[40,512]{1,0:T(8,128)S(1)} %get-tuple-element.46.pr_ref, f32[8,512]{1,0:T(8,128)S(1)} %get-tuple-element.58.own_ref, ...), custom_call_target="tpu_custom_call" | custom-call | flops 1000000000 | bytes 262144 | tf_op jit(solution)/shard_map/pallas_call | solution.py:712
  31.1 0.0 collective-permute-start.7
  31.1 1.0 %collective-permute-start.8 = (f32[1,40,128]{2,1,0:T(8,128)S(1)}, f32[1,40,128]{2,1,0:T(8,128)S(1)}, u32[]{:S(2)}, u32[]{:S(2)}) collective-permute-start(f32[1,40,128]{2,1,0:T(8,128)S(1)} %get-tuple-element.60.refs_0_.own_ref), channel_id=1, source_target_pairs={{0,2},{1,3},{2,0},{3,1},{4,6},{5,7},{6,4},{7,5},{8,10},{9,11},{10,... | collective-permute-start | bytes 61448 | tf_op jit(solution)/shard_map/ppermute | solution.py:724
  32.1 3.4 %collective-permute-start.9 = (f32[1,40,128]{2,1,0:T(8,128)S(1)}, f32[1,40,128]{2,1,0:T(8,128)S(1)}, u32[]{:S(2)}, u32[]{:S(2)}) collective-permute-start(f32[1,40,128]{2,1,0:T(8,128)S(1)} %get-tuple-element.60.refs_0_.own_ref), channel_id=1, source_target_pairs={{0,3},{1,2},{2,1},{3,0},{4,7},{5,6},{6,5},{7,4},{8,11},{9,10},{10,... | collective-permute-start | bytes 61448 | tf_op jit(solution)/shard_map/ppermute | solution.py:724
  35.5 0.0 collective-permute-done.7.refs_1_
  35.5 0.4 collective-permute-done.8.refs_2_
  36.0 1.8 %collective-permute-done.9.refs_3_ = f32[1,40,128]{2,1,0:T(8,128)S(1)} collective-permute-done((f32[1,40,128]{2,1,0:T(8,128)S(1)}, f32[1,40,128]{2,1,0:T(8,128)S(1)}, u32[]{:S(2)}, u32[]{:S(2)}) %collective-permute-start.9) | collective-permute-done | bytes 20512 | tf_op jit(solution)/shard_map/ppermute | solution.py:724
  37.7 0.2 shard_map.172
  38.0 1.5 %collective-permute-start.10 = (f32[8,128]{1,0:T(8,128)S(1)}, f32[8,128]{1,0:T(8,128)S(1)}, u32[]{:S(2)}, u32[]{:S(2)}) collective-permute-start(f32[8,128]{1,0:T(8,128)S(1)} %get-tuple-element.63.rest_0_), channel_id=1, source_target_pairs={{0,8},{4,12},{8,0},{12,4},{1,9},{5,13},{9,1},{13,5},{2,10},{6,14},... | collective-permute-start | bytes 12296 | tf_op jit(solution)/shard_map/ppermute | solution.py:724
  39.5 0.0 collective-permute-start.11
  39.5 0.7 %collective-permute-start.12 = (f32[8,128]{1,0:T(8,128)S(1)}, f32[8,128]{1,0:T(8,128)S(1)}, u32[]{:S(2)}, u32[]{:S(2)}) collective-permute-start(f32[8,128]{1,0:T(8,128)S(1)} %get-tuple-element.63.rest_0_), channel_id=1, source_target_pairs={{0,4},{4,0},{8,12},{12,8},{1,5},{5,1},{9,13},{13,9},{2,6},{6,2},{1... | collective-permute-start | bytes 12296 | tf_op jit(solution)/shard_map/ppermute | solution.py:724
  40.2 1.5 %collective-permute-done.10.rest_1_ = f32[8,128]{1,0:T(8,128)S(1)} collective-permute-done((f32[8,128]{1,0:T(8,128)S(1)}, f32[8,128]{1,0:T(8,128)S(1)}, u32[]{:S(2)}, u32[]{:S(2)}) %collective-permute-start.10) | collective-permute-done | bytes 4128 | tf_op jit(solution)/shard_map/ppermute | solution.py:724
  41.6 0.9 %collective-permute-done.11.rest_2_ = f32[8,128]{1,0:T(8,128)S(1)} collective-permute-done((f32[8,128]{1,0:T(8,128)S(1)}, f32[8,128]{1,0:T(8,128)S(1)}, u32[]{:S(2)}, u32[]{:S(2)}) %collective-permute-start.11) | collective-permute-done | bytes 4128 | tf_op jit(solution)/shard_map/ppermute | solution.py:724
  42.5 0.0 collective-permute-done.12.rest_3_
  42.5 0.7 %shard_map.173 = (f32[3,1,512]{2,1,0:T(1,128)}, f32[3,1,512]{2,1,0:T(1,128)}, f32[2,1,2]{2,1,0:T(1,128)}, f32[1,1]{1,0:T(1,128)}) custom-call(f32[1,40,128]{2,1,0:T(8,128)S(1)} %get-tuple-element.60.refs_0_.own_ref, f32[3,128]{1,0:T(4,128)S(1)} %get-tuple-element.61.record_ref, f32[40,128]{1,0:T(8,128)S(1)} %get-tuple-element.62.state_ref, ...), custom_call_target="tpu_custom_call" | custom-call | bytes 262144 | tf_op jit(solution)/shard_map/pallas_call | solution.py:712
Async XLA Ops:
  2.5 6.9 %collective-permute-start = (f32[40,512]{1,0:T(8,128)}, f32[40,512]{1,0:T(8,128)S(1)}, u32[]{:S(2)}, u32[]{:S(2)}) collective-permute-start(f32[40,512]{1,0:T(8,128)} %get-tuple-element.38), channel_id=1, source_target_pairs={{0,4},{4,0},{8,12},{12,8},{1,5},{5,1},{9,13},{13,9},{2,6},{6,2},{1... | collective-permute-start | bytes 245768 | tf_op jit(solution)/shard_map/ppermute | solution.py:724
  3.0 6.4 %collective-permute-start.1 = (f32[40,512]{1,0:T(8,128)}, f32[40,512]{1,0:T(8,128)S(1)}, u32[]{:S(2)}, u32[]{:S(2)}) collective-permute-start(f32[40,512]{1,0:T(8,128)} %get-tuple-element.38), channel_id=1, source_target_pairs={{0,12},{4,8},{8,4},{12,0},{1,13},{5,9},{9,5},{13,1},{2,14},{6,10},... | collective-permute-start | bytes 245768 | tf_op jit(solution)/shard_map/ppermute | solution.py:724
  5.7 0.9 %copy-start = (f32[112,512]{1,0:T(8,128)S(1)}, f32[112,512]{1,0:T(8,128)}, u32[]{:S(2)}) copy-start(f32[112,512]{1,0:T(8,128)} %get-tuple-element.36.po_ref) | copy-start | bytes 688132
  7.8 11.4 %collective-permute-start.2 = (f32[3,1,512]{2,1,0:T(1,128)S(1)}, f32[3,1,512]{2,1,0:T(1,128)S(1)}, u32[]{:S(2)}, u32[]{:S(2)}) collective-permute-start(f32[3,1,512]{2,1,0:T(1,128)S(1)} %get-tuple-element.37.x_ref), channel_id=1, source_target_pairs={{0,1},{1,2},{2,3},{3,0},{4,5},{5,6},{6,7},{7,4},{8,9},{9,10},{10,1... | collective-permute-start | bytes 18440 | tf_op jit(solution)/shard_map/ppermute | solution.py:724
  10.7 8.5 %collective-permute-start.3 = (f32[3,1,512]{2,1,0:T(1,128)S(1)}, f32[3,1,512]{2,1,0:T(1,128)S(1)}, u32[]{:S(2)}, u32[]{:S(2)}) collective-permute-start(f32[3,1,512]{2,1,0:T(1,128)S(1)} %get-tuple-element.57), channel_id=1, source_target_pairs={{0,3},{1,0},{2,1},{3,2},{4,7},{5,4},{6,5},{7,6},{8,11},{9,8},{10,9... | collective-permute-start | bytes 18440 | tf_op jit(solution)/shard_map/ppermute | solution.py:724
  13.4 9.4 %copy-start.2 = (s32[2,1]{0,1:T(1,128)S(1)}, s32[2,1]{0,1:T(1,128)}, u32[]{:S(2)}) copy-start(s32[2,1]{0,1:T(1,128)} %param.17) | copy-start | bytes 28
  13.4 11.1 %copy-start.1 = (f32[112,512]{1,0:T(8,128)S(1)}, f32[112,512]{1,0:T(8,128)}, u32[]{:S(2)}) copy-start(f32[112,512]{1,0:T(8,128)} %get-tuple-element.36.po_ref) | copy-start | bytes 688132
  19.3 5.2 %collective-permute-start.4 = (f32[8,512]{1,0:T(8,128)S(1)}, f32[8,512]{1,0:T(8,128)S(1)}, u32[]{:S(2)}, u32[]{:S(2)}) collective-permute-start(f32[8,512]{1,0:T(8,128)S(1)} %get-tuple-element.58.own_ref), channel_id=1, source_target_pairs={{0,4},{4,0},{8,12},{12,8},{1,5},{5,1},{9,13},{13,9},{2,6},{6,2},{1... | collective-permute-start | bytes 49160 | tf_op jit(solution)/shard_map/ppermute | solution.py:724
  19.5 5.1 %collective-permute-start.5 = (f32[8,512]{1,0:T(8,128)S(1)}, f32[8,512]{1,0:T(8,128)S(1)}, u32[]{:S(2)}, u32[]{:S(2)}) collective-permute-start(f32[8,512]{1,0:T(8,128)S(1)} %get-tuple-element.58.own_ref), channel_id=1, source_target_pairs={{0,12},{4,8},{8,4},{12,0},{1,13},{5,9},{9,5},{13,1},{2,14},{6,10},... | collective-permute-start | bytes 49160 | tf_op jit(solution)/shard_map/ppermute | solution.py:724
  20.9 3.6 %collective-permute-start.6 = (f32[8,128]{1,0:T(8,128)S(1)}, f32[8,128]{1,0:T(8,128)S(1)}, u32[]{:S(2)}, u32[]{:S(2)}) collective-permute-start(f32[8,128]{1,0:T(8,128)S(1)} %get-tuple-element.59.rest_0_), channel_id=1, source_target_pairs={{0,8},{4,12},{8,0},{12,4},{1,9},{5,13},{9,1},{13,5},{2,10},{6,14},... | collective-permute-start | bytes 12296 | tf_op jit(solution)/shard_map/ppermute | solution.py:724
  31.1 4.4 %collective-permute-start.7 = (f32[1,40,128]{2,1,0:T(8,128)S(1)}, f32[1,40,128]{2,1,0:T(8,128)S(1)}, u32[]{:S(2)}, u32[]{:S(2)}) collective-permute-start(f32[1,40,128]{2,1,0:T(8,128)S(1)} %get-tuple-element.60.refs_0_.own_ref), channel_id=1, source_target_pairs={{0,1},{1,0},{2,3},{3,2},{4,5},{5,4},{6,7},{7,6},{8,9},{9,8},{10,11... | collective-permute-start | bytes 61448 | tf_op jit(solution)/shard_map/ppermute | solution.py:724
  31.1 4.8 %collective-permute-start.8 = (f32[1,40,128]{2,1,0:T(8,128)S(1)}, f32[1,40,128]{2,1,0:T(8,128)S(1)}, u32[]{:S(2)}, u32[]{:S(2)}) collective-permute-start(f32[1,40,128]{2,1,0:T(8,128)S(1)} %get-tuple-element.60.refs_0_.own_ref), channel_id=1, source_target_pairs={{0,2},{1,3},{2,0},{3,1},{4,6},{5,7},{6,4},{7,5},{8,10},{9,11},{10,... | collective-permute-start | bytes 61448 | tf_op jit(solution)/shard_map/ppermute | solution.py:724
  32.1 5.6 %collective-permute-start.9 = (f32[1,40,128]{2,1,0:T(8,128)S(1)}, f32[1,40,128]{2,1,0:T(8,128)S(1)}, u32[]{:S(2)}, u32[]{:S(2)}) collective-permute-start(f32[1,40,128]{2,1,0:T(8,128)S(1)} %get-tuple-element.60.refs_0_.own_ref), channel_id=1, source_target_pairs={{0,3},{1,2},{2,1},{3,0},{4,7},{5,6},{6,5},{7,4},{8,11},{9,10},{10,... | collective-permute-start | bytes 61448 | tf_op jit(solution)/shard_map/ppermute | solution.py:724
  38.0 3.7 %collective-permute-start.10 = (f32[8,128]{1,0:T(8,128)S(1)}, f32[8,128]{1,0:T(8,128)S(1)}, u32[]{:S(2)}, u32[]{:S(2)}) collective-permute-start(f32[8,128]{1,0:T(8,128)S(1)} %get-tuple-element.63.rest_0_), channel_id=1, source_target_pairs={{0,8},{4,12},{8,0},{12,4},{1,9},{5,13},{9,1},{13,5},{2,10},{6,14},... | collective-permute-start | bytes 12296 | tf_op jit(solution)/shard_map/ppermute | solution.py:724
  39.5 3.0 %collective-permute-start.11 = (f32[8,128]{1,0:T(8,128)S(1)}, f32[8,128]{1,0:T(8,128)S(1)}, u32[]{:S(2)}, u32[]{:S(2)}) collective-permute-start(f32[8,128]{1,0:T(8,128)S(1)} %get-tuple-element.63.rest_0_), channel_id=1, source_target_pairs={{0,12},{4,8},{8,4},{12,0},{1,13},{5,9},{9,5},{13,1},{2,14},{6,10},... | collective-permute-start | bytes 12296 | tf_op jit(solution)/shard_map/ppermute | solution.py:724
  39.5 3.0 %collective-permute-start.12 = (f32[8,128]{1,0:T(8,128)S(1)}, f32[8,128]{1,0:T(8,128)S(1)}, u32[]{:S(2)}, u32[]{:S(2)}) collective-permute-start(f32[8,128]{1,0:T(8,128)S(1)} %get-tuple-element.63.rest_0_), channel_id=1, source_target_pairs={{0,4},{4,0},{8,12},{12,8},{1,5},{5,1},{9,13},{13,9},{2,6},{6,2},{1... | collective-permute-start | bytes 12296 | tf_op jit(solution)/shard_map/ppermute | solution.py:724

commit v11 on v9

--- a/solution.py
+++ b/solution.py
@@ -265,14 +265,13 @@
     (widx, kinds, geo, bst, bps, bpr, sent_all, slope) = kept
     slot = lax.broadcasted_iota(jnp.int32, (SLOTS, LANES), 0)
 
-    def spread(left, b, first, last, sums):
-        ws = reach(b, first, last)
+    def marks(b, ws):
         if b in SIDE_START:
             start = SIDE_START[b] + (ws[0] - reach(b, 3, 8)[0]) * LANES
-            picked = side_hot[start : start + len(ws) * LANES, :]
-        else:
-            picked = own_hot[b - 4, ws[0] * LANES : (ws[-1] + 1) * LANES, :]
-        out = mm_nt(picked, left)
+            return side_hot.at[start : start + len(ws) * LANES]
+        return own_hot.at[b - 4, ws[0] * LANES : (ws[-1] + 1) * LANES]
+
+    def add_rows(sums, first, b, ws, out):
         for i, w in enumerate(ws):
             target = b - 1 + w
             piece = out[i * LANES : (i + 1) * LANES]
@@ -285,7 +284,7 @@
 
     started = set()
 
-    def gather_and_return(b):
+    def block_work(b):
         index = widx[b]
         inner, part = index & (LANES - 1), index >> 7
         basis = bst[b]
@@ -318,13 +317,31 @@
                 if 3 <= b <= 8:
                     pull = got[k] * back * steepness[rows, cols]
                     total[k] = total[k] + pull[0:8] + pull[8:16]
-        spread(value[...], b, 3, 8, dg)
+            yield
         if 3 <= b <= 8:
             for k in range(SLOTS):
                 pulls[b, :, k * LANES : (k + 1) * LANES] = total[k]
 
-    for b in range(2, 10):
-        gather_and_return(b)
+    def scatter_work(b):
+        ws = reach(b, 3, 8)
+        chosen, value = marks(b, ws), held.at[b % 2]
+        out = None
+        for u in range(4):
+            cols = slice(u * 2 * LANES, (u + 1) * 2 * LANES)
+            one = mm_nt(chosen[:, cols], value[:, cols])
+            out = one if out is None else out + one
+            yield
+        add_rows(dg, 3, b, ws, out)
+
+    def together(*works):
+        works = list(works)
+        while works:
+            works = [work for work in works if next(work, "end") != "end"]
+
+    together(block_work(2))
+    for b in range(3, 10):
+        together(scatter_work(b - 1), block_work(b))
+    together(scatter_work(9))
 
     def finish(b, sums):
         kind = kinds[b]
@@ -344,7 +361,20 @@
         for h in range(2):
             for c in range(3):
                 lines.append(jnp.concatenate([jnp.where(slot == k, pieces[c][h], 0.0) for k in range(SLOTS)], axis=1))
-        spread(jnp.concatenate(lines, axis=0).astype(BF16), b, 4, 7, met)
+        ws = reach(b, 4, 7)
+        out = mm_nt(jnp.concatenate(lines, axis=0).astype(BF16), marks(b, ws)[...])
+        for c in range(3):
+            both = out[8 * c : 8 * c + 8] + out[24 + 8 * c : 32 + 8 * c]
+            for i, w in enumerate(ws):
+                target = b - 5 + w
+                piece = both[:, i * LANES : (i + 1) * LANES]
+                if (c, target) in met_blocks:
+                    met[target, c] += piece
+                else:
+                    met[target, c] = piece
+                    met_blocks.add((c, target))
+
+    met_blocks = set()
 
     for b in range(3, 9, 2):
         cols = slice(b * LANES, (b + 2) * LANES)
@@ -355,14 +385,11 @@
         for i in range(2):
             finish(b + i, sums[:, i * LANES : (i + 1) * LANES])
 
-    high, low = split(met[...])
-    column = lax.broadcasted_iota(jnp.int32, (16, 6 * SLOTS), 1)
-    column = jnp.where(column < 3 * SLOTS, column, column - 3 * SLOTS)
-    first = SLOTS * lax.broadcasted_iota(jnp.int32, (16, 6 * SLOTS), 0)
-    choose = jnp.where((column >= first) & (column < first + SLOTS), 1.0, 0.0).astype(BF16)
-    back = mm_nt(choose, high.astype(BF16)) + mm_nt(choose, low.astype(BF16))
-    away = [jnp.concatenate([acc[i, c] for i in range(SLAB_BLOCKS)], axis=1) for c in range(3)]
-    return jnp.concatenate(away, axis=0) - back[0:3]
+    away = []
+    for c in range(3):
+        back = [acc[i, c] - jnp.sum(met[i, c], axis=0, keepdims=True) for i in range(SLAB_BLOCKS)]
+        away.append(jnp.concatenate(back, axis=1))
+    return jnp.concatenate(away, axis=0)
 
 
 def fill_region(xs, packs, rows_of):
@@ -404,7 +431,7 @@
     return [
         pltpu.VMEM((6 * LANES, 2 * CHANNELS), F32),
         pltpu.VMEM((12, 8, SLOTS * LANES), F32),
-        pltpu.VMEM((SLAB_BLOCKS * LANES, 6 * SLOTS), F32),
+        pltpu.VMEM((SLAB_BLOCKS, 3, SLOTS, LANES), F32),
         pltpu.VMEM((SLAB_BLOCKS, 3, 1, LANES), F32),
         pltpu.VMEM((2, 2 * CHANNELS, SLOTS * LANES), BF16),
     ]

time: 42.2 us -> 41.9 us (level)
  no operation moved by 1% of the time
where the time goes in v11:
time: 41.9 us; the launch traced here: 41.7 us
  Pallas kernels  16.6 us (40%)
  starting transfers between devices  16.3 us (39%)
  waiting for transfers between devices  5.8 us (14%)
  between operations  2.03 us (5%)
  local copies, waits for them, and re-layouts  0.95 us (2%)
    pallas_call x9, Pallas kernels, call(): pl.pallas_call(body, out_shape=outs, in_specs=[SMEM_SPEC] * len(scalars)...  16.6 us
    ppermute x13, starting transfers between devices, swap(): lax.ppermute(array, axis, [(i, partner(i)) for i in range(lax.axis_size(a...  16.3 us
    ppermute x13, waiting for transfers between devices, swap(): lax.ppermute(array, axis, [(i, partner(i)) for i in range(lax.axis_size(a...  5.8 us
    unnamed x6, local copies, waits for them, and re-layouts  0.95 us
  transfers between devices with their start and end apart: 13, of which 5 were waited for; matrix products, arithmetic and copies ran while one was open for 0% of the time, Pallas kernels for 19%

profile of v11, /device:TPU:0, one launch (start us, length us, event | category | flops | bytes accessed | tf_op | source)
XLA Modules:
  0.0 41.7 jit_solution(16520776202838914784)
XLA Ops:
  0.6 1.9 %shard_map.166 = (f32[40,512]{1,0:T(8,128)}, f32[112,512]{1,0:T(8,128)}) custom-call(f32[3,1,512]{2,1,0:T(1,128)} %bitcast.12, f32[3,1,512]{2,1,0:T(1,128)} %bitcast.13, s32[512]{0:T(512)} %refs_2_.1, s32[8,512]{1,0:T(8,128)} %refs_3_.1, s32[512]{0:T(512)} %refs_4_.1, f32[2,64]{1,0:T(2,128)} %refs_5_.1, f32[64]{0:T(128)} %refs_6_.1, f32[2,8,64]{2,1,0:T(8,128)} %refs_7_.1, ...), custom_call_target="tpu_custom_call" | custom-call | bytes 262144 | tf_op jit(solution)/shard_map/pallas_call | solution.py:720
  2.5 0.5 %collective-permute-start = (f32[40,512]{1,0:T(8,128)}, f32[40,512]{1,0:T(8,128)S(1)}, u32[]{:S(2)}, u32[]{:S(2)}) collective-permute-start(f32[40,512]{1,0:T(8,128)} %get-tuple-element.38), channel_id=1, source_target_pairs={{0,4},{4,0},{8,12},{12,8},{1,5},{5,1},{9,13},{13,9},{2,6},{6,2},{1... | collective-permute-start | bytes 245768 | tf_op jit(solution)/shard_map/ppermute | solution.py:732
  3.0 2.6 %collective-permute-start.1 = (f32[40,512]{1,0:T(8,128)}, f32[40,512]{1,0:T(8,128)S(1)}, u32[]{:S(2)}, u32[]{:S(2)}) collective-permute-start(f32[40,512]{1,0:T(8,128)} %get-tuple-element.38), channel_id=1, source_target_pairs={{0,12},{4,8},{8,4},{12,0},{1,13},{5,9},{9,5},{13,1},{2,14},{6,10},... | collective-permute-start | bytes 245768 | tf_op jit(solution)/shard_map/ppermute | solution.py:732
  5.7 0.0 copy-start
  5.7 0.9 %copy-done = f32[112,512]{1,0:T(8,128)S(1)} copy-done((f32[112,512]{1,0:T(8,128)S(1)}, f32[112,512]{1,0:T(8,128)}, u32[]{:S(2)}) %copy-start) | copy-done | bytes 229400
  6.6 1.2 %shard_map.167 = (bf16[4,384,1024]{2,1,0:T(8,128)(2,1)S(1)}, bf16[64,48]{1,0:T(8,128)(2,1)S(1)}, bf16[64,192]{1,0:T(8,128)(2,1)S(1)}, bf16[64,32]{1,0:T(8,128)(2...) custom-call(f32[112,512]{1,0:T(8,128)S(1)} %copy-done), custom_call_target="tpu_custom_call" | custom-call | flops 100000000 | bytes 262144 | tf_op jit(solution)/shard_map/pallas_call | solution.py:720
  7.8 1.6 %collective-permute-start.2 = (f32[3,1,512]{2,1,0:T(1,128)S(1)}, f32[3,1,512]{2,1,0:T(1,128)S(1)}, u32[]{:S(2)}, u32[]{:S(2)}) collective-permute-start(f32[3,1,512]{2,1,0:T(1,128)S(1)} %get-tuple-element.37.x_ref), channel_id=1, source_target_pairs={{0,1},{1,2},{2,3},{3,0},{4,5},{5,6},{6,7},{7,4},{8,9},{9,10},{10,1... | collective-permute-start | bytes 18440 | tf_op jit(solution)/shard_map/ppermute | solution.py:732
  9.4 0.0 collective-permute-done.sibling_ref
  9.4 0.0 collective-permute-done.1.across_ref
  9.4 1.3 %shard_map.168 = (f32[40,512]{1,0:T(8,128)S(1)}, f32[40,512]{1,0:T(8,128)S(1)}, bf16[768,1024]{1,0:T(8,128)(2,1)S(1)}, f32[3,1,512]{2,1,0:T(1,128)S(1)}, s32[12,...) custom-call(f32[3,1,512]{2,1,0:T(1,128)S(1)} %get-tuple-element.37.x, ...), custom_call_target="tpu_custom_call" | custom-call | flops 1000000000 | bytes 262144 | tf_op jit(solution)/shard_map/pallas_call | solution.py:720
  10.7 2.7 %collective-permute-start.3 = (f32[3,1,512]{2,1,0:T(1,128)S(1)}, f32[3,1,512]{2,1,0:T(1,128)S(1)}, u32[]{:S(2)}, u32[]{:S(2)}) collective-permute-start(f32[3,1,512]{2,1,0:T(1,128)S(1)} %get-tuple-element.57), channel_id=1, source_target_pairs={{0,3},{1,0},{2,1},{3,2},{4,7},{5,4},{6,5},{7,6},{8,11},{9,8},{10,9... | collective-permute-start | bytes 18440 | tf_op jit(solution)/shard_map/ppermute | solution.py:732
  13.4 0.0 copy-start.2
  13.4 0.0 copy-start.1
  13.4 5.0 %shard_map.169.force_ref = f32[3,512]{1,0:T(4,128)S(1)} custom-call(bf16[4,384,1024]{2,1,0:T(8,128)(2,1)S(1)} %get-tuple-element.47.own_hot.rest_2_, bf16[768,1024]{1,0:T(8,128)(2,1)S(1)} %get-tuple-element.48.side_hot.rest_3_, bf16[64,48]{1,0:T(8,128)(2,1)S(1)} %get-tuple-element.39.rest_0_.rest_4_, bf16[64,192]{1,0:T(8,128)(2,1)S(1)} %get-tuple-element.40.rest_1_.rest_5_, ...), custom_call_target="tpu_custom_call" | custom-call | flops 1000000000 | bytes 262144 | tf_op jit(solution)/shard_map/pallas_call | solution.py:720
  18.4 0.0 collective-permute-done.2.before_ref
  18.4 0.0 collective-permute-done.3.after_ref
  18.4 0.1 shard_map.170
  18.5 0.2 collective-permute-start.4
  18.7 1.5 %collective-permute-start.5 = (f32[8,512]{1,0:T(8,128)S(1)}, f32[8,512]{1,0:T(8,128)S(1)}, u32[]{:S(2)}, u32[]{:S(2)}) collective-permute-start(f32[8,512]{1,0:T(8,128)S(1)} %get-tuple-element.58.own_ref), channel_id=1, source_target_pairs={{0,12},{4,8},{8,4},{12,0},{1,13},{5,9},{9,5},{13,1},{2,14},{6,10},... | collective-permute-start | bytes 49160 | tf_op jit(solution)/shard_map/ppermute | solution.py:732
  20.1 0.5 %collective-permute-start.6 = (f32[8,128]{1,0:T(8,128)S(1)}, f32[8,128]{1,0:T(8,128)S(1)}, u32[]{:S(2)}, u32[]{:S(2)}) collective-permute-start(f32[8,128]{1,0:T(8,128)S(1)} %get-tuple-element.59.rest_0_), channel_id=1, source_target_pairs={{0,8},{4,12},{8,0},{12,4},{1,9},{5,13},{9,1},{13,5},{2,10},{6,14},... | collective-permute-start | bytes 12296 | tf_op jit(solution)/shard_map/ppermute | solution.py:732
  22.0 0.0 copy-done.2
  22.0 0.5 %shard_map.165.number_ref = f32[8,128]{1,0:T(8,128)S(1)} custom-call(f32[1]{0:T(128)S(6)} %copy.19.dt_ref, s32[1,2]{1,0:T(1,128)S(1)} %bitcast.10, s32[1]{0:T(128)S(6)} %copy.20.climb_ref), custom_call_target="tpu_custom_call" | custom-call | bytes 262144 | tf_op jit(solution)/shard_map/pallas_call | solution.py:720
  22.5 1.2 %collective-permute-done.6.rest_1_ = f32[8,128]{1,0:T(8,128)S(1)} collective-permute-done((f32[8,128]{1,0:T(8,128)S(1)}, f32[8,128]{1,0:T(8,128)S(1)}, u32[]{:S(2)}, u32[]{:S(2)}) %collective-permute-start.6) | collective-permute-done | bytes 4128 | tf_op jit(solution)/shard_map/ppermute | solution.py:732
  23.8 0.0 collective-permute-done.4.near_ref
  23.8 0.0 collective-permute-done.5.far_ref
  23.8 0.0 copy-done.1
  23.8 5.7 %shard_map.171 = (f32[1,40,128]{2,1,0:T(8,128)S(1)}, f32[3,128]{1,0:T(4,128)S(1)}) custom-call(f32[8,128]{1,0:T(8,128)S(1)} %shard_map.165.number_ref, f32[40,512]{1,0:T(8,128)S(1)} %get-tuple-element.45.pl_ref, f32[112,512]{1,0:T(8,128)S(1)} %copy-done.1, f32[40,512]{1,0:T(8,128)S(1)} %get-tuple-element.46.pr_ref, f32[8,512]{1,0:T(8,128)S(1)} %get-tuple-element.58.own_ref, ...), custom_call_target="tpu_custom_call" | custom-call | flops 1000000000 | bytes 262144 | tf_op jit(solution)/shard_map/pallas_call | solution.py:720
  29.5 0.1 collective-permute-start.7
  29.6 1.0 %collective-permute-start.8 = (f32[1,40,128]{2,1,0:T(8,128)S(1)}, f32[1,40,128]{2,1,0:T(8,128)S(1)}, u32[]{:S(2)}, u32[]{:S(2)}) collective-permute-start(f32[1,40,128]{2,1,0:T(8,128)S(1)} %get-tuple-element.60.refs_0_.own_ref), channel_id=1, source_target_pairs={{0,2},{1,3},{2,0},{3,1},{4,6},{5,7},{6,4},{7,5},{8,10},{9,11},{10,... | collective-permute-start | bytes 61448 | tf_op jit(solution)/shard_map/ppermute | solution.py:732
  30.6 3.4 %collective-permute-start.9 = (f32[1,40,128]{2,1,0:T(8,128)S(1)}, f32[1,40,128]{2,1,0:T(8,128)S(1)}, u32[]{:S(2)}, u32[]{:S(2)}) collective-permute-start(f32[1,40,128]{2,1,0:T(8,128)S(1)} %get-tuple-element.60.refs_0_.own_ref), channel_id=1, source_target_pairs={{0,3},{1,2},{2,1},{3,0},{4,7},{5,6},{6,5},{7,4},{8,11},{9,10},{10,... | collective-permute-start | bytes 61448 | tf_op jit(solution)/shard_map/ppermute | solution.py:732
  33.9 0.0 collective-permute-done.7.refs_1_
  33.9 0.4 %collective-permute-done.8.refs_2_ = f32[1,40,128]{2,1,0:T(8,128)S(1)} collective-permute-done((f32[1,40,128]{2,1,0:T(8,128)S(1)}, f32[1,40,128]{2,1,0:T(8,128)S(1)}, u32[]{:S(2)}, u32[]{:S(2)}) %collective-permute-start.8) | collective-permute-done | bytes 20512 | tf_op jit(solution)/shard_map/ppermute | solution.py:732
  34.4 1.8 %collective-permute-done.9.refs_3_ = f32[1,40,128]{2,1,0:T(8,128)S(1)} collective-permute-done((f32[1,40,128]{2,1,0:T(8,128)S(1)}, f32[1,40,128]{2,1,0:T(8,128)S(1)}, u32[]{:S(2)}, u32[]{:S(2)}) %collective-permute-start.9) | collective-permute-done | bytes 20512 | tf_op jit(solution)/shard_map/ppermute | solution.py:732
  36.1 0.2 shard_map.172
  36.4 1.5 %collective-permute-start.10 = (f32[8,128]{1,0:T(8,128)S(1)}, f32[8,128]{1,0:T(8,128)S(1)}, u32[]{:S(2)}, u32[]{:S(2)}) collective-permute-start(f32[8,128]{1,0:T(8,128)S(1)} %get-tuple-element.63.rest_0_), channel_id=1, source_target_pairs={{0,8},{4,12},{8,0},{12,4},{1,9},{5,13},{9,1},{13,5},{2,10},{6,14},... | collective-permute-start | bytes 12296 | tf_op jit(solution)/shard_map/ppermute | solution.py:732
  37.9 0.0 collective-permute-start.11
  37.9 0.7 %collective-permute-start.12 = (f32[8,128]{1,0:T(8,128)S(1)}, f32[8,128]{1,0:T(8,128)S(1)}, u32[]{:S(2)}, u32[]{:S(2)}) collective-permute-start(f32[8,128]{1,0:T(8,128)S(1)} %get-tuple-element.63.rest_0_), channel_id=1, source_target_pairs={{0,4},{4,0},{8,12},{12,8},{1,5},{5,1},{9,13},{13,9},{2,6},{6,2},{1... | collective-permute-start | bytes 12296 | tf_op jit(solution)/shard_map/ppermute | solution.py:732
  38.6 1.5 %collective-permute-done.10.rest_1_ = f32[8,128]{1,0:T(8,128)S(1)} collective-permute-done((f32[8,128]{1,0:T(8,128)S(1)}, f32[8,128]{1,0:T(8,128)S(1)}, u32[]{:S(2)}, u32[]{:S(2)}) %collective-permute-start.10) | collective-permute-done | bytes 4128 | tf_op jit(solution)/shard_map/ppermute | solution.py:732
  40.0 0.9 %collective-permute-done.11.rest_2_ = f32[8,128]{1,0:T(8,128)S(1)} collective-permute-done((f32[8,128]{1,0:T(8,128)S(1)}, f32[8,128]{1,0:T(8,128)S(1)}, u32[]{:S(2)}, u32[]{:S(2)}) %collective-permute-start.11) | collective-permute-done | bytes 4128 | tf_op jit(solution)/shard_map/ppermute | solution.py:732
  40.9 0.0 collective-permute-done.12.rest_3_
  40.9 0.7 %shard_map.173 = (f32[3,1,512]{2,1,0:T(1,128)}, f32[3,1,512]{2,1,0:T(1,128)}, f32[2,1,2]{2,1,0:T(1,128)}, f32[1,1]{1,0:T(1,128)}) custom-call(f32[1,40,128]{2,1,0:T(8,128)S(1)} %get-tuple-element.60.refs_0_.own_ref, f32[3,128]{1,0:T(4,128)S(1)} %get-tuple-element.61.record_ref, f32[40,128]{1,0:T(8,128)S(1)} %get-tuple-element.62.state_ref, ...), custom_call_target="tpu_custom_call" | custom-call | bytes 262144 | tf_op jit(solution)/shard_map/pallas_call | solution.py:720
Async XLA Ops:
  2.5 6.9 %collective-permute-start = (f32[40,512]{1,0:T(8,128)}, f32[40,512]{1,0:T(8,128)S(1)}, u32[]{:S(2)}, u32[]{:S(2)}) collective-permute-start(f32[40,512]{1,0:T(8,128)} %get-tuple-element.38), channel_id=1, source_target_pairs={{0,4},{4,0},{8,12},{12,8},{1,5},{5,1},{9,13},{13,9},{2,6},{6,2},{1... | collective-permute-start | bytes 245768 | tf_op jit(solution)/shard_map/ppermute | solution.py:732
  3.0 6.4 %collective-permute-start.1 = (f32[40,512]{1,0:T(8,128)}, f32[40,512]{1,0:T(8,128)S(1)}, u32[]{:S(2)}, u32[]{:S(2)}) collective-permute-start(f32[40,512]{1,0:T(8,128)} %get-tuple-element.38), channel_id=1, source_target_pairs={{0,12},{4,8},{8,4},{12,0},{1,13},{5,9},{9,5},{13,1},{2,14},{6,10},... | collective-permute-start | bytes 245768 | tf_op jit(solution)/shard_map/ppermute | solution.py:732
  5.7 0.9 %copy-start = (f32[112,512]{1,0:T(8,128)S(1)}, f32[112,512]{1,0:T(8,128)}, u32[]{:S(2)}) copy-start(f32[112,512]{1,0:T(8,128)} %get-tuple-element.36.po_ref) | copy-start | bytes 688132
  7.8 10.6 %collective-permute-start.2 = (f32[3,1,512]{2,1,0:T(1,128)S(1)}, f32[3,1,512]{2,1,0:T(1,128)S(1)}, u32[]{:S(2)}, u32[]{:S(2)}) collective-permute-start(f32[3,1,512]{2,1,0:T(1,128)S(1)} %get-tuple-element.37.x_ref), channel_id=1, source_target_pairs={{0,1},{1,2},{2,3},{3,0},{4,5},{5,6},{6,7},{7,4},{8,9},{9,10},{10,1... | collective-permute-start | bytes 18440 | tf_op jit(solution)/shard_map/ppermute | solution.py:732
  10.7 7.7 %collective-permute-start.3 = (f32[3,1,512]{2,1,0:T(1,128)S(1)}, f32[3,1,512]{2,1,0:T(1,128)S(1)}, u32[]{:S(2)}, u32[]{:S(2)}) collective-permute-start(f32[3,1,512]{2,1,0:T(1,128)S(1)} %get-tuple-element.57), channel_id=1, source_target_pairs={{0,3},{1,0},{2,1},{3,2},{4,7},{5,4},{6,5},{7,6},{8,11},{9,8},{10,9... | collective-permute-start | bytes 18440 | tf_op jit(solution)/shard_map/ppermute | solution.py:732
  13.4 8.6 %copy-start.2 = (s32[2,1]{0,1:T(1,128)S(1)}, s32[2,1]{0,1:T(1,128)}, u32[]{:S(2)}) copy-start(s32[2,1]{0,1:T(1,128)} %param.17) | copy-start | bytes 28
  13.4 10.4 %copy-start.1 = (f32[112,512]{1,0:T(8,128)S(1)}, f32[112,512]{1,0:T(8,128)}, u32[]{:S(2)}) copy-start(f32[112,512]{1,0:T(8,128)} %get-tuple-element.36.po_ref) | copy-start | bytes 688132
  18.5 5.2 %collective-permute-start.4 = (f32[8,512]{1,0:T(8,128)S(1)}, f32[8,512]{1,0:T(8,128)S(1)}, u32[]{:S(2)}, u32[]{:S(2)}) collective-permute-start(f32[8,512]{1,0:T(8,128)S(1)} %get-tuple-element.58.own_ref), channel_id=1, source_target_pairs={{0,4},{4,0},{8,12},{12,8},{1,5},{5,1},{9,13},{13,9},{2,6},{6,2},{1... | collective-permute-start | bytes 49160 | tf_op jit(solution)/shard_map/ppermute | solution.py:732
  18.7 5.1 %collective-permute-start.5 = (f32[8,512]{1,0:T(8,128)S(1)}, f32[8,512]{1,0:T(8,128)S(1)}, u32[]{:S(2)}, u32[]{:S(2)}) collective-permute-start(f32[8,512]{1,0:T(8,128)S(1)} %get-tuple-element.58.own_ref), channel_id=1, source_target_pairs={{0,12},{4,8},{8,4},{12,0},{1,13},{5,9},{9,5},{13,1},{2,14},{6,10},... | collective-permute-start | bytes 49160 | tf_op jit(solution)/shard_map/ppermute | solution.py:732
  20.1 3.6 %collective-permute-start.6 = (f32[8,128]{1,0:T(8,128)S(1)}, f32[8,128]{1,0:T(8,128)S(1)}, u32[]{:S(2)}, u32[]{:S(2)}) collective-permute-start(f32[8,128]{1,0:T(8,128)S(1)} %get-tuple-element.59.rest_0_), channel_id=1, source_target_pairs={{0,8},{4,12},{8,0},{12,4},{1,9},{5,13},{9,1},{13,5},{2,10},{6,14},... | collective-permute-start | bytes 12296 | tf_op jit(solution)/shard_map/ppermute | solution.py:732
  29.5 4.5 %collective-permute-start.7 = (f32[1,40,128]{2,1,0:T(8,128)S(1)}, f32[1,40,128]{2,1,0:T(8,128)S(1)}, u32[]{:S(2)}, u32[]{:S(2)}) collective-permute-start(f32[1,40,128]{2,1,0:T(8,128)S(1)} %get-tuple-element.60.refs_0_.own_ref), channel_id=1, source_target_pairs={{0,1},{1,0},{2,3},{3,2},{4,5},{5,4},{6,7},{7,6},{8,9},{9,8},{10,11... | collective-permute-start | bytes 61448 | tf_op jit(solution)/shard_map/ppermute | solution.py:732
  29.6 4.8 %collective-permute-start.8 = (f32[1,40,128]{2,1,0:T(8,128)S(1)}, f32[1,40,128]{2,1,0:T(8,128)S(1)}, u32[]{:S(2)}, u32[]{:S(2)}) collective-permute-start(f32[1,40,128]{2,1,0:T(8,128)S(1)} %get-tuple-element.60.refs_0_.own_ref), channel_id=1, source_target_pairs={{0,2},{1,3},{2,0},{3,1},{4,6},{5,7},{6,4},{7,5},{8,10},{9,11},{10,... | collective-permute-start | bytes 61448 | tf_op jit(solution)/shard_map/ppermute | solution.py:732
  30.6 5.6 %collective-permute-start.9 = (f32[1,40,128]{2,1,0:T(8,128)S(1)}, f32[1,40,128]{2,1,0:T(8,128)S(1)}, u32[]{:S(2)}, u32[]{:S(2)}) collective-permute-start(f32[1,40,128]{2,1,0:T(8,128)S(1)} %get-tuple-element.60.refs_0_.own_ref), channel_id=1, source_target_pairs={{0,3},{1,2},{2,1},{3,0},{4,7},{5,6},{6,5},{7,4},{8,11},{9,10},{10,... | collective-permute-start | bytes 61448 | tf_op jit(solution)/shard_map/ppermute | solution.py:732
  36.4 3.7 %collective-permute-start.10 = (f32[8,128]{1,0:T(8,128)S(1)}, f32[8,128]{1,0:T(8,128)S(1)}, u32[]{:S(2)}, u32[]{:S(2)}) collective-permute-start(f32[8,128]{1,0:T(8,128)S(1)} %get-tuple-element.63.rest_0_), channel_id=1, source_target_pairs={{0,8},{4,12},{8,0},{12,4},{1,9},{5,13},{9,1},{13,5},{2,10},{6,14},... | collective-permute-start | bytes 12296 | tf_op jit(solution)/shard_map/ppermute | solution.py:732
  37.9 3.0 %collective-permute-start.11 = (f32[8,128]{1,0:T(8,128)S(1)}, f32[8,128]{1,0:T(8,128)S(1)}, u32[]{:S(2)}, u32[]{:S(2)}) collective-permute-start(f32[8,128]{1,0:T(8,128)S(1)} %get-tuple-element.63.rest_0_), channel_id=1, source_target_pairs={{0,12},{4,8},{8,4},{12,0},{1,13},{5,9},{9,5},{13,1},{2,14},{6,10},... | collective-permute-start | bytes 12296 | tf_op jit(solution)/shard_map/ppermute | solution.py:732
  37.9 3.0 %collective-permute-start.12 = (f32[8,128]{1,0:T(8,128)S(1)}, f32[8,128]{1,0:T(8,128)S(1)}, u32[]{:S(2)}, u32[]{:S(2)}) collective-permute-start(f32[8,128]{1,0:T(8,128)S(1)} %get-tuple-element.63.rest_0_), channel_id=1, source_target_pairs={{0,4},{4,0},{8,12},{12,8},{1,5},{5,1},{9,13},{13,9},{2,6},{6,2},{1... | collective-permute-start | bytes 12296 | tf_op jit(solution)/shard_map/ppermute | solution.py:732

commit v12 on v11

--- a/solution.py
+++ b/solution.py
@@ -187,7 +187,7 @@
 
 def forward_parts(packs, weights, xs, sst, kept):
     l1, l2, l3, l5, l6, col = weights
-    (widx, kinds, geo, bst, bps, bpr, sent_all, slope) = kept
+    (widx, kinds, geo, bst, bps, bpr, sent_all, sent_pair, slope) = kept
     centre = 2.0 + 0.5 * lax.broadcasted_iota(jnp.int32, (BASIS, LANES), 0).astype(F32)
     slot = lax.broadcasted_iota(jnp.int32, (SLOTS, LANES), 0)
 
@@ -257,12 +257,14 @@
             one = sent[:, i * LANES : (i + 1) * LANES]
             one = one + col[0] + col[1] * jnp.broadcast_to(xs[b + i, 3:4, :], (CHANNELS, LANES))
             sent_all[:, (b + i) * LANES : (b + i + 1) * LANES] = one
+            if 3 <= b + i <= 8:
+                sent_pair[:, (b + i) * LANES : (b + i + 1) * LANES] = pair_stack(one)
         slope[:, cols] = steep
 
 
 def force_parts(weights, own_hot, side_hot, kept, dg, pulls, met, acc, held):
     l1, l2, l3, l5, l6, col = weights
-    (widx, kinds, geo, bst, bps, bpr, sent_all, slope) = kept
+    (widx, kinds, geo, bst, bps, bpr, sent_all, sent_pair, slope) = kept
     slot = lax.broadcasted_iota(jnp.int32, (SLOTS, LANES), 0)
 
     def marks(b, ws):
@@ -294,6 +296,9 @@
             steepness = mm(l3[...], jnp.concatenate([basis, basis], axis=0))
         lanes = [jnp.broadcast_to(inner[k : k + 1, :], (16, LANES)) for k in range(SLOTS)]
         parts = [jnp.broadcast_to(part[k : k + 1, :], (16, LANES)) for k in range(SLOTS)]
+        own = 4 <= b <= 7
+        if own:
+            found_all = mm(sent_pair[:, (b - 1) * LANES : (b + 2) * LANES], own_hot[b - 4])
         value = held.at[b % 2]
         total = [jnp.zeros((8, LANES), F32)] * SLOTS
         for u in range(CHANNELS // 16):
@@ -304,8 +309,11 @@
             message = jnp.zeros((16, LANES), F32)
             for k in range(SLOTS):
                 cols = slice(k * LANES, (k + 1) * LANES)
-                found = [pick(window, lanes[k]) for window in windows]
-                got.append(jnp.where(parts[k] == 0, found[0], jnp.where(parts[k] == 1, found[1], found[2])))
+                if own:
+                    got.append(found_all[rows, cols] + found_all[low_rows, cols])
+                else:
+                    found = [pick(window, lanes[k]) for window in windows]
+                    got.append(jnp.where(parts[k] == 0, found[0], jnp.where(parts[k] == 1, found[1], found[2])))
                 message = message + radial[rows, cols] * got[k]
             _, steep = silu_parts(message)
             back = col[3, rows] * steep
@@ -419,6 +427,7 @@
         ((12, 16, SLOTS * LANES), BF16),
         ((12, 8, SLOTS * LANES), F32),
         ((CHANNELS, wide), F32),
+        ((2 * CHANNELS, wide), BF16),
         ((CHANNELS, wide), F32),
     ]
 
@@ -443,7 +452,7 @@
 
 
 def first_kernel(x_ref, sibling_ref, po_ref, across_ref, *rest):
-    weights, (pl_ref, pr_ref, side_hot, copy_ref), kept, (xs, sst) = rest[:6], rest[6:10], rest[10:18], rest[18:]
+    weights, (pl_ref, pr_ref, side_hot, copy_ref), kept, (xs, sst) = rest[:6], rest[6:10], rest[10:19], rest[19:]
     copy_ref[...] = x_ref[...]
     pl_ref[...], pr_ref[...] = by_parity(sibling_ref[...], across_ref[...])
     packs = [pl_ref, po_ref, pr_ref]
@@ -453,7 +462,7 @@
 
 
 def first_back_kernel(own_hot, side_hot, *rest):
-    weights, kept, out_ref, scr = rest[:6], rest[6:14], rest[14], rest[15:]
+    weights, kept, out_ref, scr = rest[:6], rest[6:15], rest[15], rest[16:]
     out_ref[...] = force_parts(weights, own_hot, side_hot, kept, *scr)
 
 
@@ -575,10 +584,10 @@
         for p, m in zip(packs, messages)
     ]
     moved = [p[ROW_X : ROW_X + 3, :] + wide(dt) * s for p, s in zip(packs, speeds)]
-    xs, sst, kept = scr[0], scr[1], scr[2:10]
+    xs, sst, kept = scr[0], scr[1], scr[2:11]
     fill_region(xs, packs, lambda s: moved[s])
     forward_parts(packs, weights, xs, sst, kept)
-    force = force_parts(weights, own_hot, side_hot, kept, *scr[10:])
+    force = force_parts(weights, own_hot, side_hot, kept, *scr[11:])
     for c in range(3):
         for i in range(SLAB_BLOCKS):
             lanes = slice(i * LANES, (i + 1) * LANES)

time: 41.9 us -> 41.3 us (0.986)
  Pallas kernels: 16.6 us -> 16 us
    pallas_call x9, Pallas kernels: 16.6 us -> 16 us  [call(): pl.pallas_call(body, out_shape=outs, in_specs=[SMEM_SPEC] * len(scalars)...]
where the time goes in v12:
time: 41.3 us; the launch traced here: 41 us
  starting transfers between devices  16.3 us (39%)
  Pallas kernels  16 us (39%)
  waiting for transfers between devices  5.8 us (14%)
  between operations  2.03 us (5%)
  local copies, waits for them, and re-layouts  0.95 us (2%)
    ppermute x13, starting transfers between devices, swap(): lax.ppermute(array, axis, [(i, partner(i)) for i in range(lax.axis_size(a...  16.3 us
    pallas_call x9, Pallas kernels, call(): pl.pallas_call(body, out_shape=outs, in_specs=[SMEM_SPEC] * len(scalars)...  16 us
    ppermute x13, waiting for transfers between devices, swap(): lax.ppermute(array, axis, [(i, partner(i)) for i in range(lax.axis_size(a...  5.8 us
    unnamed x6, local copies, waits for them, and re-layouts  0.95 us
  transfers between devices with their start and end apart: 13, of which 5 were waited for; matrix products, arithmetic and copies ran while one was open for 0% of the time, Pallas kernels for 19%

profile of v12, /device:TPU:0, one launch (start us, length us, event | category | flops | bytes accessed | tf_op | source)
XLA Modules:
  0.0 41.0 jit_solution(13847382905605783374)
XLA Ops:
  0.6 1.9 %shard_map.166 = (f32[40,512]{1,0:T(8,128)}, f32[112,512]{1,0:T(8,128)}) custom-call(f32[3,1,512]{2,1,0:T(1,128)} %bitcast.12, f32[3,1,512]{2,1,0:T(1,128)} %bitcast.13, s32[512]{0:T(512)} %refs_2_.1, s32[8,512]{1,0:T(8,128)} %refs_3_.1, s32[512]{0:T(512)} %refs_4_.1, f32[2,64]{1,0:T(2,128)} %refs_5_.1, f32[64]{0:T(128)} %refs_6_.1, f32[2,8,64]{2,1,0:T(8,128)} %refs_7_.1, ...), custom_call_target="tpu_custom_call" | custom-call | bytes 262144 | tf_op jit(solution)/shard_map/pallas_call | solution.py:729
  2.5 0.5 %collective-permute-start = (f32[40,512]{1,0:T(8,128)}, f32[40,512]{1,0:T(8,128)S(1)}, u32[]{:S(2)}, u32[]{:S(2)}) collective-permute-start(f32[40,512]{1,0:T(8,128)} %get-tuple-element.39), channel_id=1, source_target_pairs={{0,4},{4,0},{8,12},{12,8},{1,5},{5,1},{9,13},{13,9},{2,6},{6,2},{1... | collective-permute-start | bytes 245768 | tf_op jit(solution)/shard_map/ppermute | solution.py:741
  3.0 2.6 %collective-permute-start.1 = (f32[40,512]{1,0:T(8,128)}, f32[40,512]{1,0:T(8,128)S(1)}, u32[]{:S(2)}, u32[]{:S(2)}) collective-permute-start(f32[40,512]{1,0:T(8,128)} %get-tuple-element.39), channel_id=1, source_target_pairs={{0,12},{4,8},{8,4},{12,0},{1,13},{5,9},{9,5},{13,1},{2,14},{6,10},... | collective-permute-start | bytes 245768 | tf_op jit(solution)/shard_map/ppermute | solution.py:741
  5.7 0.0 copy-start
  5.7 0.9 %copy-done = f32[112,512]{1,0:T(8,128)S(1)} copy-done((f32[112,512]{1,0:T(8,128)S(1)}, f32[112,512]{1,0:T(8,128)}, u32[]{:S(2)}) %copy-start) | copy-done | bytes 229400
  6.6 1.2 %shard_map.167 = (bf16[4,384,1024]{2,1,0:T(8,128)(2,1)S(1)}, bf16[64,48]{1,0:T(8,128)(2,1)S(1)}, bf16[64,192]{1,0:T(8,128)(2,1)S(1)}, bf16[64,32]{1,0:T(8,128)(2...) custom-call(f32[112,512]{1,0:T(8,128)S(1)} %copy-done), custom_call_target="tpu_custom_call" | custom-call | flops 100000000 | bytes 262144 | tf_op jit(solution)/shard_map/pallas_call | solution.py:729
  7.8 1.6 %collective-permute-start.2 = (f32[3,1,512]{2,1,0:T(1,128)S(1)}, f32[3,1,512]{2,1,0:T(1,128)S(1)}, u32[]{:S(2)}, u32[]{:S(2)}) collective-permute-start(f32[3,1,512]{2,1,0:T(1,128)S(1)} %get-tuple-element.38.x_ref), channel_id=1, source_target_pairs={{0,1},{1,2},{2,3},{3,0},{4,5},{5,6},{6,7},{7,4},{8,9},{9,10},{10,1... | collective-permute-start | bytes 18440 | tf_op jit(solution)/shard_map/ppermute | solution.py:741
  9.4 0.0 collective-permute-done.sibling_ref
  9.4 0.0 collective-permute-done.1.across_ref
  9.4 1.3 %shard_map.168 = (f32[40,512]{1,0:T(8,128)S(1)}, f32[40,512]{1,0:T(8,128)S(1)}, bf16[768,1024]{1,0:T(8,128)(2,1)S(1)}, f32[3,1,512]{2,1,0:T(1,128)S(1)}, s32[12,...) custom-call(f32[3,1,512]{2,1,0:T(1,128)S(1)} %get-tuple-element.38.x, ...), custom_call_target="tpu_custom_call" | custom-call | flops 1000000000 | bytes 262144 | tf_op jit(solution)/shard_map/pallas_call | solution.py:729
  10.7 2.7 %collective-permute-start.3 = (f32[3,1,512]{2,1,0:T(1,128)S(1)}, f32[3,1,512]{2,1,0:T(1,128)S(1)}, u32[]{:S(2)}, u32[]{:S(2)}) collective-permute-start(f32[3,1,512]{2,1,0:T(1,128)S(1)} %get-tuple-element.59), channel_id=1, source_target_pairs={{0,3},{1,0},{2,1},{3,2},{4,7},{5,4},{6,5},{7,6},{8,11},{9,8},{10,9... | collective-permute-start | bytes 18440 | tf_op jit(solution)/shard_map/ppermute | solution.py:741
  13.4 0.0 copy-start.2
  13.4 0.0 copy-start.1
  13.4 4.7 %shard_map.169.force_ref = f32[3,512]{1,0:T(4,128)S(1)} custom-call(bf16[4,384,1024]{2,1,0:T(8,128)(2,1)S(1)} %get-tuple-element.48.own_hot.rest_2_, bf16[768,1024]{1,0:T(8,128)(2,1)S(1)} %get-tuple-element.49.side_hot.rest_3_, bf16[64,48]{1,0:T(8,128)(2,1)S(1)} %get-tuple-element.40.rest_0_.rest_4_, bf16[64,192]{1,0:T(8,128)(2,1)S(1)} %get-tuple-element.41.rest_1_.rest_5_, ...), custom_call_target="tpu_custom_call" | custom-call | flops 1000000000 | bytes 262144 | tf_op jit(solution)/shard_map/pallas_call | solution.py:729
  18.1 0.0 collective-permute-done.2.before_ref
  18.1 0.0 collective-permute-done.3.after_ref
  18.1 0.1 shard_map.170
  18.2 0.1 collective-permute-start.4
  18.4 1.5 %collective-permute-start.5 = (f32[8,512]{1,0:T(8,128)S(1)}, f32[8,512]{1,0:T(8,128)S(1)}, u32[]{:S(2)}, u32[]{:S(2)}) collective-permute-start(f32[8,512]{1,0:T(8,128)S(1)} %get-tuple-element.60.own_ref), channel_id=1, source_target_pairs={{0,12},{4,8},{8,4},{12,0},{1,13},{5,9},{9,5},{13,1},{2,14},{6,10},... | collective-permute-start | bytes 49160 | tf_op jit(solution)/shard_map/ppermute | solution.py:741
  19.8 0.5 %collective-permute-start.6 = (f32[8,128]{1,0:T(8,128)S(1)}, f32[8,128]{1,0:T(8,128)S(1)}, u32[]{:S(2)}, u32[]{:S(2)}) collective-permute-start(f32[8,128]{1,0:T(8,128)S(1)} %get-tuple-element.61.rest_0_), channel_id=1, source_target_pairs={{0,8},{4,12},{8,0},{12,4},{1,9},{5,13},{9,1},{13,5},{2,10},{6,14},... | collective-permute-start | bytes 12296 | tf_op jit(solution)/shard_map/ppermute | solution.py:741
  21.7 0.0 copy-done.2
  21.7 0.5 %shard_map.165.number_ref = f32[8,128]{1,0:T(8,128)S(1)} custom-call(f32[1]{0:T(128)S(6)} %copy.19.dt_ref, s32[1,2]{1,0:T(1,128)S(1)} %bitcast.10, s32[1]{0:T(128)S(6)} %copy.20.climb_ref), custom_call_target="tpu_custom_call" | custom-call | bytes 262144 | tf_op jit(solution)/shard_map/pallas_call | solution.py:729
  22.2 1.2 %collective-permute-done.6.rest_1_ = f32[8,128]{1,0:T(8,128)S(1)} collective-permute-done((f32[8,128]{1,0:T(8,128)S(1)}, f32[8,128]{1,0:T(8,128)S(1)}, u32[]{:S(2)}, u32[]{:S(2)}) %collective-permute-start.6) | collective-permute-done | bytes 4128 | tf_op jit(solution)/shard_map/ppermute | solution.py:741
  23.4 0.0 collective-permute-done.4.near_ref
  23.5 0.0 collective-permute-done.5.far_ref
  23.5 0.0 copy-done.1
  23.5 5.3 %shard_map.171 = (f32[1,40,128]{2,1,0:T(8,128)S(1)}, f32[3,128]{1,0:T(4,128)S(1)}) custom-call(f32[8,128]{1,0:T(8,128)S(1)} %shard_map.165.number_ref, f32[40,512]{1,0:T(8,128)S(1)} %get-tuple-element.46.pl_ref, f32[112,512]{1,0:T(8,128)S(1)} %copy-done.1, f32[40,512]{1,0:T(8,128)S(1)} %get-tuple-element.47.pr_ref, f32[8,512]{1,0:T(8,128)S(1)} %get-tuple-element.60.own_ref, ...), custom_call_target="tpu_custom_call" | custom-call | flops 1000000000 | bytes 262144 | tf_op jit(solution)/shard_map/pallas_call | solution.py:729
  28.8 0.1 collective-permute-start.7
  28.9 1.3 %collective-permute-start.8 = (f32[1,40,128]{2,1,0:T(8,128)S(1)}, f32[1,40,128]{2,1,0:T(8,128)S(1)}, u32[]{:S(2)}, u32[]{:S(2)}) collective-permute-start(f32[1,40,128]{2,1,0:T(8,128)S(1)} %get-tuple-element.62.refs_0_.own_ref), channel_id=1, source_target_pairs={{0,2},{1,3},{2,0},{3,1},{4,6},{5,7},{6,4},{7,5},{8,10},{9,11},{10,... | collective-permute-start | bytes 61448 | tf_op jit(solution)/shard_map/ppermute | solution.py:741
  30.2 3.1 %collective-permute-start.9 = (f32[1,40,128]{2,1,0:T(8,128)S(1)}, f32[1,40,128]{2,1,0:T(8,128)S(1)}, u32[]{:S(2)}, u32[]{:S(2)}) collective-permute-start(f32[1,40,128]{2,1,0:T(8,128)S(1)} %get-tuple-element.62.refs_0_.own_ref), channel_id=1, source_target_pairs={{0,3},{1,2},{2,1},{3,0},{4,7},{5,6},{6,5},{7,4},{8,11},{9,10},{10,... | collective-permute-start | bytes 61448 | tf_op jit(solution)/shard_map/ppermute | solution.py:741
  33.3 0.0 collective-permute-done.7.refs_1_
  33.3 0.4 %collective-permute-done.8.refs_2_ = f32[1,40,128]{2,1,0:T(8,128)S(1)} collective-permute-done((f32[1,40,128]{2,1,0:T(8,128)S(1)}, f32[1,40,128]{2,1,0:T(8,128)S(1)}, u32[]{:S(2)}, u32[]{:S(2)}) %collective-permute-start.8) | collective-permute-done | bytes 20512 | tf_op jit(solution)/shard_map/ppermute | solution.py:741
  33.7 2.0 %collective-permute-done.9.refs_3_ = f32[1,40,128]{2,1,0:T(8,128)S(1)} collective-permute-done((f32[1,40,128]{2,1,0:T(8,128)S(1)}, f32[1,40,128]{2,1,0:T(8,128)S(1)}, u32[]{:S(2)}, u32[]{:S(2)}) %collective-permute-start.9) | collective-permute-done | bytes 20512 | tf_op jit(solution)/shard_map/ppermute | solution.py:741
  35.7 0.2 shard_map.172
  36.0 1.3 %collective-permute-start.10 = (f32[8,128]{1,0:T(8,128)S(1)}, f32[8,128]{1,0:T(8,128)S(1)}, u32[]{:S(2)}, u32[]{:S(2)}) collective-permute-start(f32[8,128]{1,0:T(8,128)S(1)} %get-tuple-element.65.rest_0_), channel_id=1, source_target_pairs={{0,8},{4,12},{8,0},{12,4},{1,9},{5,13},{9,1},{13,5},{2,10},{6,14},... | collective-permute-start | bytes 12296 | tf_op jit(solution)/shard_map/ppermute | solution.py:741
  37.2 0.0 collective-permute-start.11
  37.2 0.9 %collective-permute-start.12 = (f32[8,128]{1,0:T(8,128)S(1)}, f32[8,128]{1,0:T(8,128)S(1)}, u32[]{:S(2)}, u32[]{:S(2)}) collective-permute-start(f32[8,128]{1,0:T(8,128)S(1)} %get-tuple-element.65.rest_0_), channel_id=1, source_target_pairs={{0,4},{4,0},{8,12},{12,8},{1,5},{5,1},{9,13},{13,9},{2,6},{6,2},{1... | collective-permute-start | bytes 12296 | tf_op jit(solution)/shard_map/ppermute | solution.py:741
  38.2 1.5 %collective-permute-done.10.rest_1_ = f32[8,128]{1,0:T(8,128)S(1)} collective-permute-done((f32[8,128]{1,0:T(8,128)S(1)}, f32[8,128]{1,0:T(8,128)S(1)}, u32[]{:S(2)}, u32[]{:S(2)}) %collective-permute-start.10) | collective-permute-done | bytes 4128 | tf_op jit(solution)/shard_map/ppermute | solution.py:741
  39.6 0.6 %collective-permute-done.11.rest_2_ = f32[8,128]{1,0:T(8,128)S(1)} collective-permute-done((f32[8,128]{1,0:T(8,128)S(1)}, f32[8,128]{1,0:T(8,128)S(1)}, u32[]{:S(2)}, u32[]{:S(2)}) %collective-permute-start.11) | collective-permute-done | bytes 4128 | tf_op jit(solution)/shard_map/ppermute | solution.py:741
  40.3 0.0 collective-permute-done.12.rest_3_
  40.3 0.7 %shard_map.173 = (f32[3,1,512]{2,1,0:T(1,128)}, f32[3,1,512]{2,1,0:T(1,128)}, f32[2,1,2]{2,1,0:T(1,128)}, f32[1,1]{1,0:T(1,128)}) custom-call(f32[1,40,128]{2,1,0:T(8,128)S(1)} %get-tuple-element.62.refs_0_.own_ref, f32[3,128]{1,0:T(4,128)S(1)} %get-tuple-element.63.record_ref, f32[40,128]{1,0:T(8,128)S(1)} %get-tuple-element.64.state_ref, ...), custom_call_target="tpu_custom_call" | custom-call | bytes 262144 | tf_op jit(solution)/shard_map/pallas_call | solution.py:729
Async XLA Ops:
  2.5 6.9 %collective-permute-start = (f32[40,512]{1,0:T(8,128)}, f32[40,512]{1,0:T(8,128)S(1)}, u32[]{:S(2)}, u32[]{:S(2)}) collective-permute-start(f32[40,512]{1,0:T(8,128)} %get-tuple-element.39), channel_id=1, source_target_pairs={{0,4},{4,0},{8,12},{12,8},{1,5},{5,1},{9,13},{13,9},{2,6},{6,2},{1... | collective-permute-start | bytes 245768 | tf_op jit(solution)/shard_map/ppermute | solution.py:741
  3.0 6.4 %collective-permute-start.1 = (f32[40,512]{1,0:T(8,128)}, f32[40,512]{1,0:T(8,128)S(1)}, u32[]{:S(2)}, u32[]{:S(2)}) collective-permute-start(f32[40,512]{1,0:T(8,128)} %get-tuple-element.39), channel_id=1, source_target_pairs={{0,12},{4,8},{8,4},{12,0},{1,13},{5,9},{9,5},{13,1},{2,14},{6,10},... | collective-permute-start | bytes 245768 | tf_op jit(solution)/shard_map/ppermute | solution.py:741
  5.7 0.9 %copy-start = (f32[112,512]{1,0:T(8,128)S(1)}, f32[112,512]{1,0:T(8,128)}, u32[]{:S(2)}) copy-start(f32[112,512]{1,0:T(8,128)} %get-tuple-element.37.po_ref) | copy-start | bytes 688132
  7.8 10.3 %collective-permute-start.2 = (f32[3,1,512]{2,1,0:T(1,128)S(1)}, f32[3,1,512]{2,1,0:T(1,128)S(1)}, u32[]{:S(2)}, u32[]{:S(2)}) collective-permute-start(f32[3,1,512]{2,1,0:T(1,128)S(1)} %get-tuple-element.38.x_ref), channel_id=1, source_target_pairs={{0,1},{1,2},{2,3},{3,0},{4,5},{5,6},{6,7},{7,4},{8,9},{9,10},{10,1... | collective-permute-start | bytes 18440 | tf_op jit(solution)/shard_map/ppermute | solution.py:741
  10.7 7.4 %collective-permute-start.3 = (f32[3,1,512]{2,1,0:T(1,128)S(1)}, f32[3,1,512]{2,1,0:T(1,128)S(1)}, u32[]{:S(2)}, u32[]{:S(2)}) collective-permute-start(f32[3,1,512]{2,1,0:T(1,128)S(1)} %get-tuple-element.59), channel_id=1, source_target_pairs={{0,3},{1,0},{2,1},{3,2},{4,7},{5,4},{6,5},{7,6},{8,11},{9,8},{10,9... | collective-permute-start | bytes 18440 | tf_op jit(solution)/shard_map/ppermute | solution.py:741
  13.4 8.3 %copy-start.2 = (s32[2,1]{0,1:T(1,128)S(1)}, s32[2,1]{0,1:T(1,128)}, u32[]{:S(2)}) copy-start(s32[2,1]{0,1:T(1,128)} %param.17) | copy-start | bytes 28
  13.4 10.0 %copy-start.1 = (f32[112,512]{1,0:T(8,128)S(1)}, f32[112,512]{1,0:T(8,128)}, u32[]{:S(2)}) copy-start(f32[112,512]{1,0:T(8,128)} %get-tuple-element.37.po_ref) | copy-start | bytes 688132
  18.2 5.2 %collective-permute-start.4 = (f32[8,512]{1,0:T(8,128)S(1)}, f32[8,512]{1,0:T(8,128)S(1)}, u32[]{:S(2)}, u32[]{:S(2)}) collective-permute-start(f32[8,512]{1,0:T(8,128)S(1)} %get-tuple-element.60.own_ref), channel_id=1, source_target_pairs={{0,4},{4,0},{8,12},{12,8},{1,5},{5,1},{9,13},{13,9},{2,6},{6,2},{1... | collective-permute-start | bytes 49160 | tf_op jit(solution)/shard_map/ppermute | solution.py:741
  18.4 5.1 %collective-permute-start.5 = (f32[8,512]{1,0:T(8,128)S(1)}, f32[8,512]{1,0:T(8,128)S(1)}, u32[]{:S(2)}, u32[]{:S(2)}) collective-permute-start(f32[8,512]{1,0:T(8,128)S(1)} %get-tuple-element.60.own_ref), channel_id=1, source_target_pairs={{0,12},{4,8},{8,4},{12,0},{1,13},{5,9},{9,5},{13,1},{2,14},{6,10},... | collective-permute-start | bytes 49160 | tf_op jit(solution)/shard_map/ppermute | solution.py:741
  19.8 3.6 %collective-permute-start.6 = (f32[8,128]{1,0:T(8,128)S(1)}, f32[8,128]{1,0:T(8,128)S(1)}, u32[]{:S(2)}, u32[]{:S(2)}) collective-permute-start(f32[8,128]{1,0:T(8,128)S(1)} %get-tuple-element.61.rest_0_), channel_id=1, source_target_pairs={{0,8},{4,12},{8,0},{12,4},{1,9},{5,13},{9,1},{13,5},{2,10},{6,14},... | collective-permute-start | bytes 12296 | tf_op jit(solution)/shard_map/ppermute | solution.py:741
  28.8 4.5 %collective-permute-start.7 = (f32[1,40,128]{2,1,0:T(8,128)S(1)}, f32[1,40,128]{2,1,0:T(8,128)S(1)}, u32[]{:S(2)}, u32[]{:S(2)}) collective-permute-start(f32[1,40,128]{2,1,0:T(8,128)S(1)} %get-tuple-element.62.refs_0_.own_ref), channel_id=1, source_target_pairs={{0,1},{1,0},{2,3},{3,2},{4,5},{5,4},{6,7},{7,6},{8,9},{9,8},{10,11... | collective-permute-start | bytes 61448 | tf_op jit(solution)/shard_map/ppermute | solution.py:741
  28.9 4.8 %collective-permute-start.8 = (f32[1,40,128]{2,1,0:T(8,128)S(1)}, f32[1,40,128]{2,1,0:T(8,128)S(1)}, u32[]{:S(2)}, u32[]{:S(2)}) collective-permute-start(f32[1,40,128]{2,1,0:T(8,128)S(1)} %get-tuple-element.62.refs_0_.own_ref), channel_id=1, source_target_pairs={{0,2},{1,3},{2,0},{3,1},{4,6},{5,7},{6,4},{7,5},{8,10},{9,11},{10,... | collective-permute-start | bytes 61448 | tf_op jit(solution)/shard_map/ppermute | solution.py:741
  30.2 5.6 %collective-permute-start.9 = (f32[1,40,128]{2,1,0:T(8,128)S(1)}, f32[1,40,128]{2,1,0:T(8,128)S(1)}, u32[]{:S(2)}, u32[]{:S(2)}) collective-permute-start(f32[1,40,128]{2,1,0:T(8,128)S(1)} %get-tuple-element.62.refs_0_.own_ref), channel_id=1, source_target_pairs={{0,3},{1,2},{2,1},{3,0},{4,7},{5,6},{6,5},{7,4},{8,11},{9,10},{10,... | collective-permute-start | bytes 61448 | tf_op jit(solution)/shard_map/ppermute | solution.py:741
  36.0 3.7 %collective-permute-start.10 = (f32[8,128]{1,0:T(8,128)S(1)}, f32[8,128]{1,0:T(8,128)S(1)}, u32[]{:S(2)}, u32[]{:S(2)}) collective-permute-start(f32[8,128]{1,0:T(8,128)S(1)} %get-tuple-element.65.rest_0_), channel_id=1, source_target_pairs={{0,8},{4,12},{8,0},{12,4},{1,9},{5,13},{9,1},{13,5},{2,10},{6,14},... | collective-permute-start | bytes 12296 | tf_op jit(solution)/shard_map/ppermute | solution.py:741
  37.2 3.0 %collective-permute-start.11 = (f32[8,128]{1,0:T(8,128)S(1)}, f32[8,128]{1,0:T(8,128)S(1)}, u32[]{:S(2)}, u32[]{:S(2)}) collective-permute-start(f32[8,128]{1,0:T(8,128)S(1)} %get-tuple-element.65.rest_0_), channel_id=1, source_target_pairs={{0,12},{4,8},{8,4},{12,0},{1,13},{5,9},{9,5},{13,1},{2,14},{6,10},... | collective-permute-start | bytes 12296 | tf_op jit(solution)/shard_map/ppermute | solution.py:741
  37.2 3.0 %collective-permute-start.12 = (f32[8,128]{1,0:T(8,128)S(1)}, f32[8,128]{1,0:T(8,128)S(1)}, u32[]{:S(2)}, u32[]{:S(2)}) collective-permute-start(f32[8,128]{1,0:T(8,128)S(1)} %get-tuple-element.65.rest_0_), channel_id=1, source_target_pairs={{0,4},{4,0},{8,12},{12,8},{1,5},{5,1},{9,13},{13,9},{2,6},{6,2},{1... | collective-permute-start | bytes 12296 | tf_op jit(solution)/shard_map/ppermute | solution.py:741

commit v13 on v12

--- a/solution.py
+++ b/solution.py
@@ -90,8 +90,7 @@
     own_hot, l1_ref, l2_ref, l3_ref, l5_ref, l6_ref, col_ref, copy_ref = rest
     for b in range(SLAB_BLOCKS):
         mark(window_index(po_ref, b), [0, 1, 2], own_hot.at[b])
-    for c in range(3):
-        copy_ref[c] = po_ref[ROW_X + c : ROW_X + c + 1, :]
+    copy_ref[...] = po_ref[ROW_X : ROW_X + 8, :]
 
     def raw(first, count, i):
         return po_ref[first : first + count, i * LANES : i * LANES + CHANNELS]
@@ -451,23 +450,15 @@
     return jnp.where(even, across, sibling), jnp.where(even, sibling, across)
 
 
-def first_kernel(x_ref, sibling_ref, po_ref, across_ref, *rest):
-    weights, (pl_ref, pr_ref, side_hot, copy_ref), kept, (xs, sst) = rest[:6], rest[6:10], rest[10:19], rest[19:]
-    copy_ref[...] = x_ref[...]
+def first_kernel(sibling_ref, po_ref, across_ref, own_hot, *rest):
+    weights, (out_ref, pl_ref, pr_ref, side_hot), scr = rest[:6], rest[6:10], rest[10:]
+    xs, sst, kept = scr[0], scr[1], scr[2:11]
     pl_ref[...], pr_ref[...] = by_parity(sibling_ref[...], across_ref[...])
     packs = [pl_ref, po_ref, pr_ref]
     mark_sides(packs, side_hot)
     fill_region(xs, packs, lambda s: packs[s][ROW_X : ROW_X + 3, :])
     forward_parts(packs, weights, xs, sst, kept)
-
-
-def first_back_kernel(own_hot, side_hot, *rest):
-    weights, kept, out_ref, scr = rest[:6], rest[6:15], rest[15], rest[16:]
-    out_ref[...] = force_parts(weights, own_hot, side_hot, kept, *scr)
-
-
-def rows_of(ref):
-    return jnp.concatenate([ref[c] for c in range(3)], axis=0)
+    out_ref[...] = force_parts(weights, own_hot, side_hot, kept, *scr[11:])
 
 
 def block_row(*values):
@@ -475,13 +466,15 @@
     return jnp.concatenate(values, axis=1)
 
 
-def blend_kernel(images, force_ref, po_ref, before_ref, after_ref, out_ref, sums_ref):
+def blend_kernel(images, force_ref, po_ref, all_ref, out_ref, sums_ref):
     x = po_ref[ROW_X : ROW_X + 3, :]
     v = po_ref[ROW_V : ROW_V + 3, :]
     force = force_ref[...]
     here = lax.axis_index("img")
-    before = jnp.where(here > 0, rows_of(before_ref), 0.0)
-    after = jnp.where(here < images - 1, rows_of(after_ref), 0.0)
+    before = all_ref[pl.ds(pl.multiple_of(8 * jnp.maximum(here - 1, 0), 8), 8), :][0:3]
+    after = all_ref[pl.ds(pl.multiple_of(8 * jnp.minimum(here + 1, images - 1), 8), 8), :][0:3]
+    before = jnp.where(here > 0, before, 0.0)
+    after = jnp.where(here < images - 1, after, 0.0)
     tangent = after - before
     plus = after - x
     minus = x - before
@@ -813,41 +806,32 @@
             shape((CHANNELS, 3 * LANES), BF16),
             shape((16, 192), BF16),
             shape((4, CHANNELS, LANES), F32),
-            shape(x.shape, F32),
+            shape((8, atoms), F32),
         ),
         (),
         (pack,),
         flops=100000000,
     )
-    before = swap(x_copy, "img", lambda i: (i + 1) % images)
-    left, right, side_hot, x_copy, *kept = call(
+    everyone = lax.all_gather(x_copy, "img", tiled=True)
+    force_scratch = forward_scratch() + [pltpu.VMEM(*one) for one in kept_shapes()] + back_scratch()
+    force, left, right, side_hot = call(
         first_kernel,
         (
+            shape((3, atoms), F32),
             shape(sent.shape, F32),
             shape(sent.shape, F32),
             shape((SIDE_ROWS, SLOTS * LANES), BF16),
-            shape(x.shape, F32),
-            *[shape(*one) for one in kept_shapes()],
         ),
         (),
-        (x_copy, sibling, pack, across, *weights),
-        forward_scratch(),
-        flops=1000000000,
-    )
-    after = swap(x_copy, "img", lambda i: (i - 1) % images)
-    force = call(
-        first_back_kernel,
-        shape((3, atoms), F32),
-        (),
-        (own_hot, side_hot, *weights, *kept),
-        back_scratch(),
+        (sibling, pack, across, own_hot, *weights),
+        force_scratch,
         flops=1000000000,
     )
     message, sums = call(
         functools.partial(blend_kernel, images),
         (shape((8, atoms), F32), shape((8, LANES), F32)),
         (),
-        (force, pack, before, after),
+        (force, pack, everyone),
     )
     far = swap(message, "dom", lambda i: (i + 2 * (i % 2) - 1) % domains)
     if domains == 4:
@@ -861,7 +845,7 @@
         (shape((1, 40, LANES), F32), shape((3, LANES), F32)),
         (),
         (numbers, left, pack, right, message, near, far, *parts, own_hot, side_hot, *weights),
-        forward_scratch() + [pltpu.VMEM(*one) for one in kept_shapes()] + back_scratch(),
+        force_scratch,
         flops=1000000000,
     )
     rows = 8 * ((images + 7) // 8)

time: 41.3 us -> 52.8 us (1.28)
  blocking collectives: 0 us -> 13.4 us
  starting transfers between devices: 16.3 us -> 11.7 us
  waiting for transfers between devices: 5.8 us -> 8.07 us
  local copies, waits for them, and re-layouts: 0.95 us -> 1.88 us
    all_gather x0 -> x1, blocking collectives: none -> 13.4 us  [local(): everyone = lax.all_gather(x_copy, 'img', tiled=True)]
    ppermute x13 -> x11, starting transfers between devices: 16.3 us -> 11.7 us  [swap(): lax.ppermute(array, axis, [(i, partner(i)) for i in range(lax.axis_size(a...]
    ppermute x13 -> x11, waiting for transfers between devices: 5.8 us -> 8.07 us  [swap(): lax.ppermute(array, axis, [(i, partner(i)) for i in range(lax.axis_size(a...]
    unnamed x6 -> x8, local copies, waits for them, and re-layouts: 0.95 us -> 1.88 us
    pallas_call x9 -> x8, Pallas kernels: 16 us -> 15.5 us  [call(): pl.pallas_call(body, out_shape=outs, in_specs=[SMEM_SPEC] * len(scalars)...]
  transfers between devices with their start and end apart: 13 -> 11, of which waited for: 5 -> 5; matrix products, arithmetic and copies ran while one was open for 0% -> 0% of each run, Pallas kernels for 19% -> 3%
where the time goes in v13:
time: 52.8 us; the launch traced here: 52.6 us
  Pallas kernels  15.5 us (29%)
  blocking collectives  13.4 us (25%)
  starting transfers between devices  11.7 us (22%)
  waiting for transfers between devices  8.07 us (15%)
  between operations  2.03 us (4%)
  local copies, waits for them, and re-layouts  1.88 us (4%)
    pallas_call x8, Pallas kernels, call(): pl.pallas_call(body, out_shape=outs, in_specs=[SMEM_SPEC] * len(scalars)...  15.5 us
    all_gather x1, blocking collectives, local(): everyone = lax.all_gather(x_copy, 'img', tiled=True)  13.4 us
    ppermute x11, starting transfers between devices, swap(): lax.ppermute(array, axis, [(i, partner(i)) for i in range(lax.axis_size(a...  11.7 us
    ppermute x11, waiting for transfers between devices, swap(): lax.ppermute(array, axis, [(i, partner(i)) for i in range(lax.axis_size(a...  8.07 us
    unnamed x8, local copies, waits for them, and re-layouts  1.88 us
  transfers between devices with their start and end apart: 11, of which 5 were waited for; matrix products, arithmetic and copies ran while one was open for 0% of the time, Pallas kernels for 3%

profile of v13, /device:TPU:0, one launch (start us, length us, event | category | flops | bytes accessed | tf_op | source)
XLA Modules:
  0.0 52.6 jit_solution(11650532482577303945)
XLA Ops:
  0.6 0.0 copy-start.3
  0.6 1.9 %shard_map.166 = (f32[40,512]{1,0:T(8,128)}, f32[112,512]{1,0:T(8,128)}) custom-call(f32[3,1,512]{2,1,0:T(1,128)} %bitcast.12, f32[3,1,512]{2,1,0:T(1,128)} %bitcast.13, s32[512]{0:T(512)} %refs_2_.1, s32[8,512]{1,0:T(8,128)} %refs_3_.1, s32[512]{0:T(512)} %refs_4_.1, f32[2,64]{1,0:T(2,128)} %refs_5_.1, f32[64]{0:T(128)} %refs_6_.1, f32[2,8,64]{2,1,0:T(8,128)} %refs_7_.1, ...), custom_call_target="tpu_custom_call" | custom-call | bytes 262144 | tf_op jit(solution)/shard_map/pallas_call | solution.py:722
  2.5 0.5 collective-permute-start
  3.1 2.6 %collective-permute-start.1 = (f32[40,512]{1,0:T(8,128)}, f32[40,512]{1,0:T(8,128)S(1)}, u32[]{:S(2)}, u32[]{:S(2)}) collective-permute-start(f32[40,512]{1,0:T(8,128)} %get-tuple-element.28), channel_id=1, source_target_pairs={{0,12},{4,8},{8,4},{12,0},{1,13},{5,9},{9,5},{13,1},{2,14},{6,10},... | collective-permute-start | bytes 245768 | tf_op jit(solution)/shard_map/ppermute | solution.py:734
  5.7 0.0 copy-start
  5.7 0.9 %copy-done = f32[112,512]{1,0:T(8,128)S(1)} copy-done((f32[112,512]{1,0:T(8,128)S(1)}, f32[112,512]{1,0:T(8,128)}, u32[]{:S(2)}) %copy-start) | copy-done | bytes 229400
  6.6 0.0 copy-start.2
  6.6 1.2 %shard_map.167 = (bf16[4,384,1024]{2,1,0:T(8,128)(2,1)S(1)}, bf16[64,48]{1,0:T(8,128)(2,1)S(1)}, bf16[64,192]{1,0:T(8,128)(2,1)S(1)}, bf16[64,32]{1,0:T(8,128)(2...) custom-call(f32[112,512]{1,0:T(8,128)S(1)} %copy-done), custom_call_target="tpu_custom_call" | custom-call | flops 100000000 | bytes 262144 | tf_op jit(solution)/shard_map/pallas_call | solution.py:722
  7.8 13.4 %all_gather.3.all_ref = f32[32,512]{1,0:T(8,128)S(1)} all-gather(f32[8,512]{1,0:T(8,128)S(1)} %get-tuple-element.40), channel_id=1, replica_groups=mesh['group'=2,'dom'=4,'img'=4] {'img'}, dimensions={0}, use_global_device_ids=true | all-gather | bytes 81920 | tf_op jit(solution)/shard_map/all_gather | solution.py:815
  21.2 0.0 collective-permute-done.sibling_ref
  21.2 0.0 collective-permute-done.1.across_ref
  21.2 0.0 copy-start.1
  21.2 0.9 %copy-done.1 = f32[112,512]{1,0:T(8,128)S(1)} copy-done((f32[112,512]{1,0:T(8,128)S(1)}, f32[112,512]{1,0:T(8,128)}, u32[]{:S(2)}) %copy-start.1) | copy-done | bytes 229400
  22.2 5.4 %shard_map.168 = (f32[3,512]{1,0:T(4,128)S(1)}, f32[40,512]{1,0:T(8,128)S(1)}, f32[40,512]{1,0:T(8,128)S(1)}, bf16[768,1024]{1,0:T(8,128)(2,1)S(1)}) custom-call(f32[40,512]{1,0:T(8,128)S(1)} %collective-permute-done.sibling_ref, f32[112,512]{1,0:T(8,128)S(1)} %copy-done.1, f32[40,512]{1,0:T(8,128)S(1)} %collective-permute-done.1.across_ref, ...), custom_call_target="tpu_custom_call" | custom-call | flops 1000000000 | bytes 262144 | tf_op jit(solution)/shard_map/pallas_call | solution.py:722
  27.6 0.1 shard_map.169
  27.7 0.0 collective-permute-start.2
  27.7 0.7 %collective-permute-start.3 = (f32[8,512]{1,0:T(8,128)S(1)}, f32[8,512]{1,0:T(8,128)S(1)}, u32[]{:S(2)}, u32[]{:S(2)}) collective-permute-start(f32[8,512]{1,0:T(8,128)S(1)} %get-tuple-element.41.own_ref), channel_id=1, source_target_pairs={{0,12},{4,8},{8,4},{12,0},{1,13},{5,9},{9,5},{13,1},{2,14},{6,10},... | collective-permute-start | bytes 49160 | tf_op jit(solution)/shard_map/ppermute | solution.py:734
  28.4 1.5 %collective-permute-start.4 = (f32[8,128]{1,0:T(8,128)S(1)}, f32[8,128]{1,0:T(8,128)S(1)}, u32[]{:S(2)}, u32[]{:S(2)}) collective-permute-start(f32[8,128]{1,0:T(8,128)S(1)} %get-tuple-element.42.rest_0_), channel_id=1, source_target_pairs={{0,8},{4,12},{8,0},{12,4},{1,9},{5,13},{9,1},{13,5},{2,10},{6,14},... | collective-permute-start | bytes 12296 | tf_op jit(solution)/shard_map/ppermute | solution.py:734
  31.2 0.0 copy-done.3
  31.2 0.5 %shard_map.165.number_ref = f32[8,128]{1,0:T(8,128)S(1)} custom-call(f32[1]{0:T(128)S(6)} %copy.19.dt_ref, s32[1,2]{1,0:T(1,128)S(1)} %bitcast.10, s32[1]{0:T(128)S(6)} %copy.20.climb_ref), custom_call_target="tpu_custom_call" | custom-call | bytes 262144 | tf_op jit(solution)/shard_map/pallas_call | solution.py:722
  31.7 0.3 collective-permute-done.4.rest_1_
  32.0 0.0 collective-permute-done.2.near_ref
  32.0 0.0 collective-permute-done.3.far_ref
  32.0 0.0 copy-done.2
  32.0 5.4 %shard_map.170 = (f32[1,40,128]{2,1,0:T(8,128)S(1)}, f32[3,128]{1,0:T(4,128)S(1)}) custom-call(f32[8,128]{1,0:T(8,128)S(1)} %shard_map.165.number_ref, f32[40,512]{1,0:T(8,128)S(1)} %get-tuple-element.37.pl_ref, f32[112,512]{1,0:T(8,128)S(1)} %copy-done.2, f32[40,512]{1,0:T(8,128)S(1)} %get-tuple-element.38.pr_ref, f32[8,512]{1,0:T(8,128)S(1)} %get-tuple-element.41.own_ref, ...), custom_call_target="tpu_custom_call" | custom-call | flops 1000000000 | bytes 262144 | tf_op jit(solution)/shard_map/pallas_call | solution.py:722
  37.4 1.6 %collective-permute-start.5 = (f32[1,40,128]{2,1,0:T(8,128)S(1)}, f32[1,40,128]{2,1,0:T(8,128)S(1)}, u32[]{:S(2)}, u32[]{:S(2)}) collective-permute-start(f32[1,40,128]{2,1,0:T(8,128)S(1)} %get-tuple-element.44.refs_0_.own_ref), channel_id=1, source_target_pairs={{0,1},{1,0},{2,3},{3,2},{4,5},{5,4},{6,7},{7,6},{8,9},{9,8},{10,11... | collective-permute-start | bytes 61448 | tf_op jit(solution)/shard_map/ppermute | solution.py:734
  39.0 2.4 %collective-permute-start.6 = (f32[1,40,128]{2,1,0:T(8,128)S(1)}, f32[1,40,128]{2,1,0:T(8,128)S(1)}, u32[]{:S(2)}, u32[]{:S(2)}) collective-permute-start(f32[1,40,128]{2,1,0:T(8,128)S(1)} %get-tuple-element.44.refs_0_.own_ref), channel_id=1, source_target_pairs={{0,2},{1,3},{2,0},{3,1},{4,6},{5,7},{6,4},{7,5},{8,10},{9,11},{10,... | collective-permute-start | bytes 61448 | tf_op jit(solution)/shard_map/ppermute | solution.py:734
  41.4 0.5 collective-permute-start.7
  41.9 0.0 collective-permute-done.5.refs_1_
  41.9 2.0 %collective-permute-done.6.refs_2_ = f32[1,40,128]{2,1,0:T(8,128)S(1)} collective-permute-done((f32[1,40,128]{2,1,0:T(8,128)S(1)}, f32[1,40,128]{2,1,0:T(8,128)S(1)}, u32[]{:S(2)}, u32[]{:S(2)}) %collective-permute-start.6) | collective-permute-done | bytes 20512 | tf_op jit(solution)/shard_map/ppermute | solution.py:734
  43.8 3.1 %collective-permute-done.7.refs_3_ = f32[1,40,128]{2,1,0:T(8,128)S(1)} collective-permute-done((f32[1,40,128]{2,1,0:T(8,128)S(1)}, f32[1,40,128]{2,1,0:T(8,128)S(1)}, u32[]{:S(2)}, u32[]{:S(2)}) %collective-permute-start.7) | collective-permute-done | bytes 20512 | tf_op jit(solution)/shard_map/ppermute | solution.py:734
  46.9 0.2 shard_map.171
  47.2 0.1 collective-permute-start.10
  47.3 1.6 %collective-permute-start.8 = (f32[8,128]{1,0:T(8,128)S(1)}, f32[8,128]{1,0:T(8,128)S(1)}, u32[]{:S(2)}, u32[]{:S(2)}) collective-permute-start(f32[8,128]{1,0:T(8,128)S(1)} %get-tuple-element.47.rest_0_), channel_id=1, source_target_pairs={{0,8},{4,12},{8,0},{12,4},{1,9},{5,13},{9,1},{13,5},{2,10},{6,14},... | collective-permute-start | bytes 12296 | tf_op jit(solution)/shard_map/ppermute | solution.py:734
  48.8 0.3 collective-permute-start.9
  49.1 0.0 collective-permute-done.10.rest_3_
  49.1 1.8 %collective-permute-done.8.rest_1_ = f32[8,128]{1,0:T(8,128)S(1)} collective-permute-done((f32[8,128]{1,0:T(8,128)S(1)}, f32[8,128]{1,0:T(8,128)S(1)}, u32[]{:S(2)}, u32[]{:S(2)}) %collective-permute-start.8) | collective-permute-done | bytes 4128 | tf_op jit(solution)/shard_map/ppermute | solution.py:734
  50.9 0.9 %collective-permute-done.9.rest_2_ = f32[8,128]{1,0:T(8,128)S(1)} collective-permute-done((f32[8,128]{1,0:T(8,128)S(1)}, f32[8,128]{1,0:T(8,128)S(1)}, u32[]{:S(2)}, u32[]{:S(2)}) %collective-permute-start.9) | collective-permute-done | bytes 4128 | tf_op jit(solution)/shard_map/ppermute | solution.py:734
  51.8 0.7 %shard_map.172 = (f32[3,1,512]{2,1,0:T(1,128)}, f32[3,1,512]{2,1,0:T(1,128)}, f32[2,1,2]{2,1,0:T(1,128)}, f32[1,1]{1,0:T(1,128)}) custom-call(f32[1,40,128]{2,1,0:T(8,128)S(1)} %get-tuple-element.44.refs_0_.own_ref, f32[3,128]{1,0:T(4,128)S(1)} %get-tuple-element.45.record_ref, f32[40,128]{1,0:T(8,128)S(1)} %get-tuple-element.46.state_ref, ...), custom_call_target="tpu_custom_call" | custom-call | bytes 262144 | tf_op jit(solution)/shard_map/pallas_call | solution.py:722
Async XLA Ops:
  0.6 30.5 %copy-start.3 = (s32[2,1]{0,1:T(1,128)S(1)}, s32[2,1]{0,1:T(1,128)}, u32[]{:S(2)}) copy-start(s32[2,1]{0,1:T(1,128)} %param.17) | copy-start | bytes 28
  2.5 18.7 %collective-permute-start = (f32[40,512]{1,0:T(8,128)}, f32[40,512]{1,0:T(8,128)S(1)}, u32[]{:S(2)}, u32[]{:S(2)}) collective-permute-start(f32[40,512]{1,0:T(8,128)} %get-tuple-element.28), channel_id=1, source_target_pairs={{0,4},{4,0},{8,12},{12,8},{1,5},{5,1},{9,13},{13,9},{2,6},{6,2},{1... | collective-permute-start | bytes 245768 | tf_op jit(solution)/shard_map/ppermute | solution.py:734
  3.1 18.2 %collective-permute-start.1 = (f32[40,512]{1,0:T(8,128)}, f32[40,512]{1,0:T(8,128)S(1)}, u32[]{:S(2)}, u32[]{:S(2)}) collective-permute-start(f32[40,512]{1,0:T(8,128)} %get-tuple-element.28), channel_id=1, source_target_pairs={{0,12},{4,8},{8,4},{12,0},{1,13},{5,9},{9,5},{13,1},{2,14},{6,10},... | collective-permute-start | bytes 245768 | tf_op jit(solution)/shard_map/ppermute | solution.py:734
  5.7 0.9 %copy-start = (f32[112,512]{1,0:T(8,128)S(1)}, f32[112,512]{1,0:T(8,128)}, u32[]{:S(2)}) copy-start(f32[112,512]{1,0:T(8,128)} %get-tuple-element.29.po_ref) | copy-start | bytes 688132
  6.6 25.4 %copy-start.2 = (f32[112,512]{1,0:T(8,128)S(1)}, f32[112,512]{1,0:T(8,128)}, u32[]{:S(2)}) copy-start(f32[112,512]{1,0:T(8,128)} %get-tuple-element.29.po_ref) | copy-start | bytes 688132
  21.2 0.9 %copy-start.1 = (f32[112,512]{1,0:T(8,128)S(1)}, f32[112,512]{1,0:T(8,128)}, u32[]{:S(2)}) copy-start(f32[112,512]{1,0:T(8,128)} %get-tuple-element.29.po_ref) | copy-start | bytes 688132
  27.7 4.3 %collective-permute-start.2 = (f32[8,512]{1,0:T(8,128)S(1)}, f32[8,512]{1,0:T(8,128)S(1)}, u32[]{:S(2)}, u32[]{:S(2)}) collective-permute-start(f32[8,512]{1,0:T(8,128)S(1)} %get-tuple-element.41.own_ref), channel_id=1, source_target_pairs={{0,4},{4,0},{8,12},{12,8},{1,5},{5,1},{9,13},{13,9},{2,6},{6,2},{1... | collective-permute-start | bytes 49160 | tf_op jit(solution)/shard_map/ppermute | solution.py:734
  27.7 4.3 %collective-permute-start.3 = (f32[8,512]{1,0:T(8,128)S(1)}, f32[8,512]{1,0:T(8,128)S(1)}, u32[]{:S(2)}, u32[]{:S(2)}) collective-permute-start(f32[8,512]{1,0:T(8,128)S(1)} %get-tuple-element.41.own_ref), channel_id=1, source_target_pairs={{0,12},{4,8},{8,4},{12,0},{1,13},{5,9},{9,5},{13,1},{2,14},{6,10},... | collective-permute-start | bytes 49160 | tf_op jit(solution)/shard_map/ppermute | solution.py:734
  28.4 3.6 %collective-permute-start.4 = (f32[8,128]{1,0:T(8,128)S(1)}, f32[8,128]{1,0:T(8,128)S(1)}, u32[]{:S(2)}, u32[]{:S(2)}) collective-permute-start(f32[8,128]{1,0:T(8,128)S(1)} %get-tuple-element.42.rest_0_), channel_id=1, source_target_pairs={{0,8},{4,12},{8,0},{12,4},{1,9},{5,13},{9,1},{13,5},{2,10},{6,14},... | collective-permute-start | bytes 12296 | tf_op jit(solution)/shard_map/ppermute | solution.py:734
  37.4 4.5 %collective-permute-start.5 = (f32[1,40,128]{2,1,0:T(8,128)S(1)}, f32[1,40,128]{2,1,0:T(8,128)S(1)}, u32[]{:S(2)}, u32[]{:S(2)}) collective-permute-start(f32[1,40,128]{2,1,0:T(8,128)S(1)} %get-tuple-element.44.refs_0_.own_ref), channel_id=1, source_target_pairs={{0,1},{1,0},{2,3},{3,2},{4,5},{5,4},{6,7},{7,6},{8,9},{9,8},{10,11... | collective-permute-start | bytes 61448 | tf_op jit(solution)/shard_map/ppermute | solution.py:734
  39.0 4.9 %collective-permute-start.6 = (f32[1,40,128]{2,1,0:T(8,128)S(1)}, f32[1,40,128]{2,1,0:T(8,128)S(1)}, u32[]{:S(2)}, u32[]{:S(2)}) collective-permute-start(f32[1,40,128]{2,1,0:T(8,128)S(1)} %get-tuple-element.44.refs_0_.own_ref), channel_id=1, source_target_pairs={{0,2},{1,3},{2,0},{3,1},{4,6},{5,7},{6,4},{7,5},{8,10},{9,11},{10,... | collective-permute-start | bytes 61448 | tf_op jit(solution)/shard_map/ppermute | solution.py:734
  41.4 5.6 %collective-permute-start.7 = (f32[1,40,128]{2,1,0:T(8,128)S(1)}, f32[1,40,128]{2,1,0:T(8,128)S(1)}, u32[]{:S(2)}, u32[]{:S(2)}) collective-permute-start(f32[1,40,128]{2,1,0:T(8,128)S(1)} %get-tuple-element.44.refs_0_.own_ref), channel_id=1, source_target_pairs={{0,3},{1,2},{2,1},{3,0},{4,7},{5,6},{6,5},{7,4},{8,11},{9,10},{10,... | collective-permute-start | bytes 61448 | tf_op jit(solution)/shard_map/ppermute | solution.py:734
  47.2 1.9 %collective-permute-start.10 = (f32[8,128]{1,0:T(8,128)S(1)}, f32[8,128]{1,0:T(8,128)S(1)}, u32[]{:S(2)}, u32[]{:S(2)}) collective-permute-start(f32[8,128]{1,0:T(8,128)S(1)} %get-tuple-element.47.rest_0_), channel_id=1, source_target_pairs={{0,4},{4,0},{8,12},{12,8},{1,5},{5,1},{9,13},{13,9},{2,6},{6,2},{1... | collective-permute-start | bytes 12296 | tf_op jit(solution)/shard_map/ppermute | solution.py:734
  47.3 3.7 %collective-permute-start.8 = (f32[8,128]{1,0:T(8,128)S(1)}, f32[8,128]{1,0:T(8,128)S(1)}, u32[]{:S(2)}, u32[]{:S(2)}) collective-permute-start(f32[8,128]{1,0:T(8,128)S(1)} %get-tuple-element.47.rest_0_), channel_id=1, source_target_pairs={{0,8},{4,12},{8,0},{12,4},{1,9},{5,13},{9,1},{13,5},{2,10},{6,14},... | collective-permute-start | bytes 12296 | tf_op jit(solution)/shard_map/ppermute | solution.py:734
  48.8 3.0 %collective-permute-start.9 = (f32[8,128]{1,0:T(8,128)S(1)}, f32[8,128]{1,0:T(8,128)S(1)}, u32[]{:S(2)}, u32[]{:S(2)}) collective-permute-start(f32[8,128]{1,0:T(8,128)S(1)} %get-tuple-element.47.rest_0_), channel_id=1, source_target_pairs={{0,12},{4,8},{8,4},{12,0},{1,13},{5,9},{9,5},{13,1},{2,14},{6,10},... | collective-permute-start | bytes 12296 | tf_op jit(solution)/shard_map/ppermute | solution.py:734

commit v14 on v11

--- a/solution.py
+++ b/solution.py
@@ -160,8 +160,7 @@
     return [w for w in range(3) if first <= b - 1 + w <= last]
 
 
-SIDE_START = {2: 0, 3: LANES, 8: 3 * LANES, 9: 5 * LANES}
-SIDE_ROWS = 6 * LANES
+SIDES = {2: 0, 3: 1, 8: 2, 9: 3}
 
 
 def mark(index, ws, target):
@@ -180,14 +179,13 @@
 
 
 def mark_sides(packs, side):
-    for b, start in SIDE_START.items():
-        ws = reach(b, 3, 8)
-        mark(window_index(packs[b // 4], b), ws, side.at[start : start + len(ws) * LANES])
+    for b, place in SIDES.items():
+        mark(window_index(packs[b // 4], b), [0, 1, 2], side.at[place])
 
 
 def forward_parts(packs, weights, xs, sst, kept):
     l1, l2, l3, l5, l6, col = weights
-    (widx, kinds, geo, bst, bps, bpr, sent_all, slope) = kept
+    (kinds, geo, bst, bps, bpr, sent_pair, slope) = kept
     centre = 2.0 + 0.5 * lax.broadcasted_iota(jnp.int32, (BASIS, LANES), 0).astype(F32)
     slot = lax.broadcasted_iota(jnp.int32, (SLOTS, LANES), 0)
 
@@ -199,7 +197,6 @@
         pack = packs[b // 4]
         lanes = slice((b % 4) * LANES, (b % 4 + 1) * LANES)
         index = window_index(pack, b)
-        widx[b] = index
         inner = index & (LANES - 1)
         part = index >> 7
 
@@ -256,20 +253,18 @@
         for i in range(2):
             one = sent[:, i * LANES : (i + 1) * LANES]
             one = one + col[0] + col[1] * jnp.broadcast_to(xs[b + i, 3:4, :], (CHANNELS, LANES))
-            sent_all[:, (b + i) * LANES : (b + i + 1) * LANES] = one
+            sent_pair[:, (b + i) * LANES : (b + i + 1) * LANES] = pair_stack(one)
         slope[:, cols] = steep
 
 
 def force_parts(weights, own_hot, side_hot, kept, dg, pulls, met, acc, held):
     l1, l2, l3, l5, l6, col = weights
-    (widx, kinds, geo, bst, bps, bpr, sent_all, slope) = kept
+    (kinds, geo, bst, bps, bpr, sent_pair, slope) = kept
     slot = lax.broadcasted_iota(jnp.int32, (SLOTS, LANES), 0)
 
     def marks(b, ws):
-        if b in SIDE_START:
-            start = SIDE_START[b] + (ws[0] - reach(b, 3, 8)[0]) * LANES
-            return side_hot.at[start : start + len(ws) * LANES]
-        return own_hot.at[b - 4, ws[0] * LANES : (ws[-1] + 1) * LANES]
+        rows = slice(ws[0] * LANES, (ws[-1] + 1) * LANES)
+        return side_hot.at[SIDES[b], rows] if b in SIDES else own_hot.at[b - 4, rows]
 
     def add_rows(sums, first, b, ws, out):
         for i, w in enumerate(ws):
@@ -285,27 +280,22 @@
     started = set()
 
     def block_work(b):
-        index = widx[b]
-        inner, part = index & (LANES - 1), index >> 7
+        found = mm(sent_pair[:, (b - 1) * LANES : (b + 2) * LANES], marks(b, [0, 1, 2])[...])
         basis = bst[b]
         radial = mm(l3[...], jnp.concatenate([basis, basis], axis=0))
         if 3 <= b <= 8:
             basis = bps[b]
             steepness = mm(l3[...], jnp.concatenate([basis, basis], axis=0))
-        lanes = [jnp.broadcast_to(inner[k : k + 1, :], (16, LANES)) for k in range(SLOTS)]
-        parts = [jnp.broadcast_to(part[k : k + 1, :], (16, LANES)) for k in range(SLOTS)]
         value = held.at[b % 2]
         total = [jnp.zeros((8, LANES), F32)] * SLOTS
         for u in range(CHANNELS // 16):
             rows = slice(16 * u, 16 * u + 16)
             low_rows = slice(CHANNELS + 16 * u, CHANNELS + 16 * u + 16)
-            windows = [sent_all[rows, (b - 1 + w) * LANES : (b + w) * LANES] for w in range(3)]
             got = []
             message = jnp.zeros((16, LANES), F32)
             for k in range(SLOTS):
                 cols = slice(k * LANES, (k + 1) * LANES)
-                found = [pick(window, lanes[k]) for window in windows]
-                got.append(jnp.where(parts[k] == 0, found[0], jnp.where(parts[k] == 1, found[1], found[2])))
+                got.append(found[rows, cols] + found[low_rows, cols])
                 message = message + radial[rows, cols] * got[k]
             _, steep = silu_parts(message)
             back = col[3, rows] * steep
@@ -412,13 +402,12 @@
 def kept_shapes():
     wide = 12 * LANES
     return [
-        ((12, 8, LANES), jnp.int32),
         ((12, 8, LANES), F32),
         ((12, 4, 8, LANES), F32),
         ((12, 16, SLOTS * LANES), BF16),
         ((12, 16, SLOTS * LANES), BF16),
         ((12, 8, SLOTS * LANES), F32),
-        ((CHANNELS, wide), F32),
+        ((2 * CHANNELS, wide), BF16),
         ((CHANNELS, wide), F32),
     ]
 
@@ -443,7 +432,7 @@
 
 
 def first_kernel(x_ref, sibling_ref, po_ref, across_ref, *rest):
-    weights, (pl_ref, pr_ref, side_hot, copy_ref), kept, (xs, sst) = rest[:6], rest[6:10], rest[10:18], rest[18:]
+    weights, (pl_ref, pr_ref, side_hot, copy_ref), kept, (xs, sst) = rest[:6], rest[6:10], rest[10:17], rest[17:]
     copy_ref[...] = x_ref[...]
     pl_ref[...], pr_ref[...] = by_parity(sibling_ref[...], across_ref[...])
     packs = [pl_ref, po_ref, pr_ref]
@@ -453,7 +442,7 @@
 
 
 def first_back_kernel(own_hot, side_hot, *rest):
-    weights, kept, out_ref, scr = rest[:6], rest[6:14], rest[14], rest[15:]
+    weights, kept, out_ref, scr = rest[:6], rest[6:13], rest[13], rest[14:]
     out_ref[...] = force_parts(weights, own_hot, side_hot, kept, *scr)
 
 
@@ -575,10 +564,10 @@
         for p, m in zip(packs, messages)
     ]
     moved = [p[ROW_X : ROW_X + 3, :] + wide(dt) * s for p, s in zip(packs, speeds)]
-    xs, sst, kept = scr[0], scr[1], scr[2:10]
+    xs, sst, kept = scr[0], scr[1], scr[2:9]
     fill_region(xs, packs, lambda s: moved[s])
     forward_parts(packs, weights, xs, sst, kept)
-    force = force_parts(weights, own_hot, side_hot, kept, *scr[10:])
+    force = force_parts(weights, own_hot, side_hot, kept, *scr[9:])
     for c in range(3):
         for i in range(SLAB_BLOCKS):
             lanes = slice(i * LANES, (i + 1) * LANES)
@@ -816,7 +805,7 @@
         (
             shape(sent.shape, F32),
             shape(sent.shape, F32),
-            shape((SIDE_ROWS, SLOTS * LANES), BF16),
+            shape((len(SIDES), 3 * LANES, SLOTS * LANES), BF16),
             shape(x.shape, F32),
             *[shape(*one) for one in kept_shapes()],
         ),

time: 41.9 us -> 42.3 us (level)
  transfers between devices with their start and end apart: 13 -> 13, of which waited for: 5 -> 5; matrix products, arithmetic and copies ran while one was open for 0% -> 0% of each run, Pallas kernels for 19% -> 20%
where the time goes in v14:
time: 42.3 us; the launch traced here: 42 us
  Pallas kernels  17 us (40%)
  starting transfers between devices  16.3 us (39%)
  waiting for transfers between devices  5.8 us (14%)
  between operations  2.03 us (5%)
  local copies, waits for them, and re-layouts  0.95 us (2%)
    pallas_call x9, Pallas kernels, call(): pl.pallas_call(body, out_shape=outs, in_specs=[SMEM_SPEC] * len(scalars)...  17 us
    ppermute x13, starting transfers between devices, swap(): lax.ppermute(array, axis, [(i, partner(i)) for i in range(lax.axis_size(a...  16.3 us
    ppermute x13, waiting for transfers between devices, swap(): lax.ppermute(array, axis, [(i, partner(i)) for i in range(lax.axis_size(a...  5.8 us
    unnamed x6, local copies, waits for them, and re-layouts  0.95 us
  transfers between devices with their start and end apart: 13, of which 5 were waited for; matrix products, arithmetic and copies ran while one was open for 0% of the time, Pallas kernels for 20%

profile of v14, /device:TPU:0, one launch (start us, length us, event | category | flops | bytes accessed | tf_op | source)
XLA Modules:
  0.0 42.0 jit_solution(16691401301539674979)
XLA Ops:
  0.6 1.9 %shard_map.166 = (f32[40,512]{1,0:T(8,128)}, f32[112,512]{1,0:T(8,128)}) custom-call(f32[3,1,512]{2,1,0:T(1,128)} %bitcast.12, f32[3,1,512]{2,1,0:T(1,128)} %bitcast.13, s32[512]{0:T(512)} %refs_2_.1, s32[8,512]{1,0:T(8,128)} %refs_3_.1, s32[512]{0:T(512)} %refs_4_.1, f32[2,64]{1,0:T(2,128)} %refs_5_.1, f32[64]{0:T(128)} %refs_6_.1, f32[2,8,64]{2,1,0:T(8,128)} %refs_7_.1, ...), custom_call_target="tpu_custom_call" | custom-call | bytes 262144 | tf_op jit(solution)/shard_map/pallas_call | solution.py:709
  2.5 0.5 %collective-permute-start = (f32[40,512]{1,0:T(8,128)}, f32[40,512]{1,0:T(8,128)S(1)}, u32[]{:S(2)}, u32[]{:S(2)}) collective-permute-start(f32[40,512]{1,0:T(8,128)} %get-tuple-element.37), channel_id=1, source_target_pairs={{0,4},{4,0},{8,12},{12,8},{1,5},{5,1},{9,13},{13,9},{2,6},{6,2},{1... | collective-permute-start | bytes 245768 | tf_op jit(solution)/shard_map/ppermute | solution.py:721
  3.0 2.6 %collective-permute-start.1 = (f32[40,512]{1,0:T(8,128)}, f32[40,512]{1,0:T(8,128)S(1)}, u32[]{:S(2)}, u32[]{:S(2)}) collective-permute-start(f32[40,512]{1,0:T(8,128)} %get-tuple-element.37), channel_id=1, source_target_pairs={{0,12},{4,8},{8,4},{12,0},{1,13},{5,9},{9,5},{13,1},{2,14},{6,10},... | collective-permute-start | bytes 245768 | tf_op jit(solution)/shard_map/ppermute | solution.py:721
  5.7 0.0 copy-start
  5.7 0.9 %copy-done = f32[112,512]{1,0:T(8,128)S(1)} copy-done((f32[112,512]{1,0:T(8,128)S(1)}, f32[112,512]{1,0:T(8,128)}, u32[]{:S(2)}) %copy-start) | copy-done | bytes 229400
  6.6 1.2 %shard_map.167 = (bf16[4,384,1024]{2,1,0:T(8,128)(2,1)S(1)}, bf16[64,48]{1,0:T(8,128)(2,1)S(1)}, bf16[64,192]{1,0:T(8,128)(2,1)S(1)}, bf16[64,32]{1,0:T(8,128)(2...) custom-call(f32[112,512]{1,0:T(8,128)S(1)} %copy-done), custom_call_target="tpu_custom_call" | custom-call | flops 100000000 | bytes 262144 | tf_op jit(solution)/shard_map/pallas_call | solution.py:709
  7.8 1.6 %collective-permute-start.2 = (f32[3,1,512]{2,1,0:T(1,128)S(1)}, f32[3,1,512]{2,1,0:T(1,128)S(1)}, u32[]{:S(2)}, u32[]{:S(2)}) collective-permute-start(f32[3,1,512]{2,1,0:T(1,128)S(1)} %get-tuple-element.36.x_ref), channel_id=1, source_target_pairs={{0,1},{1,2},{2,3},{3,0},{4,5},{5,6},{6,7},{7,4},{8,9},{9,10},{10,1... | collective-permute-start | bytes 18440 | tf_op jit(solution)/shard_map/ppermute | solution.py:721
  9.4 0.0 collective-permute-done.sibling_ref
  9.4 0.0 collective-permute-done.1.across_ref
  9.4 1.7 %shard_map.168 = (f32[40,512]{1,0:T(8,128)S(1)}, f32[40,512]{1,0:T(8,128)S(1)}, bf16[4,384,1024]{2,1,0:T(8,128)(2,1)S(1)}, f32[3,1,512]{2,1,0:T(1,128)S(1)}, f32...) custom-call(f32[3,1,512]{2,1,0:T(1,128)S(1)} %get-tuple-element.36.x, ...), custom_call_target="tpu_custom_call" | custom-call | flops 1000000000 | bytes 262144 | tf_op jit(solution)/shard_map/pallas_call | solution.py:709
  11.1 2.7 %collective-permute-start.3 = (f32[3,1,512]{2,1,0:T(1,128)S(1)}, f32[3,1,512]{2,1,0:T(1,128)S(1)}, u32[]{:S(2)}, u32[]{:S(2)}) collective-permute-start(f32[3,1,512]{2,1,0:T(1,128)S(1)} %get-tuple-element.55), channel_id=1, source_target_pairs={{0,3},{1,0},{2,1},{3,2},{4,7},{5,4},{6,5},{7,6},{8,11},{9,8},{10,9... | collective-permute-start | bytes 18440 | tf_op jit(solution)/shard_map/ppermute | solution.py:721
  13.9 0.0 copy-start.2
  13.9 0.0 copy-start.1
  13.9 4.9 %shard_map.169.force_ref = f32[3,512]{1,0:T(4,128)S(1)} custom-call(bf16[4,384,1024]{2,1,0:T(8,128)(2,1)S(1)} %get-tuple-element.46.own_hot.rest_2_, bf16[4,384,1024]{2,1,0:T(8,128)(2,1)S(1)} %get-tuple-element.47.side_hot.rest_3_, bf16[64,48]{1,0:T(8,128)(2,1)S(1)} %get-tuple-element.38.rest_0_.rest_4_, ...), custom_call_target="tpu_custom_call" | custom-call | flops 1000000000 | bytes 262144 | tf_op jit(solution)/shard_map/pallas_call | solution.py:709
  18.8 0.0 collective-permute-done.2.before_ref
  18.8 0.0 collective-permute-done.3.after_ref
  18.8 0.1 shard_map.170
  18.9 0.2 collective-permute-start.4
  19.1 1.5 %collective-permute-start.5 = (f32[8,512]{1,0:T(8,128)S(1)}, f32[8,512]{1,0:T(8,128)S(1)}, u32[]{:S(2)}, u32[]{:S(2)}) collective-permute-start(f32[8,512]{1,0:T(8,128)S(1)} %get-tuple-element.56.own_ref), channel_id=1, source_target_pairs={{0,12},{4,8},{8,4},{12,0},{1,13},{5,9},{9,5},{13,1},{2,14},{6,10},... | collective-permute-start | bytes 49160 | tf_op jit(solution)/shard_map/ppermute | solution.py:721
  20.5 0.5 %collective-permute-start.6 = (f32[8,128]{1,0:T(8,128)S(1)}, f32[8,128]{1,0:T(8,128)S(1)}, u32[]{:S(2)}, u32[]{:S(2)}) collective-permute-start(f32[8,128]{1,0:T(8,128)S(1)} %get-tuple-element.57.rest_0_), channel_id=1, source_target_pairs={{0,8},{4,12},{8,0},{12,4},{1,9},{5,13},{9,1},{13,5},{2,10},{6,14},... | collective-permute-start | bytes 12296 | tf_op jit(solution)/shard_map/ppermute | solution.py:721
  22.4 0.0 copy-done.2
  22.4 0.5 %shard_map.165.number_ref = f32[8,128]{1,0:T(8,128)S(1)} custom-call(f32[1]{0:T(128)S(6)} %copy.19.dt_ref, s32[1,2]{1,0:T(1,128)S(1)} %bitcast.10, s32[1]{0:T(128)S(6)} %copy.20.climb_ref), custom_call_target="tpu_custom_call" | custom-call | bytes 262144 | tf_op jit(solution)/shard_map/pallas_call | solution.py:709
  22.9 1.2 %collective-permute-done.6.rest_1_ = f32[8,128]{1,0:T(8,128)S(1)} collective-permute-done((f32[8,128]{1,0:T(8,128)S(1)}, f32[8,128]{1,0:T(8,128)S(1)}, u32[]{:S(2)}, u32[]{:S(2)}) %collective-permute-start.6) | collective-permute-done | bytes 4128 | tf_op jit(solution)/shard_map/ppermute | solution.py:721
  24.1 0.0 collective-permute-done.4.near_ref
  24.2 0.0 collective-permute-done.5.far_ref
  24.2 0.0 copy-done.1
  24.2 5.6 %shard_map.171 = (f32[1,40,128]{2,1,0:T(8,128)S(1)}, f32[3,128]{1,0:T(4,128)S(1)}) custom-call(f32[8,128]{1,0:T(8,128)S(1)} %shard_map.165.number_ref, f32[40,512]{1,0:T(8,128)S(1)} %get-tuple-element.44.pl_ref, f32[112,512]{1,0:T(8,128)S(1)} %copy-done.1, f32[40,512]{1,0:T(8,128)S(1)} %get-tuple-element.45.pr_ref, f32[8,512]{1,0:T(8,128)S(1)} %get-tuple-element.56.own_ref, ...), custom_call_target="tpu_custom_call" | custom-call | flops 1000000000 | bytes 262144 | tf_op jit(solution)/shard_map/pallas_call | solution.py:709
  29.8 0.1 collective-permute-start.7
  29.9 1.1 %collective-permute-start.8 = (f32[1,40,128]{2,1,0:T(8,128)S(1)}, f32[1,40,128]{2,1,0:T(8,128)S(1)}, u32[]{:S(2)}, u32[]{:S(2)}) collective-permute-start(f32[1,40,128]{2,1,0:T(8,128)S(1)} %get-tuple-element.58.refs_0_.own_ref), channel_id=1, source_target_pairs={{0,2},{1,3},{2,0},{3,1},{4,6},{5,7},{6,4},{7,5},{8,10},{9,11},{10,... | collective-permute-start | bytes 61448 | tf_op jit(solution)/shard_map/ppermute | solution.py:721
  31.0 3.3 %collective-permute-start.9 = (f32[1,40,128]{2,1,0:T(8,128)S(1)}, f32[1,40,128]{2,1,0:T(8,128)S(1)}, u32[]{:S(2)}, u32[]{:S(2)}) collective-permute-start(f32[1,40,128]{2,1,0:T(8,128)S(1)} %get-tuple-element.58.refs_0_.own_ref), channel_id=1, source_target_pairs={{0,3},{1,2},{2,1},{3,0},{4,7},{5,6},{6,5},{7,4},{8,11},{9,10},{10,... | collective-permute-start | bytes 61448 | tf_op jit(solution)/shard_map/ppermute | solution.py:721
  34.3 0.0 collective-permute-done.7.refs_1_
  34.3 0.4 %collective-permute-done.8.refs_2_ = f32[1,40,128]{2,1,0:T(8,128)S(1)} collective-permute-done((f32[1,40,128]{2,1,0:T(8,128)S(1)}, f32[1,40,128]{2,1,0:T(8,128)S(1)}, u32[]{:S(2)}, u32[]{:S(2)}) %collective-permute-start.8) | collective-permute-done | bytes 20512 | tf_op jit(solution)/shard_map/ppermute | solution.py:721
  34.7 1.8 %collective-permute-done.9.refs_3_ = f32[1,40,128]{2,1,0:T(8,128)S(1)} collective-permute-done((f32[1,40,128]{2,1,0:T(8,128)S(1)}, f32[1,40,128]{2,1,0:T(8,128)S(1)}, u32[]{:S(2)}, u32[]{:S(2)}) %collective-permute-start.9) | collective-permute-done | bytes 20512 | tf_op jit(solution)/shard_map/ppermute | solution.py:721
  36.5 0.2 shard_map.172
  36.8 1.5 %collective-permute-start.10 = (f32[8,128]{1,0:T(8,128)S(1)}, f32[8,128]{1,0:T(8,128)S(1)}, u32[]{:S(2)}, u32[]{:S(2)}) collective-permute-start(f32[8,128]{1,0:T(8,128)S(1)} %get-tuple-element.61.rest_0_), channel_id=1, source_target_pairs={{0,8},{4,12},{8,0},{12,4},{1,9},{5,13},{9,1},{13,5},{2,10},{6,14},... | collective-permute-start | bytes 12296 | tf_op jit(solution)/shard_map/ppermute | solution.py:721
  38.2 0.0 collective-permute-start.11
  38.2 0.7 %collective-permute-start.12 = (f32[8,128]{1,0:T(8,128)S(1)}, f32[8,128]{1,0:T(8,128)S(1)}, u32[]{:S(2)}, u32[]{:S(2)}) collective-permute-start(f32[8,128]{1,0:T(8,128)S(1)} %get-tuple-element.61.rest_0_), channel_id=1, source_target_pairs={{0,4},{4,0},{8,12},{12,8},{1,5},{5,1},{9,13},{13,9},{2,6},{6,2},{1... | collective-permute-start | bytes 12296 | tf_op jit(solution)/shard_map/ppermute | solution.py:721
  39.0 1.5 %collective-permute-done.10.rest_1_ = f32[8,128]{1,0:T(8,128)S(1)} collective-permute-done((f32[8,128]{1,0:T(8,128)S(1)}, f32[8,128]{1,0:T(8,128)S(1)}, u32[]{:S(2)}, u32[]{:S(2)}) %collective-permute-start.10) | collective-permute-done | bytes 4128 | tf_op jit(solution)/shard_map/ppermute | solution.py:721
  40.4 0.8 %collective-permute-done.11.rest_2_ = f32[8,128]{1,0:T(8,128)S(1)} collective-permute-done((f32[8,128]{1,0:T(8,128)S(1)}, f32[8,128]{1,0:T(8,128)S(1)}, u32[]{:S(2)}, u32[]{:S(2)}) %collective-permute-start.11) | collective-permute-done | bytes 4128 | tf_op jit(solution)/shard_map/ppermute | solution.py:721
  41.3 0.0 collective-permute-done.12.rest_3_
  41.3 0.7 %shard_map.173 = (f32[3,1,512]{2,1,0:T(1,128)}, f32[3,1,512]{2,1,0:T(1,128)}, f32[2,1,2]{2,1,0:T(1,128)}, f32[1,1]{1,0:T(1,128)}) custom-call(f32[1,40,128]{2,1,0:T(8,128)S(1)} %get-tuple-element.58.refs_0_.own_ref, f32[3,128]{1,0:T(4,128)S(1)} %get-tuple-element.59.record_ref, f32[40,128]{1,0:T(8,128)S(1)} %get-tuple-element.60.state_ref, ...), custom_call_target="tpu_custom_call" | custom-call | bytes 262144 | tf_op jit(solution)/shard_map/pallas_call | solution.py:709
Async XLA Ops:
  2.5 6.9 %collective-permute-start = (f32[40,512]{1,0:T(8,128)}, f32[40,512]{1,0:T(8,128)S(1)}, u32[]{:S(2)}, u32[]{:S(2)}) collective-permute-start(f32[40,512]{1,0:T(8,128)} %get-tuple-element.37), channel_id=1, source_target_pairs={{0,4},{4,0},{8,12},{12,8},{1,5},{5,1},{9,13},{13,9},{2,6},{6,2},{1... | collective-permute-start | bytes 245768 | tf_op jit(solution)/shard_map/ppermute | solution.py:721
  3.0 6.4 %collective-permute-start.1 = (f32[40,512]{1,0:T(8,128)}, f32[40,512]{1,0:T(8,128)S(1)}, u32[]{:S(2)}, u32[]{:S(2)}) collective-permute-start(f32[40,512]{1,0:T(8,128)} %get-tuple-element.37), channel_id=1, source_target_pairs={{0,12},{4,8},{8,4},{12,0},{1,13},{5,9},{9,5},{13,1},{2,14},{6,10},... | collective-permute-start | bytes 245768 | tf_op jit(solution)/shard_map/ppermute | solution.py:721
  5.7 0.9 %copy-start = (f32[112,512]{1,0:T(8,128)S(1)}, f32[112,512]{1,0:T(8,128)}, u32[]{:S(2)}) copy-start(f32[112,512]{1,0:T(8,128)} %get-tuple-element.35.po_ref) | copy-start | bytes 688132
  7.8 11.0 %collective-permute-start.2 = (f32[3,1,512]{2,1,0:T(1,128)S(1)}, f32[3,1,512]{2,1,0:T(1,128)S(1)}, u32[]{:S(2)}, u32[]{:S(2)}) collective-permute-start(f32[3,1,512]{2,1,0:T(1,128)S(1)} %get-tuple-element.36.x_ref), channel_id=1, source_target_pairs={{0,1},{1,2},{2,3},{3,0},{4,5},{5,6},{6,7},{7,4},{8,9},{9,10},{10,1... | collective-permute-start | bytes 18440 | tf_op jit(solution)/shard_map/ppermute | solution.py:721
  11.1 7.7 %collective-permute-start.3 = (f32[3,1,512]{2,1,0:T(1,128)S(1)}, f32[3,1,512]{2,1,0:T(1,128)S(1)}, u32[]{:S(2)}, u32[]{:S(2)}) collective-permute-start(f32[3,1,512]{2,1,0:T(1,128)S(1)} %get-tuple-element.55), channel_id=1, source_target_pairs={{0,3},{1,0},{2,1},{3,2},{4,7},{5,4},{6,5},{7,6},{8,11},{9,8},{10,9... | collective-permute-start | bytes 18440 | tf_op jit(solution)/shard_map/ppermute | solution.py:721
  13.9 8.5 %copy-start.2 = (s32[2,1]{0,1:T(1,128)S(1)}, s32[2,1]{0,1:T(1,128)}, u32[]{:S(2)}) copy-start(s32[2,1]{0,1:T(1,128)} %param.17) | copy-start | bytes 28
  13.9 10.3 %copy-start.1 = (f32[112,512]{1,0:T(8,128)S(1)}, f32[112,512]{1,0:T(8,128)}, u32[]{:S(2)}) copy-start(f32[112,512]{1,0:T(8,128)} %get-tuple-element.35.po_ref) | copy-start | bytes 688132
  18.9 5.2 %collective-permute-start.4 = (f32[8,512]{1,0:T(8,128)S(1)}, f32[8,512]{1,0:T(8,128)S(1)}, u32[]{:S(2)}, u32[]{:S(2)}) collective-permute-start(f32[8,512]{1,0:T(8,128)S(1)} %get-tuple-element.56.own_ref), channel_id=1, source_target_pairs={{0,4},{4,0},{8,12},{12,8},{1,5},{5,1},{9,13},{13,9},{2,6},{6,2},{1... | collective-permute-start | bytes 49160 | tf_op jit(solution)/shard_map/ppermute | solution.py:721
  19.1 5.1 %collective-permute-start.5 = (f32[8,512]{1,0:T(8,128)S(1)}, f32[8,512]{1,0:T(8,128)S(1)}, u32[]{:S(2)}, u32[]{:S(2)}) collective-permute-start(f32[8,512]{1,0:T(8,128)S(1)} %get-tuple-element.56.own_ref), channel_id=1, source_target_pairs={{0,12},{4,8},{8,4},{12,0},{1,13},{5,9},{9,5},{13,1},{2,14},{6,10},... | collective-permute-start | bytes 49160 | tf_op jit(solution)/shard_map/ppermute | solution.py:721
  20.5 3.6 %collective-permute-start.6 = (f32[8,128]{1,0:T(8,128)S(1)}, f32[8,128]{1,0:T(8,128)S(1)}, u32[]{:S(2)}, u32[]{:S(2)}) collective-permute-start(f32[8,128]{1,0:T(8,128)S(1)} %get-tuple-element.57.rest_0_), channel_id=1, source_target_pairs={{0,8},{4,12},{8,0},{12,4},{1,9},{5,13},{9,1},{13,5},{2,10},{6,14},... | collective-permute-start | bytes 12296 | tf_op jit(solution)/shard_map/ppermute | solution.py:721
  29.8 4.5 %collective-permute-start.7 = (f32[1,40,128]{2,1,0:T(8,128)S(1)}, f32[1,40,128]{2,1,0:T(8,128)S(1)}, u32[]{:S(2)}, u32[]{:S(2)}) collective-permute-start(f32[1,40,128]{2,1,0:T(8,128)S(1)} %get-tuple-element.58.refs_0_.own_ref), channel_id=1, source_target_pairs={{0,1},{1,0},{2,3},{3,2},{4,5},{5,4},{6,7},{7,6},{8,9},{9,8},{10,11... | collective-permute-start | bytes 61448 | tf_op jit(solution)/shard_map/ppermute | solution.py:721
  29.9 4.8 %collective-permute-start.8 = (f32[1,40,128]{2,1,0:T(8,128)S(1)}, f32[1,40,128]{2,1,0:T(8,128)S(1)}, u32[]{:S(2)}, u32[]{:S(2)}) collective-permute-start(f32[1,40,128]{2,1,0:T(8,128)S(1)} %get-tuple-element.58.refs_0_.own_ref), channel_id=1, source_target_pairs={{0,2},{1,3},{2,0},{3,1},{4,6},{5,7},{6,4},{7,5},{8,10},{9,11},{10,... | collective-permute-start | bytes 61448 | tf_op jit(solution)/shard_map/ppermute | solution.py:721
  31.0 5.6 %collective-permute-start.9 = (f32[1,40,128]{2,1,0:T(8,128)S(1)}, f32[1,40,128]{2,1,0:T(8,128)S(1)}, u32[]{:S(2)}, u32[]{:S(2)}) collective-permute-start(f32[1,40,128]{2,1,0:T(8,128)S(1)} %get-tuple-element.58.refs_0_.own_ref), channel_id=1, source_target_pairs={{0,3},{1,2},{2,1},{3,0},{4,7},{5,6},{6,5},{7,4},{8,11},{9,10},{10,... | collective-permute-start | bytes 61448 | tf_op jit(solution)/shard_map/ppermute | solution.py:721
  36.8 3.7 %collective-permute-start.10 = (f32[8,128]{1,0:T(8,128)S(1)}, f32[8,128]{1,0:T(8,128)S(1)}, u32[]{:S(2)}, u32[]{:S(2)}) collective-permute-start(f32[8,128]{1,0:T(8,128)S(1)} %get-tuple-element.61.rest_0_), channel_id=1, source_target_pairs={{0,8},{4,12},{8,0},{12,4},{1,9},{5,13},{9,1},{13,5},{2,10},{6,14},... | collective-permute-start | bytes 12296 | tf_op jit(solution)/shard_map/ppermute | solution.py:721
  38.2 3.0 %collective-permute-start.11 = (f32[8,128]{1,0:T(8,128)S(1)}, f32[8,128]{1,0:T(8,128)S(1)}, u32[]{:S(2)}, u32[]{:S(2)}) collective-permute-start(f32[8,128]{1,0:T(8,128)S(1)} %get-tuple-element.61.rest_0_), channel_id=1, source_target_pairs={{0,12},{4,8},{8,4},{12,0},{1,13},{5,9},{9,5},{13,1},{2,14},{6,10},... | collective-permute-start | bytes 12296 | tf_op jit(solution)/shard_map/ppermute | solution.py:721
  38.2 3.0 %collective-permute-start.12 = (f32[8,128]{1,0:T(8,128)S(1)}, f32[8,128]{1,0:T(8,128)S(1)}, u32[]{:S(2)}, u32[]{:S(2)}) collective-permute-start(f32[8,128]{1,0:T(8,128)S(1)} %get-tuple-element.61.rest_0_), channel_id=1, source_target_pairs={{0,4},{4,0},{8,12},{12,8},{1,5},{5,1},{9,13},{13,9},{2,6},{6,2},{1... | collective-permute-start | bytes 12296 | tf_op jit(solution)/shard_map/ppermute | solution.py:721

commit v15 on v12

--- a/solution.py
+++ b/solution.py
@@ -532,12 +532,6 @@
     out_ref[...] = a_ref[...] + b_ref[...]
 
 
-def join_kernel(a_ref, b_ref, out_ref):
-    count = a_ref.shape[0]
-    out_ref[0:count] = a_ref[...]
-    out_ref[count : 2 * count] = b_ref[...]
-
-
 def number_kernel(dt_ref, flag_ref, climb_ref, out_ref):
     flags = [flag_ref[0, s].astype(F32) for s in range(flag_ref.shape[1])]
     for i, value in enumerate([dt_ref[0], climb_ref[0].astype(F32)] + flags):
@@ -622,7 +616,7 @@
     zero = jnp.zeros((1, LANES), F32)
 
     def gathered(row):
-        return jnp.concatenate([messages_ref[here ^ i, row : row + 1, :] for i in range(images)] + blank, axis=0)
+        return jnp.concatenate([messages_ref[lax.rem(here + images - i, images), row : row + 1, :] for i in range(images)] + blank, axis=0)
 
     def earlier(value):
         return jnp.concatenate([zero, value[0 : rows - 1]], axis=0)
@@ -755,16 +749,7 @@
 
 def collected(array, axis):
     count = lax.axis_size(axis)
-    if count == 4:
-        far = [swap(array, axis, lambda i, by=by: i ^ by) for by in (3, 2, 1)]
-        return [array] + far[::-1]
-    distance = 1
-    while distance < count:
-        more = swap(array, axis, lambda i, by=distance: i ^ by)
-        shape = jax.ShapeDtypeStruct((2 * distance,) + array.shape[1:], F32)
-        array = call(join_kernel, shape, (), (array, more))
-        distance *= 2
-    return [array]
+    return [array] + [swap(array, axis, lambda i, by=by: (i + by) % count) for by in range(1, count)]
 
 
 def local(

time: 41.3 us -> 39.9 us (0.966)
  waiting for transfers between devices: 5.8 us -> 5.02 us
  starting transfers between devices: 16.3 us -> 15.7 us
    ppermute x13, waiting for transfers between devices: 5.8 us -> 5.02 us  [swap(): lax.ppermute(array, axis, [(i, partner(i)) for i in range(lax.axis_size(a...]
    ppermute x13, starting transfers between devices: 16.3 us -> 15.7 us  [swap(): lax.ppermute(array, axis, [(i, partner(i)) for i in range(lax.axis_size(a...]
  transfers between devices with their start and end apart: 13 -> 13, of which waited for: 5 -> 4; matrix products, arithmetic and copies ran while one was open for 0% -> 0% of each run, Pallas kernels for 19% -> 19%
where the time goes in v15:
time: 39.9 us; the launch traced here: 39.7 us
  Pallas kernels  16 us (40%)
  starting transfers between devices  15.7 us (39%)
  waiting for transfers between devices  5.02 us (13%)
  between operations  2.03 us (5%)
  local copies, waits for them, and re-layouts  0.95 us (2%)
    pallas_call x9, Pallas kernels, call(): pl.pallas_call(body, out_shape=outs, in_specs=[SMEM_SPEC] * len(scalars)...  16 us
    ppermute x13, starting transfers between devices, swap(): lax.ppermute(array, axis, [(i, partner(i)) for i in range(lax.axis_size(a...  15.7 us
    ppermute x13, waiting for transfers between devices, swap(): lax.ppermute(array, axis, [(i, partner(i)) for i in range(lax.axis_size(a...  5.02 us
    unnamed x6, local copies, waits for them, and re-layouts  0.95 us
  transfers between devices with their start and end apart: 13, of which 4 were waited for; matrix products, arithmetic and copies ran while one was open for 0% of the time, Pallas kernels for 19%

profile of v15, /device:TPU:0, one launch (start us, length us, event | category | flops | bytes accessed | tf_op | source)
XLA Modules:
  0.0 39.7 jit_solution(16773759665074704204)
XLA Ops:
  0.6 1.9 %shard_map.166 = (f32[40,512]{1,0:T(8,128)}, f32[112,512]{1,0:T(8,128)}) custom-call(f32[3,1,512]{2,1,0:T(1,128)} %bitcast.12, f32[3,1,512]{2,1,0:T(1,128)} %bitcast.13, s32[512]{0:T(512)} %refs_2_.1, s32[8,512]{1,0:T(8,128)} %refs_3_.1, s32[512]{0:T(512)} %refs_4_.1, f32[2,64]{1,0:T(2,128)} %refs_5_.1, f32[64]{0:T(128)} %refs_6_.1, f32[2,8,64]{2,1,0:T(8,128)} %refs_7_.1, ...), custom_call_target="tpu_custom_call" | custom-call | bytes 262144 | tf_op jit(solution)/shard_map/pallas_call | solution.py:723
  2.5 0.5 %collective-permute-start = (f32[40,512]{1,0:T(8,128)}, f32[40,512]{1,0:T(8,128)S(1)}, u32[]{:S(2)}, u32[]{:S(2)}) collective-permute-start(f32[40,512]{1,0:T(8,128)} %get-tuple-element.39), channel_id=1, source_target_pairs={{0,4},{4,0},{8,12},{12,8},{1,5},{5,1},{9,13},{13,9},{2,6},{6,2},{1... | collective-permute-start | bytes 245768 | tf_op jit(solution)/shard_map/ppermute | solution.py:735
  3.0 2.6 %collective-permute-start.1 = (f32[40,512]{1,0:T(8,128)}, f32[40,512]{1,0:T(8,128)S(1)}, u32[]{:S(2)}, u32[]{:S(2)}) collective-permute-start(f32[40,512]{1,0:T(8,128)} %get-tuple-element.39), channel_id=1, source_target_pairs={{0,12},{4,8},{8,4},{12,0},{1,13},{5,9},{9,5},{13,1},{2,14},{6,10},... | collective-permute-start | bytes 245768 | tf_op jit(solution)/shard_map/ppermute | solution.py:735
  5.7 0.0 copy-start
  5.7 0.9 %copy-done = f32[112,512]{1,0:T(8,128)S(1)} copy-done((f32[112,512]{1,0:T(8,128)S(1)}, f32[112,512]{1,0:T(8,128)}, u32[]{:S(2)}) %copy-start) | copy-done | bytes 229400
  6.6 1.2 %shard_map.167 = (bf16[4,384,1024]{2,1,0:T(8,128)(2,1)S(1)}, bf16[64,48]{1,0:T(8,128)(2,1)S(1)}, bf16[64,192]{1,0:T(8,128)(2,1)S(1)}, bf16[64,32]{1,0:T(8,128)(2...) custom-call(f32[112,512]{1,0:T(8,128)S(1)} %copy-done), custom_call_target="tpu_custom_call" | custom-call | flops 100000000 | bytes 262144 | tf_op jit(solution)/shard_map/pallas_call | solution.py:723
  7.8 1.6 %collective-permute-start.2 = (f32[3,1,512]{2,1,0:T(1,128)S(1)}, f32[3,1,512]{2,1,0:T(1,128)S(1)}, u32[]{:S(2)}, u32[]{:S(2)}) collective-permute-start(f32[3,1,512]{2,1,0:T(1,128)S(1)} %get-tuple-element.38.x_ref), channel_id=1, source_target_pairs={{0,1},{1,2},{2,3},{3,0},{4,5},{5,6},{6,7},{7,4},{8,9},{9,10},{10,1... | collective-permute-start | bytes 18440 | tf_op jit(solution)/shard_map/ppermute | solution.py:735
  9.4 0.0 collective-permute-done.sibling_ref
  9.4 0.0 collective-permute-done.1.across_ref
  9.4 1.3 %shard_map.168 = (f32[40,512]{1,0:T(8,128)S(1)}, f32[40,512]{1,0:T(8,128)S(1)}, bf16[768,1024]{1,0:T(8,128)(2,1)S(1)}, f32[3,1,512]{2,1,0:T(1,128)S(1)}, s32[12,...) custom-call(f32[3,1,512]{2,1,0:T(1,128)S(1)} %get-tuple-element.38.x, ...), custom_call_target="tpu_custom_call" | custom-call | flops 1000000000 | bytes 262144 | tf_op jit(solution)/shard_map/pallas_call | solution.py:723
  10.7 2.7 %collective-permute-start.3 = (f32[3,1,512]{2,1,0:T(1,128)S(1)}, f32[3,1,512]{2,1,0:T(1,128)S(1)}, u32[]{:S(2)}, u32[]{:S(2)}) collective-permute-start(f32[3,1,512]{2,1,0:T(1,128)S(1)} %get-tuple-element.59), channel_id=1, source_target_pairs={{0,3},{1,0},{2,1},{3,2},{4,7},{5,4},{6,5},{7,6},{8,11},{9,8},{10,9... | collective-permute-start | bytes 18440 | tf_op jit(solution)/shard_map/ppermute | solution.py:735
  13.4 0.0 copy-start.2
  13.4 0.0 copy-start.1
  13.4 4.7 %shard_map.169.force_ref = f32[3,512]{1,0:T(4,128)S(1)} custom-call(bf16[4,384,1024]{2,1,0:T(8,128)(2,1)S(1)} %get-tuple-element.48.own_hot.rest_2_, bf16[768,1024]{1,0:T(8,128)(2,1)S(1)} %get-tuple-element.49.side_hot.rest_3_, bf16[64,48]{1,0:T(8,128)(2,1)S(1)} %get-tuple-element.40.rest_0_.rest_4_, bf16[64,192]{1,0:T(8,128)(2,1)S(1)} %get-tuple-element.41.rest_1_.rest_5_, ...), custom_call_target="tpu_custom_call" | custom-call | flops 1000000000 | bytes 262144 | tf_op jit(solution)/shard_map/pallas_call | solution.py:723
  18.1 0.0 collective-permute-done.2.before_ref
  18.1 0.0 collective-permute-done.3.after_ref
  18.1 0.1 shard_map.170
  18.2 0.1 collective-permute-start.4
  18.4 1.5 %collective-permute-start.5 = (f32[8,512]{1,0:T(8,128)S(1)}, f32[8,512]{1,0:T(8,128)S(1)}, u32[]{:S(2)}, u32[]{:S(2)}) collective-permute-start(f32[8,512]{1,0:T(8,128)S(1)} %get-tuple-element.60.own_ref), channel_id=1, source_target_pairs={{0,12},{4,8},{8,4},{12,0},{1,13},{5,9},{9,5},{13,1},{2,14},{6,10},... | collective-permute-start | bytes 49160 | tf_op jit(solution)/shard_map/ppermute | solution.py:735
  19.8 0.5 %collective-permute-start.6 = (f32[8,128]{1,0:T(8,128)S(1)}, f32[8,128]{1,0:T(8,128)S(1)}, u32[]{:S(2)}, u32[]{:S(2)}) collective-permute-start(f32[8,128]{1,0:T(8,128)S(1)} %get-tuple-element.61.rest_0_), channel_id=1, source_target_pairs={{0,8},{4,12},{8,0},{12,4},{1,9},{5,13},{9,1},{13,5},{2,10},{6,14},... | collective-permute-start | bytes 12296 | tf_op jit(solution)/shard_map/ppermute | solution.py:735
  21.7 0.0 copy-done.2
  21.7 0.5 %shard_map.165.number_ref = f32[8,128]{1,0:T(8,128)S(1)} custom-call(f32[1]{0:T(128)S(6)} %copy.19.dt_ref, s32[1,2]{1,0:T(1,128)S(1)} %bitcast.10, s32[1]{0:T(128)S(6)} %copy.20.climb_ref), custom_call_target="tpu_custom_call" | custom-call | bytes 262144 | tf_op jit(solution)/shard_map/pallas_call | solution.py:723
  22.2 1.2 %collective-permute-done.6.rest_1_ = f32[8,128]{1,0:T(8,128)S(1)} collective-permute-done((f32[8,128]{1,0:T(8,128)S(1)}, f32[8,128]{1,0:T(8,128)S(1)}, u32[]{:S(2)}, u32[]{:S(2)}) %collective-permute-start.6) | collective-permute-done | bytes 4128 | tf_op jit(solution)/shard_map/ppermute | solution.py:735
  23.4 0.0 collective-permute-done.4.near_ref
  23.5 0.0 collective-permute-done.5.far_ref
  23.5 0.0 copy-done.1
  23.5 5.3 %shard_map.171 = (f32[1,40,128]{2,1,0:T(8,128)S(1)}, f32[3,128]{1,0:T(4,128)S(1)}) custom-call(f32[8,128]{1,0:T(8,128)S(1)} %shard_map.165.number_ref, f32[40,512]{1,0:T(8,128)S(1)} %get-tuple-element.46.pl_ref, f32[112,512]{1,0:T(8,128)S(1)} %copy-done.1, f32[40,512]{1,0:T(8,128)S(1)} %get-tuple-element.47.pr_ref, f32[8,512]{1,0:T(8,128)S(1)} %get-tuple-element.60.own_ref, ...), custom_call_target="tpu_custom_call" | custom-call | flops 1000000000 | bytes 262144 | tf_op jit(solution)/shard_map/pallas_call | solution.py:723
  28.8 0.1 collective-permute-start.7
  28.9 1.3 %collective-permute-start.8 = (f32[1,40,128]{2,1,0:T(8,128)S(1)}, f32[1,40,128]{2,1,0:T(8,128)S(1)}, u32[]{:S(2)}, u32[]{:S(2)}) collective-permute-start(f32[1,40,128]{2,1,0:T(8,128)S(1)} %get-tuple-element.62.refs_0_.own_ref), channel_id=1, source_target_pairs={{0,2},{1,3},{2,0},{3,1},{4,6},{5,7},{6,4},{7,5},{8,10},{9,11},{10,... | collective-permute-start | bytes 61448 | tf_op jit(solution)/shard_map/ppermute | solution.py:735
  30.2 2.5 %collective-permute-start.9 = (f32[1,40,128]{2,1,0:T(8,128)S(1)}, f32[1,40,128]{2,1,0:T(8,128)S(1)}, u32[]{:S(2)}, u32[]{:S(2)}) collective-permute-start(f32[1,40,128]{2,1,0:T(8,128)S(1)} %get-tuple-element.62.refs_0_.own_ref), channel_id=1, source_target_pairs={{0,3},{1,0},{2,1},{3,2},{4,7},{5,4},{6,5},{7,6},{8,11},{9,8},{10,9... | collective-permute-start | bytes 61448 | tf_op jit(solution)/shard_map/ppermute | solution.py:735
  32.7 1.8 %collective-permute-done.7.refs_1_ = f32[1,40,128]{2,1,0:T(8,128)S(1)} collective-permute-done((f32[1,40,128]{2,1,0:T(8,128)S(1)}, f32[1,40,128]{2,1,0:T(8,128)S(1)}, u32[]{:S(2)}, u32[]{:S(2)}) %collective-permute-start.7) | collective-permute-done | bytes 20512 | tf_op jit(solution)/shard_map/ppermute | solution.py:735
  34.4 0.0 collective-permute-done.8.refs_2_
  34.4 0.6 %collective-permute-done.9.refs_3_ = f32[1,40,128]{2,1,0:T(8,128)S(1)} collective-permute-done((f32[1,40,128]{2,1,0:T(8,128)S(1)}, f32[1,40,128]{2,1,0:T(8,128)S(1)}, u32[]{:S(2)}, u32[]{:S(2)}) %collective-permute-start.9) | collective-permute-done | bytes 20512 | tf_op jit(solution)/shard_map/ppermute | solution.py:735
  35.0 0.2 shard_map.172
  35.2 0.6 %collective-permute-start.10 = (f32[8,128]{1,0:T(8,128)S(1)}, f32[8,128]{1,0:T(8,128)S(1)}, u32[]{:S(2)}, u32[]{:S(2)}) collective-permute-start(f32[8,128]{1,0:T(8,128)S(1)} %get-tuple-element.65.rest_0_), channel_id=1, source_target_pairs={{0,8},{4,12},{8,0},{12,4},{1,9},{5,13},{9,1},{13,5},{2,10},{6,14},... | collective-permute-start | bytes 12296 | tf_op jit(solution)/shard_map/ppermute | solution.py:735
  35.8 0.0 collective-permute-start.11
  35.8 1.6 %collective-permute-start.12 = (f32[8,128]{1,0:T(8,128)S(1)}, f32[8,128]{1,0:T(8,128)S(1)}, u32[]{:S(2)}, u32[]{:S(2)}) collective-permute-start(f32[8,128]{1,0:T(8,128)S(1)} %get-tuple-element.65.rest_0_), channel_id=1, source_target_pairs={{0,4},{4,0},{8,12},{12,8},{1,5},{5,1},{9,13},{13,9},{2,6},{6,2},{1... | collective-permute-start | bytes 12296 | tf_op jit(solution)/shard_map/ppermute | solution.py:735
  37.4 1.5 %collective-permute-done.10.rest_1_ = f32[8,128]{1,0:T(8,128)S(1)} collective-permute-done((f32[8,128]{1,0:T(8,128)S(1)}, f32[8,128]{1,0:T(8,128)S(1)}, u32[]{:S(2)}, u32[]{:S(2)}) %collective-permute-start.10) | collective-permute-done | bytes 4128 | tf_op jit(solution)/shard_map/ppermute | solution.py:735
  38.9 0.0 collective-permute-done.11.rest_2_
  38.9 0.0 collective-permute-done.12.rest_3_
  38.9 0.7 %shard_map.173 = (f32[3,1,512]{2,1,0:T(1,128)}, f32[3,1,512]{2,1,0:T(1,128)}, f32[2,1,2]{2,1,0:T(1,128)}, f32[1,1]{1,0:T(1,128)}) custom-call(f32[1,40,128]{2,1,0:T(8,128)S(1)} %get-tuple-element.62.refs_0_.own_ref, f32[3,128]{1,0:T(4,128)S(1)} %get-tuple-element.63.record_ref, f32[40,128]{1,0:T(8,128)S(1)} %get-tuple-element.64.state_ref, ...), custom_call_target="tpu_custom_call" | custom-call | bytes 262144 | tf_op jit(solution)/shard_map/pallas_call | solution.py:723
Async XLA Ops:
  2.5 6.9 %collective-permute-start = (f32[40,512]{1,0:T(8,128)}, f32[40,512]{1,0:T(8,128)S(1)}, u32[]{:S(2)}, u32[]{:S(2)}) collective-permute-start(f32[40,512]{1,0:T(8,128)} %get-tuple-element.39), channel_id=1, source_target_pairs={{0,4},{4,0},{8,12},{12,8},{1,5},{5,1},{9,13},{13,9},{2,6},{6,2},{1... | collective-permute-start | bytes 245768 | tf_op jit(solution)/shard_map/ppermute | solution.py:735
  3.0 6.4 %collective-permute-start.1 = (f32[40,512]{1,0:T(8,128)}, f32[40,512]{1,0:T(8,128)S(1)}, u32[]{:S(2)}, u32[]{:S(2)}) collective-permute-start(f32[40,512]{1,0:T(8,128)} %get-tuple-element.39), channel_id=1, source_target_pairs={{0,12},{4,8},{8,4},{12,0},{1,13},{5,9},{9,5},{13,1},{2,14},{6,10},... | collective-permute-start | bytes 245768 | tf_op jit(solution)/shard_map/ppermute | solution.py:735
  5.7 0.9 %copy-start = (f32[112,512]{1,0:T(8,128)S(1)}, f32[112,512]{1,0:T(8,128)}, u32[]{:S(2)}) copy-start(f32[112,512]{1,0:T(8,128)} %get-tuple-element.37.po_ref) | copy-start | bytes 688132
  7.8 10.3 %collective-permute-start.2 = (f32[3,1,512]{2,1,0:T(1,128)S(1)}, f32[3,1,512]{2,1,0:T(1,128)S(1)}, u32[]{:S(2)}, u32[]{:S(2)}) collective-permute-start(f32[3,1,512]{2,1,0:T(1,128)S(1)} %get-tuple-element.38.x_ref), channel_id=1, source_target_pairs={{0,1},{1,2},{2,3},{3,0},{4,5},{5,6},{6,7},{7,4},{8,9},{9,10},{10,1... | collective-permute-start | bytes 18440 | tf_op jit(solution)/shard_map/ppermute | solution.py:735
  10.7 7.4 %collective-permute-start.3 = (f32[3,1,512]{2,1,0:T(1,128)S(1)}, f32[3,1,512]{2,1,0:T(1,128)S(1)}, u32[]{:S(2)}, u32[]{:S(2)}) collective-permute-start(f32[3,1,512]{2,1,0:T(1,128)S(1)} %get-tuple-element.59), channel_id=1, source_target_pairs={{0,3},{1,0},{2,1},{3,2},{4,7},{5,4},{6,5},{7,6},{8,11},{9,8},{10,9... | collective-permute-start | bytes 18440 | tf_op jit(solution)/shard_map/ppermute | solution.py:735
  13.4 8.3 %copy-start.2 = (s32[2,1]{0,1:T(1,128)S(1)}, s32[2,1]{0,1:T(1,128)}, u32[]{:S(2)}) copy-start(s32[2,1]{0,1:T(1,128)} %param.17) | copy-start | bytes 28
  13.4 10.0 %copy-start.1 = (f32[112,512]{1,0:T(8,128)S(1)}, f32[112,512]{1,0:T(8,128)}, u32[]{:S(2)}) copy-start(f32[112,512]{1,0:T(8,128)} %get-tuple-element.37.po_ref) | copy-start | bytes 688132
  18.2 5.2 %collective-permute-start.4 = (f32[8,512]{1,0:T(8,128)S(1)}, f32[8,512]{1,0:T(8,128)S(1)}, u32[]{:S(2)}, u32[]{:S(2)}) collective-permute-start(f32[8,512]{1,0:T(8,128)S(1)} %get-tuple-element.60.own_ref), channel_id=1, source_target_pairs={{0,4},{4,0},{8,12},{12,8},{1,5},{5,1},{9,13},{13,9},{2,6},{6,2},{1... | collective-permute-start | bytes 49160 | tf_op jit(solution)/shard_map/ppermute | solution.py:735
  18.4 5.1 %collective-permute-start.5 = (f32[8,512]{1,0:T(8,128)S(1)}, f32[8,512]{1,0:T(8,128)S(1)}, u32[]{:S(2)}, u32[]{:S(2)}) collective-permute-start(f32[8,512]{1,0:T(8,128)S(1)} %get-tuple-element.60.own_ref), channel_id=1, source_target_pairs={{0,12},{4,8},{8,4},{12,0},{1,13},{5,9},{9,5},{13,1},{2,14},{6,10},... | collective-permute-start | bytes 49160 | tf_op jit(solution)/shard_map/ppermute | solution.py:735
  19.8 3.6 %collective-permute-start.6 = (f32[8,128]{1,0:T(8,128)S(1)}, f32[8,128]{1,0:T(8,128)S(1)}, u32[]{:S(2)}, u32[]{:S(2)}) collective-permute-start(f32[8,128]{1,0:T(8,128)S(1)} %get-tuple-element.61.rest_0_), channel_id=1, source_target_pairs={{0,8},{4,12},{8,0},{12,4},{1,9},{5,13},{9,1},{13,5},{2,10},{6,14},... | collective-permute-start | bytes 12296 | tf_op jit(solution)/shard_map/ppermute | solution.py:735
  28.8 5.6 %collective-permute-start.7 = (f32[1,40,128]{2,1,0:T(8,128)S(1)}, f32[1,40,128]{2,1,0:T(8,128)S(1)}, u32[]{:S(2)}, u32[]{:S(2)}) collective-permute-start(f32[1,40,128]{2,1,0:T(8,128)S(1)} %get-tuple-element.62.refs_0_.own_ref), channel_id=1, source_target_pairs={{0,1},{1,2},{2,3},{3,0},{4,5},{5,6},{6,7},{7,4},{8,9},{9,10},{10,1... | collective-permute-start | bytes 61448 | tf_op jit(solution)/shard_map/ppermute | solution.py:735
  28.9 5.6 %collective-permute-start.8 = (f32[1,40,128]{2,1,0:T(8,128)S(1)}, f32[1,40,128]{2,1,0:T(8,128)S(1)}, u32[]{:S(2)}, u32[]{:S(2)}) collective-permute-start(f32[1,40,128]{2,1,0:T(8,128)S(1)} %get-tuple-element.62.refs_0_.own_ref), channel_id=1, source_target_pairs={{0,2},{1,3},{2,0},{3,1},{4,6},{5,7},{6,4},{7,5},{8,10},{9,11},{10,... | collective-permute-start | bytes 61448 | tf_op jit(solution)/shard_map/ppermute | solution.py:735
  30.2 4.9 %collective-permute-start.9 = (f32[1,40,128]{2,1,0:T(8,128)S(1)}, f32[1,40,128]{2,1,0:T(8,128)S(1)}, u32[]{:S(2)}, u32[]{:S(2)}) collective-permute-start(f32[1,40,128]{2,1,0:T(8,128)S(1)} %get-tuple-element.62.refs_0_.own_ref), channel_id=1, source_target_pairs={{0,3},{1,0},{2,1},{3,2},{4,7},{5,4},{6,5},{7,6},{8,11},{9,8},{10,9... | collective-permute-start | bytes 61448 | tf_op jit(solution)/shard_map/ppermute | solution.py:735
  35.2 3.7 %collective-permute-start.10 = (f32[8,128]{1,0:T(8,128)S(1)}, f32[8,128]{1,0:T(8,128)S(1)}, u32[]{:S(2)}, u32[]{:S(2)}) collective-permute-start(f32[8,128]{1,0:T(8,128)S(1)} %get-tuple-element.65.rest_0_), channel_id=1, source_target_pairs={{0,8},{4,12},{8,0},{12,4},{1,9},{5,13},{9,1},{13,5},{2,10},{6,14},... | collective-permute-start | bytes 12296 | tf_op jit(solution)/shard_map/ppermute | solution.py:735
  35.8 3.1 %collective-permute-start.11 = (f32[8,128]{1,0:T(8,128)S(1)}, f32[8,128]{1,0:T(8,128)S(1)}, u32[]{:S(2)}, u32[]{:S(2)}) collective-permute-start(f32[8,128]{1,0:T(8,128)S(1)} %get-tuple-element.65.rest_0_), channel_id=1, source_target_pairs={{0,12},{4,8},{8,4},{12,0},{1,13},{5,9},{9,5},{13,1},{2,14},{6,10},... | collective-permute-start | bytes 12296 | tf_op jit(solution)/shard_map/ppermute | solution.py:735
  35.8 3.1 %collective-permute-start.12 = (f32[8,128]{1,0:T(8,128)S(1)}, f32[8,128]{1,0:T(8,128)S(1)}, u32[]{:S(2)}, u32[]{:S(2)}) collective-permute-start(f32[8,128]{1,0:T(8,128)S(1)} %get-tuple-element.65.rest_0_), channel_id=1, source_target_pairs={{0,4},{4,0},{8,12},{12,8},{1,5},{5,1},{9,13},{13,9},{2,6},{6,2},{1... | collective-permute-start | bytes 12296 | tf_op jit(solution)/shard_map/ppermute | solution.py:735

commit v16 on v15

--- a/solution.py
+++ b/solution.py
@@ -451,19 +451,15 @@
     return jnp.where(even, across, sibling), jnp.where(even, sibling, across)
 
 
-def first_kernel(x_ref, sibling_ref, po_ref, across_ref, *rest):
-    weights, (pl_ref, pr_ref, side_hot, copy_ref), kept, (xs, sst) = rest[:6], rest[6:10], rest[10:19], rest[19:]
-    copy_ref[...] = x_ref[...]
+def first_kernel(sibling_ref, po_ref, across_ref, own_hot, *rest):
+    weights, (out_ref, pl_ref, pr_ref, side_hot), scr = rest[:6], rest[6:10], rest[10:]
+    xs, sst, kept = scr[0], scr[1], scr[2:11]
     pl_ref[...], pr_ref[...] = by_parity(sibling_ref[...], across_ref[...])
     packs = [pl_ref, po_ref, pr_ref]
     mark_sides(packs, side_hot)
     fill_region(xs, packs, lambda s: packs[s][ROW_X : ROW_X + 3, :])
     forward_parts(packs, weights, xs, sst, kept)
-
-
-def first_back_kernel(own_hot, side_hot, *rest):
-    weights, kept, out_ref, scr = rest[:6], rest[6:15], rest[15], rest[16:]
-    out_ref[...] = force_parts(weights, own_hot, side_hot, kept, *scr)
+    out_ref[...] = force_parts(weights, own_hot, side_hot, kept, *scr[11:])
 
 
 def rows_of(ref):
@@ -805,27 +801,19 @@
         flops=100000000,
     )
     before = swap(x_copy, "img", lambda i: (i + 1) % images)
-    left, right, side_hot, x_copy, *kept = call(
+    after = swap(x_copy, "img", lambda i: (i - 1) % images)
+    force_scratch = forward_scratch() + [pltpu.VMEM(*one) for one in kept_shapes()] + back_scratch()
+    force, left, right, side_hot = call(
         first_kernel,
         (
+            shape((3, atoms), F32),
             shape(sent.shape, F32),
             shape(sent.shape, F32),
             shape((SIDE_ROWS, SLOTS * LANES), BF16),
-            shape(x.shape, F32),
-            *[shape(*one) for one in kept_shapes()],
         ),
         (),
-        (x_copy, sibling, pack, across, *weights),
-        forward_scratch(),
-        flops=1000000000,
-    )
-    after = swap(x_copy, "img", lambda i: (i - 1) % images)
-    force = call(
-        first_back_kernel,
-        shape((3, atoms), F32),
-        (),
-        (own_hot, side_hot, *weights, *kept),
-        back_scratch(),
+        (sibling, pack, across, own_hot, *weights),
+        force_scratch,
         flops=1000000000,
     )
     message, sums = call(
@@ -846,7 +834,7 @@
         (shape((1, 40, LANES), F32), shape((3, LANES), F32)),
         (),
         (numbers, left, pack, right, message, near, far, *parts, own_hot, side_hot, *weights),
-        forward_scratch() + [pltpu.VMEM(*one) for one in kept_shapes()] + back_scratch(),
+        force_scratch,
         flops=1000000000,
     )
     rows = 8 * ((images + 7) // 8)

time: 39.9 us -> 39.9 us (level)
  local copies, waits for them, and re-layouts: 0.95 us -> 1.88 us
  Pallas kernels: 16 us -> 15.5 us
  starting transfers between devices: 15.7 us -> 15.3 us
    unnamed x6 -> x8, local copies, waits for them, and re-layouts: 0.95 us -> 1.88 us
    pallas_call x9 -> x8, Pallas kernels: 16 us -> 15.5 us  [call(): pl.pallas_call(body, out_shape=outs, in_specs=[SMEM_SPEC] * len(scalars)...]
    ppermute x13, starting transfers between devices: 15.7 us -> 15.3 us  [swap(): lax.ppermute(array, axis, [(i, partner(i)) for i in range(lax.axis_size(a...]
  transfers between devices with their start and end apart: 13 -> 13, of which waited for: 4 -> 5; matrix products, arithmetic and copies ran while one was open for 0% -> 0% of each run, Pallas kernels for 19% -> 18%
where the time goes in v16:
time: 39.9 us; the launch traced here: 39.6 us
  Pallas kernels  15.5 us (39%)
  starting transfers between devices  15.3 us (38%)
  waiting for transfers between devices  4.94 us (12%)
  between operations  2.04 us (5%)
  local copies, waits for them, and re-layouts  1.88 us (5%)
    pallas_call x8, Pallas kernels, call(): pl.pallas_call(body, out_shape=outs, in_specs=[SMEM_SPEC] * len(scalars)...  15.5 us
    ppermute x13, starting transfers between devices, swap(): lax.ppermute(array, axis, [(i, partner(i)) for i in range(lax.axis_size(a...  15.3 us
    ppermute x13, waiting for transfers between devices, swap(): lax.ppermute(array, axis, [(i, partner(i)) for i in range(lax.axis_size(a...  4.94 us
    unnamed x8, local copies, waits for them, and re-layouts  1.88 us
  transfers between devices with their start and end apart: 13, of which 5 were waited for; matrix products, arithmetic and copies ran while one was open for 0% of the time, Pallas kernels for 18%

profile of v16, /device:TPU:0, one launch (start us, length us, event | category | flops | bytes accessed | tf_op | source)
XLA Modules:
  0.0 39.6 jit_solution(9761269031466184996)
XLA Ops:
  0.6 0.0 copy-start.3
  0.6 1.9 %shard_map.166 = (f32[40,512]{1,0:T(8,128)}, f32[112,512]{1,0:T(8,128)}) custom-call(f32[3,1,512]{2,1,0:T(1,128)} %bitcast.12, f32[3,1,512]{2,1,0:T(1,128)} %bitcast.13, s32[512]{0:T(512)} %refs_2_.1, s32[8,512]{1,0:T(8,128)} %refs_3_.1, s32[512]{0:T(512)} %refs_4_.1, f32[2,64]{1,0:T(2,128)} %refs_5_.1, f32[64]{0:T(128)} %refs_6_.1, f32[2,8,64]{2,1,0:T(8,128)} %refs_7_.1, ...), custom_call_target="tpu_custom_call" | custom-call | bytes 262144 | tf_op jit(solution)/shard_map/pallas_call | solution.py:719
  2.5 0.5 %collective-permute-start = (f32[40,512]{1,0:T(8,128)}, f32[40,512]{1,0:T(8,128)S(1)}, u32[]{:S(2)}, u32[]{:S(2)}) collective-permute-start(f32[40,512]{1,0:T(8,128)} %get-tuple-element.28), channel_id=1, source_target_pairs={{0,4},{4,0},{8,12},{12,8},{1,5},{5,1},{9,13},{13,9},{2,6},{6,2},{1... | collective-permute-start | bytes 245768 | tf_op jit(solution)/shard_map/ppermute | solution.py:731
  3.1 2.6 %collective-permute-start.1 = (f32[40,512]{1,0:T(8,128)}, f32[40,512]{1,0:T(8,128)S(1)}, u32[]{:S(2)}, u32[]{:S(2)}) collective-permute-start(f32[40,512]{1,0:T(8,128)} %get-tuple-element.28), channel_id=1, source_target_pairs={{0,12},{4,8},{8,4},{12,0},{1,13},{5,9},{9,5},{13,1},{2,14},{6,10},... | collective-permute-start | bytes 245768 | tf_op jit(solution)/shard_map/ppermute | solution.py:731
  5.7 0.0 copy-start
  5.7 0.9 %copy-done = f32[112,512]{1,0:T(8,128)S(1)} copy-done((f32[112,512]{1,0:T(8,128)S(1)}, f32[112,512]{1,0:T(8,128)}, u32[]{:S(2)}) %copy-start) | copy-done | bytes 229400
  6.6 0.0 copy-start.2
  6.6 1.2 %shard_map.167 = (bf16[4,384,1024]{2,1,0:T(8,128)(2,1)S(1)}, bf16[64,48]{1,0:T(8,128)(2,1)S(1)}, bf16[64,192]{1,0:T(8,128)(2,1)S(1)}, bf16[64,32]{1,0:T(8,128)(2...) custom-call(f32[112,512]{1,0:T(8,128)S(1)} %copy-done), custom_call_target="tpu_custom_call" | custom-call | flops 100000000 | bytes 262144 | tf_op jit(solution)/shard_map/pallas_call | solution.py:719
  7.8 1.6 %collective-permute-start.2 = (f32[3,1,512]{2,1,0:T(1,128)S(1)}, f32[3,1,512]{2,1,0:T(1,128)S(1)}, u32[]{:S(2)}, u32[]{:S(2)}) collective-permute-start(f32[3,1,512]{2,1,0:T(1,128)S(1)} %get-tuple-element.40), channel_id=1, source_target_pairs={{0,1},{1,2},{2,3},{3,0},{4,5},{5,6},{6,7},{7,4},{8,9},{9,10},{10,1... | collective-permute-start | bytes 18440 | tf_op jit(solution)/shard_map/ppermute | solution.py:731
  9.4 2.2 %collective-permute-start.3 = (f32[3,1,512]{2,1,0:T(1,128)S(1)}, f32[3,1,512]{2,1,0:T(1,128)S(1)}, u32[]{:S(2)}, u32[]{:S(2)}) collective-permute-start(f32[3,1,512]{2,1,0:T(1,128)S(1)} %get-tuple-element.40), channel_id=1, source_target_pairs={{0,3},{1,0},{2,1},{3,2},{4,7},{5,4},{6,5},{7,6},{8,11},{9,8},{10,9... | collective-permute-start | bytes 18440 | tf_op jit(solution)/shard_map/ppermute | solution.py:731
  11.7 0.0 collective-permute-done.sibling_ref
  11.7 0.0 collective-permute-done.1.across_ref
  11.7 0.0 copy-start.1
  11.7 0.9 %copy-done.1 = f32[112,512]{1,0:T(8,128)S(1)} copy-done((f32[112,512]{1,0:T(8,128)S(1)}, f32[112,512]{1,0:T(8,128)}, u32[]{:S(2)}) %copy-start.1) | copy-done | bytes 229400
  12.6 5.4 %shard_map.168 = (f32[3,512]{1,0:T(4,128)S(1)}, f32[40,512]{1,0:T(8,128)S(1)}, f32[40,512]{1,0:T(8,128)S(1)}, bf16[768,1024]{1,0:T(8,128)(2,1)S(1)}) custom-call(f32[40,512]{1,0:T(8,128)S(1)} %collective-permute-done.sibling_ref, f32[112,512]{1,0:T(8,128)S(1)} %copy-done.1, f32[40,512]{1,0:T(8,128)S(1)} %collective-permute-done.1.across_ref, ...), custom_call_target="tpu_custom_call" | custom-call | flops 1000000000 | bytes 262144 | tf_op jit(solution)/shard_map/pallas_call | solution.py:719
  18.0 0.0 collective-permute-done.2.before_ref
  18.0 0.0 collective-permute-done.3.after_ref
  18.0 0.1 shard_map.169
  18.2 0.0 collective-permute-start.4
  18.2 0.5 %collective-permute-start.5 = (f32[8,512]{1,0:T(8,128)S(1)}, f32[8,512]{1,0:T(8,128)S(1)}, u32[]{:S(2)}, u32[]{:S(2)}) collective-permute-start(f32[8,512]{1,0:T(8,128)S(1)} %get-tuple-element.41.own_ref), channel_id=1, source_target_pairs={{0,12},{4,8},{8,4},{12,0},{1,13},{5,9},{9,5},{13,1},{2,14},{6,10},... | collective-permute-start | bytes 49160 | tf_op jit(solution)/shard_map/ppermute | solution.py:731
  18.7 1.6 %collective-permute-start.6 = (f32[8,128]{1,0:T(8,128)S(1)}, f32[8,128]{1,0:T(8,128)S(1)}, u32[]{:S(2)}, u32[]{:S(2)}) collective-permute-start(f32[8,128]{1,0:T(8,128)S(1)} %get-tuple-element.42.rest_0_), channel_id=1, source_target_pairs={{0,8},{4,12},{8,0},{12,4},{1,9},{5,13},{9,1},{13,5},{2,10},{6,14},... | collective-permute-start | bytes 12296 | tf_op jit(solution)/shard_map/ppermute | solution.py:731
  21.6 0.0 copy-done.3
  21.6 0.5 %shard_map.165.number_ref = f32[8,128]{1,0:T(8,128)S(1)} custom-call(f32[1]{0:T(128)S(6)} %copy.19.dt_ref, s32[1,2]{1,0:T(1,128)S(1)} %bitcast.10, s32[1]{0:T(128)S(6)} %copy.20.climb_ref), custom_call_target="tpu_custom_call" | custom-call | bytes 262144 | tf_op jit(solution)/shard_map/pallas_call | solution.py:719
  22.2 0.1 collective-permute-done.6.rest_1_
  22.3 0.0 collective-permute-done.4.near_ref
  22.3 0.0 collective-permute-done.5.far_ref
  22.3 0.0 copy-done.2
  22.3 5.4 %shard_map.170 = (f32[1,40,128]{2,1,0:T(8,128)S(1)}, f32[3,128]{1,0:T(4,128)S(1)}) custom-call(f32[8,128]{1,0:T(8,128)S(1)} %shard_map.165.number_ref, f32[40,512]{1,0:T(8,128)S(1)} %get-tuple-element.37.pl_ref, f32[112,512]{1,0:T(8,128)S(1)} %copy-done.2, f32[40,512]{1,0:T(8,128)S(1)} %get-tuple-element.38.pr_ref, f32[8,512]{1,0:T(8,128)S(1)} %get-tuple-element.41.own_ref, ...), custom_call_target="tpu_custom_call" | custom-call | flops 1000000000 | bytes 262144 | tf_op jit(solution)/shard_map/pallas_call | solution.py:719
  27.7 0.1 collective-permute-start.7
  27.8 2.5 %collective-permute-start.8 = (f32[1,40,128]{2,1,0:T(8,128)S(1)}, f32[1,40,128]{2,1,0:T(8,128)S(1)}, u32[]{:S(2)}, u32[]{:S(2)}) collective-permute-start(f32[1,40,128]{2,1,0:T(8,128)S(1)} %get-tuple-element.44.refs_0_.own_ref), channel_id=1, source_target_pairs={{0,2},{1,3},{2,0},{3,1},{4,6},{5,7},{6,4},{7,5},{8,10},{9,11},{10,... | collective-permute-start | bytes 61448 | tf_op jit(solution)/shard_map/ppermute | solution.py:731
  30.3 1.3 %collective-permute-start.9 = (f32[1,40,128]{2,1,0:T(8,128)S(1)}, f32[1,40,128]{2,1,0:T(8,128)S(1)}, u32[]{:S(2)}, u32[]{:S(2)}) collective-permute-start(f32[1,40,128]{2,1,0:T(8,128)S(1)} %get-tuple-element.44.refs_0_.own_ref), channel_id=1, source_target_pairs={{0,3},{1,0},{2,1},{3,2},{4,7},{5,4},{6,5},{7,6},{8,11},{9,8},{10,9... | collective-permute-start | bytes 61448 | tf_op jit(solution)/shard_map/ppermute | solution.py:731
  31.6 1.7 %collective-permute-done.7.refs_1_ = f32[1,40,128]{2,1,0:T(8,128)S(1)} collective-permute-done((f32[1,40,128]{2,1,0:T(8,128)S(1)}, f32[1,40,128]{2,1,0:T(8,128)S(1)}, u32[]{:S(2)}, u32[]{:S(2)}) %collective-permute-start.7) | collective-permute-done | bytes 20512 | tf_op jit(solution)/shard_map/ppermute | solution.py:731
  33.4 0.0 collective-permute-done.8.refs_2_
  33.4 0.7 %collective-permute-done.9.refs_3_ = f32[1,40,128]{2,1,0:T(8,128)S(1)} collective-permute-done((f32[1,40,128]{2,1,0:T(8,128)S(1)}, f32[1,40,128]{2,1,0:T(8,128)S(1)}, u32[]{:S(2)}, u32[]{:S(2)}) %collective-permute-start.9) | collective-permute-done | bytes 20512 | tf_op jit(solution)/shard_map/ppermute | solution.py:731
  34.1 0.2 shard_map.171
  34.3 1.6 %collective-permute-start.10 = (f32[8,128]{1,0:T(8,128)S(1)}, f32[8,128]{1,0:T(8,128)S(1)}, u32[]{:S(2)}, u32[]{:S(2)}) collective-permute-start(f32[8,128]{1,0:T(8,128)S(1)} %get-tuple-element.47.rest_0_), channel_id=1, source_target_pairs={{0,8},{4,12},{8,0},{12,4},{1,9},{5,13},{9,1},{13,5},{2,10},{6,14},... | collective-permute-start | bytes 12296 | tf_op jit(solution)/shard_map/ppermute | solution.py:731
  35.9 0.0 collective-permute-start.11
  35.9 0.6 %collective-permute-start.12 = (f32[8,128]{1,0:T(8,128)S(1)}, f32[8,128]{1,0:T(8,128)S(1)}, u32[]{:S(2)}, u32[]{:S(2)}) collective-permute-start(f32[8,128]{1,0:T(8,128)S(1)} %get-tuple-element.47.rest_0_), channel_id=1, source_target_pairs={{0,4},{4,0},{8,12},{12,8},{1,5},{5,1},{9,13},{13,9},{2,6},{6,2},{1... | collective-permute-start | bytes 12296 | tf_op jit(solution)/shard_map/ppermute | solution.py:731
  36.5 1.5 %collective-permute-done.10.rest_1_ = f32[8,128]{1,0:T(8,128)S(1)} collective-permute-done((f32[8,128]{1,0:T(8,128)S(1)}, f32[8,128]{1,0:T(8,128)S(1)}, u32[]{:S(2)}, u32[]{:S(2)}) %collective-permute-start.10) | collective-permute-done | bytes 4128 | tf_op jit(solution)/shard_map/ppermute | solution.py:731
  38.0 0.9 %collective-permute-done.11.rest_2_ = f32[8,128]{1,0:T(8,128)S(1)} collective-permute-done((f32[8,128]{1,0:T(8,128)S(1)}, f32[8,128]{1,0:T(8,128)S(1)}, u32[]{:S(2)}, u32[]{:S(2)}) %collective-permute-start.11) | collective-permute-done | bytes 4128 | tf_op jit(solution)/shard_map/ppermute | solution.py:731
  38.9 0.0 collective-permute-done.12.rest_3_
  38.9 0.7 %shard_map.172 = (f32[3,1,512]{2,1,0:T(1,128)}, f32[3,1,512]{2,1,0:T(1,128)}, f32[2,1,2]{2,1,0:T(1,128)}, f32[1,1]{1,0:T(1,128)}) custom-call(f32[1,40,128]{2,1,0:T(8,128)S(1)} %get-tuple-element.44.refs_0_.own_ref, f32[3,128]{1,0:T(4,128)S(1)} %get-tuple-element.45.record_ref, f32[40,128]{1,0:T(8,128)S(1)} %get-tuple-element.46.state_ref, ...), custom_call_target="tpu_custom_call" | custom-call | bytes 262144 | tf_op jit(solution)/shard_map/pallas_call | solution.py:719
Async XLA Ops:
  0.6 21.0 %copy-start.3 = (s32[2,1]{0,1:T(1,128)S(1)}, s32[2,1]{0,1:T(1,128)}, u32[]{:S(2)}) copy-start(s32[2,1]{0,1:T(1,128)} %param.17) | copy-start | bytes 28
  2.5 9.1 %collective-permute-start = (f32[40,512]{1,0:T(8,128)}, f32[40,512]{1,0:T(8,128)S(1)}, u32[]{:S(2)}, u32[]{:S(2)}) collective-permute-start(f32[40,512]{1,0:T(8,128)} %get-tuple-element.28), channel_id=1, source_target_pairs={{0,4},{4,0},{8,12},{12,8},{1,5},{5,1},{9,13},{13,9},{2,6},{6,2},{1... | collective-permute-start | bytes 245768 | tf_op jit(solution)/shard_map/ppermute | solution.py:731
  3.1 8.6 %collective-permute-start.1 = (f32[40,512]{1,0:T(8,128)}, f32[40,512]{1,0:T(8,128)S(1)}, u32[]{:S(2)}, u32[]{:S(2)}) collective-permute-start(f32[40,512]{1,0:T(8,128)} %get-tuple-element.28), channel_id=1, source_target_pairs={{0,12},{4,8},{8,4},{12,0},{1,13},{5,9},{9,5},{13,1},{2,14},{6,10},... | collective-permute-start | bytes 245768 | tf_op jit(solution)/shard_map/ppermute | solution.py:731
  5.7 0.9 %copy-start = (f32[112,512]{1,0:T(8,128)S(1)}, f32[112,512]{1,0:T(8,128)}, u32[]{:S(2)}) copy-start(f32[112,512]{1,0:T(8,128)} %get-tuple-element.29.po_ref) | copy-start | bytes 688132
  6.6 15.7 %copy-start.2 = (f32[112,512]{1,0:T(8,128)S(1)}, f32[112,512]{1,0:T(8,128)}, u32[]{:S(2)}) copy-start(f32[112,512]{1,0:T(8,128)} %get-tuple-element.29.po_ref) | copy-start | bytes 688132
  7.8 10.2 %collective-permute-start.2 = (f32[3,1,512]{2,1,0:T(1,128)S(1)}, f32[3,1,512]{2,1,0:T(1,128)S(1)}, u32[]{:S(2)}, u32[]{:S(2)}) collective-permute-start(f32[3,1,512]{2,1,0:T(1,128)S(1)} %get-tuple-element.40), channel_id=1, source_target_pairs={{0,1},{1,2},{2,3},{3,0},{4,5},{5,6},{6,7},{7,4},{8,9},{9,10},{10,1... | collective-permute-start | bytes 18440 | tf_op jit(solution)/shard_map/ppermute | solution.py:731
  9.4 8.6 %collective-permute-start.3 = (f32[3,1,512]{2,1,0:T(1,128)S(1)}, f32[3,1,512]{2,1,0:T(1,128)S(1)}, u32[]{:S(2)}, u32[]{:S(2)}) collective-permute-start(f32[3,1,512]{2,1,0:T(1,128)S(1)} %get-tuple-element.40), channel_id=1, source_target_pairs={{0,3},{1,0},{2,1},{3,2},{4,7},{5,4},{6,5},{7,6},{8,11},{9,8},{10,9... | collective-permute-start | bytes 18440 | tf_op jit(solution)/shard_map/ppermute | solution.py:731
  11.7 0.9 %copy-start.1 = (f32[112,512]{1,0:T(8,128)S(1)}, f32[112,512]{1,0:T(8,128)}, u32[]{:S(2)}) copy-start(f32[112,512]{1,0:T(8,128)} %get-tuple-element.29.po_ref) | copy-start | bytes 688132
  18.2 4.1 %collective-permute-start.4 = (f32[8,512]{1,0:T(8,128)S(1)}, f32[8,512]{1,0:T(8,128)S(1)}, u32[]{:S(2)}, u32[]{:S(2)}) collective-permute-start(f32[8,512]{1,0:T(8,128)S(1)} %get-tuple-element.41.own_ref), channel_id=1, source_target_pairs={{0,4},{4,0},{8,12},{12,8},{1,5},{5,1},{9,13},{13,9},{2,6},{6,2},{1... | collective-permute-start | bytes 49160 | tf_op jit(solution)/shard_map/ppermute | solution.py:731
  18.2 4.1 %collective-permute-start.5 = (f32[8,512]{1,0:T(8,128)S(1)}, f32[8,512]{1,0:T(8,128)S(1)}, u32[]{:S(2)}, u32[]{:S(2)}) collective-permute-start(f32[8,512]{1,0:T(8,128)S(1)} %get-tuple-element.41.own_ref), channel_id=1, source_target_pairs={{0,12},{4,8},{8,4},{12,0},{1,13},{5,9},{9,5},{13,1},{2,14},{6,10},... | collective-permute-start | bytes 49160 | tf_op jit(solution)/shard_map/ppermute | solution.py:731
  18.7 3.6 %collective-permute-start.6 = (f32[8,128]{1,0:T(8,128)S(1)}, f32[8,128]{1,0:T(8,128)S(1)}, u32[]{:S(2)}, u32[]{:S(2)}) collective-permute-start(f32[8,128]{1,0:T(8,128)S(1)} %get-tuple-element.42.rest_0_), channel_id=1, source_target_pairs={{0,8},{4,12},{8,0},{12,4},{1,9},{5,13},{9,1},{13,5},{2,10},{6,14},... | collective-permute-start | bytes 12296 | tf_op jit(solution)/shard_map/ppermute | solution.py:731
  27.7 5.6 %collective-permute-start.7 = (f32[1,40,128]{2,1,0:T(8,128)S(1)}, f32[1,40,128]{2,1,0:T(8,128)S(1)}, u32[]{:S(2)}, u32[]{:S(2)}) collective-permute-start(f32[1,40,128]{2,1,0:T(8,128)S(1)} %get-tuple-element.44.refs_0_.own_ref), channel_id=1, source_target_pairs={{0,1},{1,2},{2,3},{3,0},{4,5},{5,6},{6,7},{7,4},{8,9},{9,10},{10,1... | collective-permute-start | bytes 61448 | tf_op jit(solution)/shard_map/ppermute | solution.py:731
  27.8 5.6 %collective-permute-start.8 = (f32[1,40,128]{2,1,0:T(8,128)S(1)}, f32[1,40,128]{2,1,0:T(8,128)S(1)}, u32[]{:S(2)}, u32[]{:S(2)}) collective-permute-start(f32[1,40,128]{2,1,0:T(8,128)S(1)} %get-tuple-element.44.refs_0_.own_ref), channel_id=1, source_target_pairs={{0,2},{1,3},{2,0},{3,1},{4,6},{5,7},{6,4},{7,5},{8,10},{9,11},{10,... | collective-permute-start | bytes 61448 | tf_op jit(solution)/shard_map/ppermute | solution.py:731
  30.3 3.8 %collective-permute-start.9 = (f32[1,40,128]{2,1,0:T(8,128)S(1)}, f32[1,40,128]{2,1,0:T(8,128)S(1)}, u32[]{:S(2)}, u32[]{:S(2)}) collective-permute-start(f32[1,40,128]{2,1,0:T(8,128)S(1)} %get-tuple-element.44.refs_0_.own_ref), channel_id=1, source_target_pairs={{0,3},{1,0},{2,1},{3,2},{4,7},{5,4},{6,5},{7,6},{8,11},{9,8},{10,9... | collective-permute-start | bytes 61448 | tf_op jit(solution)/shard_map/ppermute | solution.py:731
  34.3 3.7 %collective-permute-start.10 = (f32[8,128]{1,0:T(8,128)S(1)}, f32[8,128]{1,0:T(8,128)S(1)}, u32[]{:S(2)}, u32[]{:S(2)}) collective-permute-start(f32[8,128]{1,0:T(8,128)S(1)} %get-tuple-element.47.rest_0_), channel_id=1, source_target_pairs={{0,8},{4,12},{8,0},{12,4},{1,9},{5,13},{9,1},{13,5},{2,10},{6,14},... | collective-permute-start | bytes 12296 | tf_op jit(solution)/shard_map/ppermute | solution.py:731
  35.9 3.0 %collective-permute-start.11 = (f32[8,128]{1,0:T(8,128)S(1)}, f32[8,128]{1,0:T(8,128)S(1)}, u32[]{:S(2)}, u32[]{:S(2)}) collective-permute-start(f32[8,128]{1,0:T(8,128)S(1)} %get-tuple-element.47.rest_0_), channel_id=1, source_target_pairs={{0,12},{4,8},{8,4},{12,0},{1,13},{5,9},{9,5},{13,1},{2,14},{6,10},... | collective-permute-start | bytes 12296 | tf_op jit(solution)/shard_map/ppermute | solution.py:731
  35.9 3.0 %collective-permute-start.12 = (f32[8,128]{1,0:T(8,128)S(1)}, f32[8,128]{1,0:T(8,128)S(1)}, u32[]{:S(2)}, u32[]{:S(2)}) collective-permute-start(f32[8,128]{1,0:T(8,128)S(1)} %get-tuple-element.47.rest_0_), channel_id=1, source_target_pairs={{0,4},{4,0},{8,12},{12,8},{1,5},{5,1},{9,13},{13,9},{2,6},{6,2},{1... | collective-permute-start | bytes 12296 | tf_op jit(solution)/shard_map/ppermute | solution.py:731

commit v17 on v16

--- a/solution.py
+++ b/solution.py
@@ -87,7 +87,8 @@
 
 
 def prepare_kernel(po_ref, *rest):
-    own_hot, l1_ref, l2_ref, l3_ref, l5_ref, l6_ref, col_ref, copy_ref = rest
+    own_hot, l1_ref, l2_ref, l3_ref, l5_ref, l6_ref, col_ref, copy_ref, pack_ref = rest
+    pack_ref[...] = po_ref[0:PACK_ROWS, :]
     for b in range(SLAB_BLOCKS):
         mark(window_index(po_ref, b), [0, 1, 2], own_hot.at[b])
     for c in range(3):
@@ -773,7 +774,7 @@
     x = jnp.transpose(disp, (1, 0, 2))
     v = jnp.transpose(veloc, (1, 0, 2))
     small = (x, v, species, neighbours, counts, embed, readout, radial_weight, mix_weight, update_weight)
-    sent, pack = call(
+    sent, kept_pack = call(
         pack_kernel,
         (shape((PACK_ROWS, atoms), F32), shape((OWN_ROWS, atoms), F32)),
         (),
@@ -784,7 +785,7 @@
     )
     sibling = swap(sent, "dom", lambda i: i ^ 1)
     across = swap(sent, "dom", lambda i: (i + 2 * (i % 2) - 1) % domains)
-    own_hot, *weights, x_copy = call(
+    own_hot, *weights, x_copy, pack = call(
         prepare_kernel,
         (
             shape((SLAB_BLOCKS, 3 * LANES, SLOTS * LANES), BF16),
@@ -795,9 +796,10 @@
             shape((16, 192), BF16),
             shape((4, CHANNELS, LANES), F32),
             shape(x.shape, F32),
+            shape(sent.shape, F32),
         ),
         (),
-        (pack,),
+        (kept_pack,),
         flops=100000000,
     )
     before = swap(x_copy, "img", lambda i: (i + 1) % images)

time: 39.9 us -> 38.9 us (0.975)
  local copies, waits for them, and re-layouts: 1.88 us -> 0.94 us
    unnamed x8 -> x4, local copies, waits for them, and re-layouts: 1.88 us -> 0.94 us
where the time goes in v17:
time: 38.9 us; the launch traced here: 38.7 us
  Pallas kernels  15.5 us (40%)
  starting transfers between devices  15.3 us (39%)
  waiting for transfers between devices  4.93 us (13%)
  between operations  2.03 us (5%)
  local copies, waits for them, and re-layouts  0.94 us (2%)
    pallas_call x8, Pallas kernels, call(): pl.pallas_call(body, out_shape=outs, in_specs=[SMEM_SPEC] * len(scalars)...  15.5 us
    ppermute x13, starting transfers between devices, swap(): lax.ppermute(array, axis, [(i, partner(i)) for i in range(lax.axis_size(a...  15.3 us
    ppermute x13, waiting for transfers between devices, swap(): lax.ppermute(array, axis, [(i, partner(i)) for i in range(lax.axis_size(a...  4.93 us
    unnamed x4, local copies, waits for them, and re-layouts  0.94 us
  transfers between devices with their start and end apart: 13, of which 5 were waited for; matrix products, arithmetic and copies ran while one was open for 0% of the time, Pallas kernels for 18%

profile of v17, /device:TPU:0, one launch (start us, length us, event | category | flops | bytes accessed | tf_op | source)
XLA Modules:
  0.0 38.7 jit_solution(16007768333877323366)
XLA Ops:
  0.6 0.0 copy-start
  0.6 1.9 %shard_map.166 = (f32[40,512]{1,0:T(8,128)}, f32[112,512]{1,0:T(8,128)}) custom-call(f32[3,1,512]{2,1,0:T(1,128)} %bitcast.12, f32[3,1,512]{2,1,0:T(1,128)} %bitcast.13, s32[512]{0:T(512)} %refs_2_.1, s32[8,512]{1,0:T(8,128)} %refs_3_.1, s32[512]{0:T(512)} %refs_4_.1, f32[2,64]{1,0:T(2,128)} %refs_5_.1, f32[64]{0:T(128)} %refs_6_.1, f32[2,8,64]{2,1,0:T(8,128)} %refs_7_.1, ...), custom_call_target="tpu_custom_call" | custom-call | bytes 262144 | tf_op jit(solution)/shard_map/pallas_call | solution.py:720
  2.5 0.5 %collective-permute-start = (f32[40,512]{1,0:T(8,128)}, f32[40,512]{1,0:T(8,128)S(1)}, u32[]{:S(2)}, u32[]{:S(2)}) collective-permute-start(f32[40,512]{1,0:T(8,128)} %get-tuple-element.29), channel_id=1, source_target_pairs={{0,4},{4,0},{8,12},{12,8},{1,5},{5,1},{9,13},{13,9},{2,6},{6,2},{1... | collective-permute-start | bytes 245768 | tf_op jit(solution)/shard_map/ppermute | solution.py:732
  3.1 2.6 %collective-permute-start.1 = (f32[40,512]{1,0:T(8,128)}, f32[40,512]{1,0:T(8,128)S(1)}, u32[]{:S(2)}, u32[]{:S(2)}) collective-permute-start(f32[40,512]{1,0:T(8,128)} %get-tuple-element.29), channel_id=1, source_target_pairs={{0,12},{4,8},{8,4},{12,0},{1,13},{5,9},{9,5},{13,1},{2,14},{6,10},... | collective-permute-start | bytes 245768 | tf_op jit(solution)/shard_map/ppermute | solution.py:732
  5.7 0.0 copy-start.1
  5.7 0.9 %copy-done.1 = f32[112,512]{1,0:T(8,128)S(1)} copy-done((f32[112,512]{1,0:T(8,128)S(1)}, f32[112,512]{1,0:T(8,128)}, u32[]{:S(2)}) %copy-start.1) | copy-done | bytes 229400
  6.6 1.2 %shard_map.167 = (bf16[4,384,1024]{2,1,0:T(8,128)(2,1)S(1)}, bf16[64,48]{1,0:T(8,128)(2,1)S(1)}, bf16[64,192]{1,0:T(8,128)(2,1)S(1)}, bf16[64,32]{1,0:T(8,128)(2...) custom-call(f32[112,512]{1,0:T(8,128)S(1)} %copy-done.1), custom_call_target="tpu_custom_call" | custom-call | flops 100000000 | bytes 262144 | tf_op jit(solution)/shard_map/pallas_call | solution.py:720
  7.8 1.6 %collective-permute-start.2 = (f32[3,1,512]{2,1,0:T(1,128)S(1)}, f32[3,1,512]{2,1,0:T(1,128)S(1)}, u32[]{:S(2)}, u32[]{:S(2)}) collective-permute-start(f32[3,1,512]{2,1,0:T(1,128)S(1)} %get-tuple-element.42), channel_id=1, source_target_pairs={{0,1},{1,2},{2,3},{3,0},{4,5},{5,6},{6,7},{7,4},{8,9},{9,10},{10,1... | collective-permute-start | bytes 18440 | tf_op jit(solution)/shard_map/ppermute | solution.py:732
  9.4 2.2 %collective-permute-start.3 = (f32[3,1,512]{2,1,0:T(1,128)S(1)}, f32[3,1,512]{2,1,0:T(1,128)S(1)}, u32[]{:S(2)}, u32[]{:S(2)}) collective-permute-start(f32[3,1,512]{2,1,0:T(1,128)S(1)} %get-tuple-element.42), channel_id=1, source_target_pairs={{0,3},{1,0},{2,1},{3,2},{4,7},{5,4},{6,5},{7,6},{8,11},{9,8},{10,9... | collective-permute-start | bytes 18440 | tf_op jit(solution)/shard_map/ppermute | solution.py:732
  11.7 0.0 collective-permute-done.sibling_ref
  11.7 0.0 collective-permute-done.1.across_ref
  11.7 5.4 %shard_map.168 = (f32[3,512]{1,0:T(4,128)S(1)}, f32[40,512]{1,0:T(8,128)S(1)}, f32[40,512]{1,0:T(8,128)S(1)}, bf16[768,1024]{1,0:T(8,128)(2,1)S(1)}) custom-call(f32[40,512]{1,0:T(8,128)S(1)} %collective-permute-done.sibling_ref, f32[40,512]{1,0:T(8,128)S(1)} %get-tuple-element.31.po_ref, f32[40,512]{1,0:T(8,128)S(1)} %collective-permute-done.1.across_ref, ...), custom_call_target="tpu_custom_call" | custom-call | flops 1000000000 | bytes 262144 | tf_op jit(solution)/shard_map/pallas_call | solution.py:720
  17.1 0.0 collective-permute-done.2.before_ref
  17.1 0.0 collective-permute-done.3.after_ref
  17.1 0.1 shard_map.169
  17.2 0.0 collective-permute-start.4
  17.2 0.5 %collective-permute-start.5 = (f32[8,512]{1,0:T(8,128)S(1)}, f32[8,512]{1,0:T(8,128)S(1)}, u32[]{:S(2)}, u32[]{:S(2)}) collective-permute-start(f32[8,512]{1,0:T(8,128)S(1)} %get-tuple-element.43.own_ref), channel_id=1, source_target_pairs={{0,12},{4,8},{8,4},{12,0},{1,13},{5,9},{9,5},{13,1},{2,14},{6,10},... | collective-permute-start | bytes 49160 | tf_op jit(solution)/shard_map/ppermute | solution.py:732
  17.7 1.6 %collective-permute-start.6 = (f32[8,128]{1,0:T(8,128)S(1)}, f32[8,128]{1,0:T(8,128)S(1)}, u32[]{:S(2)}, u32[]{:S(2)}) collective-permute-start(f32[8,128]{1,0:T(8,128)S(1)} %get-tuple-element.44.rest_0_), channel_id=1, source_target_pairs={{0,8},{4,12},{8,0},{12,4},{1,9},{5,13},{9,1},{13,5},{2,10},{6,14},... | collective-permute-start | bytes 12296 | tf_op jit(solution)/shard_map/ppermute | solution.py:732
  20.7 0.0 copy-done
  20.7 0.5 %shard_map.165.number_ref = f32[8,128]{1,0:T(8,128)S(1)} custom-call(f32[1]{0:T(128)S(6)} %copy.19.dt_ref, s32[1,2]{1,0:T(1,128)S(1)} %bitcast.10, s32[1]{0:T(128)S(6)} %copy.20.climb_ref), custom_call_target="tpu_custom_call" | custom-call | bytes 262144 | tf_op jit(solution)/shard_map/pallas_call | solution.py:720
  21.2 0.1 collective-permute-done.6.rest_1_
  21.3 0.0 collective-permute-done.4.near_ref
  21.3 0.0 collective-permute-done.5.far_ref
  21.3 5.4 %shard_map.170 = (f32[1,40,128]{2,1,0:T(8,128)S(1)}, f32[3,128]{1,0:T(4,128)S(1)}) custom-call(f32[8,128]{1,0:T(8,128)S(1)} %shard_map.165.number_ref, f32[40,512]{1,0:T(8,128)S(1)} %get-tuple-element.39.pl_ref, f32[40,512]{1,0:T(8,128)S(1)} %get-tuple-element.31.po_ref, f32[40,512]{1,0:T(8,128)S(1)} %get-tuple-element.40.pr_ref, ...), custom_call_target="tpu_custom_call" | custom-call | flops 1000000000 | bytes 262144 | tf_op jit(solution)/shard_map/pallas_call | solution.py:720
  26.7 0.1 collective-permute-start.7
  26.8 2.5 %collective-permute-start.8 = (f32[1,40,128]{2,1,0:T(8,128)S(1)}, f32[1,40,128]{2,1,0:T(8,128)S(1)}, u32[]{:S(2)}, u32[]{:S(2)}) collective-permute-start(f32[1,40,128]{2,1,0:T(8,128)S(1)} %get-tuple-element.46.refs_0_.own_ref), channel_id=1, source_target_pairs={{0,2},{1,3},{2,0},{3,1},{4,6},{5,7},{6,4},{7,5},{8,10},{9,11},{10,... | collective-permute-start | bytes 61448 | tf_op jit(solution)/shard_map/ppermute | solution.py:732
  29.3 1.3 %collective-permute-start.9 = (f32[1,40,128]{2,1,0:T(8,128)S(1)}, f32[1,40,128]{2,1,0:T(8,128)S(1)}, u32[]{:S(2)}, u32[]{:S(2)}) collective-permute-start(f32[1,40,128]{2,1,0:T(8,128)S(1)} %get-tuple-element.46.refs_0_.own_ref), channel_id=1, source_target_pairs={{0,3},{1,0},{2,1},{3,2},{4,7},{5,4},{6,5},{7,6},{8,11},{9,8},{10,9... | collective-permute-start | bytes 61448 | tf_op jit(solution)/shard_map/ppermute | solution.py:732
  30.7 1.7 %collective-permute-done.7.refs_1_ = f32[1,40,128]{2,1,0:T(8,128)S(1)} collective-permute-done((f32[1,40,128]{2,1,0:T(8,128)S(1)}, f32[1,40,128]{2,1,0:T(8,128)S(1)}, u32[]{:S(2)}, u32[]{:S(2)}) %collective-permute-start.7) | collective-permute-done | bytes 20512 | tf_op jit(solution)/shard_map/ppermute | solution.py:732
  32.4 0.0 collective-permute-done.8.refs_2_
  32.4 0.7 %collective-permute-done.9.refs_3_ = f32[1,40,128]{2,1,0:T(8,128)S(1)} collective-permute-done((f32[1,40,128]{2,1,0:T(8,128)S(1)}, f32[1,40,128]{2,1,0:T(8,128)S(1)}, u32[]{:S(2)}, u32[]{:S(2)}) %collective-permute-start.9) | collective-permute-done | bytes 20512 | tf_op jit(solution)/shard_map/ppermute | solution.py:732
  33.1 0.2 shard_map.171
  33.3 1.6 %collective-permute-start.10 = (f32[8,128]{1,0:T(8,128)S(1)}, f32[8,128]{1,0:T(8,128)S(1)}, u32[]{:S(2)}, u32[]{:S(2)}) collective-permute-start(f32[8,128]{1,0:T(8,128)S(1)} %get-tuple-element.49.rest_0_), channel_id=1, source_target_pairs={{0,8},{4,12},{8,0},{12,4},{1,9},{5,13},{9,1},{13,5},{2,10},{6,14},... | collective-permute-start | bytes 12296 | tf_op jit(solution)/shard_map/ppermute | solution.py:732
  34.9 0.0 collective-permute-start.11
  34.9 0.6 %collective-permute-start.12 = (f32[8,128]{1,0:T(8,128)S(1)}, f32[8,128]{1,0:T(8,128)S(1)}, u32[]{:S(2)}, u32[]{:S(2)}) collective-permute-start(f32[8,128]{1,0:T(8,128)S(1)} %get-tuple-element.49.rest_0_), channel_id=1, source_target_pairs={{0,4},{4,0},{8,12},{12,8},{1,5},{5,1},{9,13},{13,9},{2,6},{6,2},{1... | collective-permute-start | bytes 12296 | tf_op jit(solution)/shard_map/ppermute | solution.py:732
  35.5 1.5 %collective-permute-done.10.rest_1_ = f32[8,128]{1,0:T(8,128)S(1)} collective-permute-done((f32[8,128]{1,0:T(8,128)S(1)}, f32[8,128]{1,0:T(8,128)S(1)}, u32[]{:S(2)}, u32[]{:S(2)}) %collective-permute-start.10) | collective-permute-done | bytes 4128 | tf_op jit(solution)/shard_map/ppermute | solution.py:732
  37.0 0.9 %collective-permute-done.11.rest_2_ = f32[8,128]{1,0:T(8,128)S(1)} collective-permute-done((f32[8,128]{1,0:T(8,128)S(1)}, f32[8,128]{1,0:T(8,128)S(1)}, u32[]{:S(2)}, u32[]{:S(2)}) %collective-permute-start.11) | collective-permute-done | bytes 4128 | tf_op jit(solution)/shard_map/ppermute | solution.py:732
  37.9 0.0 collective-permute-done.12.rest_3_
  37.9 0.7 %shard_map.172 = (f32[3,1,512]{2,1,0:T(1,128)}, f32[3,1,512]{2,1,0:T(1,128)}, f32[2,1,2]{2,1,0:T(1,128)}, f32[1,1]{1,0:T(1,128)}) custom-call(f32[1,40,128]{2,1,0:T(8,128)S(1)} %get-tuple-element.46.refs_0_.own_ref, f32[3,128]{1,0:T(4,128)S(1)} %get-tuple-element.47.record_ref, f32[40,128]{1,0:T(8,128)S(1)} %get-tuple-element.48.state_ref, ...), custom_call_target="tpu_custom_call" | custom-call | bytes 262144 | tf_op jit(solution)/shard_map/pallas_call | solution.py:720
Async XLA Ops:
  0.6 20.0 %copy-start = (s32[2,1]{0,1:T(1,128)S(1)}, s32[2,1]{0,1:T(1,128)}, u32[]{:S(2)}) copy-start(s32[2,1]{0,1:T(1,128)} %param.17) | copy-start | bytes 28
  2.5 9.1 %collective-permute-start = (f32[40,512]{1,0:T(8,128)}, f32[40,512]{1,0:T(8,128)S(1)}, u32[]{:S(2)}, u32[]{:S(2)}) collective-permute-start(f32[40,512]{1,0:T(8,128)} %get-tuple-element.29), channel_id=1, source_target_pairs={{0,4},{4,0},{8,12},{12,8},{1,5},{5,1},{9,13},{13,9},{2,6},{6,2},{1... | collective-permute-start | bytes 245768 | tf_op jit(solution)/shard_map/ppermute | solution.py:732
  3.1 8.6 %collective-permute-start.1 = (f32[40,512]{1,0:T(8,128)}, f32[40,512]{1,0:T(8,128)S(1)}, u32[]{:S(2)}, u32[]{:S(2)}) collective-permute-start(f32[40,512]{1,0:T(8,128)} %get-tuple-element.29), channel_id=1, source_target_pairs={{0,12},{4,8},{8,4},{12,0},{1,13},{5,9},{9,5},{13,1},{2,14},{6,10},... | collective-permute-start | bytes 245768 | tf_op jit(solution)/shard_map/ppermute | solution.py:732
  5.7 0.9 %copy-start.1 = (f32[112,512]{1,0:T(8,128)S(1)}, f32[112,512]{1,0:T(8,128)}, u32[]{:S(2)}) copy-start(f32[112,512]{1,0:T(8,128)} %get-tuple-element.30.po_ref) | copy-start | bytes 688132
  7.8 9.2 %collective-permute-start.2 = (f32[3,1,512]{2,1,0:T(1,128)S(1)}, f32[3,1,512]{2,1,0:T(1,128)S(1)}, u32[]{:S(2)}, u32[]{:S(2)}) collective-permute-start(f32[3,1,512]{2,1,0:T(1,128)S(1)} %get-tuple-element.42), channel_id=1, source_target_pairs={{0,1},{1,2},{2,3},{3,0},{4,5},{5,6},{6,7},{7,4},{8,9},{9,10},{10,1... | collective-permute-start | bytes 18440 | tf_op jit(solution)/shard_map/ppermute | solution.py:732
  9.4 7.6 %collective-permute-start.3 = (f32[3,1,512]{2,1,0:T(1,128)S(1)}, f32[3,1,512]{2,1,0:T(1,128)S(1)}, u32[]{:S(2)}, u32[]{:S(2)}) collective-permute-start(f32[3,1,512]{2,1,0:T(1,128)S(1)} %get-tuple-element.42), channel_id=1, source_target_pairs={{0,3},{1,0},{2,1},{3,2},{4,7},{5,4},{6,5},{7,6},{8,11},{9,8},{10,9... | collective-permute-start | bytes 18440 | tf_op jit(solution)/shard_map/ppermute | solution.py:732
  17.2 4.1 %collective-permute-start.4 = (f32[8,512]{1,0:T(8,128)S(1)}, f32[8,512]{1,0:T(8,128)S(1)}, u32[]{:S(2)}, u32[]{:S(2)}) collective-permute-start(f32[8,512]{1,0:T(8,128)S(1)} %get-tuple-element.43.own_ref), channel_id=1, source_target_pairs={{0,4},{4,0},{8,12},{12,8},{1,5},{5,1},{9,13},{13,9},{2,6},{6,2},{1... | collective-permute-start | bytes 49160 | tf_op jit(solution)/shard_map/ppermute | solution.py:732
  17.2 4.1 %collective-permute-start.5 = (f32[8,512]{1,0:T(8,128)S(1)}, f32[8,512]{1,0:T(8,128)S(1)}, u32[]{:S(2)}, u32[]{:S(2)}) collective-permute-start(f32[8,512]{1,0:T(8,128)S(1)} %get-tuple-element.43.own_ref), channel_id=1, source_target_pairs={{0,12},{4,8},{8,4},{12,0},{1,13},{5,9},{9,5},{13,1},{2,14},{6,10},... | collective-permute-start | bytes 49160 | tf_op jit(solution)/shard_map/ppermute | solution.py:732
  17.7 3.6 %collective-permute-start.6 = (f32[8,128]{1,0:T(8,128)S(1)}, f32[8,128]{1,0:T(8,128)S(1)}, u32[]{:S(2)}, u32[]{:S(2)}) collective-permute-start(f32[8,128]{1,0:T(8,128)S(1)} %get-tuple-element.44.rest_0_), channel_id=1, source_target_pairs={{0,8},{4,12},{8,0},{12,4},{1,9},{5,13},{9,1},{13,5},{2,10},{6,14},... | collective-permute-start | bytes 12296 | tf_op jit(solution)/shard_map/ppermute | solution.py:732
  26.7 5.6 %collective-permute-start.7 = (f32[1,40,128]{2,1,0:T(8,128)S(1)}, f32[1,40,128]{2,1,0:T(8,128)S(1)}, u32[]{:S(2)}, u32[]{:S(2)}) collective-permute-start(f32[1,40,128]{2,1,0:T(8,128)S(1)} %get-tuple-element.46.refs_0_.own_ref), channel_id=1, source_target_pairs={{0,1},{1,2},{2,3},{3,0},{4,5},{5,6},{6,7},{7,4},{8,9},{9,10},{10,1... | collective-permute-start | bytes 61448 | tf_op jit(solution)/shard_map/ppermute | solution.py:732
  26.8 5.6 %collective-permute-start.8 = (f32[1,40,128]{2,1,0:T(8,128)S(1)}, f32[1,40,128]{2,1,0:T(8,128)S(1)}, u32[]{:S(2)}, u32[]{:S(2)}) collective-permute-start(f32[1,40,128]{2,1,0:T(8,128)S(1)} %get-tuple-element.46.refs_0_.own_ref), channel_id=1, source_target_pairs={{0,2},{1,3},{2,0},{3,1},{4,6},{5,7},{6,4},{7,5},{8,10},{9,11},{10,... | collective-permute-start | bytes 61448 | tf_op jit(solution)/shard_map/ppermute | solution.py:732
  29.3 3.8 %collective-permute-start.9 = (f32[1,40,128]{2,1,0:T(8,128)S(1)}, f32[1,40,128]{2,1,0:T(8,128)S(1)}, u32[]{:S(2)}, u32[]{:S(2)}) collective-permute-start(f32[1,40,128]{2,1,0:T(8,128)S(1)} %get-tuple-element.46.refs_0_.own_ref), channel_id=1, source_target_pairs={{0,3},{1,0},{2,1},{3,2},{4,7},{5,4},{6,5},{7,6},{8,11},{9,8},{10,9... | collective-permute-start | bytes 61448 | tf_op jit(solution)/shard_map/ppermute | solution.py:732
  33.3 3.7 %collective-permute-start.10 = (f32[8,128]{1,0:T(8,128)S(1)}, f32[8,128]{1,0:T(8,128)S(1)}, u32[]{:S(2)}, u32[]{:S(2)}) collective-permute-start(f32[8,128]{1,0:T(8,128)S(1)} %get-tuple-element.49.rest_0_), channel_id=1, source_target_pairs={{0,8},{4,12},{8,0},{12,4},{1,9},{5,13},{9,1},{13,5},{2,10},{6,14},... | collective-permute-start | bytes 12296 | tf_op jit(solution)/shard_map/ppermute | solution.py:732
  34.9 3.0 %collective-permute-start.11 = (f32[8,128]{1,0:T(8,128)S(1)}, f32[8,128]{1,0:T(8,128)S(1)}, u32[]{:S(2)}, u32[]{:S(2)}) collective-permute-start(f32[8,128]{1,0:T(8,128)S(1)} %get-tuple-element.49.rest_0_), channel_id=1, source_target_pairs={{0,12},{4,8},{8,4},{12,0},{1,13},{5,9},{9,5},{13,1},{2,14},{6,10},... | collective-permute-start | bytes 12296 | tf_op jit(solution)/shard_map/ppermute | solution.py:732
  34.9 3.0 %collective-permute-start.12 = (f32[8,128]{1,0:T(8,128)S(1)}, f32[8,128]{1,0:T(8,128)S(1)}, u32[]{:S(2)}, u32[]{:S(2)}) collective-permute-start(f32[8,128]{1,0:T(8,128)S(1)} %get-tuple-element.49.rest_0_), channel_id=1, source_target_pairs={{0,4},{4,0},{8,12},{12,8},{1,5},{5,1},{9,13},{13,9},{2,6},{6,2},{1... | collective-permute-start | bytes 12296 | tf_op jit(solution)/shard_map/ppermute | solution.py:732

commit v18 on v17

--- a/solution.py
+++ b/solution.py
@@ -602,18 +602,26 @@
 
 
 def gram_kernel(images, *refs):
-    parts, (out_ref, state_ref, messages_ref) = refs[:-3], refs[-3:]
+    parts, after_ref, (out_ref, state_ref, messages_ref) = refs[:-4], refs[-4], refs[-3:]
     rows = out_ref.shape[0]
-    place = 0
-    for part in parts:
-        messages_ref[place : place + part.shape[0]] = part[...]
-        place += part.shape[0]
     here = lax.axis_index("img")
+    if images == 4:
+        places = [here, lax.rem(here + 3, 4), jnp.where(here < 2, 3 - here, here - 2)]
+        messages_ref[...] = jnp.zeros(messages_ref.shape, F32)
+        follower = lax.rem(here + 1, 4)
+        for c in range(3):
+            for i in range(SLAB_BLOCKS):
+                row = 24 + 4 * c + i
+                messages_ref[follower, row : row + 1, :] = after_ref[c][:, i * LANES : (i + 1) * LANES]
+    else:
+        places = [lax.rem(here + images - s, images) for s in range(images)]
+    for place, part in zip(places, parts):
+        messages_ref[place] = part[0]
     blank = [jnp.zeros((rows - images, LANES), F32)] if rows > images else []
     zero = jnp.zeros((1, LANES), F32)
 
     def gathered(row):
-        return jnp.concatenate([messages_ref[lax.rem(here + images - i, images), row : row + 1, :] for i in range(images)] + blank, axis=0)
+        return jnp.concatenate([messages_ref[i, row : row + 1, :] for i in range(images)] + blank, axis=0)
 
     def earlier(value):
         return jnp.concatenate([zero, value[0 : rows - 1]], axis=0)
@@ -744,9 +752,11 @@
     return [sums]
 
 
-def collected(array, axis):
+def collected(state, axis, after):
     count = lax.axis_size(axis)
-    return [array] + [swap(array, axis, lambda i, by=by: (i + by) % count) for by in range(1, count)]
+    if count == 4:
+        return [state, swap(state, axis, lambda i: (i + 1) % 4), swap(state, axis, lambda i: (2, 3, 1, 0)[i]), after]
+    return [state] + [swap(state, axis, lambda i, by=by: (i + by) % count) for by in range(1, count)] + [after]
 
 
 def local(
@@ -844,7 +854,7 @@
         functools.partial(gram_kernel, images),
         (shape((rows, LANES), F32), shape((16 + 3 * rows, LANES), F32)),
         (),
-        collected(state, "img"),
+        collected(state, "img", after),
         [pltpu.VMEM((images, 40, LANES), F32)],
     )
     new_x, new_v, records, path = call(

time: 38.9 us -> 39 us (level)
    ppermute x13 -> x12, starting transfers between devices: 15.3 us -> 15.5 us  [swap(): lax.ppermute(array, axis, [(i, partner(i)) for i in range(lax.axis_size(a...]
    ppermute x13 -> x12, waiting for transfers between devices: 4.93 us -> 4.83 us  [swap(): lax.ppermute(array, axis, [(i, partner(i)) for i in range(lax.axis_size(a...]
  transfers between devices with their start and end apart: 13 -> 12, of which waited for: 5 -> 5; matrix products, arithmetic and copies ran while one was open for 0% -> 0% of each run, Pallas kernels for 18% -> 18%
where the time goes in v18:
time: 39 us; the launch traced here: 38.8 us
  Pallas kernels  15.5 us (40%)
  starting transfers between devices  15.5 us (40%)
  waiting for transfers between devices  4.83 us (12%)
  between operations  2.03 us (5%)
  local copies, waits for them, and re-layouts  0.94 us (2%)
    ppermute x12, starting transfers between devices, swap(): lax.ppermute(array, axis, [(i, partner(i)) for i in range(lax.axis_size(a...  15.5 us
    pallas_call x8, Pallas kernels, call(): pl.pallas_call(body, out_shape=outs, in_specs=[SMEM_SPEC] * len(scalars)...  15.5 us
    ppermute x12, waiting for transfers between devices, swap(): lax.ppermute(array, axis, [(i, partner(i)) for i in range(lax.axis_size(a...  4.83 us
    unnamed x4, local copies, waits for them, and re-layouts  0.94 us
  transfers between devices with their start and end apart: 12, of which 5 were waited for; matrix products, arithmetic and copies ran while one was open for 0% of the time, Pallas kernels for 18%

profile of v18, /device:TPU:0, one launch (start us, length us, event | category | flops | bytes accessed | tf_op | source)
XLA Modules:
  0.0 38.8 jit_solution(7196191209264612208)
XLA Ops:
  0.6 0.0 copy-start
  0.6 1.9 %shard_map.166 = (f32[40,512]{1,0:T(8,128)}, f32[112,512]{1,0:T(8,128)}) custom-call(f32[3,1,512]{2,1,0:T(1,128)} %bitcast.12, f32[3,1,512]{2,1,0:T(1,128)} %bitcast.13, s32[512]{0:T(512)} %refs_2_.1, s32[8,512]{1,0:T(8,128)} %refs_3_.1, s32[512]{0:T(512)} %refs_4_.1, f32[2,64]{1,0:T(2,128)} %refs_5_.1, f32[64]{0:T(128)} %refs_6_.1, f32[2,8,64]{2,1,0:T(8,128)} %refs_7_.1, ...), custom_call_target="tpu_custom_call" | custom-call | bytes 262144 | tf_op jit(solution)/shard_map/pallas_call | solution.py:728
  2.5 0.5 %collective-permute-start = (f32[40,512]{1,0:T(8,128)}, f32[40,512]{1,0:T(8,128)S(1)}, u32[]{:S(2)}, u32[]{:S(2)}) collective-permute-start(f32[40,512]{1,0:T(8,128)} %get-tuple-element.29), channel_id=1, source_target_pairs={{0,4},{4,0},{8,12},{12,8},{1,5},{5,1},{9,13},{13,9},{2,6},{6,2},{1... | collective-permute-start | bytes 245768 | tf_op jit(solution)/shard_map/ppermute | solution.py:740
  3.0 2.6 %collective-permute-start.1 = (f32[40,512]{1,0:T(8,128)}, f32[40,512]{1,0:T(8,128)S(1)}, u32[]{:S(2)}, u32[]{:S(2)}) collective-permute-start(f32[40,512]{1,0:T(8,128)} %get-tuple-element.29), channel_id=1, source_target_pairs={{0,12},{4,8},{8,4},{12,0},{1,13},{5,9},{9,5},{13,1},{2,14},{6,10},... | collective-permute-start | bytes 245768 | tf_op jit(solution)/shard_map/ppermute | solution.py:740
  5.7 0.0 copy-start.1
  5.7 0.9 %copy-done.1 = f32[112,512]{1,0:T(8,128)S(1)} copy-done((f32[112,512]{1,0:T(8,128)S(1)}, f32[112,512]{1,0:T(8,128)}, u32[]{:S(2)}) %copy-start.1) | copy-done | bytes 229400
  6.6 1.2 %shard_map.167 = (bf16[4,384,1024]{2,1,0:T(8,128)(2,1)S(1)}, bf16[64,48]{1,0:T(8,128)(2,1)S(1)}, bf16[64,192]{1,0:T(8,128)(2,1)S(1)}, bf16[64,32]{1,0:T(8,128)(2...) custom-call(f32[112,512]{1,0:T(8,128)S(1)} %copy-done.1), custom_call_target="tpu_custom_call" | custom-call | flops 100000000 | bytes 262144 | tf_op jit(solution)/shard_map/pallas_call | solution.py:728
  7.8 3.6 %collective-permute-start.3 = (f32[3,1,512]{2,1,0:T(1,128)S(1)}, f32[3,1,512]{2,1,0:T(1,128)S(1)}, u32[]{:S(2)}, u32[]{:S(2)}) collective-permute-start(f32[3,1,512]{2,1,0:T(1,128)S(1)} %get-tuple-element.42), channel_id=1, source_target_pairs={{0,3},{1,0},{2,1},{3,2},{4,7},{5,4},{6,5},{7,6},{8,11},{9,8},{10,9... | collective-permute-start | bytes 18440 | tf_op jit(solution)/shard_map/ppermute | solution.py:740
  11.4 0.0 collective-permute-start.2
  11.5 0.0 collective-permute-done.sibling_ref
  11.5 0.0 collective-permute-done.1.across_ref
  11.5 5.4 %shard_map.168 = (f32[3,512]{1,0:T(4,128)S(1)}, f32[40,512]{1,0:T(8,128)S(1)}, f32[40,512]{1,0:T(8,128)S(1)}, bf16[768,1024]{1,0:T(8,128)(2,1)S(1)}) custom-call(f32[40,512]{1,0:T(8,128)S(1)} %collective-permute-done.sibling_ref, f32[40,512]{1,0:T(8,128)S(1)} %get-tuple-element.31.po_ref, f32[40,512]{1,0:T(8,128)S(1)} %collective-permute-done.1.across_ref, ...), custom_call_target="tpu_custom_call" | custom-call | flops 1000000000 | bytes 262144 | tf_op jit(solution)/shard_map/pallas_call | solution.py:728
  16.8 0.0 collective-permute-done.3.after_ref.refs_3_
  16.9 0.0 collective-permute-done.2.before_ref
  16.9 0.1 shard_map.169
  17.0 0.0 collective-permute-start.4
  17.0 0.6 %collective-permute-start.5 = (f32[8,512]{1,0:T(8,128)S(1)}, f32[8,512]{1,0:T(8,128)S(1)}, u32[]{:S(2)}, u32[]{:S(2)}) collective-permute-start(f32[8,512]{1,0:T(8,128)S(1)} %get-tuple-element.43.own_ref), channel_id=1, source_target_pairs={{0,12},{4,8},{8,4},{12,0},{1,13},{5,9},{9,5},{13,1},{2,14},{6,10},... | collective-permute-start | bytes 49160 | tf_op jit(solution)/shard_map/ppermute | solution.py:740
  17.6 1.5 %collective-permute-start.6 = (f32[8,128]{1,0:T(8,128)S(1)}, f32[8,128]{1,0:T(8,128)S(1)}, u32[]{:S(2)}, u32[]{:S(2)}) collective-permute-start(f32[8,128]{1,0:T(8,128)S(1)} %get-tuple-element.44.rest_0_), channel_id=1, source_target_pairs={{0,8},{4,12},{8,0},{12,4},{1,9},{5,13},{9,1},{13,5},{2,10},{6,14},... | collective-permute-start | bytes 12296 | tf_op jit(solution)/shard_map/ppermute | solution.py:740
  20.4 0.0 copy-done
  20.4 0.5 %shard_map.165.number_ref = f32[8,128]{1,0:T(8,128)S(1)} custom-call(f32[1]{0:T(128)S(6)} %copy.19.dt_ref, s32[1,2]{1,0:T(1,128)S(1)} %bitcast.10, s32[1]{0:T(128)S(6)} %copy.20.climb_ref), custom_call_target="tpu_custom_call" | custom-call | bytes 262144 | tf_op jit(solution)/shard_map/pallas_call | solution.py:728
  21.0 0.3 collective-permute-done.6.rest_1_
  21.3 0.0 collective-permute-done.4.near_ref
  21.3 0.0 collective-permute-done.5.far_ref
  21.3 5.4 %shard_map.170 = (f32[1,40,128]{2,1,0:T(8,128)S(1)}, f32[3,128]{1,0:T(4,128)S(1)}) custom-call(f32[8,128]{1,0:T(8,128)S(1)} %shard_map.165.number_ref, f32[40,512]{1,0:T(8,128)S(1)} %get-tuple-element.39.pl_ref, f32[40,512]{1,0:T(8,128)S(1)} %get-tuple-element.31.po_ref, f32[40,512]{1,0:T(8,128)S(1)} %get-tuple-element.40.pr_ref, ...), custom_call_target="tpu_custom_call" | custom-call | flops 1000000000 | bytes 262144 | tf_op jit(solution)/shard_map/pallas_call | solution.py:728
  26.7 0.1 collective-permute-start.7
  26.7 4.4 %collective-permute-start.8 = (f32[1,40,128]{2,1,0:T(8,128)S(1)}, f32[1,40,128]{2,1,0:T(8,128)S(1)}, u32[]{:S(2)}, u32[]{:S(2)}) collective-permute-start(f32[1,40,128]{2,1,0:T(8,128)S(1)} %get-tuple-element.46.refs_0_.own_ref), channel_id=1, source_target_pairs={{0,2},{1,3},{2,1},{3,0},{4,6},{5,7},{6,5},{7,4},{8,10},{9,11},{10,... | collective-permute-start | bytes 61448 | tf_op jit(solution)/shard_map/ppermute | solution.py:740
  31.1 1.2 %collective-permute-done.7.refs_1_ = f32[1,40,128]{2,1,0:T(8,128)S(1)} collective-permute-done((f32[1,40,128]{2,1,0:T(8,128)S(1)}, f32[1,40,128]{2,1,0:T(8,128)S(1)}, u32[]{:S(2)}, u32[]{:S(2)}) %collective-permute-start.7) | collective-permute-done | bytes 20512 | tf_op jit(solution)/shard_map/ppermute | solution.py:740
  32.3 0.3 collective-permute-done.8.refs_2_
  32.6 0.2 shard_map.171
  32.8 0.1 collective-permute-start.10
  32.9 1.6 %collective-permute-start.11 = (f32[8,128]{1,0:T(8,128)S(1)}, f32[8,128]{1,0:T(8,128)S(1)}, u32[]{:S(2)}, u32[]{:S(2)}) collective-permute-start(f32[8,128]{1,0:T(8,128)S(1)} %get-tuple-element.49.rest_0_), channel_id=1, source_target_pairs={{0,4},{4,0},{8,12},{12,8},{1,5},{5,1},{9,13},{13,9},{2,6},{6,2},{1... | collective-permute-start | bytes 12296 | tf_op jit(solution)/shard_map/ppermute | solution.py:740
  34.5 0.5 %collective-permute-start.9 = (f32[8,128]{1,0:T(8,128)S(1)}, f32[8,128]{1,0:T(8,128)S(1)}, u32[]{:S(2)}, u32[]{:S(2)}) collective-permute-start(f32[8,128]{1,0:T(8,128)S(1)} %get-tuple-element.49.rest_0_), channel_id=1, source_target_pairs={{0,8},{4,12},{8,0},{12,4},{1,9},{5,13},{9,1},{13,5},{2,10},{6,14},... | collective-permute-start | bytes 12296 | tf_op jit(solution)/shard_map/ppermute | solution.py:740
  35.0 0.9 %collective-permute-done.10.rest_2_ = f32[8,128]{1,0:T(8,128)S(1)} collective-permute-done((f32[8,128]{1,0:T(8,128)S(1)}, f32[8,128]{1,0:T(8,128)S(1)}, u32[]{:S(2)}, u32[]{:S(2)}) %collective-permute-start.10) | collective-permute-done | bytes 4128 | tf_op jit(solution)/shard_map/ppermute | solution.py:740
  35.9 0.0 collective-permute-done.11.rest_3_
  35.9 2.2 %collective-permute-done.9.rest_1_ = f32[8,128]{1,0:T(8,128)S(1)} collective-permute-done((f32[8,128]{1,0:T(8,128)S(1)}, f32[8,128]{1,0:T(8,128)S(1)}, u32[]{:S(2)}, u32[]{:S(2)}) %collective-permute-start.9) | collective-permute-done | bytes 4128 | tf_op jit(solution)/shard_map/ppermute | solution.py:740
  38.1 0.7 %shard_map.172 = (f32[3,1,512]{2,1,0:T(1,128)}, f32[3,1,512]{2,1,0:T(1,128)}, f32[2,1,2]{2,1,0:T(1,128)}, f32[1,1]{1,0:T(1,128)}) custom-call(f32[1,40,128]{2,1,0:T(8,128)S(1)} %get-tuple-element.46.refs_0_.own_ref, f32[3,128]{1,0:T(4,128)S(1)} %get-tuple-element.47.record_ref, f32[40,128]{1,0:T(8,128)S(1)} %get-tuple-element.48.state_ref, ...), custom_call_target="tpu_custom_call" | custom-call | bytes 262144 | tf_op jit(solution)/shard_map/pallas_call | solution.py:728
Async XLA Ops:
  0.6 19.8 %copy-start = (s32[2,1]{0,1:T(1,128)S(1)}, s32[2,1]{0,1:T(1,128)}, u32[]{:S(2)}) copy-start(s32[2,1]{0,1:T(1,128)} %param.17) | copy-start | bytes 28
  2.5 8.9 %collective-permute-start = (f32[40,512]{1,0:T(8,128)}, f32[40,512]{1,0:T(8,128)S(1)}, u32[]{:S(2)}, u32[]{:S(2)}) collective-permute-start(f32[40,512]{1,0:T(8,128)} %get-tuple-element.29), channel_id=1, source_target_pairs={{0,4},{4,0},{8,12},{12,8},{1,5},{5,1},{9,13},{13,9},{2,6},{6,2},{1... | collective-permute-start | bytes 245768 | tf_op jit(solution)/shard_map/ppermute | solution.py:740
  3.0 8.4 %collective-permute-start.1 = (f32[40,512]{1,0:T(8,128)}, f32[40,512]{1,0:T(8,128)S(1)}, u32[]{:S(2)}, u32[]{:S(2)}) collective-permute-start(f32[40,512]{1,0:T(8,128)} %get-tuple-element.29), channel_id=1, source_target_pairs={{0,12},{4,8},{8,4},{12,0},{1,13},{5,9},{9,5},{13,1},{2,14},{6,10},... | collective-permute-start | bytes 245768 | tf_op jit(solution)/shard_map/ppermute | solution.py:740
  5.7 0.9 %copy-start.1 = (f32[112,512]{1,0:T(8,128)S(1)}, f32[112,512]{1,0:T(8,128)}, u32[]{:S(2)}) copy-start(f32[112,512]{1,0:T(8,128)} %get-tuple-element.30.po_ref) | copy-start | bytes 688132
  7.8 9.0 %collective-permute-start.3 = (f32[3,1,512]{2,1,0:T(1,128)S(1)}, f32[3,1,512]{2,1,0:T(1,128)S(1)}, u32[]{:S(2)}, u32[]{:S(2)}) collective-permute-start(f32[3,1,512]{2,1,0:T(1,128)S(1)} %get-tuple-element.42), channel_id=1, source_target_pairs={{0,3},{1,0},{2,1},{3,2},{4,7},{5,4},{6,5},{7,6},{8,11},{9,8},{10,9... | collective-permute-start | bytes 18440 | tf_op jit(solution)/shard_map/ppermute | solution.py:740
  11.4 5.4 %collective-permute-start.2 = (f32[3,1,512]{2,1,0:T(1,128)S(1)}, f32[3,1,512]{2,1,0:T(1,128)S(1)}, u32[]{:S(2)}, u32[]{:S(2)}) collective-permute-start(f32[3,1,512]{2,1,0:T(1,128)S(1)} %get-tuple-element.42), channel_id=1, source_target_pairs={{0,1},{1,2},{2,3},{3,0},{4,5},{5,6},{6,7},{7,4},{8,9},{9,10},{10,1... | collective-permute-start | bytes 18440 | tf_op jit(solution)/shard_map/ppermute | solution.py:740
  17.0 4.3 %collective-permute-start.4 = (f32[8,512]{1,0:T(8,128)S(1)}, f32[8,512]{1,0:T(8,128)S(1)}, u32[]{:S(2)}, u32[]{:S(2)}) collective-permute-start(f32[8,512]{1,0:T(8,128)S(1)} %get-tuple-element.43.own_ref), channel_id=1, source_target_pairs={{0,4},{4,0},{8,12},{12,8},{1,5},{5,1},{9,13},{13,9},{2,6},{6,2},{1... | collective-permute-start | bytes 49160 | tf_op jit(solution)/shard_map/ppermute | solution.py:740
  17.0 4.3 %collective-permute-start.5 = (f32[8,512]{1,0:T(8,128)S(1)}, f32[8,512]{1,0:T(8,128)S(1)}, u32[]{:S(2)}, u32[]{:S(2)}) collective-permute-start(f32[8,512]{1,0:T(8,128)S(1)} %get-tuple-element.43.own_ref), channel_id=1, source_target_pairs={{0,12},{4,8},{8,4},{12,0},{1,13},{5,9},{9,5},{13,1},{2,14},{6,10},... | collective-permute-start | bytes 49160 | tf_op jit(solution)/shard_map/ppermute | solution.py:740
  17.6 3.6 %collective-permute-start.6 = (f32[8,128]{1,0:T(8,128)S(1)}, f32[8,128]{1,0:T(8,128)S(1)}, u32[]{:S(2)}, u32[]{:S(2)}) collective-permute-start(f32[8,128]{1,0:T(8,128)S(1)} %get-tuple-element.44.rest_0_), channel_id=1, source_target_pairs={{0,8},{4,12},{8,0},{12,4},{1,9},{5,13},{9,1},{13,5},{2,10},{6,14},... | collective-permute-start | bytes 12296 | tf_op jit(solution)/shard_map/ppermute | solution.py:740
  26.7 5.6 %collective-permute-start.7 = (f32[1,40,128]{2,1,0:T(8,128)S(1)}, f32[1,40,128]{2,1,0:T(8,128)S(1)}, u32[]{:S(2)}, u32[]{:S(2)}) collective-permute-start(f32[1,40,128]{2,1,0:T(8,128)S(1)} %get-tuple-element.46.refs_0_.own_ref), channel_id=1, source_target_pairs={{0,1},{1,2},{2,3},{3,0},{4,5},{5,6},{6,7},{7,4},{8,9},{9,10},{10,1... | collective-permute-start | bytes 61448 | tf_op jit(solution)/shard_map/ppermute | solution.py:740
  26.7 5.8 %collective-permute-start.8 = (f32[1,40,128]{2,1,0:T(8,128)S(1)}, f32[1,40,128]{2,1,0:T(8,128)S(1)}, u32[]{:S(2)}, u32[]{:S(2)}) collective-permute-start(f32[1,40,128]{2,1,0:T(8,128)S(1)} %get-tuple-element.46.refs_0_.own_ref), channel_id=1, source_target_pairs={{0,2},{1,3},{2,1},{3,0},{4,6},{5,7},{6,5},{7,4},{8,10},{9,11},{10,... | collective-permute-start | bytes 61448 | tf_op jit(solution)/shard_map/ppermute | solution.py:740
  32.8 3.1 %collective-permute-start.10 = (f32[8,128]{1,0:T(8,128)S(1)}, f32[8,128]{1,0:T(8,128)S(1)}, u32[]{:S(2)}, u32[]{:S(2)}) collective-permute-start(f32[8,128]{1,0:T(8,128)S(1)} %get-tuple-element.49.rest_0_), channel_id=1, source_target_pairs={{0,12},{4,8},{8,4},{12,0},{1,13},{5,9},{9,5},{13,1},{2,14},{6,10},... | collective-permute-start | bytes 12296 | tf_op jit(solution)/shard_map/ppermute | solution.py:740
  32.9 3.0 %collective-permute-start.11 = (f32[8,128]{1,0:T(8,128)S(1)}, f32[8,128]{1,0:T(8,128)S(1)}, u32[]{:S(2)}, u32[]{:S(2)}) collective-permute-start(f32[8,128]{1,0:T(8,128)S(1)} %get-tuple-element.49.rest_0_), channel_id=1, source_target_pairs={{0,4},{4,0},{8,12},{12,8},{1,5},{5,1},{9,13},{13,9},{2,6},{6,2},{1... | collective-permute-start | bytes 12296 | tf_op jit(solution)/shard_map/ppermute | solution.py:740
  34.5 3.6 %collective-permute-start.9 = (f32[8,128]{1,0:T(8,128)S(1)}, f32[8,128]{1,0:T(8,128)S(1)}, u32[]{:S(2)}, u32[]{:S(2)}) collective-permute-start(f32[8,128]{1,0:T(8,128)S(1)} %get-tuple-element.49.rest_0_), channel_id=1, source_target_pairs={{0,8},{4,12},{8,0},{12,4},{1,9},{5,13},{9,1},{13,5},{2,10},{6,14},... | collective-permute-start | bytes 12296 | tf_op jit(solution)/shard_map/ppermute | solution.py:740

commit v19 on v18

--- a/solution.py
+++ b/solution.py
@@ -602,17 +602,17 @@
 
 
 def gram_kernel(images, *refs):
-    parts, after_ref, (out_ref, state_ref, messages_ref) = refs[:-4], refs[-4], refs[-3:]
+    parts, (before_ref, after_ref), (out_ref, state_ref, messages_ref) = refs[:-5], refs[-5:-3], refs[-3:]
     rows = out_ref.shape[0]
     here = lax.axis_index("img")
     if images == 4:
         places = [here, lax.rem(here + 3, 4), jnp.where(here < 2, 3 - here, here - 2)]
         messages_ref[...] = jnp.zeros(messages_ref.shape, F32)
-        follower = lax.rem(here + 1, 4)
-        for c in range(3):
-            for i in range(SLAB_BLOCKS):
-                row = 24 + 4 * c + i
-                messages_ref[follower, row : row + 1, :] = after_ref[c][:, i * LANES : (i + 1) * LANES]
+        for place, beside in [(lax.rem(here + 3, 4), before_ref), (lax.rem(here + 1, 4), after_ref)]:
+            for c in range(3):
+                for i in range(SLAB_BLOCKS):
+                    row = 24 + 4 * c + i
+                    messages_ref[place, row : row + 1, :] = beside[c][:, i * LANES : (i + 1) * LANES]
     else:
         places = [lax.rem(here + images - s, images) for s in range(images)]
     for place, part in zip(places, parts):
@@ -752,11 +752,11 @@
     return [sums]
 
 
-def collected(state, axis, after):
+def collected(state, axis, before, after):
     count = lax.axis_size(axis)
     if count == 4:
-        return [state, swap(state, axis, lambda i: (i + 1) % 4), swap(state, axis, lambda i: (2, 3, 1, 0)[i]), after]
-    return [state] + [swap(state, axis, lambda i, by=by: (i + by) % count) for by in range(1, count)] + [after]
+        return [state, swap(state, axis, lambda i: (i + 1) % 4), swap(state, axis, lambda i: (2, 3, 1, 0)[i]), before, after]
+    return [state] + [swap(state, axis, lambda i, by=by: (i + by) % count) for by in range(1, count)] + [before, after]
 
 
 def local(
@@ -854,7 +854,7 @@
         functools.partial(gram_kernel, images),
         (shape((rows, LANES), F32), shape((16 + 3 * rows, LANES), F32)),
         (),
-        collected(state, "img", after),
+        collected(state, "img", before, after),
         [pltpu.VMEM((images, 40, LANES), F32)],
     )
     new_x, new_v, records, path = call(

time: 39 us -> 39.2 us (level)
  waiting for transfers between devices: 4.83 us -> 6.62 us
  starting transfers between devices: 15.5 us -> 13.9 us
    ppermute x12, waiting for transfers between devices: 4.83 us -> 6.62 us  [swap(): lax.ppermute(array, axis, [(i, partner(i)) for i in range(lax.axis_size(a...]
    ppermute x12, starting transfers between devices: 15.5 us -> 13.9 us  [swap(): lax.ppermute(array, axis, [(i, partner(i)) for i in range(lax.axis_size(a...]
where the time goes in v19:
time: 39.2 us; the launch traced here: 39 us
  Pallas kernels  15.5 us (40%)
  starting transfers between devices  13.9 us (35%)
  waiting for transfers between devices  6.62 us (17%)
  between operations  2.04 us (5%)
  local copies, waits for them, and re-layouts  0.94 us (2%)
    pallas_call x8, Pallas kernels, call(): pl.pallas_call(body, out_shape=outs, in_specs=[SMEM_SPEC] * len(scalars)...  15.5 us
    ppermute x12, starting transfers between devices, swap(): lax.ppermute(array, axis, [(i, partner(i)) for i in range(lax.axis_size(a...  13.9 us
    ppermute x12, waiting for transfers between devices, swap(): lax.ppermute(array, axis, [(i, partner(i)) for i in range(lax.axis_size(a...  6.62 us
    unnamed x4, local copies, waits for them, and re-layouts  0.94 us
  transfers between devices with their start and end apart: 12, of which 5 were waited for; matrix products, arithmetic and copies ran while one was open for 0% of the time, Pallas kernels for 18%

profile of v19, /device:TPU:0, one launch (start us, length us, event | category | flops | bytes accessed | tf_op | source)
XLA Modules:
  0.0 39.0 jit_solution(9316641809890515286)
XLA Ops:
  0.6 0.0 copy-start
  0.6 1.9 %shard_map.166 = (f32[40,512]{1,0:T(8,128)}, f32[112,512]{1,0:T(8,128)}) custom-call(f32[3,1,512]{2,1,0:T(1,128)} %bitcast.12, f32[3,1,512]{2,1,0:T(1,128)} %bitcast.13, s32[512]{0:T(512)} %refs_2_.1, s32[8,512]{1,0:T(8,128)} %refs_3_.1, s32[512]{0:T(512)} %refs_4_.1, f32[2,64]{1,0:T(2,128)} %refs_5_.1, f32[64]{0:T(128)} %refs_6_.1, f32[2,8,64]{2,1,0:T(8,128)} %refs_7_.1, ...), custom_call_target="tpu_custom_call" | custom-call | bytes 262144 | tf_op jit(solution)/shard_map/pallas_call | solution.py:728
  2.5 0.5 %collective-permute-start = (f32[40,512]{1,0:T(8,128)}, f32[40,512]{1,0:T(8,128)S(1)}, u32[]{:S(2)}, u32[]{:S(2)}) collective-permute-start(f32[40,512]{1,0:T(8,128)} %get-tuple-element.29), channel_id=1, source_target_pairs={{0,4},{4,0},{8,12},{12,8},{1,5},{5,1},{9,13},{13,9},{2,6},{6,2},{1... | collective-permute-start | bytes 245768 | tf_op jit(solution)/shard_map/ppermute | solution.py:740
  3.0 2.6 %collective-permute-start.1 = (f32[40,512]{1,0:T(8,128)}, f32[40,512]{1,0:T(8,128)S(1)}, u32[]{:S(2)}, u32[]{:S(2)}) collective-permute-start(f32[40,512]{1,0:T(8,128)} %get-tuple-element.29), channel_id=1, source_target_pairs={{0,12},{4,8},{8,4},{12,0},{1,13},{5,9},{9,5},{13,1},{2,14},{6,10},... | collective-permute-start | bytes 245768 | tf_op jit(solution)/shard_map/ppermute | solution.py:740
  5.7 0.0 copy-start.1
  5.7 0.9 %copy-done.1 = f32[112,512]{1,0:T(8,128)S(1)} copy-done((f32[112,512]{1,0:T(8,128)S(1)}, f32[112,512]{1,0:T(8,128)}, u32[]{:S(2)}) %copy-start.1) | copy-done | bytes 229400
  6.6 1.2 %shard_map.167 = (bf16[4,384,1024]{2,1,0:T(8,128)(2,1)S(1)}, bf16[64,48]{1,0:T(8,128)(2,1)S(1)}, bf16[64,192]{1,0:T(8,128)(2,1)S(1)}, bf16[64,32]{1,0:T(8,128)(2...) custom-call(f32[112,512]{1,0:T(8,128)S(1)} %copy-done.1), custom_call_target="tpu_custom_call" | custom-call | flops 100000000 | bytes 262144 | tf_op jit(solution)/shard_map/pallas_call | solution.py:728
  7.8 1.6 %collective-permute-start.2 = (f32[3,1,512]{2,1,0:T(1,128)S(1)}, f32[3,1,512]{2,1,0:T(1,128)S(1)}, u32[]{:S(2)}, u32[]{:S(2)}) collective-permute-start(f32[3,1,512]{2,1,0:T(1,128)S(1)} %get-tuple-element.42), channel_id=1, source_target_pairs={{0,1},{1,2},{2,3},{3,0},{4,5},{5,6},{6,7},{7,4},{8,9},{9,10},{10,1... | collective-permute-start | bytes 18440 | tf_op jit(solution)/shard_map/ppermute | solution.py:740
  9.4 2.2 %collective-permute-start.3 = (f32[3,1,512]{2,1,0:T(1,128)S(1)}, f32[3,1,512]{2,1,0:T(1,128)S(1)}, u32[]{:S(2)}, u32[]{:S(2)}) collective-permute-start(f32[3,1,512]{2,1,0:T(1,128)S(1)} %get-tuple-element.42), channel_id=1, source_target_pairs={{0,3},{1,0},{2,1},{3,2},{4,7},{5,4},{6,5},{7,6},{8,11},{9,8},{10,9... | collective-permute-start | bytes 18440 | tf_op jit(solution)/shard_map/ppermute | solution.py:740
  11.7 0.0 collective-permute-done.sibling_ref
  11.7 0.0 collective-permute-done.1.across_ref
  11.7 5.4 %shard_map.168 = (f32[3,512]{1,0:T(4,128)S(1)}, f32[40,512]{1,0:T(8,128)S(1)}, f32[40,512]{1,0:T(8,128)S(1)}, bf16[768,1024]{1,0:T(8,128)(2,1)S(1)}) custom-call(f32[40,512]{1,0:T(8,128)S(1)} %collective-permute-done.sibling_ref, f32[40,512]{1,0:T(8,128)S(1)} %get-tuple-element.31.po_ref, f32[40,512]{1,0:T(8,128)S(1)} %collective-permute-done.1.across_ref, ...), custom_call_target="tpu_custom_call" | custom-call | flops 1000000000 | bytes 262144 | tf_op jit(solution)/shard_map/pallas_call | solution.py:728
  17.1 0.0 collective-permute-done.2.before_ref.refs_3_
  17.1 0.0 collective-permute-done.3.after_ref.refs_4_
  17.1 0.1 shard_map.169
  17.2 0.0 collective-permute-start.4
  17.2 0.5 %collective-permute-start.5 = (f32[8,512]{1,0:T(8,128)S(1)}, f32[8,512]{1,0:T(8,128)S(1)}, u32[]{:S(2)}, u32[]{:S(2)}) collective-permute-start(f32[8,512]{1,0:T(8,128)S(1)} %get-tuple-element.43.own_ref), channel_id=1, source_target_pairs={{0,12},{4,8},{8,4},{12,0},{1,13},{5,9},{9,5},{13,1},{2,14},{6,10},... | collective-permute-start | bytes 49160 | tf_op jit(solution)/shard_map/ppermute | solution.py:740
  17.7 1.6 %collective-permute-start.6 = (f32[8,128]{1,0:T(8,128)S(1)}, f32[8,128]{1,0:T(8,128)S(1)}, u32[]{:S(2)}, u32[]{:S(2)}) collective-permute-start(f32[8,128]{1,0:T(8,128)S(1)} %get-tuple-element.44.rest_0_), channel_id=1, source_target_pairs={{0,8},{4,12},{8,0},{12,4},{1,9},{5,13},{9,1},{13,5},{2,10},{6,14},... | collective-permute-start | bytes 12296 | tf_op jit(solution)/shard_map/ppermute | solution.py:740
  20.7 0.0 copy-done
  20.7 0.5 %shard_map.165.number_ref = f32[8,128]{1,0:T(8,128)S(1)} custom-call(f32[1]{0:T(128)S(6)} %copy.19.dt_ref, s32[1,2]{1,0:T(1,128)S(1)} %bitcast.10, s32[1]{0:T(128)S(6)} %copy.20.climb_ref), custom_call_target="tpu_custom_call" | custom-call | bytes 262144 | tf_op jit(solution)/shard_map/pallas_call | solution.py:728
  21.2 0.1 collective-permute-done.6.rest_1_
  21.3 0.0 collective-permute-done.4.near_ref
  21.3 0.0 collective-permute-done.5.far_ref
  21.3 5.4 %shard_map.170 = (f32[1,40,128]{2,1,0:T(8,128)S(1)}, f32[3,128]{1,0:T(4,128)S(1)}) custom-call(f32[8,128]{1,0:T(8,128)S(1)} %shard_map.165.number_ref, f32[40,512]{1,0:T(8,128)S(1)} %get-tuple-element.39.pl_ref, f32[40,512]{1,0:T(8,128)S(1)} %get-tuple-element.31.po_ref, f32[40,512]{1,0:T(8,128)S(1)} %get-tuple-element.40.pr_ref, ...), custom_call_target="tpu_custom_call" | custom-call | flops 1000000000 | bytes 262144 | tf_op jit(solution)/shard_map/pallas_call | solution.py:728
  26.7 0.1 collective-permute-start.7
  26.8 2.5 %collective-permute-start.8 = (f32[1,40,128]{2,1,0:T(8,128)S(1)}, f32[1,40,128]{2,1,0:T(8,128)S(1)}, u32[]{:S(2)}, u32[]{:S(2)}) collective-permute-start(f32[1,40,128]{2,1,0:T(8,128)S(1)} %get-tuple-element.46.refs_0_.own_ref), channel_id=1, source_target_pairs={{0,2},{1,3},{2,1},{3,0},{4,6},{5,7},{6,5},{7,4},{8,10},{9,11},{10,... | collective-permute-start | bytes 61448 | tf_op jit(solution)/shard_map/ppermute | solution.py:740
  29.3 3.1 %collective-permute-done.7.refs_1_ = f32[1,40,128]{2,1,0:T(8,128)S(1)} collective-permute-done((f32[1,40,128]{2,1,0:T(8,128)S(1)}, f32[1,40,128]{2,1,0:T(8,128)S(1)}, u32[]{:S(2)}, u32[]{:S(2)}) %collective-permute-start.7) | collective-permute-done | bytes 20512 | tf_op jit(solution)/shard_map/ppermute | solution.py:740
  32.4 0.2 collective-permute-done.8.refs_2_
  32.6 0.2 shard_map.171
  32.8 0.1 collective-permute-start.10
  32.9 1.8 %collective-permute-start.11 = (f32[8,128]{1,0:T(8,128)S(1)}, f32[8,128]{1,0:T(8,128)S(1)}, u32[]{:S(2)}, u32[]{:S(2)}) collective-permute-start(f32[8,128]{1,0:T(8,128)S(1)} %get-tuple-element.49.rest_0_), channel_id=1, source_target_pairs={{0,4},{4,0},{8,12},{12,8},{1,5},{5,1},{9,13},{13,9},{2,6},{6,2},{1... | collective-permute-start | bytes 12296 | tf_op jit(solution)/shard_map/ppermute | solution.py:740
  34.6 0.4 collective-permute-start.9
  35.0 0.9 %collective-permute-done.10.rest_2_ = f32[8,128]{1,0:T(8,128)S(1)} collective-permute-done((f32[8,128]{1,0:T(8,128)S(1)}, f32[8,128]{1,0:T(8,128)S(1)}, u32[]{:S(2)}, u32[]{:S(2)}) %collective-permute-start.10) | collective-permute-done | bytes 4128 | tf_op jit(solution)/shard_map/ppermute | solution.py:740
  35.9 0.0 collective-permute-done.11.rest_3_
  35.9 2.3 %collective-permute-done.9.rest_1_ = f32[8,128]{1,0:T(8,128)S(1)} collective-permute-done((f32[8,128]{1,0:T(8,128)S(1)}, f32[8,128]{1,0:T(8,128)S(1)}, u32[]{:S(2)}, u32[]{:S(2)}) %collective-permute-start.9) | collective-permute-done | bytes 4128 | tf_op jit(solution)/shard_map/ppermute | solution.py:740
  38.3 0.7 %shard_map.172 = (f32[3,1,512]{2,1,0:T(1,128)}, f32[3,1,512]{2,1,0:T(1,128)}, f32[2,1,2]{2,1,0:T(1,128)}, f32[1,1]{1,0:T(1,128)}) custom-call(f32[1,40,128]{2,1,0:T(8,128)S(1)} %get-tuple-element.46.refs_0_.own_ref, f32[3,128]{1,0:T(4,128)S(1)} %get-tuple-element.47.record_ref, f32[40,128]{1,0:T(8,128)S(1)} %get-tuple-element.48.state_ref, ...), custom_call_target="tpu_custom_call" | custom-call | bytes 262144 | tf_op jit(solution)/shard_map/pallas_call | solution.py:728
Async XLA Ops:
  0.6 20.0 %copy-start = (s32[2,1]{0,1:T(1,128)S(1)}, s32[2,1]{0,1:T(1,128)}, u32[]{:S(2)}) copy-start(s32[2,1]{0,1:T(1,128)} %param.17) | copy-start | bytes 28
  2.5 9.1 %collective-permute-start = (f32[40,512]{1,0:T(8,128)}, f32[40,512]{1,0:T(8,128)S(1)}, u32[]{:S(2)}, u32[]{:S(2)}) collective-permute-start(f32[40,512]{1,0:T(8,128)} %get-tuple-element.29), channel_id=1, source_target_pairs={{0,4},{4,0},{8,12},{12,8},{1,5},{5,1},{9,13},{13,9},{2,6},{6,2},{1... | collective-permute-start | bytes 245768 | tf_op jit(solution)/shard_map/ppermute | solution.py:740
  3.0 8.6 %collective-permute-start.1 = (f32[40,512]{1,0:T(8,128)}, f32[40,512]{1,0:T(8,128)S(1)}, u32[]{:S(2)}, u32[]{:S(2)}) collective-permute-start(f32[40,512]{1,0:T(8,128)} %get-tuple-element.29), channel_id=1, source_target_pairs={{0,12},{4,8},{8,4},{12,0},{1,13},{5,9},{9,5},{13,1},{2,14},{6,10},... | collective-permute-start | bytes 245768 | tf_op jit(solution)/shard_map/ppermute | solution.py:740
  5.7 0.9 %copy-start.1 = (f32[112,512]{1,0:T(8,128)S(1)}, f32[112,512]{1,0:T(8,128)}, u32[]{:S(2)}) copy-start(f32[112,512]{1,0:T(8,128)} %get-tuple-element.30.po_ref) | copy-start | bytes 688132
  7.8 9.3 %collective-permute-start.2 = (f32[3,1,512]{2,1,0:T(1,128)S(1)}, f32[3,1,512]{2,1,0:T(1,128)S(1)}, u32[]{:S(2)}, u32[]{:S(2)}) collective-permute-start(f32[3,1,512]{2,1,0:T(1,128)S(1)} %get-tuple-element.42), channel_id=1, source_target_pairs={{0,1},{1,2},{2,3},{3,0},{4,5},{5,6},{6,7},{7,4},{8,9},{9,10},{10,1... | collective-permute-start | bytes 18440 | tf_op jit(solution)/shard_map/ppermute | solution.py:740
  9.4 7.6 %collective-permute-start.3 = (f32[3,1,512]{2,1,0:T(1,128)S(1)}, f32[3,1,512]{2,1,0:T(1,128)S(1)}, u32[]{:S(2)}, u32[]{:S(2)}) collective-permute-start(f32[3,1,512]{2,1,0:T(1,128)S(1)} %get-tuple-element.42), channel_id=1, source_target_pairs={{0,3},{1,0},{2,1},{3,2},{4,7},{5,4},{6,5},{7,6},{8,11},{9,8},{10,9... | collective-permute-start | bytes 18440 | tf_op jit(solution)/shard_map/ppermute | solution.py:740
  17.2 4.1 %collective-permute-start.4 = (f32[8,512]{1,0:T(8,128)S(1)}, f32[8,512]{1,0:T(8,128)S(1)}, u32[]{:S(2)}, u32[]{:S(2)}) collective-permute-start(f32[8,512]{1,0:T(8,128)S(1)} %get-tuple-element.43.own_ref), channel_id=1, source_target_pairs={{0,4},{4,0},{8,12},{12,8},{1,5},{5,1},{9,13},{13,9},{2,6},{6,2},{1... | collective-permute-start | bytes 49160 | tf_op jit(solution)/shard_map/ppermute | solution.py:740
  17.2 4.1 %collective-permute-start.5 = (f32[8,512]{1,0:T(8,128)S(1)}, f32[8,512]{1,0:T(8,128)S(1)}, u32[]{:S(2)}, u32[]{:S(2)}) collective-permute-start(f32[8,512]{1,0:T(8,128)S(1)} %get-tuple-element.43.own_ref), channel_id=1, source_target_pairs={{0,12},{4,8},{8,4},{12,0},{1,13},{5,9},{9,5},{13,1},{2,14},{6,10},... | collective-permute-start | bytes 49160 | tf_op jit(solution)/shard_map/ppermute | solution.py:740
  17.7 3.6 %collective-permute-start.6 = (f32[8,128]{1,0:T(8,128)S(1)}, f32[8,128]{1,0:T(8,128)S(1)}, u32[]{:S(2)}, u32[]{:S(2)}) collective-permute-start(f32[8,128]{1,0:T(8,128)S(1)} %get-tuple-element.44.rest_0_), channel_id=1, source_target_pairs={{0,8},{4,12},{8,0},{12,4},{1,9},{5,13},{9,1},{13,5},{2,10},{6,14},... | collective-permute-start | bytes 12296 | tf_op jit(solution)/shard_map/ppermute | solution.py:740
  26.7 5.6 %collective-permute-start.7 = (f32[1,40,128]{2,1,0:T(8,128)S(1)}, f32[1,40,128]{2,1,0:T(8,128)S(1)}, u32[]{:S(2)}, u32[]{:S(2)}) collective-permute-start(f32[1,40,128]{2,1,0:T(8,128)S(1)} %get-tuple-element.46.refs_0_.own_ref), channel_id=1, source_target_pairs={{0,1},{1,2},{2,3},{3,0},{4,5},{5,6},{6,7},{7,4},{8,9},{9,10},{10,1... | collective-permute-start | bytes 61448 | tf_op jit(solution)/shard_map/ppermute | solution.py:740
  26.8 5.8 %collective-permute-start.8 = (f32[1,40,128]{2,1,0:T(8,128)S(1)}, f32[1,40,128]{2,1,0:T(8,128)S(1)}, u32[]{:S(2)}, u32[]{:S(2)}) collective-permute-start(f32[1,40,128]{2,1,0:T(8,128)S(1)} %get-tuple-element.46.refs_0_.own_ref), channel_id=1, source_target_pairs={{0,2},{1,3},{2,1},{3,0},{4,6},{5,7},{6,5},{7,4},{8,10},{9,11},{10,... | collective-permute-start | bytes 61448 | tf_op jit(solution)/shard_map/ppermute | solution.py:740
  32.8 3.1 %collective-permute-start.10 = (f32[8,128]{1,0:T(8,128)S(1)}, f32[8,128]{1,0:T(8,128)S(1)}, u32[]{:S(2)}, u32[]{:S(2)}) collective-permute-start(f32[8,128]{1,0:T(8,128)S(1)} %get-tuple-element.49.rest_0_), channel_id=1, source_target_pairs={{0,12},{4,8},{8,4},{12,0},{1,13},{5,9},{9,5},{13,1},{2,14},{6,10},... | collective-permute-start | bytes 12296 | tf_op jit(solution)/shard_map/ppermute | solution.py:740
  32.9 3.0 %collective-permute-start.11 = (f32[8,128]{1,0:T(8,128)S(1)}, f32[8,128]{1,0:T(8,128)S(1)}, u32[]{:S(2)}, u32[]{:S(2)}) collective-permute-start(f32[8,128]{1,0:T(8,128)S(1)} %get-tuple-element.49.rest_0_), channel_id=1, source_target_pairs={{0,4},{4,0},{8,12},{12,8},{1,5},{5,1},{9,13},{13,9},{2,6},{6,2},{1... | collective-permute-start | bytes 12296 | tf_op jit(solution)/shard_map/ppermute | solution.py:740
  34.6 3.6 %collective-permute-start.9 = (f32[8,128]{1,0:T(8,128)S(1)}, f32[8,128]{1,0:T(8,128)S(1)}, u32[]{:S(2)}, u32[]{:S(2)}) collective-permute-start(f32[8,128]{1,0:T(8,128)S(1)} %get-tuple-element.49.rest_0_), channel_id=1, source_target_pairs={{0,8},{4,12},{8,0},{12,4},{1,9},{5,13},{9,1},{13,5},{2,10},{6,14},... | collective-permute-start | bytes 12296 | tf_op jit(solution)/shard_map/ppermute | solution.py:740

commit v20 on v19

--- a/solution.py
+++ b/solution.py
@@ -743,7 +743,7 @@
 def exchanged(sums, axis):
     count = lax.axis_size(axis)
     if count == 4:
-        return [sums] + [swap(sums, axis, lambda i, by=by: i ^ by) for by in (2, 3, 1)]
+        return [sums] + [swap(sums, axis, lambda i, by=by: i ^ by) for by in (1, 2, 3)]
     distance = 1
     while distance < count:
         more = swap(sums, axis, lambda i, by=distance: i ^ by)

time: 39.2 us -> 38.5 us (0.982)
  waiting for transfers between devices: 6.62 us -> 5.93 us
    ppermute x12, waiting for transfers between devices: 6.62 us -> 5.93 us  [swap(): lax.ppermute(array, axis, [(i, partner(i)) for i in range(lax.axis_size(a...]
  transfers between devices with their start and end apart: 12 -> 12, of which waited for: 5 -> 5; matrix products, arithmetic and copies ran while one was open for 0% -> 0% of each run, Pallas kernels for 18% -> 19%
where the time goes in v20:
time: 38.5 us; the launch traced here: 38.3 us
  Pallas kernels  15.5 us (40%)
  starting transfers between devices  13.9 us (36%)
  waiting for transfers between devices  5.93 us (15%)
  between operations  2.03 us (5%)
  local copies, waits for them, and re-layouts  0.94 us (2%)
    pallas_call x8, Pallas kernels, call(): pl.pallas_call(body, out_shape=outs, in_specs=[SMEM_SPEC] * len(scalars)...  15.5 us
    ppermute x12, starting transfers between devices, swap(): lax.ppermute(array, axis, [(i, partner(i)) for i in range(lax.axis_size(a...  13.9 us
    ppermute x12, waiting for transfers between devices, swap(): lax.ppermute(array, axis, [(i, partner(i)) for i in range(lax.axis_size(a...  5.93 us
    unnamed x4, local copies, waits for them, and re-layouts  0.94 us
  transfers between devices with their start and end apart: 12, of which 5 were waited for; matrix products, arithmetic and copies ran while one was open for 0% of the time, Pallas kernels for 19%

profile of v20, /device:TPU:0, one launch (start us, length us, event | category | flops | bytes accessed | tf_op | source)
XLA Modules:
  0.0 38.3 jit_solution(1426221731290723103)
XLA Ops:
  0.6 0.0 copy-start
  0.6 1.9 %shard_map.166 = (f32[40,512]{1,0:T(8,128)}, f32[112,512]{1,0:T(8,128)}) custom-call(f32[3,1,512]{2,1,0:T(1,128)} %bitcast.12, f32[3,1,512]{2,1,0:T(1,128)} %bitcast.13, s32[512]{0:T(512)} %refs_2_.1, s32[8,512]{1,0:T(8,128)} %refs_3_.1, s32[512]{0:T(512)} %refs_4_.1, f32[2,64]{1,0:T(2,128)} %refs_5_.1, f32[64]{0:T(128)} %refs_6_.1, f32[2,8,64]{2,1,0:T(8,128)} %refs_7_.1, ...), custom_call_target="tpu_custom_call" | custom-call | bytes 262144 | tf_op jit(solution)/shard_map/pallas_call | solution.py:728
  2.5 0.5 %collective-permute-start = (f32[40,512]{1,0:T(8,128)}, f32[40,512]{1,0:T(8,128)S(1)}, u32[]{:S(2)}, u32[]{:S(2)}) collective-permute-start(f32[40,512]{1,0:T(8,128)} %get-tuple-element.29), channel_id=1, source_target_pairs={{0,4},{4,0},{8,12},{12,8},{1,5},{5,1},{9,13},{13,9},{2,6},{6,2},{1... | collective-permute-start | bytes 245768 | tf_op jit(solution)/shard_map/ppermute | solution.py:740
  3.0 2.6 %collective-permute-start.1 = (f32[40,512]{1,0:T(8,128)}, f32[40,512]{1,0:T(8,128)S(1)}, u32[]{:S(2)}, u32[]{:S(2)}) collective-permute-start(f32[40,512]{1,0:T(8,128)} %get-tuple-element.29), channel_id=1, source_target_pairs={{0,12},{4,8},{8,4},{12,0},{1,13},{5,9},{9,5},{13,1},{2,14},{6,10},... | collective-permute-start | bytes 245768 | tf_op jit(solution)/shard_map/ppermute | solution.py:740
  5.7 0.0 copy-start.1
  5.7 0.9 %copy-done.1 = f32[112,512]{1,0:T(8,128)S(1)} copy-done((f32[112,512]{1,0:T(8,128)S(1)}, f32[112,512]{1,0:T(8,128)}, u32[]{:S(2)}) %copy-start.1) | copy-done | bytes 229400
  6.6 1.2 %shard_map.167 = (bf16[4,384,1024]{2,1,0:T(8,128)(2,1)S(1)}, bf16[64,48]{1,0:T(8,128)(2,1)S(1)}, bf16[64,192]{1,0:T(8,128)(2,1)S(1)}, bf16[64,32]{1,0:T(8,128)(2...) custom-call(f32[112,512]{1,0:T(8,128)S(1)} %copy-done.1), custom_call_target="tpu_custom_call" | custom-call | flops 100000000 | bytes 262144 | tf_op jit(solution)/shard_map/pallas_call | solution.py:728
  7.8 1.6 %collective-permute-start.2 = (f32[3,1,512]{2,1,0:T(1,128)S(1)}, f32[3,1,512]{2,1,0:T(1,128)S(1)}, u32[]{:S(2)}, u32[]{:S(2)}) collective-permute-start(f32[3,1,512]{2,1,0:T(1,128)S(1)} %get-tuple-element.42), channel_id=1, source_target_pairs={{0,1},{1,2},{2,3},{3,0},{4,5},{5,6},{6,7},{7,4},{8,9},{9,10},{10,1... | collective-permute-start | bytes 18440 | tf_op jit(solution)/shard_map/ppermute | solution.py:740
  9.4 2.2 %collective-permute-start.3 = (f32[3,1,512]{2,1,0:T(1,128)S(1)}, f32[3,1,512]{2,1,0:T(1,128)S(1)}, u32[]{:S(2)}, u32[]{:S(2)}) collective-permute-start(f32[3,1,512]{2,1,0:T(1,128)S(1)} %get-tuple-element.42), channel_id=1, source_target_pairs={{0,3},{1,0},{2,1},{3,2},{4,7},{5,4},{6,5},{7,6},{8,11},{9,8},{10,9... | collective-permute-start | bytes 18440 | tf_op jit(solution)/shard_map/ppermute | solution.py:740
  11.7 0.0 collective-permute-done.sibling_ref
  11.7 0.0 collective-permute-done.1.across_ref
  11.7 5.4 %shard_map.168 = (f32[3,512]{1,0:T(4,128)S(1)}, f32[40,512]{1,0:T(8,128)S(1)}, f32[40,512]{1,0:T(8,128)S(1)}, bf16[768,1024]{1,0:T(8,128)(2,1)S(1)}) custom-call(f32[40,512]{1,0:T(8,128)S(1)} %collective-permute-done.sibling_ref, f32[40,512]{1,0:T(8,128)S(1)} %get-tuple-element.31.po_ref, f32[40,512]{1,0:T(8,128)S(1)} %collective-permute-done.1.across_ref, ...), custom_call_target="tpu_custom_call" | custom-call | flops 1000000000 | bytes 262144 | tf_op jit(solution)/shard_map/pallas_call | solution.py:728
  17.1 0.0 collective-permute-done.2.before_ref.refs_3_
  17.1 0.0 collective-permute-done.3.after_ref.refs_4_
  17.1 0.1 shard_map.169
  17.2 0.0 collective-permute-start.4
  17.2 0.5 %collective-permute-start.5 = (f32[8,512]{1,0:T(8,128)S(1)}, f32[8,512]{1,0:T(8,128)S(1)}, u32[]{:S(2)}, u32[]{:S(2)}) collective-permute-start(f32[8,512]{1,0:T(8,128)S(1)} %get-tuple-element.43.own_ref), channel_id=1, source_target_pairs={{0,12},{4,8},{8,4},{12,0},{1,13},{5,9},{9,5},{13,1},{2,14},{6,10},... | collective-permute-start | bytes 49160 | tf_op jit(solution)/shard_map/ppermute | solution.py:740
  17.7 1.6 %collective-permute-start.6 = (f32[8,128]{1,0:T(8,128)S(1)}, f32[8,128]{1,0:T(8,128)S(1)}, u32[]{:S(2)}, u32[]{:S(2)}) collective-permute-start(f32[8,128]{1,0:T(8,128)S(1)} %get-tuple-element.44.rest_0_), channel_id=1, source_target_pairs={{0,8},{4,12},{8,0},{12,4},{1,9},{5,13},{9,1},{13,5},{2,10},{6,14},... | collective-permute-start | bytes 12296 | tf_op jit(solution)/shard_map/ppermute | solution.py:740
  20.7 0.0 copy-done
  20.7 0.5 %shard_map.165.number_ref = f32[8,128]{1,0:T(8,128)S(1)} custom-call(f32[1]{0:T(128)S(6)} %copy.19.dt_ref, s32[1,2]{1,0:T(1,128)S(1)} %bitcast.10, s32[1]{0:T(128)S(6)} %copy.20.climb_ref), custom_call_target="tpu_custom_call" | custom-call | bytes 262144 | tf_op jit(solution)/shard_map/pallas_call | solution.py:728
  21.2 0.1 collective-permute-done.6.rest_1_
  21.3 0.0 collective-permute-done.4.near_ref
  21.3 0.0 collective-permute-done.5.far_ref
  21.3 5.4 %shard_map.170 = (f32[1,40,128]{2,1,0:T(8,128)S(1)}, f32[3,128]{1,0:T(4,128)S(1)}) custom-call(f32[8,128]{1,0:T(8,128)S(1)} %shard_map.165.number_ref, f32[40,512]{1,0:T(8,128)S(1)} %get-tuple-element.39.pl_ref, f32[40,512]{1,0:T(8,128)S(1)} %get-tuple-element.31.po_ref, f32[40,512]{1,0:T(8,128)S(1)} %get-tuple-element.40.pr_ref, ...), custom_call_target="tpu_custom_call" | custom-call | flops 1000000000 | bytes 262144 | tf_op jit(solution)/shard_map/pallas_call | solution.py:728
  26.7 0.1 collective-permute-start.7
  26.8 2.5 %collective-permute-start.8 = (f32[1,40,128]{2,1,0:T(8,128)S(1)}, f32[1,40,128]{2,1,0:T(8,128)S(1)}, u32[]{:S(2)}, u32[]{:S(2)}) collective-permute-start(f32[1,40,128]{2,1,0:T(8,128)S(1)} %get-tuple-element.46.refs_0_.own_ref), channel_id=1, source_target_pairs={{0,2},{1,3},{2,1},{3,0},{4,6},{5,7},{6,5},{7,4},{8,10},{9,11},{10,... | collective-permute-start | bytes 61448 | tf_op jit(solution)/shard_map/ppermute | solution.py:740
  29.3 3.1 %collective-permute-done.7.refs_1_ = f32[1,40,128]{2,1,0:T(8,128)S(1)} collective-permute-done((f32[1,40,128]{2,1,0:T(8,128)S(1)}, f32[1,40,128]{2,1,0:T(8,128)S(1)}, u32[]{:S(2)}, u32[]{:S(2)}) %collective-permute-start.7) | collective-permute-done | bytes 20512 | tf_op jit(solution)/shard_map/ppermute | solution.py:740
  32.4 0.2 collective-permute-done.8.refs_2_
  32.6 0.2 shard_map.171
  32.8 1.7 %collective-permute-start.10 = (f32[8,128]{1,0:T(8,128)S(1)}, f32[8,128]{1,0:T(8,128)S(1)}, u32[]{:S(2)}, u32[]{:S(2)}) collective-permute-start(f32[8,128]{1,0:T(8,128)S(1)} %get-tuple-element.49.rest_0_), channel_id=1, source_target_pairs={{0,8},{4,12},{8,0},{12,4},{1,9},{5,13},{9,1},{13,5},{2,10},{6,14},... | collective-permute-start | bytes 12296 | tf_op jit(solution)/shard_map/ppermute | solution.py:740
  34.5 0.0 collective-permute-start.11
  34.5 0.5 %collective-permute-start.9 = (f32[8,128]{1,0:T(8,128)S(1)}, f32[8,128]{1,0:T(8,128)S(1)}, u32[]{:S(2)}, u32[]{:S(2)}) collective-permute-start(f32[8,128]{1,0:T(8,128)S(1)} %get-tuple-element.49.rest_0_), channel_id=1, source_target_pairs={{0,4},{4,0},{8,12},{12,8},{1,5},{5,1},{9,13},{13,9},{2,6},{6,2},{1... | collective-permute-start | bytes 12296 | tf_op jit(solution)/shard_map/ppermute | solution.py:740
  35.0 1.5 %collective-permute-done.10.rest_2_ = f32[8,128]{1,0:T(8,128)S(1)} collective-permute-done((f32[8,128]{1,0:T(8,128)S(1)}, f32[8,128]{1,0:T(8,128)S(1)}, u32[]{:S(2)}, u32[]{:S(2)}) %collective-permute-start.10) | collective-permute-done | bytes 4128 | tf_op jit(solution)/shard_map/ppermute | solution.py:740
  36.5 1.1 %collective-permute-done.11.rest_3_ = f32[8,128]{1,0:T(8,128)S(1)} collective-permute-done((f32[8,128]{1,0:T(8,128)S(1)}, f32[8,128]{1,0:T(8,128)S(1)}, u32[]{:S(2)}, u32[]{:S(2)}) %collective-permute-start.11) | collective-permute-done | bytes 4128 | tf_op jit(solution)/shard_map/ppermute | solution.py:740
  37.6 0.0 collective-permute-done.9.rest_1_
  37.6 0.7 %shard_map.172 = (f32[3,1,512]{2,1,0:T(1,128)}, f32[3,1,512]{2,1,0:T(1,128)}, f32[2,1,2]{2,1,0:T(1,128)}, f32[1,1]{1,0:T(1,128)}) custom-call(f32[1,40,128]{2,1,0:T(8,128)S(1)} %get-tuple-element.46.refs_0_.own_ref, f32[3,128]{1,0:T(4,128)S(1)} %get-tuple-element.47.record_ref, f32[40,128]{1,0:T(8,128)S(1)} %get-tuple-element.48.state_ref, ...), custom_call_target="tpu_custom_call" | custom-call | bytes 262144 | tf_op jit(solution)/shard_map/pallas_call | solution.py:728
Async XLA Ops:
  0.6 20.0 %copy-start = (s32[2,1]{0,1:T(1,128)S(1)}, s32[2,1]{0,1:T(1,128)}, u32[]{:S(2)}) copy-start(s32[2,1]{0,1:T(1,128)} %param.17) | copy-start | bytes 28
  2.5 9.1 %collective-permute-start = (f32[40,512]{1,0:T(8,128)}, f32[40,512]{1,0:T(8,128)S(1)}, u32[]{:S(2)}, u32[]{:S(2)}) collective-permute-start(f32[40,512]{1,0:T(8,128)} %get-tuple-element.29), channel_id=1, source_target_pairs={{0,4},{4,0},{8,12},{12,8},{1,5},{5,1},{9,13},{13,9},{2,6},{6,2},{1... | collective-permute-start | bytes 245768 | tf_op jit(solution)/shard_map/ppermute | solution.py:740
  3.0 8.6 %collective-permute-start.1 = (f32[40,512]{1,0:T(8,128)}, f32[40,512]{1,0:T(8,128)S(1)}, u32[]{:S(2)}, u32[]{:S(2)}) collective-permute-start(f32[40,512]{1,0:T(8,128)} %get-tuple-element.29), channel_id=1, source_target_pairs={{0,12},{4,8},{8,4},{12,0},{1,13},{5,9},{9,5},{13,1},{2,14},{6,10},... | collective-permute-start | bytes 245768 | tf_op jit(solution)/shard_map/ppermute | solution.py:740
  5.7 0.9 %copy-start.1 = (f32[112,512]{1,0:T(8,128)S(1)}, f32[112,512]{1,0:T(8,128)}, u32[]{:S(2)}) copy-start(f32[112,512]{1,0:T(8,128)} %get-tuple-element.30.po_ref) | copy-start | bytes 688132
  7.8 9.3 %collective-permute-start.2 = (f32[3,1,512]{2,1,0:T(1,128)S(1)}, f32[3,1,512]{2,1,0:T(1,128)S(1)}, u32[]{:S(2)}, u32[]{:S(2)}) collective-permute-start(f32[3,1,512]{2,1,0:T(1,128)S(1)} %get-tuple-element.42), channel_id=1, source_target_pairs={{0,1},{1,2},{2,3},{3,0},{4,5},{5,6},{6,7},{7,4},{8,9},{9,10},{10,1... | collective-permute-start | bytes 18440 | tf_op jit(solution)/shard_map/ppermute | solution.py:740
  9.4 7.6 %collective-permute-start.3 = (f32[3,1,512]{2,1,0:T(1,128)S(1)}, f32[3,1,512]{2,1,0:T(1,128)S(1)}, u32[]{:S(2)}, u32[]{:S(2)}) collective-permute-start(f32[3,1,512]{2,1,0:T(1,128)S(1)} %get-tuple-element.42), channel_id=1, source_target_pairs={{0,3},{1,0},{2,1},{3,2},{4,7},{5,4},{6,5},{7,6},{8,11},{9,8},{10,9... | collective-permute-start | bytes 18440 | tf_op jit(solution)/shard_map/ppermute | solution.py:740
  17.2 4.1 %collective-permute-start.4 = (f32[8,512]{1,0:T(8,128)S(1)}, f32[8,512]{1,0:T(8,128)S(1)}, u32[]{:S(2)}, u32[]{:S(2)}) collective-permute-start(f32[8,512]{1,0:T(8,128)S(1)} %get-tuple-element.43.own_ref), channel_id=1, source_target_pairs={{0,4},{4,0},{8,12},{12,8},{1,5},{5,1},{9,13},{13,9},{2,6},{6,2},{1... | collective-permute-start | bytes 49160 | tf_op jit(solution)/shard_map/ppermute | solution.py:740
  17.2 4.1 %collective-permute-start.5 = (f32[8,512]{1,0:T(8,128)S(1)}, f32[8,512]{1,0:T(8,128)S(1)}, u32[]{:S(2)}, u32[]{:S(2)}) collective-permute-start(f32[8,512]{1,0:T(8,128)S(1)} %get-tuple-element.43.own_ref), channel_id=1, source_target_pairs={{0,12},{4,8},{8,4},{12,0},{1,13},{5,9},{9,5},{13,1},{2,14},{6,10},... | collective-permute-start | bytes 49160 | tf_op jit(solution)/shard_map/ppermute | solution.py:740
  17.7 3.6 %collective-permute-start.6 = (f32[8,128]{1,0:T(8,128)S(1)}, f32[8,128]{1,0:T(8,128)S(1)}, u32[]{:S(2)}, u32[]{:S(2)}) collective-permute-start(f32[8,128]{1,0:T(8,128)S(1)} %get-tuple-element.44.rest_0_), channel_id=1, source_target_pairs={{0,8},{4,12},{8,0},{12,4},{1,9},{5,13},{9,1},{13,5},{2,10},{6,14},... | collective-permute-start | bytes 12296 | tf_op jit(solution)/shard_map/ppermute | solution.py:740
  26.7 5.6 %collective-permute-start.7 = (f32[1,40,128]{2,1,0:T(8,128)S(1)}, f32[1,40,128]{2,1,0:T(8,128)S(1)}, u32[]{:S(2)}, u32[]{:S(2)}) collective-permute-start(f32[1,40,128]{2,1,0:T(8,128)S(1)} %get-tuple-element.46.refs_0_.own_ref), channel_id=1, source_target_pairs={{0,1},{1,2},{2,3},{3,0},{4,5},{5,6},{6,7},{7,4},{8,9},{9,10},{10,1... | collective-permute-start | bytes 61448 | tf_op jit(solution)/shard_map/ppermute | solution.py:740
  26.8 5.8 %collective-permute-start.8 = (f32[1,40,128]{2,1,0:T(8,128)S(1)}, f32[1,40,128]{2,1,0:T(8,128)S(1)}, u32[]{:S(2)}, u32[]{:S(2)}) collective-permute-start(f32[1,40,128]{2,1,0:T(8,128)S(1)} %get-tuple-element.46.refs_0_.own_ref), channel_id=1, source_target_pairs={{0,2},{1,3},{2,1},{3,0},{4,6},{5,7},{6,5},{7,4},{8,10},{9,11},{10,... | collective-permute-start | bytes 61448 | tf_op jit(solution)/shard_map/ppermute | solution.py:740
  32.8 3.7 %collective-permute-start.10 = (f32[8,128]{1,0:T(8,128)S(1)}, f32[8,128]{1,0:T(8,128)S(1)}, u32[]{:S(2)}, u32[]{:S(2)}) collective-permute-start(f32[8,128]{1,0:T(8,128)S(1)} %get-tuple-element.49.rest_0_), channel_id=1, source_target_pairs={{0,8},{4,12},{8,0},{12,4},{1,9},{5,13},{9,1},{13,5},{2,10},{6,14},... | collective-permute-start | bytes 12296 | tf_op jit(solution)/shard_map/ppermute | solution.py:740
  34.5 3.0 %collective-permute-start.11 = (f32[8,128]{1,0:T(8,128)S(1)}, f32[8,128]{1,0:T(8,128)S(1)}, u32[]{:S(2)}, u32[]{:S(2)}) collective-permute-start(f32[8,128]{1,0:T(8,128)S(1)} %get-tuple-element.49.rest_0_), channel_id=1, source_target_pairs={{0,12},{4,8},{8,4},{12,0},{1,13},{5,9},{9,5},{13,1},{2,14},{6,10},... | collective-permute-start | bytes 12296 | tf_op jit(solution)/shard_map/ppermute | solution.py:740
  34.5 3.0 %collective-permute-start.9 = (f32[8,128]{1,0:T(8,128)S(1)}, f32[8,128]{1,0:T(8,128)S(1)}, u32[]{:S(2)}, u32[]{:S(2)}) collective-permute-start(f32[8,128]{1,0:T(8,128)S(1)} %get-tuple-element.49.rest_0_), channel_id=1, source_target_pairs={{0,4},{4,0},{8,12},{12,8},{1,5},{5,1},{9,13},{13,9},{2,6},{6,2},{1... | collective-permute-start | bytes 12296 | tf_op jit(solution)/shard_map/ppermute | solution.py:740

commit v21 on v20

--- a/solution.py
+++ b/solution.py
@@ -743,7 +743,7 @@
 def exchanged(sums, axis):
     count = lax.axis_size(axis)
     if count == 4:
-        return [sums] + [swap(sums, axis, lambda i, by=by: i ^ by) for by in (1, 2, 3)]
+        return [sums] + [swap(sums, axis, lambda i, by=by: i ^ by) for by in (2, 1, 3)]
     distance = 1
     while distance < count:
         more = swap(sums, axis, lambda i, by=distance: i ^ by)

time: 38.5 us -> 39.2 us (1.018)
  waiting for transfers between devices: 5.93 us -> 6.62 us
    ppermute x12, waiting for transfers between devices: 5.93 us -> 6.62 us  [swap(): lax.ppermute(array, axis, [(i, partner(i)) for i in range(lax.axis_size(a...]
  transfers between devices with their start and end apart: 12 -> 12, of which waited for: 5 -> 5; matrix products, arithmetic and copies ran while one was open for 0% -> 0% of each run, Pallas kernels for 19% -> 18%
where the time goes in v21:
time: 39.2 us; the launch traced here: 39 us
  Pallas kernels  15.5 us (40%)
  starting transfers between devices  13.9 us (35%)
  waiting for transfers between devices  6.62 us (17%)
  between operations  2.04 us (5%)
  local copies, waits for them, and re-layouts  0.94 us (2%)
    pallas_call x8, Pallas kernels, call(): pl.pallas_call(body, out_shape=outs, in_specs=[SMEM_SPEC] * len(scalars)...  15.5 us
    ppermute x12, starting transfers between devices, swap(): lax.ppermute(array, axis, [(i, partner(i)) for i in range(lax.axis_size(a...  13.9 us
    ppermute x12, waiting for transfers between devices, swap(): lax.ppermute(array, axis, [(i, partner(i)) for i in range(lax.axis_size(a...  6.62 us
    unnamed x4, local copies, waits for them, and re-layouts  0.94 us
  transfers between devices with their start and end apart: 12, of which 5 were waited for; matrix products, arithmetic and copies ran while one was open for 0% of the time, Pallas kernels for 18%

profile of v21, /device:TPU:0, one launch (start us, length us, event | category | flops | bytes accessed | tf_op | source)
XLA Modules:
  0.0 39.0 jit_solution(4402008287573453516)
XLA Ops:
  0.6 0.0 copy-start
  0.6 1.9 %shard_map.166 = (f32[40,512]{1,0:T(8,128)}, f32[112,512]{1,0:T(8,128)}) custom-call(f32[3,1,512]{2,1,0:T(1,128)} %bitcast.12, f32[3,1,512]{2,1,0:T(1,128)} %bitcast.13, s32[512]{0:T(512)} %refs_2_.1, s32[8,512]{1,0:T(8,128)} %refs_3_.1, s32[512]{0:T(512)} %refs_4_.1, f32[2,64]{1,0:T(2,128)} %refs_5_.1, f32[64]{0:T(128)} %refs_6_.1, f32[2,8,64]{2,1,0:T(8,128)} %refs_7_.1, ...), custom_call_target="tpu_custom_call" | custom-call | bytes 262144 | tf_op jit(solution)/shard_map/pallas_call | solution.py:728
  2.5 0.5 %collective-permute-start = (f32[40,512]{1,0:T(8,128)}, f32[40,512]{1,0:T(8,128)S(1)}, u32[]{:S(2)}, u32[]{:S(2)}) collective-permute-start(f32[40,512]{1,0:T(8,128)} %get-tuple-element.29), channel_id=1, source_target_pairs={{0,4},{4,0},{8,12},{12,8},{1,5},{5,1},{9,13},{13,9},{2,6},{6,2},{1... | collective-permute-start | bytes 245768 | tf_op jit(solution)/shard_map/ppermute | solution.py:740
  3.0 2.6 %collective-permute-start.1 = (f32[40,512]{1,0:T(8,128)}, f32[40,512]{1,0:T(8,128)S(1)}, u32[]{:S(2)}, u32[]{:S(2)}) collective-permute-start(f32[40,512]{1,0:T(8,128)} %get-tuple-element.29), channel_id=1, source_target_pairs={{0,12},{4,8},{8,4},{12,0},{1,13},{5,9},{9,5},{13,1},{2,14},{6,10},... | collective-permute-start | bytes 245768 | tf_op jit(solution)/shard_map/ppermute | solution.py:740
  5.7 0.0 copy-start.1
  5.7 0.9 %copy-done.1 = f32[112,512]{1,0:T(8,128)S(1)} copy-done((f32[112,512]{1,0:T(8,128)S(1)}, f32[112,512]{1,0:T(8,128)}, u32[]{:S(2)}) %copy-start.1) | copy-done | bytes 229400
  6.6 1.2 %shard_map.167 = (bf16[4,384,1024]{2,1,0:T(8,128)(2,1)S(1)}, bf16[64,48]{1,0:T(8,128)(2,1)S(1)}, bf16[64,192]{1,0:T(8,128)(2,1)S(1)}, bf16[64,32]{1,0:T(8,128)(2...) custom-call(f32[112,512]{1,0:T(8,128)S(1)} %copy-done.1), custom_call_target="tpu_custom_call" | custom-call | flops 100000000 | bytes 262144 | tf_op jit(solution)/shard_map/pallas_call | solution.py:728
  7.8 1.6 %collective-permute-start.2 = (f32[3,1,512]{2,1,0:T(1,128)S(1)}, f32[3,1,512]{2,1,0:T(1,128)S(1)}, u32[]{:S(2)}, u32[]{:S(2)}) collective-permute-start(f32[3,1,512]{2,1,0:T(1,128)S(1)} %get-tuple-element.42), channel_id=1, source_target_pairs={{0,1},{1,2},{2,3},{3,0},{4,5},{5,6},{6,7},{7,4},{8,9},{9,10},{10,1... | collective-permute-start | bytes 18440 | tf_op jit(solution)/shard_map/ppermute | solution.py:740
  9.4 2.2 %collective-permute-start.3 = (f32[3,1,512]{2,1,0:T(1,128)S(1)}, f32[3,1,512]{2,1,0:T(1,128)S(1)}, u32[]{:S(2)}, u32[]{:S(2)}) collective-permute-start(f32[3,1,512]{2,1,0:T(1,128)S(1)} %get-tuple-element.42), channel_id=1, source_target_pairs={{0,3},{1,0},{2,1},{3,2},{4,7},{5,4},{6,5},{7,6},{8,11},{9,8},{10,9... | collective-permute-start | bytes 18440 | tf_op jit(solution)/shard_map/ppermute | solution.py:740
  11.7 0.0 collective-permute-done.sibling_ref
  11.7 0.0 collective-permute-done.1.across_ref
  11.7 5.4 %shard_map.168 = (f32[3,512]{1,0:T(4,128)S(1)}, f32[40,512]{1,0:T(8,128)S(1)}, f32[40,512]{1,0:T(8,128)S(1)}, bf16[768,1024]{1,0:T(8,128)(2,1)S(1)}) custom-call(f32[40,512]{1,0:T(8,128)S(1)} %collective-permute-done.sibling_ref, f32[40,512]{1,0:T(8,128)S(1)} %get-tuple-element.31.po_ref, f32[40,512]{1,0:T(8,128)S(1)} %collective-permute-done.1.across_ref, ...), custom_call_target="tpu_custom_call" | custom-call | flops 1000000000 | bytes 262144 | tf_op jit(solution)/shard_map/pallas_call | solution.py:728
  17.1 0.0 collective-permute-done.2.before_ref.refs_3_
  17.1 0.0 collective-permute-done.3.after_ref.refs_4_
  17.1 0.1 shard_map.169
  17.2 0.0 collective-permute-start.4
  17.2 0.5 %collective-permute-start.5 = (f32[8,512]{1,0:T(8,128)S(1)}, f32[8,512]{1,0:T(8,128)S(1)}, u32[]{:S(2)}, u32[]{:S(2)}) collective-permute-start(f32[8,512]{1,0:T(8,128)S(1)} %get-tuple-element.43.own_ref), channel_id=1, source_target_pairs={{0,12},{4,8},{8,4},{12,0},{1,13},{5,9},{9,5},{13,1},{2,14},{6,10},... | collective-permute-start | bytes 49160 | tf_op jit(solution)/shard_map/ppermute | solution.py:740
  17.7 1.6 %collective-permute-start.6 = (f32[8,128]{1,0:T(8,128)S(1)}, f32[8,128]{1,0:T(8,128)S(1)}, u32[]{:S(2)}, u32[]{:S(2)}) collective-permute-start(f32[8,128]{1,0:T(8,128)S(1)} %get-tuple-element.44.rest_0_), channel_id=1, source_target_pairs={{0,8},{4,12},{8,0},{12,4},{1,9},{5,13},{9,1},{13,5},{2,10},{6,14},... | collective-permute-start | bytes 12296 | tf_op jit(solution)/shard_map/ppermute | solution.py:740
  20.7 0.0 copy-done
  20.7 0.5 %shard_map.165.number_ref = f32[8,128]{1,0:T(8,128)S(1)} custom-call(f32[1]{0:T(128)S(6)} %copy.19.dt_ref, s32[1,2]{1,0:T(1,128)S(1)} %bitcast.10, s32[1]{0:T(128)S(6)} %copy.20.climb_ref), custom_call_target="tpu_custom_call" | custom-call | bytes 262144 | tf_op jit(solution)/shard_map/pallas_call | solution.py:728
  21.2 0.1 collective-permute-done.6.rest_1_
  21.3 0.0 collective-permute-done.4.near_ref
  21.3 0.0 collective-permute-done.5.far_ref
  21.3 5.4 %shard_map.170 = (f32[1,40,128]{2,1,0:T(8,128)S(1)}, f32[3,128]{1,0:T(4,128)S(1)}) custom-call(f32[8,128]{1,0:T(8,128)S(1)} %shard_map.165.number_ref, f32[40,512]{1,0:T(8,128)S(1)} %get-tuple-element.39.pl_ref, f32[40,512]{1,0:T(8,128)S(1)} %get-tuple-element.31.po_ref, f32[40,512]{1,0:T(8,128)S(1)} %get-tuple-element.40.pr_ref, ...), custom_call_target="tpu_custom_call" | custom-call | flops 1000000000 | bytes 262144 | tf_op jit(solution)/shard_map/pallas_call | solution.py:728
  26.7 0.1 collective-permute-start.7
  26.8 2.5 %collective-permute-start.8 = (f32[1,40,128]{2,1,0:T(8,128)S(1)}, f32[1,40,128]{2,1,0:T(8,128)S(1)}, u32[]{:S(2)}, u32[]{:S(2)}) collective-permute-start(f32[1,40,128]{2,1,0:T(8,128)S(1)} %get-tuple-element.46.refs_0_.own_ref), channel_id=1, source_target_pairs={{0,2},{1,3},{2,1},{3,0},{4,6},{5,7},{6,5},{7,4},{8,10},{9,11},{10,... | collective-permute-start | bytes 61448 | tf_op jit(solution)/shard_map/ppermute | solution.py:740
  29.3 3.1 %collective-permute-done.7.refs_1_ = f32[1,40,128]{2,1,0:T(8,128)S(1)} collective-permute-done((f32[1,40,128]{2,1,0:T(8,128)S(1)}, f32[1,40,128]{2,1,0:T(8,128)S(1)}, u32[]{:S(2)}, u32[]{:S(2)}) %collective-permute-start.7) | collective-permute-done | bytes 20512 | tf_op jit(solution)/shard_map/ppermute | solution.py:740
  32.4 0.2 collective-permute-done.8.refs_2_
  32.6 0.2 shard_map.171
  32.8 0.1 collective-permute-start.10
  32.9 1.8 %collective-permute-start.11 = (f32[8,128]{1,0:T(8,128)S(1)}, f32[8,128]{1,0:T(8,128)S(1)}, u32[]{:S(2)}, u32[]{:S(2)}) collective-permute-start(f32[8,128]{1,0:T(8,128)S(1)} %get-tuple-element.49.rest_0_), channel_id=1, source_target_pairs={{0,12},{4,8},{8,4},{12,0},{1,13},{5,9},{9,5},{13,1},{2,14},{6,10},... | collective-permute-start | bytes 12296 | tf_op jit(solution)/shard_map/ppermute | solution.py:740
  34.7 0.4 collective-permute-start.9
  35.0 0.0 collective-permute-done.10.rest_2_
  35.0 1.0 %collective-permute-done.11.rest_3_ = f32[8,128]{1,0:T(8,128)S(1)} collective-permute-done((f32[8,128]{1,0:T(8,128)S(1)}, f32[8,128]{1,0:T(8,128)S(1)}, u32[]{:S(2)}, u32[]{:S(2)}) %collective-permute-start.11) | collective-permute-done | bytes 4128 | tf_op jit(solution)/shard_map/ppermute | solution.py:740
  36.0 2.3 %collective-permute-done.9.rest_1_ = f32[8,128]{1,0:T(8,128)S(1)} collective-permute-done((f32[8,128]{1,0:T(8,128)S(1)}, f32[8,128]{1,0:T(8,128)S(1)}, u32[]{:S(2)}, u32[]{:S(2)}) %collective-permute-start.9) | collective-permute-done | bytes 4128 | tf_op jit(solution)/shard_map/ppermute | solution.py:740
  38.3 0.7 %shard_map.172 = (f32[3,1,512]{2,1,0:T(1,128)}, f32[3,1,512]{2,1,0:T(1,128)}, f32[2,1,2]{2,1,0:T(1,128)}, f32[1,1]{1,0:T(1,128)}) custom-call(f32[1,40,128]{2,1,0:T(8,128)S(1)} %get-tuple-element.46.refs_0_.own_ref, f32[3,128]{1,0:T(4,128)S(1)} %get-tuple-element.47.record_ref, f32[40,128]{1,0:T(8,128)S(1)} %get-tuple-element.48.state_ref, ...), custom_call_target="tpu_custom_call" | custom-call | bytes 262144 | tf_op jit(solution)/shard_map/pallas_call | solution.py:728
Async XLA Ops:
  0.6 20.0 %copy-start = (s32[2,1]{0,1:T(1,128)S(1)}, s32[2,1]{0,1:T(1,128)}, u32[]{:S(2)}) copy-start(s32[2,1]{0,1:T(1,128)} %param.17) | copy-start | bytes 28
  2.5 9.1 %collective-permute-start = (f32[40,512]{1,0:T(8,128)}, f32[40,512]{1,0:T(8,128)S(1)}, u32[]{:S(2)}, u32[]{:S(2)}) collective-permute-start(f32[40,512]{1,0:T(8,128)} %get-tuple-element.29), channel_id=1, source_target_pairs={{0,4},{4,0},{8,12},{12,8},{1,5},{5,1},{9,13},{13,9},{2,6},{6,2},{1... | collective-permute-start | bytes 245768 | tf_op jit(solution)/shard_map/ppermute | solution.py:740
  3.0 8.6 %collective-permute-start.1 = (f32[40,512]{1,0:T(8,128)}, f32[40,512]{1,0:T(8,128)S(1)}, u32[]{:S(2)}, u32[]{:S(2)}) collective-permute-start(f32[40,512]{1,0:T(8,128)} %get-tuple-element.29), channel_id=1, source_target_pairs={{0,12},{4,8},{8,4},{12,0},{1,13},{5,9},{9,5},{13,1},{2,14},{6,10},... | collective-permute-start | bytes 245768 | tf_op jit(solution)/shard_map/ppermute | solution.py:740
  5.7 0.9 %copy-start.1 = (f32[112,512]{1,0:T(8,128)S(1)}, f32[112,512]{1,0:T(8,128)}, u32[]{:S(2)}) copy-start(f32[112,512]{1,0:T(8,128)} %get-tuple-element.30.po_ref) | copy-start | bytes 688132
  7.8 9.3 %collective-permute-start.2 = (f32[3,1,512]{2,1,0:T(1,128)S(1)}, f32[3,1,512]{2,1,0:T(1,128)S(1)}, u32[]{:S(2)}, u32[]{:S(2)}) collective-permute-start(f32[3,1,512]{2,1,0:T(1,128)S(1)} %get-tuple-element.42), channel_id=1, source_target_pairs={{0,1},{1,2},{2,3},{3,0},{4,5},{5,6},{6,7},{7,4},{8,9},{9,10},{10,1... | collective-permute-start | bytes 18440 | tf_op jit(solution)/shard_map/ppermute | solution.py:740
  9.4 7.6 %collective-permute-start.3 = (f32[3,1,512]{2,1,0:T(1,128)S(1)}, f32[3,1,512]{2,1,0:T(1,128)S(1)}, u32[]{:S(2)}, u32[]{:S(2)}) collective-permute-start(f32[3,1,512]{2,1,0:T(1,128)S(1)} %get-tuple-element.42), channel_id=1, source_target_pairs={{0,3},{1,0},{2,1},{3,2},{4,7},{5,4},{6,5},{7,6},{8,11},{9,8},{10,9... | collective-permute-start | bytes 18440 | tf_op jit(solution)/shard_map/ppermute | solution.py:740
  17.2 4.1 %collective-permute-start.4 = (f32[8,512]{1,0:T(8,128)S(1)}, f32[8,512]{1,0:T(8,128)S(1)}, u32[]{:S(2)}, u32[]{:S(2)}) collective-permute-start(f32[8,512]{1,0:T(8,128)S(1)} %get-tuple-element.43.own_ref), channel_id=1, source_target_pairs={{0,4},{4,0},{8,12},{12,8},{1,5},{5,1},{9,13},{13,9},{2,6},{6,2},{1... | collective-permute-start | bytes 49160 | tf_op jit(solution)/shard_map/ppermute | solution.py:740
  17.2 4.1 %collective-permute-start.5 = (f32[8,512]{1,0:T(8,128)S(1)}, f32[8,512]{1,0:T(8,128)S(1)}, u32[]{:S(2)}, u32[]{:S(2)}) collective-permute-start(f32[8,512]{1,0:T(8,128)S(1)} %get-tuple-element.43.own_ref), channel_id=1, source_target_pairs={{0,12},{4,8},{8,4},{12,0},{1,13},{5,9},{9,5},{13,1},{2,14},{6,10},... | collective-permute-start | bytes 49160 | tf_op jit(solution)/shard_map/ppermute | solution.py:740
  17.7 3.6 %collective-permute-start.6 = (f32[8,128]{1,0:T(8,128)S(1)}, f32[8,128]{1,0:T(8,128)S(1)}, u32[]{:S(2)}, u32[]{:S(2)}) collective-permute-start(f32[8,128]{1,0:T(8,128)S(1)} %get-tuple-element.44.rest_0_), channel_id=1, source_target_pairs={{0,8},{4,12},{8,0},{12,4},{1,9},{5,13},{9,1},{13,5},{2,10},{6,14},... | collective-permute-start | bytes 12296 | tf_op jit(solution)/shard_map/ppermute | solution.py:740
  26.7 5.6 %collective-permute-start.7 = (f32[1,40,128]{2,1,0:T(8,128)S(1)}, f32[1,40,128]{2,1,0:T(8,128)S(1)}, u32[]{:S(2)}, u32[]{:S(2)}) collective-permute-start(f32[1,40,128]{2,1,0:T(8,128)S(1)} %get-tuple-element.46.refs_0_.own_ref), channel_id=1, source_target_pairs={{0,1},{1,2},{2,3},{3,0},{4,5},{5,6},{6,7},{7,4},{8,9},{9,10},{10,1... | collective-permute-start | bytes 61448 | tf_op jit(solution)/shard_map/ppermute | solution.py:740
  26.8 5.8 %collective-permute-start.8 = (f32[1,40,128]{2,1,0:T(8,128)S(1)}, f32[1,40,128]{2,1,0:T(8,128)S(1)}, u32[]{:S(2)}, u32[]{:S(2)}) collective-permute-start(f32[1,40,128]{2,1,0:T(8,128)S(1)} %get-tuple-element.46.refs_0_.own_ref), channel_id=1, source_target_pairs={{0,2},{1,3},{2,1},{3,0},{4,6},{5,7},{6,5},{7,4},{8,10},{9,11},{10,... | collective-permute-start | bytes 61448 | tf_op jit(solution)/shard_map/ppermute | solution.py:740
  32.8 2.2 %collective-permute-start.10 = (f32[8,128]{1,0:T(8,128)S(1)}, f32[8,128]{1,0:T(8,128)S(1)}, u32[]{:S(2)}, u32[]{:S(2)}) collective-permute-start(f32[8,128]{1,0:T(8,128)S(1)} %get-tuple-element.49.rest_0_), channel_id=1, source_target_pairs={{0,4},{4,0},{8,12},{12,8},{1,5},{5,1},{9,13},{13,9},{2,6},{6,2},{1... | collective-permute-start | bytes 12296 | tf_op jit(solution)/shard_map/ppermute | solution.py:740
  32.9 3.1 %collective-permute-start.11 = (f32[8,128]{1,0:T(8,128)S(1)}, f32[8,128]{1,0:T(8,128)S(1)}, u32[]{:S(2)}, u32[]{:S(2)}) collective-permute-start(f32[8,128]{1,0:T(8,128)S(1)} %get-tuple-element.49.rest_0_), channel_id=1, source_target_pairs={{0,12},{4,8},{8,4},{12,0},{1,13},{5,9},{9,5},{13,1},{2,14},{6,10},... | collective-permute-start | bytes 12296 | tf_op jit(solution)/shard_map/ppermute | solution.py:740
  34.7 3.6 %collective-permute-start.9 = (f32[8,128]{1,0:T(8,128)S(1)}, f32[8,128]{1,0:T(8,128)S(1)}, u32[]{:S(2)}, u32[]{:S(2)}) collective-permute-start(f32[8,128]{1,0:T(8,128)S(1)} %get-tuple-element.49.rest_0_), channel_id=1, source_target_pairs={{0,8},{4,12},{8,0},{12,4},{1,9},{5,13},{9,1},{13,5},{2,10},{6,14},... | collective-permute-start | bytes 12296 | tf_op jit(solution)/shard_map/ppermute | solution.py:740

commit v22 on v21

--- a/solution.py
+++ b/solution.py
@@ -743,7 +743,7 @@
 def exchanged(sums, axis):
     count = lax.axis_size(axis)
     if count == 4:
-        return [sums] + [swap(sums, axis, lambda i, by=by: i ^ by) for by in (2, 1, 3)]
+        return [sums] + [swap(sums, axis, lambda i, by=by: i ^ by) for by in (1, 3, 2)]
     distance = 1
     while distance < count:
         more = swap(sums, axis, lambda i, by=distance: i ^ by)

time: 39.2 us -> 37.6 us (0.959)
  waiting for transfers between devices: 6.62 us -> 5.2 us
    ppermute x12, waiting for transfers between devices: 6.62 us -> 5.2 us  [swap(): lax.ppermute(array, axis, [(i, partner(i)) for i in range(lax.axis_size(a...]
  transfers between devices with their start and end apart: 12 -> 12, of which waited for: 5 -> 5; matrix products, arithmetic and copies ran while one was open for 0% -> 0% of each run, Pallas kernels for 18% -> 19%
where the time goes in v22:
time: 37.6 us; the launch traced here: 37.3 us
  Pallas kernels  15.5 us (41%)
  starting transfers between devices  13.6 us (36%)
  waiting for transfers between devices  5.2 us (14%)
  between operations  2.04 us (5%)
  local copies, waits for them, and re-layouts  0.94 us (2%)
    pallas_call x8, Pallas kernels, call(): pl.pallas_call(body, out_shape=outs, in_specs=[SMEM_SPEC] * len(scalars)...  15.5 us
    ppermute x12, starting transfers between devices, swap(): lax.ppermute(array, axis, [(i, partner(i)) for i in range(lax.axis_size(a...  13.6 us
    ppermute x12, waiting for transfers between devices, swap(): lax.ppermute(array, axis, [(i, partner(i)) for i in range(lax.axis_size(a...  5.2 us
    unnamed x4, local copies, waits for them, and re-layouts  0.94 us
  transfers between devices with their start and end apart: 12, of which 5 were waited for; matrix products, arithmetic and copies ran while one was open for 0% of the time, Pallas kernels for 19%

profile of v22, /device:TPU:0, one launch (start us, length us, event | category | flops | bytes accessed | tf_op | source)
XLA Modules:
  0.0 37.3 jit_solution(3197706728276146983)
XLA Ops:
  0.6 0.0 copy-start
  0.6 1.9 %shard_map.166 = (f32[40,512]{1,0:T(8,128)}, f32[112,512]{1,0:T(8,128)}) custom-call(f32[3,1,512]{2,1,0:T(1,128)} %bitcast.12, f32[3,1,512]{2,1,0:T(1,128)} %bitcast.13, s32[512]{0:T(512)} %refs_2_.1, s32[8,512]{1,0:T(8,128)} %refs_3_.1, s32[512]{0:T(512)} %refs_4_.1, f32[2,64]{1,0:T(2,128)} %refs_5_.1, f32[64]{0:T(128)} %refs_6_.1, f32[2,8,64]{2,1,0:T(8,128)} %refs_7_.1, ...), custom_call_target="tpu_custom_call" | custom-call | bytes 262144 | tf_op jit(solution)/shard_map/pallas_call | solution.py:728
  2.5 0.5 %collective-permute-start = (f32[40,512]{1,0:T(8,128)}, f32[40,512]{1,0:T(8,128)S(1)}, u32[]{:S(2)}, u32[]{:S(2)}) collective-permute-start(f32[40,512]{1,0:T(8,128)} %get-tuple-element.29), channel_id=1, source_target_pairs={{0,4},{4,0},{8,12},{12,8},{1,5},{5,1},{9,13},{13,9},{2,6},{6,2},{1... | collective-permute-start | bytes 245768 | tf_op jit(solution)/shard_map/ppermute | solution.py:740
  3.0 2.6 %collective-permute-start.1 = (f32[40,512]{1,0:T(8,128)}, f32[40,512]{1,0:T(8,128)S(1)}, u32[]{:S(2)}, u32[]{:S(2)}) collective-permute-start(f32[40,512]{1,0:T(8,128)} %get-tuple-element.29), channel_id=1, source_target_pairs={{0,12},{4,8},{8,4},{12,0},{1,13},{5,9},{9,5},{13,1},{2,14},{6,10},... | collective-permute-start | bytes 245768 | tf_op jit(solution)/shard_map/ppermute | solution.py:740
  5.7 0.0 copy-start.1
  5.7 0.9 %copy-done.1 = f32[112,512]{1,0:T(8,128)S(1)} copy-done((f32[112,512]{1,0:T(8,128)S(1)}, f32[112,512]{1,0:T(8,128)}, u32[]{:S(2)}) %copy-start.1) | copy-done | bytes 229400
  6.6 1.2 %shard_map.167 = (bf16[4,384,1024]{2,1,0:T(8,128)(2,1)S(1)}, bf16[64,48]{1,0:T(8,128)(2,1)S(1)}, bf16[64,192]{1,0:T(8,128)(2,1)S(1)}, bf16[64,32]{1,0:T(8,128)(2...) custom-call(f32[112,512]{1,0:T(8,128)S(1)} %copy-done.1), custom_call_target="tpu_custom_call" | custom-call | flops 100000000 | bytes 262144 | tf_op jit(solution)/shard_map/pallas_call | solution.py:728
  7.8 1.6 %collective-permute-start.2 = (f32[3,1,512]{2,1,0:T(1,128)S(1)}, f32[3,1,512]{2,1,0:T(1,128)S(1)}, u32[]{:S(2)}, u32[]{:S(2)}) collective-permute-start(f32[3,1,512]{2,1,0:T(1,128)S(1)} %get-tuple-element.42), channel_id=1, source_target_pairs={{0,1},{1,2},{2,3},{3,0},{4,5},{5,6},{6,7},{7,4},{8,9},{9,10},{10,1... | collective-permute-start | bytes 18440 | tf_op jit(solution)/shard_map/ppermute | solution.py:740
  9.4 2.2 %collective-permute-start.3 = (f32[3,1,512]{2,1,0:T(1,128)S(1)}, f32[3,1,512]{2,1,0:T(1,128)S(1)}, u32[]{:S(2)}, u32[]{:S(2)}) collective-permute-start(f32[3,1,512]{2,1,0:T(1,128)S(1)} %get-tuple-element.42), channel_id=1, source_target_pairs={{0,3},{1,0},{2,1},{3,2},{4,7},{5,4},{6,5},{7,6},{8,11},{9,8},{10,9... | collective-permute-start | bytes 18440 | tf_op jit(solution)/shard_map/ppermute | solution.py:740
  11.7 0.0 collective-permute-done.sibling_ref
  11.7 0.0 collective-permute-done.1.across_ref
  11.7 5.4 %shard_map.168 = (f32[3,512]{1,0:T(4,128)S(1)}, f32[40,512]{1,0:T(8,128)S(1)}, f32[40,512]{1,0:T(8,128)S(1)}, bf16[768,1024]{1,0:T(8,128)(2,1)S(1)}) custom-call(f32[40,512]{1,0:T(8,128)S(1)} %collective-permute-done.sibling_ref, f32[40,512]{1,0:T(8,128)S(1)} %get-tuple-element.31.po_ref, f32[40,512]{1,0:T(8,128)S(1)} %collective-permute-done.1.across_ref, ...), custom_call_target="tpu_custom_call" | custom-call | flops 1000000000 | bytes 262144 | tf_op jit(solution)/shard_map/pallas_call | solution.py:728
  17.1 0.0 collective-permute-done.2.before_ref.refs_3_
  17.1 0.0 collective-permute-done.3.after_ref.refs_4_
  17.1 0.1 shard_map.169
  17.2 0.0 collective-permute-start.4
  17.2 0.5 %collective-permute-start.5 = (f32[8,512]{1,0:T(8,128)S(1)}, f32[8,512]{1,0:T(8,128)S(1)}, u32[]{:S(2)}, u32[]{:S(2)}) collective-permute-start(f32[8,512]{1,0:T(8,128)S(1)} %get-tuple-element.43.own_ref), channel_id=1, source_target_pairs={{0,12},{4,8},{8,4},{12,0},{1,13},{5,9},{9,5},{13,1},{2,14},{6,10},... | collective-permute-start | bytes 49160 | tf_op jit(solution)/shard_map/ppermute | solution.py:740
  17.7 1.6 %collective-permute-start.6 = (f32[8,128]{1,0:T(8,128)S(1)}, f32[8,128]{1,0:T(8,128)S(1)}, u32[]{:S(2)}, u32[]{:S(2)}) collective-permute-start(f32[8,128]{1,0:T(8,128)S(1)} %get-tuple-element.44.rest_0_), channel_id=1, source_target_pairs={{0,8},{4,12},{8,0},{12,4},{1,9},{5,13},{9,1},{13,5},{2,10},{6,14},... | collective-permute-start | bytes 12296 | tf_op jit(solution)/shard_map/ppermute | solution.py:740
  20.7 0.0 copy-done
  20.7 0.5 %shard_map.165.number_ref = f32[8,128]{1,0:T(8,128)S(1)} custom-call(f32[1]{0:T(128)S(6)} %copy.19.dt_ref, s32[1,2]{1,0:T(1,128)S(1)} %bitcast.10, s32[1]{0:T(128)S(6)} %copy.20.climb_ref), custom_call_target="tpu_custom_call" | custom-call | bytes 262144 | tf_op jit(solution)/shard_map/pallas_call | solution.py:728
  21.2 0.1 collective-permute-done.6.rest_1_
  21.3 0.0 collective-permute-done.4.near_ref
  21.3 0.0 collective-permute-done.5.far_ref
  21.3 5.4 %shard_map.170 = (f32[1,40,128]{2,1,0:T(8,128)S(1)}, f32[3,128]{1,0:T(4,128)S(1)}) custom-call(f32[8,128]{1,0:T(8,128)S(1)} %shard_map.165.number_ref, f32[40,512]{1,0:T(8,128)S(1)} %get-tuple-element.39.pl_ref, f32[40,512]{1,0:T(8,128)S(1)} %get-tuple-element.31.po_ref, f32[40,512]{1,0:T(8,128)S(1)} %get-tuple-element.40.pr_ref, ...), custom_call_target="tpu_custom_call" | custom-call | flops 1000000000 | bytes 262144 | tf_op jit(solution)/shard_map/pallas_call | solution.py:728
  26.7 0.1 collective-permute-start.7
  26.8 2.5 %collective-permute-start.8 = (f32[1,40,128]{2,1,0:T(8,128)S(1)}, f32[1,40,128]{2,1,0:T(8,128)S(1)}, u32[]{:S(2)}, u32[]{:S(2)}) collective-permute-start(f32[1,40,128]{2,1,0:T(8,128)S(1)} %get-tuple-element.46.refs_0_.own_ref), channel_id=1, source_target_pairs={{0,2},{1,3},{2,1},{3,0},{4,6},{5,7},{6,5},{7,4},{8,10},{9,11},{10,... | collective-permute-start | bytes 61448 | tf_op jit(solution)/shard_map/ppermute | solution.py:740
  29.3 3.1 %collective-permute-done.7.refs_1_ = f32[1,40,128]{2,1,0:T(8,128)S(1)} collective-permute-done((f32[1,40,128]{2,1,0:T(8,128)S(1)}, f32[1,40,128]{2,1,0:T(8,128)S(1)}, u32[]{:S(2)}, u32[]{:S(2)}) %collective-permute-start.7) | collective-permute-done | bytes 20512 | tf_op jit(solution)/shard_map/ppermute | solution.py:740
  32.4 0.2 collective-permute-done.8.refs_2_
  32.6 0.2 shard_map.171
  32.8 0.1 collective-permute-start.10
  32.9 1.7 %collective-permute-start.11 = (f32[8,128]{1,0:T(8,128)S(1)}, f32[8,128]{1,0:T(8,128)S(1)}, u32[]{:S(2)}, u32[]{:S(2)}) collective-permute-start(f32[8,128]{1,0:T(8,128)S(1)} %get-tuple-element.49.rest_0_), channel_id=1, source_target_pairs={{0,8},{4,12},{8,0},{12,4},{1,9},{5,13},{9,1},{13,5},{2,10},{6,14},... | collective-permute-start | bytes 12296 | tf_op jit(solution)/shard_map/ppermute | solution.py:740
  34.6 0.1 collective-permute-start.9
  34.8 1.2 %collective-permute-done.10.rest_2_ = f32[8,128]{1,0:T(8,128)S(1)} collective-permute-done((f32[8,128]{1,0:T(8,128)S(1)}, f32[8,128]{1,0:T(8,128)S(1)}, u32[]{:S(2)}, u32[]{:S(2)}) %collective-permute-start.10) | collective-permute-done | bytes 4128 | tf_op jit(solution)/shard_map/ppermute | solution.py:740
  35.9 0.7 %collective-permute-done.11.rest_3_ = f32[8,128]{1,0:T(8,128)S(1)} collective-permute-done((f32[8,128]{1,0:T(8,128)S(1)}, f32[8,128]{1,0:T(8,128)S(1)}, u32[]{:S(2)}, u32[]{:S(2)}) %collective-permute-start.11) | collective-permute-done | bytes 4128 | tf_op jit(solution)/shard_map/ppermute | solution.py:740
  36.6 0.0 collective-permute-done.9.rest_1_
  36.6 0.7 %shard_map.172 = (f32[3,1,512]{2,1,0:T(1,128)}, f32[3,1,512]{2,1,0:T(1,128)}, f32[2,1,2]{2,1,0:T(1,128)}, f32[1,1]{1,0:T(1,128)}) custom-call(f32[1,40,128]{2,1,0:T(8,128)S(1)} %get-tuple-element.46.refs_0_.own_ref, f32[3,128]{1,0:T(4,128)S(1)} %get-tuple-element.47.record_ref, f32[40,128]{1,0:T(8,128)S(1)} %get-tuple-element.48.state_ref, ...), custom_call_target="tpu_custom_call" | custom-call | bytes 262144 | tf_op jit(solution)/shard_map/pallas_call | solution.py:728
Async XLA Ops:
  0.6 20.0 %copy-start = (s32[2,1]{0,1:T(1,128)S(1)}, s32[2,1]{0,1:T(1,128)}, u32[]{:S(2)}) copy-start(s32[2,1]{0,1:T(1,128)} %param.17) | copy-start | bytes 28
  2.5 9.1 %collective-permute-start = (f32[40,512]{1,0:T(8,128)}, f32[40,512]{1,0:T(8,128)S(1)}, u32[]{:S(2)}, u32[]{:S(2)}) collective-permute-start(f32[40,512]{1,0:T(8,128)} %get-tuple-element.29), channel_id=1, source_target_pairs={{0,4},{4,0},{8,12},{12,8},{1,5},{5,1},{9,13},{13,9},{2,6},{6,2},{1... | collective-permute-start | bytes 245768 | tf_op jit(solution)/shard_map/ppermute | solution.py:740
  3.0 8.6 %collective-permute-start.1 = (f32[40,512]{1,0:T(8,128)}, f32[40,512]{1,0:T(8,128)S(1)}, u32[]{:S(2)}, u32[]{:S(2)}) collective-permute-start(f32[40,512]{1,0:T(8,128)} %get-tuple-element.29), channel_id=1, source_target_pairs={{0,12},{4,8},{8,4},{12,0},{1,13},{5,9},{9,5},{13,1},{2,14},{6,10},... | collective-permute-start | bytes 245768 | tf_op jit(solution)/shard_map/ppermute | solution.py:740
  5.7 0.9 %copy-start.1 = (f32[112,512]{1,0:T(8,128)S(1)}, f32[112,512]{1,0:T(8,128)}, u32[]{:S(2)}) copy-start(f32[112,512]{1,0:T(8,128)} %get-tuple-element.30.po_ref) | copy-start | bytes 688132
  7.8 9.3 %collective-permute-start.2 = (f32[3,1,512]{2,1,0:T(1,128)S(1)}, f32[3,1,512]{2,1,0:T(1,128)S(1)}, u32[]{:S(2)}, u32[]{:S(2)}) collective-permute-start(f32[3,1,512]{2,1,0:T(1,128)S(1)} %get-tuple-element.42), channel_id=1, source_target_pairs={{0,1},{1,2},{2,3},{3,0},{4,5},{5,6},{6,7},{7,4},{8,9},{9,10},{10,1... | collective-permute-start | bytes 18440 | tf_op jit(solution)/shard_map/ppermute | solution.py:740
  9.4 7.6 %collective-permute-start.3 = (f32[3,1,512]{2,1,0:T(1,128)S(1)}, f32[3,1,512]{2,1,0:T(1,128)S(1)}, u32[]{:S(2)}, u32[]{:S(2)}) collective-permute-start(f32[3,1,512]{2,1,0:T(1,128)S(1)} %get-tuple-element.42), channel_id=1, source_target_pairs={{0,3},{1,0},{2,1},{3,2},{4,7},{5,4},{6,5},{7,6},{8,11},{9,8},{10,9... | collective-permute-start | bytes 18440 | tf_op jit(solution)/shard_map/ppermute | solution.py:740
  17.2 4.1 %collective-permute-start.4 = (f32[8,512]{1,0:T(8,128)S(1)}, f32[8,512]{1,0:T(8,128)S(1)}, u32[]{:S(2)}, u32[]{:S(2)}) collective-permute-start(f32[8,512]{1,0:T(8,128)S(1)} %get-tuple-element.43.own_ref), channel_id=1, source_target_pairs={{0,4},{4,0},{8,12},{12,8},{1,5},{5,1},{9,13},{13,9},{2,6},{6,2},{1... | collective-permute-start | bytes 49160 | tf_op jit(solution)/shard_map/ppermute | solution.py:740
  17.2 4.1 %collective-permute-start.5 = (f32[8,512]{1,0:T(8,128)S(1)}, f32[8,512]{1,0:T(8,128)S(1)}, u32[]{:S(2)}, u32[]{:S(2)}) collective-permute-start(f32[8,512]{1,0:T(8,128)S(1)} %get-tuple-element.43.own_ref), channel_id=1, source_target_pairs={{0,12},{4,8},{8,4},{12,0},{1,13},{5,9},{9,5},{13,1},{2,14},{6,10},... | collective-permute-start | bytes 49160 | tf_op jit(solution)/shard_map/ppermute | solution.py:740
  17.7 3.6 %collective-permute-start.6 = (f32[8,128]{1,0:T(8,128)S(1)}, f32[8,128]{1,0:T(8,128)S(1)}, u32[]{:S(2)}, u32[]{:S(2)}) collective-permute-start(f32[8,128]{1,0:T(8,128)S(1)} %get-tuple-element.44.rest_0_), channel_id=1, source_target_pairs={{0,8},{4,12},{8,0},{12,4},{1,9},{5,13},{9,1},{13,5},{2,10},{6,14},... | collective-permute-start | bytes 12296 | tf_op jit(solution)/shard_map/ppermute | solution.py:740
  26.7 5.6 %collective-permute-start.7 = (f32[1,40,128]{2,1,0:T(8,128)S(1)}, f32[1,40,128]{2,1,0:T(8,128)S(1)}, u32[]{:S(2)}, u32[]{:S(2)}) collective-permute-start(f32[1,40,128]{2,1,0:T(8,128)S(1)} %get-tuple-element.46.refs_0_.own_ref), channel_id=1, source_target_pairs={{0,1},{1,2},{2,3},{3,0},{4,5},{5,6},{6,7},{7,4},{8,9},{9,10},{10,1... | collective-permute-start | bytes 61448 | tf_op jit(solution)/shard_map/ppermute | solution.py:740
  26.8 5.8 %collective-permute-start.8 = (f32[1,40,128]{2,1,0:T(8,128)S(1)}, f32[1,40,128]{2,1,0:T(8,128)S(1)}, u32[]{:S(2)}, u32[]{:S(2)}) collective-permute-start(f32[1,40,128]{2,1,0:T(8,128)S(1)} %get-tuple-element.46.refs_0_.own_ref), channel_id=1, source_target_pairs={{0,2},{1,3},{2,1},{3,0},{4,6},{5,7},{6,5},{7,4},{8,10},{9,11},{10,... | collective-permute-start | bytes 61448 | tf_op jit(solution)/shard_map/ppermute | solution.py:740
  32.8 3.1 %collective-permute-start.10 = (f32[8,128]{1,0:T(8,128)S(1)}, f32[8,128]{1,0:T(8,128)S(1)}, u32[]{:S(2)}, u32[]{:S(2)}) collective-permute-start(f32[8,128]{1,0:T(8,128)S(1)} %get-tuple-element.49.rest_0_), channel_id=1, source_target_pairs={{0,12},{4,8},{8,4},{12,0},{1,13},{5,9},{9,5},{13,1},{2,14},{6,10},... | collective-permute-start | bytes 12296 | tf_op jit(solution)/shard_map/ppermute | solution.py:740
  32.9 3.7 %collective-permute-start.11 = (f32[8,128]{1,0:T(8,128)S(1)}, f32[8,128]{1,0:T(8,128)S(1)}, u32[]{:S(2)}, u32[]{:S(2)}) collective-permute-start(f32[8,128]{1,0:T(8,128)S(1)} %get-tuple-element.49.rest_0_), channel_id=1, source_target_pairs={{0,8},{4,12},{8,0},{12,4},{1,9},{5,13},{9,1},{13,5},{2,10},{6,14},... | collective-permute-start | bytes 12296 | tf_op jit(solution)/shard_map/ppermute | solution.py:740
  34.6 2.0 %collective-permute-start.9 = (f32[8,128]{1,0:T(8,128)S(1)}, f32[8,128]{1,0:T(8,128)S(1)}, u32[]{:S(2)}, u32[]{:S(2)}) collective-permute-start(f32[8,128]{1,0:T(8,128)S(1)} %get-tuple-element.49.rest_0_), channel_id=1, source_target_pairs={{0,4},{4,0},{8,12},{12,8},{1,5},{5,1},{9,13},{13,9},{2,6},{6,2},{1... | collective-permute-start | bytes 12296 | tf_op jit(solution)/shard_map/ppermute | solution.py:740
